TPU v7x, 32 devices: a whole 2x2x4 slice. The times are simulated.
32 devices in a mesh: row: 4 (over x, core), col: 8 (over z, y).
Axes of the slice: x: 2, y: 2, z: 4, core: 2. Of those that a mesh axis runs over, the one named last changes fastest.
Arguments:
- start_columns: bfloat16 [16384, 4096], P('row', 'col'), may hold values from -6 to 6
- hamiltonian: bfloat16 [64, 2, 256, 256], P(('row', 'col')), may hold values from -0.09375 to 0.09375
- band_pattern: int32 [64], P(('row', 'col')), may hold values 0 or 1
- coefficients: float32 [4], replicated, may hold values from -1 to 1
- tile_peer: int32 [512, 1], P(('row', 'col')), may hold values from 0 to 7; in each aligned block of 16 rows (0 to 15, 16 to 31, ...) at most 2 rows name the same one
- tile_block: int32 [512], P(('row', 'col')), may hold values from 0 to 7
- tile_count: int32 [128], P(('row', 'col')), may hold values from 1 to 4
- basis_values: bfloat16 [512, 2, 512, 128], P(('row', 'col')), may hold values from -6 to 6
- core_density: float32 [128, 128], P(('row', 'col')), may hold values from 0.5 to 3
Outputs:
- density: float32 [128, 128], P(('row', 'col'))
- h_update: bfloat16 [16384, 4096], P('row', 'col')
Inputs may be any that keep to these rules, and one draw needn't show every extreme that they name: `tile_peer`: the entries of one device name one col index at most 2 times, and on some device exactly 2 times.
All inputs are finite; a program needn't handle non-finite values. No bound on the sum of `band_pattern` on one device may be relied on, other than what follows from the above.
Results may differ from a plain program's by a relative error of at most 0.0059.
Values may be sent and summed in bfloat16 or wider, within the bound.
No kernel may reach another device: no remote copies, remote signals or barrier semaphores. Data moves between devices by JAX's collectives and lax.ppermute only.
A program may use at most 192 MiB of HBM per device.

v0:
```python
import functools
import math

import jax
import jax.numpy as jnp
from jax import lax
from jax.experimental import pallas as pl
from jax.experimental.pallas import tpu as pltpu
from jax.sharding import PartitionSpec as P

W = 256
KB = 512
DEG = 3
SLOTS = 4
CAP = 2
P_SIZE = 128
MIB = 1 << 20
LISTS = 16

exchange_factor = (3.0 / math.pi) ** (1.0 / 3.0)
HBM = pl.BlockSpec(memory_space=pltpu.HBM)
SMEM = pl.BlockSpec(memory_space=pltpu.SMEM)
VMEM = pl.BlockSpec(memory_space=pltpu.VMEM)


def partner(me, j, count):
    if count & (count - 1) == 0:
        return me ^ abs(j)
    return (me + j) % count


def piece_kernel(peers, named, counts, pattern, ham, piece, blocks, sems):
    rows = ham.shape[0]
    load = pltpu.make_async_copy(ham, blocks.at[pl.ds(0, rows)], sems.at[0])
    load.start()
    lane = lax.broadcasted_iota(jnp.int32, (LISTS, W), 1)
    lists = jnp.zeros((LISTS, W), jnp.int32)
    at = 0
    for ref in (peers, named, counts):
        for i in range(ref.shape[0]):
            lists = jnp.where(lane == at, ref[i], lists)
            at += 1
    blocks[rows:] = lists.astype(jnp.float32).astype(jnp.bfloat16)
    load.wait()
    for i in range(rows // (2 * W)):
        coupling = slice((2 * i + 1) * W, (2 * i + 2) * W)
        blocks[coupling] = blocks[coupling] * pattern[i].astype(jnp.bfloat16)
    store = pltpu.make_async_copy(blocks, piece, sems.at[1])
    store.start()
    store.wait()


def own_piece(peers, named, counts, pattern, ham):
    piece = (ham.shape[0] + LISTS, W)
    return pl.pallas_call(
        piece_kernel,
        out_shape=jax.ShapeDtypeStruct(piece, ham.dtype),
        in_specs=[SMEM] * 4 + [HBM],
        out_specs=HBM,
        scratch_shapes=[pltpu.VMEM(piece, ham.dtype), pltpu.SemaphoreType.DMA((2,))],
        compiler_params=pltpu.CompilerParams(vmem_limit_bytes=62 * MIB),
        name="own_piece",
    )(peers, named, counts, pattern, ham)


def lines_of(count):
    inner = max(count // 4, 1) if count & (count - 1) == 0 else 1
    return count // inner, inner


def swap_along(block, t):
    count = lax.axis_size("col")
    _, inner = lines_of(count)
    pairs = [(c, c - c % inner + partner(c % inner, t, inner)) for c in range(count)]
    return lax.ppermute(block, "col", pairs)


def chunk_of(home, owner, count):
    outer, inner = lines_of(count)
    return partner(home % inner, owner % inner, inner) * outer + home // inner


def pack_kernel(entries, col_count, me, peers, basis, first, *refs):
    outer, inner = lines_of(col_count)
    *sent, held, count, in_sems, out_sems = refs

    def fetch(e):
        return pltpu.make_async_copy(basis.at[e], held.at[e], in_sems.at[e])

    def send(e, p, k, act):
        line, place = lax.div(p, inner), lax.rem(p, inner)
        for t in range(inner):
            @pl.when(place == partner(lax.rem(me[0], inner), t, inner))
            def _():
                target = sent[0].at[line, k] if t == 0 else sent[1 + (t - 1) * CAP + k].at[line]
                act(pltpu.make_async_copy(held.at[e], target, out_sems.at[p, k]))

    for e in range(entries):
        fetch(e).start()
    for c in range(col_count):
        count[c] = 0
    for e in range(entries):
        p = peers[e]
        rank = count[p]
        count[p] = rank + 1
        fetch(e).wait()
        for k in range(CAP):
            @pl.when(rank == k)
            def _():
                send(e, p, k, lambda copy: copy.start())
    for c in range(col_count):
        for k in range(CAP):
            @pl.when(count[c] <= k)
            def _():
                send(0, jnp.int32(c), k, lambda copy: copy.start())
    for c in range(col_count):
        for k in range(CAP):
            pltpu.make_async_copy(basis.at[0], held.at[0], out_sems.at[c, k]).wait()


def pack(me, peers, basis, first, col_count):
    outer, inner = lines_of(col_count)
    entries = basis.shape[0]
    shapes = [(outer, CAP)] + [(outer,)] * ((inner - 1) * CAP)
    return pl.pallas_call(
        functools.partial(pack_kernel, entries, col_count),
        out_shape=tuple(
            jax.ShapeDtypeStruct(shape + basis.shape[1:], basis.dtype) for shape in shapes
        ),
        in_specs=[SMEM, SMEM, HBM, HBM],
        out_specs=(HBM,) * len(shapes),
        scratch_shapes=[
            pltpu.VMEM(basis.shape, basis.dtype),
            pltpu.SMEM((col_count,), jnp.int32),
            pltpu.SemaphoreType.DMA((entries,)),
            pltpu.SemaphoreType.DMA((col_count, CAP)),
        ],
        compiler_params=pltpu.CompilerParams(vmem_limit_bytes=62 * MIB),
        name="pack",
    )(me, peers, basis, first)


def exchange(sent, awaited):
    count = lax.axis_size("col")
    outer, inner = lines_of(count)
    groups = [[line * inner + place for line in range(outer)] for place in range(inner)]

    def between_lines(block, *others):
        return lax.all_to_all(
            after(block, *others), "col", split_axis=0, concat_axis=0,
            axis_index_groups=groups, tiled=True,
        )

    swapped = [
        [swap_along(sent[1 + (t - 1) * CAP + k], t) for k in range(CAP)] for t in range(1, inner)
    ]
    parts = [between_lines(sent[0], *awaited, *[blocks[0] for blocks in swapped])]
    for blocks in swapped:
        parts.append(between_lines(jnp.stack(blocks, axis=1), parts[-1]))
    return [part.reshape((outer * CAP,) + part.shape[2:]) for part in parts]


def after(block, *others):
    return pl.pallas_call(
        lambda *refs: None,
        out_shape=jax.ShapeDtypeStruct(block.shape, block.dtype),
        in_specs=[HBM] * (1 + len(others)),
        out_specs=HBM,
        input_output_aliases={0: 0},
        compiler_params=pltpu.CompilerParams(vmem_limit_bytes=62 * MIB),
        name="after",
    )(block, *others)


def gather_pieces(own):
    count = lax.axis_size("col")
    outer, inner = lines_of(count)
    me = lax.axis_index("col").astype(jnp.int32)
    a, b = me // inner, me % inner

    def move(block, ways):
        pairs = [(x * inner + y, z * inner + y) for x, z in ways for y in range(inner)]
        return lax.ppermute(block, "col", pairs)

    if outer == 4:
        middle, outwards = [(1, 2), (2, 1)], [(1, 0), (2, 3)]
        near = move(own, [(0, 1), (1, 0), (2, 3), (3, 2)])
        across = move(own, middle)
        far = move(near, middle)
        handed = move(across, outwards)
        last = move(far, outwards)
        within = (a == 1) | (a == 2)
        lines = [
            (own, a),
            (near, a ^ 1),
            (across + handed, jnp.where(within, a ^ 3, a ^ 2)),
            (far + last, jnp.where(within, a ^ 2, a ^ 3)),
        ]
        awaited = [far, handed]
    else:
        lines = [(own, a)] + [
            (move(own, [(x, partner(x, t, outer)) for x in range(outer)]), partner(a, -t, outer))
            for t in range(1, outer)
        ]
        awaited = [block for block, _ in lines[1:]]
    pieces, owners = [], []
    for block, line in lines:
        pieces.append(block)
        owners.append(line * inner + b)
        for t in range(1, inner):
            pieces.append(swap_along(block, t))
            owners.append(line * inner + partner(b, -t, inner))
    return pieces, jnp.stack(owners).astype(jnp.int32), awaited


def edge_kernel(col_count, depth, owners, *refs):
    pieces, (first, last, lists, sems, list_sems) = refs[:-5], refs[-5:]
    rows = pieces[0].shape[0] - LISTS
    held = rows // (2 * W)
    total = col_count * held

    def each(act):
        for i, piece in enumerate(pieces):
            for g in range(depth):
                for out, block, sem in ((first, g, 0), (last, total - depth + g, 1)):
                    source = piece.at[pl.ds(block % held * 2 * W, 2 * W)]
                    copy = pltpu.make_async_copy(source, out.at[g], sems.at[sem, g])

                    @pl.when(owners[i] == block // held)
                    def _():
                        act(copy)

            @pl.when(owners[i] >= 0)
            def _():
                act(pltpu.make_async_copy(
                    piece.at[pl.ds(rows, LISTS)], lists.at[owners[i]], list_sems.at[i]
                ))

    each(lambda copy: copy.start())
    each(lambda copy: copy.wait())


def edge_blocks(owners, pieces, col_count, depth):
    shape = jax.ShapeDtypeStruct((depth, 2 * W, W), pieces[0].dtype)
    return pl.pallas_call(
        functools.partial(edge_kernel, col_count, depth),
        out_shape=(shape, shape, jax.ShapeDtypeStruct((col_count, LISTS, W), pieces[0].dtype)),
        in_specs=[SMEM] + [HBM] * len(pieces),
        out_specs=(VMEM, VMEM, VMEM),
        scratch_shapes=[
            pltpu.SemaphoreType.DMA((2, depth)),
            pltpu.SemaphoreType.DMA((len(pieces),)),
        ],
        name="edge_blocks",
    )(owners, *pieces)


def cheb_kernel(blocks, coef, owners, v_low, v_mid, v_high, h_low, h_high, *refs):
    *pieces, out, vext, hraw, hcat, cheb_1, cheb_2, total, kern, sems, psems, osems = refs
    halo_v = DEG
    halo_h = DEG - 1
    held = (pieces[0].shape[0] - LISTS) // (2 * W)
    h_copies = [
        pltpu.make_async_copy(h_low, hraw.at[pl.ds(0, halo_h)], sems.at[0]),
        pltpu.make_async_copy(h_high, hraw.at[pl.ds(halo_h + blocks, halo_h)], sems.at[1]),
    ]
    v_copies = [
        pltpu.make_async_copy(v_low, vext.at[pl.ds(0, halo_v * W)], sems.at[2]),
        pltpu.make_async_copy(v_mid, vext.at[pl.ds(halo_v * W, blocks * W)], sems.at[3]),
        pltpu.make_async_copy(v_high, vext.at[pl.ds((halo_v + blocks) * W, halo_v * W)], sems.at[4]),
    ]

    def each_piece(act):
        for i, piece in enumerate(pieces):
            @pl.when(owners[i] >= 0)
            def _():
                for k in range(held):
                    act(pltpu.make_async_copy(
                        piece.at[pl.ds(k * 2 * W, 2 * W)],
                        hraw.at[halo_h + owners[i] * held + k],
                        psems.at[i, k],
                    ))

    each_piece(lambda copy: copy.start())
    for copy in h_copies + v_copies:
        copy.start()
    each_piece(lambda copy: copy.wait())
    for copy in h_copies:
        copy.wait()
    rows = lax.broadcasted_iota(jnp.int32, (W, W), 0)
    cols = lax.broadcasted_iota(jnp.int32, (W, W), 1)
    upper = jnp.where(rows <= cols, 1.0, 0.0).astype(jnp.bfloat16)

    def build(j, carry):
        coupling = hraw[j, W:]
        lower_band = coupling * upper
        hcat[j, :, 0:W] = lower_band
        hcat[j, :, W : 2 * W] = hraw[j, :W]
        hcat[j, :, 2 * W : 3 * W] = coupling - lower_band
        return carry

    lax.fori_loop(0, blocks + 2 * halo_h, build, 0, unroll=2)
    for copy in v_copies:
        copy.wait()

    def rows_of(j, count=1):
        return pl.ds(pl.multiple_of(j * W, W), count * W)

    def band(source, j, row):
        return jnp.dot(hcat[j], source[rows_of(row, 3), :], preferred_element_type=jnp.float32)

    def first(j, carry):
        value = band(vext, j, j)
        cheb_1[rows_of(j), :] = value.astype(jnp.bfloat16)
        total[rows_of(j), :] = value
        return carry

    lax.fori_loop(0, blocks + 4, first, 0, unroll=2)

    def second(j, carry):
        begin = vext[rows_of(j + 2), :].astype(jnp.float32)
        value = 2.0 * band(cheb_1, j + 1, j) - begin
        cheb_2[rows_of(j), :] = value.astype(jnp.bfloat16)
        total[rows_of(j + 1), :] = (
            coef[0] * begin + (coef[1] - coef[3]) * total[rows_of(j + 1), :] + coef[2] * value
        )
        return carry

    lax.fori_loop(0, blocks + 2, second, 0, unroll=2)

    def store(j):
        return pltpu.make_async_copy(kern.at[j], out.at[j], osems.at[j])

    def third(j, carry):
        for half in range(KB // W):
            i = j * (KB // W) + half
            value = total[rows_of(i + 2), :] + (2.0 * coef[3]) * band(cheb_2, i + 2, i)
            kern[j, :, half * W : (half + 1) * W] = value.astype(jnp.bfloat16).T
        store(j).start()
        return carry

    lax.fori_loop(0, blocks // (KB // W), third, 0)
    for j in range(blocks // (KB // W)):
        store(j).wait()


def chebyshev(coefficients, owners, v_low, v_mid, v_high, h_low, h_high, pieces):
    blocks = v_mid.shape[0] // W
    cols = v_mid.shape[1]
    ext = blocks + 2 * (DEG - 1)
    flops = 2 * W * 3 * W * cols * (3 * blocks + 6)
    result = (blocks * W // KB, cols, KB)
    held = (pieces[0].shape[0] - LISTS) // (2 * W)
    return pl.pallas_call(
        functools.partial(cheb_kernel, blocks),
        out_shape=jax.ShapeDtypeStruct(result, jnp.bfloat16),
        in_specs=[SMEM] * 2 + [HBM] * (5 + len(pieces)),
        out_specs=HBM,
        scratch_shapes=[
            pltpu.VMEM(((blocks + 2 * DEG) * W, cols), jnp.bfloat16),
            pltpu.VMEM((ext, 2 * W, W), jnp.bfloat16),
            pltpu.VMEM((ext, W, 3 * W), jnp.bfloat16),
            pltpu.VMEM((ext * W, cols), jnp.bfloat16),
            pltpu.VMEM(((blocks + 2) * W, cols), jnp.bfloat16),
            pltpu.VMEM((ext * W, cols), jnp.float32),
            pltpu.VMEM(result, jnp.bfloat16),
            pltpu.SemaphoreType.DMA((5,)),
            pltpu.SemaphoreType.DMA((len(pieces), held)),
            pltpu.SemaphoreType.DMA((result[0],)),
        ],
        compiler_params=pltpu.CompilerParams(vmem_limit_bytes=62 * MIB),
        cost_estimate=pl.CostEstimate(flops=flops, bytes_accessed=16 * MIB, transcendentals=0),
        name="chebyshev",
    )(coefficients, owners, v_low, v_mid, v_high, h_low, h_high, *pieces)


def entry_loads(order, parts, pair, sems):
    size = parts[0].shape[0]

    def load(p):
        return pltpu.make_async_copy(parts[0].at[0], pair.at[p], sems.at[p])

    def start(p, carry):
        n = order[p]
        for t, part in enumerate(parts):
            @pl.when((n >= t * size) & (n < (t + 1) * size))
            def _():
                pltpu.make_async_copy(part.at[n - t * size], pair.at[p], sems.at[p]).start()

        return carry

    return load, start


def by_twos(first, last, load, body):
    def step(i, carry):
        p = first + 2 * i
        q = jnp.minimum(p + 1, last - 1)
        load(p).wait()

        @pl.when(q > p)
        def _():
            load(q).wait()

        body(i, p, q)
        return carry

    lax.fori_loop(0, (last - first + 1) // 2, step, 0)


def sent_rows(slots, tiles):
    return slots + tiles + -(slots + tiles) % 8


def project_kernel(blocks, plan, order, kernel_t, core, *refs):
    *parts, out, kern, pair, rows, ksems, bsems = refs
    slots = pair.shape[0]
    load, start = entry_loads(order, parts, pair, bsems)

    def fetch(b):
        return pltpu.make_async_copy(kernel_t.at[b], kern.at[b], ksems.at[b])

    def begin(b, carry):
        first, last = plan[slots + b], plan[slots + b + 1]

        @pl.when(first < last)
        def _():
            fetch(b).start()

        return lax.fori_loop(first, last, start, carry)

    lax.fori_loop(0, blocks, begin, 0)
    rows[...] = jnp.zeros_like(rows)
    rows[slots : slots + core.shape[0]] = core[...]

    def step(b, carry):
        first, last = plan[slots + b], plan[slots + b + 1]

        @pl.when(first < last)
        def _():
            fetch(b).wait()

        def body(i, p, q):
            both = jnp.concatenate([pair[p, 0], pair[q, 0]], axis=1)
            projected = jnp.dot(kern[b], both, preferred_element_type=jnp.float32)
            other = jnp.concatenate([pair[p, 1], pair[q, 1]], axis=1).astype(jnp.float32)
            value = jnp.sum(projected * other, axis=0, keepdims=True) * (1.0 / KB)
            rows[pl.ds(order[p], 1), :] = value[:, :P_SIZE]
            rows[pl.ds(order[q], 1), :] = value[:, P_SIZE:]

        by_twos(first, last, load, body)
        return carry

    lax.fori_loop(0, blocks, step, 0)
    for c in range(out.shape[0]):
        out[c] = rows[...]


def project(plan, order, kernel_t, core, parts, col_count):
    slots = col_count * CAP
    entry = parts[0].shape[1:]
    sent = sent_rows(slots, core.shape[0])
    blocks = kernel_t.shape[0]
    return pl.pallas_call(
        functools.partial(project_kernel, blocks),
        out_shape=jax.ShapeDtypeStruct((col_count, sent, P_SIZE), jnp.float32),
        in_specs=[SMEM, SMEM, HBM, VMEM] + [HBM] * len(parts),
        out_specs=VMEM,
        scratch_shapes=[
            pltpu.VMEM(kernel_t.shape, jnp.bfloat16),
            pltpu.VMEM((slots,) + entry, jnp.bfloat16),
            pltpu.VMEM((sent, P_SIZE), jnp.float32),
            pltpu.SemaphoreType.DMA((blocks,)),
            pltpu.SemaphoreType.DMA((slots,)),
        ],
        compiler_params=pltpu.CompilerParams(vmem_limit_bytes=62 * MIB),
        name="project",
    )(plan, order, kernel_t, core, *parts)


def update_kernel(
    blocks, tiles, plan, order, tile_of, contributions, collect, *refs
):
    *parts, density_out, update_out, pair, density, potential, acc, stage, sems, osems = refs
    slots = pair.shape[0]
    live = plan[slots + blocks]
    me = plan[slots + blocks + 1]
    load, start = entry_loads(order, parts, pair, sems)
    lax.fori_loop(0, live, start, 0)
    density[...] = jnp.dot(
        collect[...],
        contributions[...],
        preferred_element_type=jnp.float32,
        precision=lax.Precision.HIGHEST,
    )
    for t in range(tiles):
        density_out[pl.ds(t, 1), :] = density[pl.ds(me * tiles + t, 1), :]
    positive = jnp.maximum(density[...], 0.1)
    root = jnp.exp(jnp.log(positive) * (1.0 / 3.0))
    root = root - (root - positive / (root * root)) * (1.0 / 3.0)
    potential[...] = -exchange_factor * root
    scale = 1.0 / math.sqrt(P_SIZE)

    def store(b):
        rows = pl.ds(pl.multiple_of(b * KB, KB), KB)
        return pltpu.make_async_copy(stage.at[b], update_out.at[rows], osems.at[b])

    def step(b, carry):
        first, last = plan[slots + b], plan[slots + b + 1]

        @pl.when(first == last)
        def _():
            stage[b] = jnp.zeros(stage.shape[1:], jnp.bfloat16)

        def body(i, p, q):
            weight_p = potential[pl.ds(tile_of[order[p]], 1), :]
            weight_q = potential[pl.ds(tile_of[order[q]], 1), :] * (q - p).astype(jnp.float32)
            weighted = jnp.concatenate(
                [
                    (pair[p, 1].astype(jnp.float32) * weight_p).astype(jnp.bfloat16),
                    (pair[q, 1].astype(jnp.float32) * weight_q).astype(jnp.bfloat16),
                ],
                axis=1,
            )
            block = lax.dot_general(
                jnp.concatenate([pair[p, 0], pair[q, 0]], axis=1),
                weighted,
                (((1,), (1,)), ((), ())),
                preferred_element_type=jnp.float32,
            )

            @pl.when(last - first <= 2)
            def _():
                stage[b] = (block * scale).astype(jnp.bfloat16)

            @pl.when((last - first > 2) & (i == 0))
            def _():
                acc[...] = block

            @pl.when(i > 0)
            def _():
                acc[...] += block

        by_twos(first, last, load, body)

        @pl.when(last - first > 2)
        def _():
            stage[b] = (acc[...] * scale).astype(jnp.bfloat16)

        store(b).start()
        return carry

    lax.fori_loop(0, blocks, step, 0)
    for b in range(blocks):
        store(b).wait()


def update(plan, order, tile_of, contributions, collect, parts, tiles, blocks, cols):
    slots = len(parts) * parts[0].shape[0]
    entry = parts[0].shape[1:]
    all_tiles = (collect.shape[0], P_SIZE)
    return pl.pallas_call(
        functools.partial(update_kernel, blocks, tiles),
        out_shape=(
            jax.ShapeDtypeStruct((tiles, P_SIZE), jnp.float32),
            jax.ShapeDtypeStruct((blocks * KB, cols), jnp.bfloat16),
        ),
        in_specs=[SMEM] * 3 + [VMEM] * 2 + [HBM] * len(parts),
        out_specs=(VMEM, HBM),
        scratch_shapes=[
            pltpu.VMEM((slots,) + entry, jnp.bfloat16),
            pltpu.VMEM(all_tiles, jnp.float32),
            pltpu.VMEM(all_tiles, jnp.float32),
            pltpu.VMEM((KB, cols), jnp.float32),
            pltpu.VMEM((blocks, KB, cols), jnp.bfloat16),
            pltpu.SemaphoreType.DMA((slots,)),
            pltpu.SemaphoreType.DMA((blocks,)),
        ],
        compiler_params=pltpu.CompilerParams(vmem_limit_bytes=62 * MIB),
        name="update",
    )(plan, order, tile_of, contributions, collect, *parts)


def shift(block, axis, step):
    count = lax.axis_size(axis)
    pairs = [(i, i + step) for i in range(count) if 0 <= i + step < count]
    return lax.ppermute(block, axis, pairs)


def make_plan(lists, me, entries, tiles, col_count, blocks):
    slots = col_count * CAP
    sent = sent_rows(slots, tiles)
    lists = lists[:, : 2 * entries + tiles].astype(jnp.int32)
    peers, named, counts = lists[:, :entries], lists[:, entries : 2 * entries], lists[:, 2 * entries :]
    index = jnp.arange(entries, dtype=jnp.int32)
    home = jnp.arange(col_count, dtype=jnp.int32)[:, None]
    earlier = (peers[:, :, None] == peers[:, None, :]) & (index[None, :] < index[:, None])
    rank = jnp.sum(earlier.astype(jnp.int32), axis=2)
    live = (index % SLOTS)[None, :] < jnp.repeat(counts, SLOTS, axis=1)
    row = jnp.where(live, peers * sent + chunk_of(home, peers, col_count) * CAP + rank, -1).reshape(col_count, tiles, SLOTS)
    core = (home * sent + slots + jnp.arange(tiles, dtype=jnp.int32))[:, :, None]
    row = jnp.concatenate([row, core], axis=2).reshape(col_count * tiles, SLOTS + 1, 1)
    picked = row == jnp.arange(col_count * sent, dtype=jnp.int32)
    collect = jnp.sum(picked.astype(jnp.float32), axis=1)
    hit = (
        (peers == me)[:, None, :]
        & (rank[:, None, :] == jnp.arange(CAP, dtype=jnp.int32)[None, :, None])
        & live[:, None, :]
    )
    at_me = chunk_of(home, me, col_count).reshape(1, col_count) == home
    tile = home * tiles + index[None, :] // SLOTS

    def of_slots(values):
        by_home = jnp.sum(jnp.where(hit, values[:, None, :], 0), axis=2)
        return jnp.sum(jnp.where(at_me[:, :, None], by_home[None], 0), axis=1).reshape(slots)

    wanted = of_slots(named + 1) - 1
    tile_of = of_slots(tile)
    key = jnp.where(wanted < 0, blocks, wanted)
    place = jnp.arange(slots, dtype=jnp.int32)
    before = (key[None, :] < key[:, None]) | (
        (key[None, :] == key[:, None]) & (place[None, :] < place[:, None])
    )
    spot = jnp.sum(before.astype(jnp.int32), axis=1)
    order = jnp.sum(jnp.where(spot[None, :] == place[:, None], place[None, :], 0), axis=1)
    starts = jnp.sum(
        (key[None, :] < jnp.arange(blocks + 1, dtype=jnp.int32)[:, None]).astype(jnp.int32), axis=1
    )
    plan = jnp.concatenate([wanted, starts, me[None]]).astype(jnp.int32)
    return collect, plan, order.astype(jnp.int32), tile_of.astype(jnp.int32)


def shards(
    start_columns,
    hamiltonian,
    band_pattern,
    coefficients,
    tile_peer,
    tile_block,
    tile_count,
    basis_values,
    core_density,
):
    col_count = lax.axis_size("col")
    entries = tile_peer.shape[0]
    tiles = core_density.shape[0]
    cols = start_columns.shape[1]
    blocks = start_columns.shape[0] // KB
    peers = tile_peer[:, 0]
    me = lax.axis_index("col").astype(jnp.int32)

    own = own_piece(peers, tile_block, tile_count, band_pattern, hamiltonian.reshape(-1, W))
    pieces, owners, awaited = gather_pieces(own)
    parts = exchange(pack(me[None], peers, basis_values, own, col_count), awaited)

    v_low = shift(start_columns[-DEG * W :], "row", 1)
    v_high = shift(start_columns[: DEG * W], "row", -1)

    first, last, lists = edge_blocks(owners, pieces, col_count, DEG - 1)
    h_low = shift(last, "row", 1)
    h_high = shift(first, "row", -1)
    kernel_t = chebyshev(
        coefficients, owners, v_low, start_columns, v_high, h_low, h_high, pieces
    )
    collect, plan, order, tile_of = make_plan(lists[:, 0], me, entries, tiles, col_count, blocks)
    partial = project(plan, order, kernel_t, core_density, parts, col_count)
    contributions = lax.all_to_all(partial, "col", split_axis=0, concat_axis=0, tiled=True)
    contributions = contributions.reshape(-1, P_SIZE)
    return update(
        plan, order, tile_of, contributions, collect, parts, tiles, blocks, cols
    )


def solution(mesh):
    return jax.shard_map(
        shards,
        mesh=mesh,
        in_specs=(
            P("row", "col"),
            P(("row", "col"), None, None, None),
            P(("row", "col")),
            P(),
            P(("row", "col"), None),
            P(("row", "col")),
            P(("row", "col")),
            P(("row", "col"), None, None, None),
            P(("row", "col"), None),
        ),
        out_specs=(P(("row", "col"), None), P("row", "col")),
        check_vma=False,
    )
```

profile of v0, /device:TPU:2, one launch (start us, length us, event | category | flops | bytes accessed | tf_op | source)
XLA Modules:
  0.0 179.7 jit_solution(4374326572995536375)
XLA Ops:
  0.6 2.6 %own_piece.1.refs_0_.first = bf16[1040,256]{1,0:T(8,128)(2,1)} custom-call(s32[16]{0:T(128)} %bitcast.35, s32[16]{0:T(128)} %named.1, s32[4]{0:T(128)} %counts.1, s32[2]{0:T(128)} %pattern.1, bf16[1024,256]{1,0:T(8,128)(2,1)} %bitcast.29), custom_call_target="tpu_custom_call" | custom-call | tf_op jit(solution)/shard_map/own_piece/pallas_call | solution.py:55
  3.2 1.5 collective-permute-start.3
  4.7 3.6 %collective-permute-start.1 = (bf16[1040,256]{1,0:T(8,128)(2,1)}, bf16[1040,256]{1,0:T(8,128)(2,1)}, u32[]{:S(2)}, u32[]{:S(2)}) collective-permute-start(bf16[1040,256]{1,0:T(8,128)(2,1)} %own_piece.1.refs_0_.first), channel_id=1, source_target_pairs={{0,2},{1,3},{2,0},{3,1},{4,6},{5,7},{6,4},{7,5},{8,10},{9,11},{10,... | collective-permute-start | bytes 1597448 | tf_op jit(solution)/shard_map/ppermute | solution.py:183
  8.3 4.5 %pack.1 = (bf16[4,2,2,512,128]{4,3,2,1,0:T(8,128)(2,1)}, bf16[4,2,512,128]{3,2,1,0:T(8,128)(2,1)}, bf16[4,2,512,128]{3,2,1,0:T(8,128)(2,1)}) custom-call(s32[1]{0:T(128)} %bitcast.11.me, s32[16]{0:T(128)} %bitcast.36, bf16[16,2,512,128]{3,2,1,0:T(8,128)(2,1)} %basis.1, bf16[1040,256]{1,0:T(8,128)(2,1)} %own_piece.1.refs_0_.first), custom_call_target="tpu_custom_call" | custom-call | tf_op jit(solution)/shard_map/pack/pallas_call | solution.py:125
  12.9 1.6 collective-permute-start.13
  14.5 1.3 collective-permute-start.4
  15.8 4.7 %collective-permute-done.1.refs_2_ = bf16[1040,256]{1,0:T(8,128)(2,1)} collective-permute-done((bf16[1040,256]{1,0:T(8,128)(2,1)}, bf16[1040,256]{1,0:T(8,128)(2,1)}, u32[]{:S(2)}, u32[]{:S(2)}) %collective-permute-start.1) | collective-permute-done | bytes 532512 | tf_op jit(solution)/shard_map/ppermute | solution.py:183
  21.2 16.3 %collective-permute-done.13.refs_3_ = bf16[4,2,512,128]{3,2,1,0:T(8,128)(2,1)S(1)} collective-permute-done((bf16[4,2,512,128]{3,2,1,0:T(8,128)(2,1)}, bf16[4,2,512,128]{3,2,1,0:T(8,128)(2,1)S(1)}, u32[]{:S(2)}, u32[]{:S(2)}) %collective-permute-start.13) | collective-permute-done | bytes 1048608 | tf_op jit(solution)/shard_map/ppermute | solution.py:75
  39.1 4.6 %all-to-all-start = ((bf16[4,2,2,512,128]{4,3,2,1,0:T(8,128)(2,1)}), bf16[4,2,2,512,128]{4,3,2,1,0:T(8,128)(2,1)}, u32[]{:S(2)}, u32[]{:S(2)}) async-start(bf16[4,2,2,512,128]{4,3,2,1,0:T(8,128)(2,1)} %after.2), calls=%async_computation | async-start | bytes 4194304 | tf_op jit(solution)/shard_map/all_to_all | solution.py:149
  43.7 1.6 collective-permute-start
  45.9 1.3 collective-permute-start.7
  47.3 2.8 %fusion.12 = (bf16[768,512]{1,0:T(8,128)(2,1)}, bf16[768,512]{1,0:T(8,128)(2,1)}) fusion(bf16[4096,512]{1,0:T(8,128)(2,1)} %v_mid.1), kind=kLoop, calls=%fused_computation.55 | loop fusion | bytes 3145728 | tf_op jit(solution)/shard_map/slice | solution.py:657
  50.0 1.5 collective-permute-start.2
  51.5 1.3 add.189.refs_4_
  53.5 26.4 %collective-permute-done.7 = bf16[1040,256]{1,0:T(8,128)(2,1)} collective-permute-done((bf16[1040,256]{1,0:T(8,128)(2,1)S(1)}, bf16[1040,256]{1,0:T(8,128)(2,1)}, u32[]{:S(2)}, u32[]{:S(2)}) %collective-permute-start.7) | collective-permute-done | bytes 532512 | tf_op jit(solution)/shard_map/ppermute | solution.py:183
  81.1 1.6 collective-permute-start.8
  83.6 1.9 %collective-permute-start.9 = (bf16[768,512]{1,0:T(8,128)(2,1)}, bf16[768,512]{1,0:T(8,128)(2,1)}, u32[]{:S(2)}, u32[]{:S(2)}) collective-permute-start(bf16[768,512]{1,0:T(8,128)(2,1)} %get-tuple-element.21), channel_id=1, source_target_pairs={{0,8},{8,16},{16,24},{1,9},{9,17},{17,25},{2,10},{10,18},{18,26},{... | collective-permute-start | bytes 2359304 | tf_op jit(solution)/shard_map/ppermute | solution.py:587
  85.5 2.8 %pad_maximum_fusion.refs_0_ = bf16[4,2,2,512,128]{4,3,2,1,0:T(8,128)(2,1)} fusion(bf16[4,1,2,512,128]{4,3,2,1,0:T(8,128)(2,1)} %bitcast.14, bf16[4,1,2,512,128]{4,3,2,1,0:T(8,128)(2,1)S(1)} %bitcast.28), kind=kLoop, calls=%fused_computation | loop fusion | flops 1048576 | bytes 4194304 | tf_op jit(solution)/shard_map/stack | solution.py:159
  88.3 2.5 %all-to-all-done.refs_1_ = bf16[4,2,2,512,128]{4,3,2,1,0:T(8,128)(2,1)} async-done(((bf16[4,2,2,512,128]{4,3,2,1,0:T(8,128)(2,1)}), bf16[4,2,2,512,128]{4,3,2,1,0:T(8,128)(2,1)}, u32[]{:S(2)}, u32[]{:S(2)}) %all-to-all-start) | async-done | bytes 2097184 | tf_op jit(solution)/shard_map/all_to_all | solution.py:149
  90.8 11.5 %all-to-all-start.1 = ((bf16[4,2,2,512,128]{4,3,2,1,0:T(8,128)(2,1)}), bf16[4,2,2,512,128]{4,3,2,1,0:T(8,128)(2,1)}, u32[]{:S(2)}, u32[]{:S(2)}) async-start(bf16[4,2,2,512,128]{4,3,2,1,0:T(8,128)(2,1)} %after.3), calls=%async_computation.1 | async-start | bytes 4194304 | tf_op jit(solution)/shard_map/all_to_all | solution.py:149
  102.3 3.4 %collective-permute-start.10 = (bf16[768,512]{1,0:T(8,128)(2,1)S(1)}, bf16[768,512]{1,0:T(8,128)(2,1)S(1)}, u32[]{:S(2)}, u32[]{:S(2)}) collective-permute-start(bf16[768,512]{1,0:T(8,128)(2,1)S(1)} %copy-done.9), channel_id=1, source_target_pairs={{8,0},{16,8},{24,16},{9,1},{17,9},{25,17},{10,2},{18,10},{26,18},{... | collective-permute-start | bytes 2359304 | tf_op jit(solution)/shard_map/ppermute | solution.py:587
  105.7 7.3 %collective-permute-done.8.refs_7_ = bf16[1040,256]{1,0:T(8,128)(2,1)} collective-permute-done((bf16[1040,256]{1,0:T(8,128)(2,1)S(1)}, bf16[1040,256]{1,0:T(8,128)(2,1)}, u32[]{:S(2)}, u32[]{:S(2)}) %collective-permute-start.8) | collective-permute-done | bytes 532512 | tf_op jit(solution)/shard_map/ppermute | solution.py:75
  113.0 3.0 %edge_blocks.1 = (bf16[2,512,256]{2,1,0:T(8,128)(2,1)}, bf16[2,512,256]{2,1,0:T(8,128)(2,1)}, bf16[8,16,256]{2,1,0:T(8,128)(2,1)}) custom-call(s32[8]{0:T(128)} %stack.44.owners, bf16[1040,256]{1,0:T(8,128)(2,1)} %own_piece.1.refs_0_.first, bf16[1040,256]{1,0:T(8,128)(2,1)} %collective-permute-done.refs_1_, ...), custom_call_target="tpu_custom_call" | custom-call | tf_op jit(solution)/shard_map/edge_blocks/pallas_call | solution.py:245
  117.9 1.9 %collective-permute-start.11 = (bf16[2,512,256]{2,1,0:T(8,128)(2,1)}, bf16[2,512,256]{2,1,0:T(8,128)(2,1)S(1)}, u32[]{:S(2)}, u32[]{:S(2)}) collective-permute-start(bf16[2,512,256]{2,1,0:T(8,128)(2,1)} %get-tuple-element.9), channel_id=1, source_target_pairs={{0,8},{8,16},{16,24},{1,9},{9,17},{17,25},{2,10},{10,18},{18,26},{... | collective-permute-start | bytes 1572872 | tf_op jit(solution)/shard_map/ppermute | solution.py:587
  119.8 3.6 %collective-permute-start.12 = (bf16[2,512,256]{2,1,0:T(8,128)(2,1)}, bf16[2,512,256]{2,1,0:T(8,128)(2,1)S(1)}, u32[]{:S(2)}, u32[]{:S(2)}) collective-permute-start(bf16[2,512,256]{2,1,0:T(8,128)(2,1)} %get-tuple-element.10), channel_id=1, source_target_pairs={{8,0},{16,8},{24,16},{9,1},{17,9},{25,17},{10,2},{18,10},{26,18},{... | collective-permute-start | bytes 1572872 | tf_op jit(solution)/shard_map/ppermute | solution.py:587
  126.8 1.8 collective-permute-done.11.h_low
  128.6 1.9 %collective-permute-done.12.h_high = bf16[2,512,256]{2,1,0:T(8,128)(2,1)S(1)} collective-permute-done((bf16[2,512,256]{2,1,0:T(8,128)(2,1)}, bf16[2,512,256]{2,1,0:T(8,128)(2,1)S(1)}, u32[]{:S(2)}, u32[]{:S(2)}) %collective-permute-start.12) | collective-permute-done | bytes 524320 | tf_op jit(solution)/shard_map/ppermute | solution.py:587
  131.3 22.2 %chebyshev.1.kernel_t = bf16[8,512,512]{2,1,0:T(8,128)(2,1)} custom-call(f32[4]{0:T(128)} %coef.1, s32[8]{0:T(128)} %stack.44.owners, bf16[768,512]{1,0:T(8,128)(2,1)} %collective-permute-done.9.v_low, bf16[4096,512]{1,0:T(8,128)(2,1)} %v_mid.1, bf16[768,512]{1,0:T(8,128)(2,1)} %copy-done.11, bf16[2,512,256]{2,1,0:T(8,128)(2,1)} %copy-done.12, ...), custom_call_target="tpu_custom_call" | custom-call | flops 10871635968 | bytes 16777216 | tf_op jit(solution)/shard_map/chebyshev/pallas_call | solution.py:354
  153.5 5.7 %project.1 = f32[8,24,128]{2,1,0:T(8,128)} custom-call(s32[26]{0:T(128)} %pad_add_fusion.1.plan, s32[16]{0:T(128)} %select_reduce_fusion.2.order, bf16[8,512,512]{2,1,0:T(8,128)(2,1)} %chebyshev.1.kernel_t, f32[4,128]{1,0:T(4,128)} %core.1, bf16[8,2,512,128]{3,2,1,0:T(8,128)(2,1)} %bitcast.12.refs_0_, bf16[8,2,512,128]{3,2,1,0:T(8,128)(2,1)} %bitcast.15.refs_1_), custom_call_target="tpu_custom_call" | custom-call | tf_op jit(solution)/shard_map/project/pallas_call | solution.py:464
  159.1 5.0 %all-to-all-start.2 = ((f32[8,24,128]{2,1,0:T(8,128)}), f32[8,24,128]{2,1,0:T(8,128)S(1)}, u32[]{:S(2)}, u32[]{:S(2)}) async-start(f32[8,24,128]{2,1,0:T(8,128)} %project.1), calls=%async_computation.2 | async-start | bytes 196608 | tf_op jit(solution)/shard_map/all_to_all | solution.py:667
  164.8 6.4 %all-to-all-done.2 = f32[8,24,128]{2,1,0:T(8,128)S(1)} async-done(((f32[8,24,128]{2,1,0:T(8,128)}), f32[8,24,128]{2,1,0:T(8,128)S(1)}, u32[]{:S(2)}, u32[]{:S(2)}) %all-to-all-start.2) | async-done | bytes 98336 | tf_op jit(solution)/shard_map/all_to_all | solution.py:667
  171.9 7.8 %update.1 = (f32[4,128]{1,0:T(4,128)}, bf16[4096,512]{1,0:T(8,128)(2,1)}) custom-call(s32[26]{0:T(128)} %pad_add_fusion.1.plan, s32[16]{0:T(128)} %select_reduce_fusion.2.order, s32[16]{0:T(128)} %reshape.285.tile_of, f32[192,128]{1,0:T(8,128)} %bitcast.30, f32[32,192]{1,0:T(8,128)} %convert_reduce_fusion.collect, bf16[8,2,512,128]{3,2,1,0:T(8,128)(2,1)} %bitcast.12.refs_0_, ...), custom_call_target="tpu_custom_call" | custom-call | tf_op jit(solution)/shard_map/update/pallas_call | solution.py:562
  (86 shorter events, 13.0 us)
Async XLA Ops:
  3.2 11.3 %collective-permute-start.3 = (bf16[1040,256]{1,0:T(8,128)(2,1)}, bf16[1040,256]{1,0:T(8,128)(2,1)}, u32[]{:S(2)}, u32[]{:S(2)}) collective-permute-start(bf16[1040,256]{1,0:T(8,128)(2,1)} %own_piece.1.refs_0_.first), channel_id=1, source_target_pairs={{2,4},{3,5},{4,2},{5,3},{10,12},{11,13},{12,10},{13,11},{18,20},{1... | collective-permute-start | bytes 1597448 | tf_op jit(solution)/shard_map/ppermute | solution.py:183
  4.7 15.8 %collective-permute-start.1 = (bf16[1040,256]{1,0:T(8,128)(2,1)}, bf16[1040,256]{1,0:T(8,128)(2,1)}, u32[]{:S(2)}, u32[]{:S(2)}) collective-permute-start(bf16[1040,256]{1,0:T(8,128)(2,1)} %own_piece.1.refs_0_.first), channel_id=1, source_target_pairs={{0,2},{1,3},{2,0},{3,1},{4,6},{5,7},{6,4},{7,5},{8,10},{9,11},{10,... | collective-permute-start | bytes 1597448 | tf_op jit(solution)/shard_map/ppermute | solution.py:183
  12.9 24.6 %collective-permute-start.13 = (bf16[4,2,512,128]{3,2,1,0:T(8,128)(2,1)}, bf16[4,2,512,128]{3,2,1,0:T(8,128)(2,1)S(1)}, u32[]{:S(2)}, u32[]{:S(2)}) collective-permute-start(bf16[4,2,512,128]{3,2,1,0:T(8,128)(2,1)} %get-tuple-element.12), channel_id=1, source_target_pairs={{0,1},{1,0},{2,3},{3,2},{4,5},{5,4},{6,7},{7,6},{8,9},{9,8},{10,11... | collective-permute-start | bytes 3145736 | tf_op jit(solution)/shard_map/ppermute | solution.py:75
  14.5 23.0 %collective-permute-start.4 = (bf16[1040,256]{1,0:T(8,128)(2,1)}, bf16[1040,256]{1,0:T(8,128)(2,1)S(1)}, u32[]{:S(2)}, u32[]{:S(2)}) collective-permute-start(bf16[1040,256]{1,0:T(8,128)(2,1)} %collective-permute-done.3), channel_id=1, source_target_pairs={{2,0},{3,1},{4,6},{5,7},{10,8},{11,9},{12,14},{13,15},{18,16},{19,... | collective-permute-start | bytes 1597448 | tf_op jit(solution)/shard_map/ppermute | solution.py:183
  20.5 17.0 %collective-permute-start.6 = (bf16[1040,256]{1,0:T(8,128)(2,1)}, bf16[1040,256]{1,0:T(8,128)(2,1)S(1)}, u32[]{:S(2)}, u32[]{:S(2)}) collective-permute-start(bf16[1040,256]{1,0:T(8,128)(2,1)} %collective-permute-done.1.refs_2_), channel_id=1, source_target_pairs={{2,4},{3,5},{4,2},{5,3},{10,12},{11,13},{12,10},{13,11},{18,20},{1... | collective-permute-start | bytes 1597448 | tf_op jit(solution)/shard_map/ppermute | solution.py:183
  37.5 1.2 copy-start.1
  37.5 0.8 copy-start.8
  38.3 0.8 copy-start.5
  39.1 4.6 %copy-start = (bf16[1040,256]{1,0:T(8,128)(2,1)S(1)}, bf16[1040,256]{1,0:T(8,128)(2,1)}, u32[]{:S(2)}) copy-start(bf16[1040,256]{1,0:T(8,128)(2,1)} %own_piece.1.refs_0_.first) | copy-start | bytes 1597444
  39.1 6.7 %copy-start.6 = (bf16[1040,256]{1,0:T(8,128)(2,1)S(1)}, bf16[1040,256]{1,0:T(8,128)(2,1)}, u32[]{:S(2)}) copy-start(bf16[1040,256]{1,0:T(8,128)(2,1)} %copy-done.5) | copy-start | bytes 1597444
  39.1 51.6 %all-to-all-start = ((bf16[4,2,2,512,128]{4,3,2,1,0:T(8,128)(2,1)}), bf16[4,2,2,512,128]{4,3,2,1,0:T(8,128)(2,1)}, u32[]{:S(2)}, u32[]{:S(2)}) async-start(bf16[4,2,2,512,128]{4,3,2,1,0:T(8,128)(2,1)} %after.2), calls=%async_computation | async-start | bytes 4194304 | tf_op jit(solution)/shard_map/all_to_all | solution.py:149
  43.7 58.5 %collective-permute-start = (bf16[1040,256]{1,0:T(8,128)(2,1)S(1)}, bf16[1040,256]{1,0:T(8,128)(2,1)}, u32[]{:S(2)}, u32[]{:S(2)}) collective-permute-start(bf16[1040,256]{1,0:T(8,128)(2,1)S(1)} %copy-done), channel_id=1, source_target_pairs={{0,1},{1,0},{2,3},{3,2},{4,5},{5,4},{6,7},{7,6},{8,9},{9,8},{10,11... | collective-permute-start | bytes 1597448 | tf_op jit(solution)/shard_map/ppermute | solution.py:75
  45.3 38.3 %collective-permute-start.14 = (bf16[4,2,512,128]{3,2,1,0:T(8,128)(2,1)}, bf16[4,2,512,128]{3,2,1,0:T(8,128)(2,1)}, u32[]{:S(2)}, u32[]{:S(2)}) collective-permute-start(bf16[4,2,512,128]{3,2,1,0:T(8,128)(2,1)} %get-tuple-element.13), channel_id=1, source_target_pairs={{0,1},{1,0},{2,3},{3,2},{4,5},{5,4},{6,7},{7,6},{8,9},{9,8},{10,11... | collective-permute-start | bytes 3145736 | tf_op jit(solution)/shard_map/ppermute | solution.py:75
  45.9 34.0 %collective-permute-start.7 = (bf16[1040,256]{1,0:T(8,128)(2,1)S(1)}, bf16[1040,256]{1,0:T(8,128)(2,1)}, u32[]{:S(2)}, u32[]{:S(2)}) collective-permute-start(bf16[1040,256]{1,0:T(8,128)(2,1)S(1)} %copy-done.6), channel_id=1, source_target_pairs={{2,0},{3,1},{4,6},{5,7},{10,8},{11,9},{12,14},{13,15},{18,16},{19,... | collective-permute-start | bytes 1597448 | tf_op jit(solution)/shard_map/ppermute | solution.py:183
  47.3 32.6 %copy-start.7 = (bf16[1040,256]{1,0:T(8,128)(2,1)S(1)}, bf16[1040,256]{1,0:T(8,128)(2,1)}, u32[]{:S(2)}) copy-start(bf16[1040,256]{1,0:T(8,128)(2,1)} %copy-done.5) | copy-start | bytes 1597444
  50.0 35.5 %copy-start.2 = (bf16[4,2,512,128]{3,2,1,0:T(8,128)(2,1)S(1)}, bf16[4,2,512,128]{3,2,1,0:T(8,128)(2,1)}, u32[]{:S(2)}) copy-start(bf16[4,2,512,128]{3,2,1,0:T(8,128)(2,1)} %copy-done.1) | copy-start | bytes 3145732
  50.0 55.7 %collective-permute-start.2 = (bf16[1040,256]{1,0:T(8,128)(2,1)}, bf16[1040,256]{1,0:T(8,128)(2,1)}, u32[]{:S(2)}, u32[]{:S(2)}) collective-permute-start(bf16[1040,256]{1,0:T(8,128)(2,1)} %collective-permute-done.1.refs_2_), channel_id=1, source_target_pairs={{0,1},{1,0},{2,3},{3,2},{4,5},{5,4},{6,7},{7,6},{8,9},{9,8},{10,11... | collective-permute-start | bytes 1597448 | tf_op jit(solution)/shard_map/ppermute | solution.py:75
  52.9 35.4 %copy-start.3 = (bf16[1040,256]{1,0:T(8,128)(2,1)}, bf16[1040,256]{1,0:T(8,128)(2,1)S(1)}, u32[]{:S(2)}) copy-start(bf16[1040,256]{1,0:T(8,128)(2,1)S(1)} %add.189.refs_4_) | copy-start | bytes 1597444
  52.9 52.8 %collective-permute-start.5 = (bf16[1040,256]{1,0:T(8,128)(2,1)S(1)}, bf16[1040,256]{1,0:T(8,128)(2,1)}, u32[]{:S(2)}, u32[]{:S(2)}) collective-permute-start(bf16[1040,256]{1,0:T(8,128)(2,1)S(1)} %add.189.refs_4_), channel_id=1, source_target_pairs={{0,1},{1,0},{2,3},{3,2},{4,5},{5,4},{6,7},{7,6},{8,9},{9,8},{10,11... | collective-permute-start | bytes 1597448 | tf_op jit(solution)/shard_map/ppermute | solution.py:75
  81.1 7.2 %copy-start.4 = (bf16[1040,256]{1,0:T(8,128)(2,1)}, bf16[1040,256]{1,0:T(8,128)(2,1)S(1)}, u32[]{:S(2)}) copy-start(bf16[1040,256]{1,0:T(8,128)(2,1)S(1)} %add.190.refs_6_) | copy-start | bytes 1597444
  81.1 31.9 %collective-permute-start.8 = (bf16[1040,256]{1,0:T(8,128)(2,1)S(1)}, bf16[1040,256]{1,0:T(8,128)(2,1)}, u32[]{:S(2)}, u32[]{:S(2)}) collective-permute-start(bf16[1040,256]{1,0:T(8,128)(2,1)S(1)} %add.190.refs_6_), channel_id=1, source_target_pairs={{0,1},{1,0},{2,3},{3,2},{4,5},{5,4},{6,7},{7,6},{8,9},{9,8},{10,11... | collective-permute-start | bytes 1597448 | tf_op jit(solution)/shard_map/ppermute | solution.py:75
  83.6 42.3 %collective-permute-start.9 = (bf16[768,512]{1,0:T(8,128)(2,1)}, bf16[768,512]{1,0:T(8,128)(2,1)}, u32[]{:S(2)}, u32[]{:S(2)}) collective-permute-start(bf16[768,512]{1,0:T(8,128)(2,1)} %get-tuple-element.21), channel_id=1, source_target_pairs={{0,8},{8,16},{16,24},{1,9},{9,17},{17,25},{2,10},{10,18},{18,26},{... | collective-permute-start | bytes 2359304 | tf_op jit(solution)/shard_map/ppermute | solution.py:587
  90.8 11.5 %copy-start.9 = (bf16[768,512]{1,0:T(8,128)(2,1)S(1)}, bf16[768,512]{1,0:T(8,128)(2,1)}, u32[]{:S(2)}) copy-start(bf16[768,512]{1,0:T(8,128)(2,1)} %get-tuple-element.20) | copy-start | bytes 2359300
  90.8 62.7 %all-to-all-start.1 = ((bf16[4,2,2,512,128]{4,3,2,1,0:T(8,128)(2,1)}), bf16[4,2,2,512,128]{4,3,2,1,0:T(8,128)(2,1)}, u32[]{:S(2)}, u32[]{:S(2)}) async-start(bf16[4,2,2,512,128]{4,3,2,1,0:T(8,128)(2,1)} %after.3), calls=%async_computation.1 | async-start | bytes 4194304 | tf_op jit(solution)/shard_map/all_to_all | solution.py:149
  102.3 23.6 %collective-permute-start.10 = (bf16[768,512]{1,0:T(8,128)(2,1)S(1)}, bf16[768,512]{1,0:T(8,128)(2,1)S(1)}, u32[]{:S(2)}, u32[]{:S(2)}) collective-permute-start(bf16[768,512]{1,0:T(8,128)(2,1)S(1)} %copy-done.9), channel_id=1, source_target_pairs={{8,0},{16,8},{24,16},{9,1},{17,9},{25,17},{10,2},{18,10},{26,18},{... | collective-permute-start | bytes 2359304 | tf_op jit(solution)/shard_map/ppermute | solution.py:587
  117.9 10.7 %collective-permute-start.11 = (bf16[2,512,256]{2,1,0:T(8,128)(2,1)}, bf16[2,512,256]{2,1,0:T(8,128)(2,1)S(1)}, u32[]{:S(2)}, u32[]{:S(2)}) collective-permute-start(bf16[2,512,256]{2,1,0:T(8,128)(2,1)} %get-tuple-element.9), channel_id=1, source_target_pairs={{0,8},{8,16},{16,24},{1,9},{9,17},{17,25},{2,10},{10,18},{18,26},{... | collective-permute-start | bytes 1572872 | tf_op jit(solution)/shard_map/ppermute | solution.py:587
  119.8 10.6 %collective-permute-start.12 = (bf16[2,512,256]{2,1,0:T(8,128)(2,1)}, bf16[2,512,256]{2,1,0:T(8,128)(2,1)S(1)}, u32[]{:S(2)}, u32[]{:S(2)}) collective-permute-start(bf16[2,512,256]{2,1,0:T(8,128)(2,1)} %get-tuple-element.10), channel_id=1, source_target_pairs={{8,0},{16,8},{24,16},{9,1},{17,9},{25,17},{10,2},{18,10},{26,18},{... | collective-permute-start | bytes 1572872 | tf_op jit(solution)/shard_map/ppermute | solution.py:587
  125.9 0.9 copy-start.11
  128.6 1.9 %copy-start.12 = (bf16[2,512,256]{2,1,0:T(8,128)(2,1)}, bf16[2,512,256]{2,1,0:T(8,128)(2,1)S(1)}, u32[]{:S(2)}) copy-start(bf16[2,512,256]{2,1,0:T(8,128)(2,1)S(1)} %collective-permute-done.11.h_low) | copy-start | bytes 1572868
  130.5 0.8 copy-start.13
  159.1 12.1 %all-to-all-start.2 = ((f32[8,24,128]{2,1,0:T(8,128)}), f32[8,24,128]{2,1,0:T(8,128)S(1)}, u32[]{:S(2)}, u32[]{:S(2)}) async-start(f32[8,24,128]{2,1,0:T(8,128)} %project.1), calls=%async_computation.2 | async-start | bytes 196608 | tf_op jit(solution)/shard_map/all_to_all | solution.py:667
  171.2 0.6 copy-start.10
where the time goes:
time: 182 us; the launch traced here: 180 us
  waiting for transfers between devices  67.3 us (37%)
  starting transfers between devices  47.6 us (26%)
  Pallas kernels  45.8 us (25%)
  local copies, waits for them, and re-layouts  9.65 us (5%)
  other arithmetic  8.42 us (5%)
    ppermute x5, waiting for transfers between devices, move(): return lax.ppermute(block, 'col', pairs)  31.1 us
    ppermute x6, waiting for transfers between devices, swap_along(): return lax.ppermute(block, 'col', pairs)  23.6 us
    pallas_call x1, Pallas kernels, chebyshev(): pl.pallas_call(functools.partial(cheb_kernel, blocks), out_shape=jax.Shap...  22.2 us
    all_to_all x2, starting transfers between devices, between_lines(): lax.all_to_all(after(block, *others), 'col', split_axis=0, concat_axis=0,...  16.1 us
    ppermute x4, starting transfers between devices, shift(): return lax.ppermute(block, axis, pairs)  10.8 us
    ppermute x5, starting transfers between devices, move(): return lax.ppermute(block, 'col', pairs)  8.39 us
    pallas_call x1, Pallas kernels, update(): pl.pallas_call(functools.partial(update_kernel, blocks, tiles), out_shape...  7.82 us
    ppermute x6, starting transfers between devices, swap_along(): return lax.ppermute(block, 'col', pairs)  7.36 us
  transfers between devices with their start and end apart: 18, of which 8 were waited for; matrix products, arithmetic and copies ran while one was open for 8% of the time, Pallas kernels for 17%

commit v1 on v0

--- a/solution.py
+++ b/solution.py
@@ -19,6 +19,7 @@
 
 exchange_factor = (3.0 / math.pi) ** (1.0 / 3.0)
 HBM = pl.BlockSpec(memory_space=pltpu.HBM)
+ANY = pl.BlockSpec(memory_space=pl.ANY)
 SMEM = pl.BlockSpec(memory_space=pltpu.SMEM)
 VMEM = pl.BlockSpec(memory_space=pltpu.VMEM)
 
@@ -80,96 +81,97 @@
     return partner(home % inner, owner % inner, inner) * outer + home // inner
 
 
-def pack_kernel(entries, col_count, me, peers, basis, first, *refs):
+def pack_kernel(entries, col_count, wanted, me, peers, basis, first, *refs):
     outer, inner = lines_of(col_count)
-    *sent, held, count, in_sems, out_sems = refs
-
-    def fetch(e):
-        return pltpu.make_async_copy(basis.at[e], held.at[e], in_sems.at[e])
-
-    def send(e, p, k, act):
-        line, place = lax.div(p, inner), lax.rem(p, inner)
-        for t in range(inner):
-            @pl.when(place == partner(lax.rem(me[0], inner), t, inner))
-            def _():
-                target = sent[0].at[line, k] if t == 0 else sent[1 + (t - 1) * CAP + k].at[line]
-                act(pltpu.make_async_copy(held.at[e], target, out_sems.at[p, k]))
-
-    for e in range(entries):
-        fetch(e).start()
+    sent, (held, owner, count, in_sems, out_sems) = refs[: len(wanted)], refs[len(wanted) :]
     for c in range(col_count):
         count[c] = 0
+        for k in range(CAP):
+            owner[c * CAP + k] = 0
     for e in range(entries):
         p = peers[e]
-        rank = count[p]
-        count[p] = rank + 1
-        fetch(e).wait()
-        for k in range(CAP):
-            @pl.when(rank == k)
-            def _():
-                send(e, p, k, lambda copy: copy.start())
-    for c in range(col_count):
-        for k in range(CAP):
-            @pl.when(count[c] <= k)
-            def _():
-                send(0, jnp.int32(c), k, lambda copy: copy.start())
-    for c in range(col_count):
-        for k in range(CAP):
-            pltpu.make_async_copy(basis.at[0], held.at[0], out_sems.at[c, k]).wait()
-
-
-def pack(me, peers, basis, first, col_count):
-    outer, inner = lines_of(col_count)
+        k = count[p]
+        count[p] = k + 1
+        owner[p * CAP + k] = e
+    place = lax.rem(me[0], inner)
+    tasks = []
+    for target, group in zip(sent, wanted):
+        for line in range(outer):
+            for i, (t, k) in enumerate(group):
+                n = len(tasks)
+                e = owner[(line * inner + partner(place, t, inner)) * CAP + k]
+                fetch = pltpu.make_async_copy(basis.at[e], held.at[n], in_sems.at[n])
+                store = pltpu.make_async_copy(held.at[n], target.at[line, i], out_sems.at[n])
+                tasks.append((fetch, store))
+    for fetch, _ in tasks:
+        fetch.start()
+    for fetch, store in tasks:
+        fetch.wait()
+        store.start()
+    for _, store in tasks:
+        store.wait()
+
+
+def pack(me, peers, basis, first, col_count, wanted):
+    outer, _ = lines_of(col_count)
     entries = basis.shape[0]
-    shapes = [(outer, CAP)] + [(outer,)] * ((inner - 1) * CAP)
-    return pl.pallas_call(
-        functools.partial(pack_kernel, entries, col_count),
+    number = sum(len(group) for group in wanted) * outer
+    return list(pl.pallas_call(
+        functools.partial(pack_kernel, entries, col_count, wanted),
         out_shape=tuple(
-            jax.ShapeDtypeStruct(shape + basis.shape[1:], basis.dtype) for shape in shapes
+            jax.ShapeDtypeStruct((outer, len(group)) + basis.shape[1:], basis.dtype)
+            for group in wanted
         ),
         in_specs=[SMEM, SMEM, HBM, HBM],
-        out_specs=(HBM,) * len(shapes),
+        out_specs=(HBM,) * len(wanted),
         scratch_shapes=[
-            pltpu.VMEM(basis.shape, basis.dtype),
+            pltpu.VMEM((number,) + basis.shape[1:], basis.dtype),
+            pltpu.SMEM((col_count * CAP,), jnp.int32),
             pltpu.SMEM((col_count,), jnp.int32),
-            pltpu.SemaphoreType.DMA((entries,)),
-            pltpu.SemaphoreType.DMA((col_count, CAP)),
+            pltpu.SemaphoreType.DMA((number,)),
+            pltpu.SemaphoreType.DMA((number,)),
         ],
         compiler_params=pltpu.CompilerParams(vmem_limit_bytes=62 * MIB),
         name="pack",
-    )(me, peers, basis, first)
-
-
-def exchange(sent, awaited):
+    )(me, peers, basis, first))
+
+
+def after(block, *others):
+    return pl.pallas_call(
+        lambda *refs: None,
+        out_shape=jax.ShapeDtypeStruct(block.shape, block.dtype),
+        in_specs=[HBM] + [ANY] * len(others),
+        out_specs=HBM,
+        input_output_aliases={0: 0},
+        compiler_params=pltpu.CompilerParams(vmem_limit_bytes=MIB),
+        name="after",
+    )(block, *others)
+
+
+def exchange(me, peers, basis, own, awaited):
     count = lax.axis_size("col")
     outer, inner = lines_of(count)
     groups = [[line * inner + place for line in range(outer)] for place in range(inner)]
 
-    def between_lines(block, *others):
+    def between_lines(blocks, *others):
+        block = jnp.concatenate(blocks, axis=1)
         return lax.all_to_all(
             after(block, *others), "col", split_axis=0, concat_axis=0,
             axis_index_groups=groups, tiled=True,
         )
 
-    swapped = [
-        [swap_along(sent[1 + (t - 1) * CAP + k], t) for k in range(CAP)] for t in range(1, inner)
-    ]
-    parts = [between_lines(sent[0], *awaited, *[blocks[0] for blocks in swapped])]
-    for blocks in swapped:
-        parts.append(between_lines(jnp.stack(blocks, axis=1), parts[-1]))
+    here = [(0, k) for k in range(CAP)]
+    ahead = [[(t, 0)] for t in range(1, inner)]
+    rest = [[(t, k)] for k in range(1, CAP) for t in range(1, inner)]
+    sent = pack(me, peers, basis, own, count, ahead) if ahead else []
+    to_lines, *later = pack(me, peers, basis, sent[0] if ahead else own, count, [here] + rest)
+    swapped = {
+        group[0]: swap_along(block, group[0][0]) for block, group in zip(sent + later, ahead + rest)
+    }
+    parts = [between_lines([to_lines], *awaited, *[swapped[group[0]] for group in ahead])]
+    for t in range(1, inner):
+        parts.append(between_lines([swapped[t, k] for k in range(CAP)], parts[-1]))
     return [part.reshape((outer * CAP,) + part.shape[2:]) for part in parts]
-
-
-def after(block, *others):
-    return pl.pallas_call(
-        lambda *refs: None,
-        out_shape=jax.ShapeDtypeStruct(block.shape, block.dtype),
-        in_specs=[HBM] * (1 + len(others)),
-        out_specs=HBM,
-        input_output_aliases={0: 0},
-        compiler_params=pltpu.CompilerParams(vmem_limit_bytes=62 * MIB),
-        name="after",
-    )(block, *others)
 
 
 def gather_pieces(own):
@@ -354,7 +356,7 @@
     return pl.pallas_call(
         functools.partial(cheb_kernel, blocks),
         out_shape=jax.ShapeDtypeStruct(result, jnp.bfloat16),
-        in_specs=[SMEM] * 2 + [HBM] * (5 + len(pieces)),
+        in_specs=[SMEM] * 2 + [ANY] * (5 + len(pieces)),
         out_specs=HBM,
         scratch_shapes=[
             pltpu.VMEM(((blocks + 2 * DEG) * W, cols), jnp.bfloat16),
@@ -368,7 +370,7 @@
             pltpu.SemaphoreType.DMA((len(pieces), held)),
             pltpu.SemaphoreType.DMA((result[0],)),
         ],
-        compiler_params=pltpu.CompilerParams(vmem_limit_bytes=62 * MIB),
+        compiler_params=pltpu.CompilerParams(vmem_limit_bytes=48 * MIB),
         cost_estimate=pl.CostEstimate(flops=flops, bytes_accessed=16 * MIB, transcendentals=0),
         name="chebyshev",
     )(coefficients, owners, v_low, v_mid, v_high, h_low, h_high, *pieces)
@@ -473,7 +475,7 @@
             pltpu.SemaphoreType.DMA((blocks,)),
             pltpu.SemaphoreType.DMA((slots,)),
         ],
-        compiler_params=pltpu.CompilerParams(vmem_limit_bytes=62 * MIB),
+        compiler_params=pltpu.CompilerParams(vmem_limit_bytes=20 * MIB),
         name="project",
     )(plan, order, kernel_t, core, *parts)
 
@@ -576,7 +578,7 @@
             pltpu.SemaphoreType.DMA((slots,)),
             pltpu.SemaphoreType.DMA((blocks,)),
         ],
-        compiler_params=pltpu.CompilerParams(vmem_limit_bytes=62 * MIB),
+        compiler_params=pltpu.CompilerParams(vmem_limit_bytes=24 * MIB),
         name="update",
     )(plan, order, tile_of, contributions, collect, *parts)
 
@@ -651,10 +653,9 @@
 
     own = own_piece(peers, tile_block, tile_count, band_pattern, hamiltonian.reshape(-1, W))
     pieces, owners, awaited = gather_pieces(own)
-    parts = exchange(pack(me[None], peers, basis_values, own, col_count), awaited)
-
     v_low = shift(start_columns[-DEG * W :], "row", 1)
     v_high = shift(start_columns[: DEG * W], "row", -1)
+    parts = exchange(me[None], peers, basis_values, own, awaited + [v_low, v_high])
 
     first, last, lists = edge_blocks(owners, pieces, col_count, DEG - 1)
     h_low = shift(last, "row", 1)

time: 182 us -> 182 us (level)
  the two profiles are of different devices: /device:TPU:2 before, /device:TPU:1 now
where the time goes in v1:
time: 182 us; the launch traced here: 181 us
  waiting for transfers between devices  75.2 us (41%)
  Pallas kernels  45.9 us (25%)
  starting transfers between devices  37.1 us (20%)
  local copies, waits for them, and re-layouts  13.2 us (7%)
  other arithmetic  8.32 us (5%)
    ppermute x5, waiting for transfers between devices, move(): return lax.ppermute(block, 'col', pairs)  34.5 us
    pallas_call x1, Pallas kernels, chebyshev(): pl.pallas_call(functools.partial(cheb_kernel, blocks), out_shape=jax.Shap...  21.8 us
    ppermute x6, waiting for transfers between devices, swap_along(): return lax.ppermute(block, 'col', pairs)  16.2 us
    ppermute x4, waiting for transfers between devices, shift(): return lax.ppermute(block, axis, pairs)  14.3 us
    ppermute x4, starting transfers between devices, shift(): return lax.ppermute(block, axis, pairs)  12.2 us
    all_to_all x2, starting transfers between devices, between_lines(): lax.all_to_all(after(block, *others), 'col', split_axis=0, concat_axis=0,...  9.56 us
    unnamed x20, local copies, waits for them, and re-layouts  8.23 us
    pallas_call x1, Pallas kernels, update(): pl.pallas_call(functools.partial(update_kernel, blocks, tiles), out_shape...  7.07 us
  transfers between devices with their start and end apart: 18, of which 11 were waited for; matrix products, arithmetic and copies ran while one was open for 7% of the time, Pallas kernels for 17%

profile of v1, /device:TPU:1, one launch (start us, length us, event | category | flops | bytes accessed | tf_op | source)
XLA Modules:
  0.0 180.7 jit_solution(15675955881669397416)
XLA Ops:
  0.6 2.6 %own_piece.1.refs_0_.first = bf16[1040,256]{1,0:T(8,128)(2,1)} custom-call(s32[16]{0:T(128)} %bitcast.34, s32[16]{0:T(128)} %named.1, s32[4]{0:T(128)} %counts.1, s32[2]{0:T(128)} %pattern.1, bf16[1024,256]{1,0:T(8,128)(2,1)} %bitcast.29), custom_call_target="tpu_custom_call" | custom-call | tf_op jit(solution)/shard_map/own_piece/pallas_call | solution.py:56
  3.2 2.2 %collective-permute-start.1 = (bf16[1040,256]{1,0:T(8,128)(2,1)}, bf16[1040,256]{1,0:T(8,128)(2,1)}, u32[]{:S(2)}, u32[]{:S(2)}) collective-permute-start(bf16[1040,256]{1,0:T(8,128)(2,1)} %own_piece.1.refs_0_.first), channel_id=1, source_target_pairs={{0,2},{1,3},{2,0},{3,1},{4,6},{5,7},{6,4},{7,5},{8,10},{9,11},{10,... | collective-permute-start | bytes 1597448 | tf_op jit(solution)/shard_map/ppermute | solution.py:185
  6.9 2.8 %pack.2.first = bf16[4,1,2,512,128]{4,3,2,1,0:T(8,128)(2,1)} custom-call(s32[1]{0:T(128)} %bitcast.11.me, s32[16]{0:T(128)} %bitcast.35, bf16[16,2,512,128]{3,2,1,0:T(8,128)(2,1)} %basis.3, bf16[1040,256]{1,0:T(8,128)(2,1)} %own_piece.1.refs_0_.first), custom_call_target="tpu_custom_call" | custom-call | tf_op jit(solution)/shard_map/pack/pallas_call | solution.py:119
  11.0 2.6 %fusion.12 = (bf16[768,512]{1,0:T(8,128)(2,1)}, bf16[768,512]{1,0:T(8,128)(2,1)}) fusion(bf16[4096,512]{1,0:T(8,128)(2,1)} %v_mid.1), kind=kLoop, calls=%fused_computation.55 | loop fusion | bytes 3145728 | tf_op jit(solution)/shard_map/slice | solution.py:657
  13.6 4.2 %collective-permute-start.9 = (bf16[768,512]{1,0:T(8,128)(2,1)}, bf16[768,512]{1,0:T(8,128)(2,1)}, u32[]{:S(2)}, u32[]{:S(2)}) collective-permute-start(bf16[768,512]{1,0:T(8,128)(2,1)} %get-tuple-element.19), channel_id=1, source_target_pairs={{0,8},{8,16},{16,24},{1,9},{9,17},{17,25},{2,10},{10,18},{18,26},{... | collective-permute-start | bytes 2359304 | tf_op jit(solution)/shard_map/ppermute | solution.py:589
  17.9 1.9 %collective-permute-start.10 = (bf16[768,512]{1,0:T(8,128)(2,1)}, bf16[768,512]{1,0:T(8,128)(2,1)}, u32[]{:S(2)}, u32[]{:S(2)}) collective-permute-start(bf16[768,512]{1,0:T(8,128)(2,1)} %get-tuple-element.18), channel_id=1, source_target_pairs={{8,0},{16,8},{24,16},{9,1},{17,9},{25,17},{10,2},{18,10},{26,18},{... | collective-permute-start | bytes 2359304 | tf_op jit(solution)/shard_map/ppermute | solution.py:589
  21.8 3.6 %pack.3 = (bf16[4,2,2,512,128]{4,3,2,1,0:T(8,128)(2,1)}, bf16[4,1,2,512,128]{4,3,2,1,0:T(8,128)(2,1)}) custom-call(s32[1]{0:T(128)} %bitcast.11.me, s32[16]{0:T(128)} %bitcast.36, bf16[16,2,512,128]{3,2,1,0:T(8,128)(2,1)} %basis.3, bf16[4,1,2,512,128]{4,3,2,1,0:T(8,128)(2,1)} %pack.2.first), custom_call_target="tpu_custom_call" | custom-call | tf_op jit(solution)/shard_map/pack/pallas_call | solution.py:119
  25.4 1.7 collective-permute-done.9.v_low.refs_3_
  27.1 4.7 %collective-permute-done.10.v_high.refs_4_ = bf16[768,512]{1,0:T(8,128)(2,1)} collective-permute-done((bf16[768,512]{1,0:T(8,128)(2,1)}, bf16[768,512]{1,0:T(8,128)(2,1)}, u32[]{:S(2)}, u32[]{:S(2)}) %collective-permute-start.10) | collective-permute-done | bytes 786464 | tf_op jit(solution)/shard_map/ppermute | solution.py:589
  31.8 2.0 %collective-permute-done.13.refs_5_ = bf16[4,1,2,512,128]{4,3,2,1,0:T(8,128)(2,1)S(1)} collective-permute-done((bf16[4,1,2,512,128]{4,3,2,1,0:T(8,128)(2,1)}, bf16[4,1,2,512,128]{4,3,2,1,0:T(8,128)(2,1)S(1)}, u32[]{:S(2)}, u32[]{:S(2)}) %collective-permute-start.13) | collective-permute-done | bytes 1048608 | tf_op jit(solution)/shard_map/ppermute | solution.py:76
  33.8 3.3 %collective-permute-done.4.refs_2_ = bf16[1040,256]{1,0:T(8,128)(2,1)} collective-permute-done((bf16[1040,256]{1,0:T(8,128)(2,1)}, bf16[1040,256]{1,0:T(8,128)(2,1)}, u32[]{:S(2)}, u32[]{:S(2)}) %collective-permute-start.4) | collective-permute-done | bytes 532512 | tf_op jit(solution)/shard_map/ppermute | solution.py:185
  37.1 1.8 copy-done.2
  40.2 5.1 %all-to-all-start = ((bf16[4,2,2,512,128]{4,3,2,1,0:T(8,128)(2,1)}), bf16[4,2,2,512,128]{4,3,2,1,0:T(8,128)(2,1)S(1)}, u32[]{:S(2)}, u32[]{:S(2)}) async-start(bf16[4,2,2,512,128]{4,3,2,1,0:T(8,128)(2,1)} %copy-done.3), calls=%async_computation | async-start | bytes 4194304 | tf_op jit(solution)/shard_map/all_to_all | solution.py:158
  48.2 2.2 %add.189.refs_4_ = bf16[1040,256]{1,0:T(8,128)(2,1)} add(bf16[1040,256]{1,0:T(8,128)(2,1)} %collective-permute-done.3, bf16[1040,256]{1,0:T(8,128)(2,1)} %collective-permute-done.4.refs_2_) | non-fusion elementwise | flops 266240 | bytes 1597440 | tf_op jit(solution)/shard_map/add | solution.py:198
  51.8 31.2 %collective-permute-done.7 = bf16[1040,256]{1,0:T(8,128)(2,1)S(1)} collective-permute-done((bf16[1040,256]{1,0:T(8,128)(2,1)}, bf16[1040,256]{1,0:T(8,128)(2,1)S(1)}, u32[]{:S(2)}, u32[]{:S(2)}) %collective-permute-start.7) | collective-permute-done | bytes 532512 | tf_op jit(solution)/shard_map/ppermute | solution.py:185
  83.0 2.0 %add.190.refs_6_ = bf16[1040,256]{1,0:T(8,128)(2,1)} add(bf16[1040,256]{1,0:T(8,128)(2,1)} %copy-done.5, bf16[1040,256]{1,0:T(8,128)(2,1)S(1)} %collective-permute-done.7) | non-fusion elementwise | flops 266240 | bytes 1597440 | tf_op jit(solution)/shard_map/add | solution.py:199
  86.0 2.8 %pad_maximum_fusion.refs_0_ = bf16[4,2,2,512,128]{4,3,2,1,0:T(8,128)(2,1)} fusion(bf16[4,1,2,512,128]{4,3,2,1,0:T(8,128)(2,1)} %collective-permute-done.14, bf16[4,1,2,512,128]{4,3,2,1,0:T(8,128)(2,1)S(1)} %collective-permute-done.13.refs_5_), kind=kLoop, calls=%fused_computation | loop fusion | flops 1048576 | bytes 4194304 | tf_op jit(solution)/shard_map/concatenate | solution.py:157
  88.8 4.3 %all-to-all-done.refs_1_ = bf16[4,2,2,512,128]{4,3,2,1,0:T(8,128)(2,1)S(1)} async-done(((bf16[4,2,2,512,128]{4,3,2,1,0:T(8,128)(2,1)}), bf16[4,2,2,512,128]{4,3,2,1,0:T(8,128)(2,1)S(1)}, u32[]{:S(2)}, u32[]{:S(2)}) %all-to-all-start) | async-done | bytes 2097184 | tf_op jit(solution)/shard_map/all_to_all | solution.py:158
  95.9 4.4 %all-to-all-start.1 = ((bf16[4,2,2,512,128]{4,3,2,1,0:T(8,128)(2,1)}), bf16[4,2,2,512,128]{4,3,2,1,0:T(8,128)(2,1)}, u32[]{:S(2)}, u32[]{:S(2)}) async-start(bf16[4,2,2,512,128]{4,3,2,1,0:T(8,128)(2,1)} %copy-done.1), calls=%async_computation.1 | async-start | bytes 4194304 | tf_op jit(solution)/shard_map/all_to_all | solution.py:158
  100.4 2.8 %collective-permute-done.5.refs_5_ = bf16[1040,256]{1,0:T(8,128)(2,1)} collective-permute-done((bf16[1040,256]{1,0:T(8,128)(2,1)}, bf16[1040,256]{1,0:T(8,128)(2,1)}, u32[]{:S(2)}, u32[]{:S(2)}) %collective-permute-start.5) | collective-permute-done | bytes 532512 | tf_op jit(solution)/shard_map/ppermute | solution.py:76
  103.2 11.4 %collective-permute-done.8.refs_7_ = bf16[1040,256]{1,0:T(8,128)(2,1)} collective-permute-done((bf16[1040,256]{1,0:T(8,128)(2,1)}, bf16[1040,256]{1,0:T(8,128)(2,1)}, u32[]{:S(2)}, u32[]{:S(2)}) %collective-permute-start.8) | collective-permute-done | bytes 532512 | tf_op jit(solution)/shard_map/ppermute | solution.py:76
  114.7 3.0 %edge_blocks.1 = (bf16[2,512,256]{2,1,0:T(8,128)(2,1)}, bf16[2,512,256]{2,1,0:T(8,128)(2,1)}, bf16[8,16,256]{2,1,0:T(8,128)(2,1)}) custom-call(s32[8]{0:T(128)} %stack.35.owners, bf16[1040,256]{1,0:T(8,128)(2,1)} %own_piece.1.refs_0_.first, bf16[1040,256]{1,0:T(8,128)(2,1)} %collective-permute-done.refs_1_, ...), custom_call_target="tpu_custom_call" | custom-call | tf_op jit(solution)/shard_map/edge_blocks/pallas_call | solution.py:247
  119.6 4.2 %collective-permute-start.11 = (bf16[2,512,256]{2,1,0:T(8,128)(2,1)}, bf16[2,512,256]{2,1,0:T(8,128)(2,1)S(1)}, u32[]{:S(2)}, u32[]{:S(2)}) collective-permute-start(bf16[2,512,256]{2,1,0:T(8,128)(2,1)} %get-tuple-element.8), channel_id=1, source_target_pairs={{0,8},{8,16},{16,24},{1,9},{9,17},{17,25},{2,10},{10,18},{18,26},{... | collective-permute-start | bytes 1572872 | tf_op jit(solution)/shard_map/ppermute | solution.py:589
  123.7 1.9 %collective-permute-start.12 = (bf16[2,512,256]{2,1,0:T(8,128)(2,1)}, bf16[2,512,256]{2,1,0:T(8,128)(2,1)S(1)}, u32[]{:S(2)}, u32[]{:S(2)}) collective-permute-start(bf16[2,512,256]{2,1,0:T(8,128)(2,1)} %get-tuple-element.9), channel_id=1, source_target_pairs={{8,0},{16,8},{24,16},{9,1},{17,9},{25,17},{10,2},{18,10},{26,18},{... | collective-permute-start | bytes 1572872 | tf_op jit(solution)/shard_map/ppermute | solution.py:589
  126.5 3.7 %collective-permute-done.11.h_low = bf16[2,512,256]{2,1,0:T(8,128)(2,1)S(1)} collective-permute-done((bf16[2,512,256]{2,1,0:T(8,128)(2,1)}, bf16[2,512,256]{2,1,0:T(8,128)(2,1)S(1)}, u32[]{:S(2)}, u32[]{:S(2)}) %collective-permute-start.11) | collective-permute-done | bytes 524320 | tf_op jit(solution)/shard_map/ppermute | solution.py:589
  130.2 4.3 %collective-permute-done.12.h_high = bf16[2,512,256]{2,1,0:T(8,128)(2,1)S(1)} collective-permute-done((bf16[2,512,256]{2,1,0:T(8,128)(2,1)}, bf16[2,512,256]{2,1,0:T(8,128)(2,1)S(1)}, u32[]{:S(2)}, u32[]{:S(2)}) %collective-permute-start.12) | collective-permute-done | bytes 524320 | tf_op jit(solution)/shard_map/ppermute | solution.py:589
  134.5 21.8 %chebyshev.1.kernel_t = bf16[8,512,512]{2,1,0:T(8,128)(2,1)} custom-call(f32[4]{0:T(128)S(1)} %copy-done.8, s32[8]{0:T(128)S(1)} %copy-done.7, bf16[768,512]{1,0:T(8,128)(2,1)} %collective-permute-done.9.v_low.refs_3_, bf16[4096,512]{1,0:T(8,128)(2,1)} %v_mid.1, bf16[768,512]{1,0:T(8,128)(2,1)} %collective-permute-done.10.v_high.refs_4_, ...), custom_call_target="tpu_custom_call" | custom-call | flops 10871635968 | bytes 16777216 | tf_op jit(solution)/shard_map/chebyshev/pallas_call | solution.py:356
  156.3 2.2 %copy-done.4 = bf16[8,512,512]{2,1,0:T(8,128)(2,1)S(1)} copy-done((bf16[8,512,512]{2,1,0:T(8,128)(2,1)S(1)}, bf16[8,512,512]{2,1,0:T(8,128)(2,1)}, u32[]{:S(2)}) %copy-start.4) | copy-done | bytes 4194328
  158.4 5.1 %project.1 = f32[8,24,128]{2,1,0:T(8,128)} custom-call(s32[26]{0:T(128)S(1)} %pad_add_fusion.1.plan, s32[16]{0:T(128)S(1)} %select_reduce_fusion.2.order, bf16[8,512,512]{2,1,0:T(8,128)(2,1)S(1)} %copy-done.4, f32[4,128]{1,0:T(4,128)S(1)} %copy-done.6, bf16[8,2,512,128]{3,2,1,0:T(8,128)(2,1)S(1)} %bitcast.26, bf16[8,2,512,128]{3,2,1,0:T(8,128)(2,1)} %bitcast.13.refs_1_), custom_call_target="tpu_custom_call" | custom-call | tf_op jit(solution)/shard_map/project/pallas_call | solution.py:466
  163.6 4.1 %all-to-all-start.2 = ((f32[8,24,128]{2,1,0:T(8,128)}), f32[8,24,128]{2,1,0:T(8,128)S(1)}, u32[]{:S(2)}, u32[]{:S(2)}) async-start(f32[8,24,128]{2,1,0:T(8,128)} %project.1), calls=%async_computation.2 | async-start | bytes 196608 | tf_op jit(solution)/shard_map/all_to_all | solution.py:668
  167.8 5.9 %all-to-all-done.2 = f32[8,24,128]{2,1,0:T(8,128)S(1)} async-done(((f32[8,24,128]{2,1,0:T(8,128)}), f32[8,24,128]{2,1,0:T(8,128)S(1)}, u32[]{:S(2)}, u32[]{:S(2)}) %all-to-all-start.2) | async-done | bytes 98336 | tf_op jit(solution)/shard_map/all_to_all | solution.py:668
  173.7 7.1 %update.1 = (f32[4,128]{1,0:T(4,128)}, bf16[4096,512]{1,0:T(8,128)(2,1)}) custom-call(s32[26]{0:T(128)S(1)} %pad_add_fusion.1.plan, s32[16]{0:T(128)S(1)} %select_reduce_fusion.2.order, s32[16]{0:T(128)S(1)} %reshape.285.tile_of, f32[192,128]{1,0:T(8,128)S(1)} %bitcast.28, f32[32,192]{1,0:T(8,128)S(1)} %convert_reduce_fusion.collect, ...), custom_call_target="tpu_custom_call" | custom-call | tf_op jit(solution)/shard_map/update/pallas_call | solution.py:564
  (77 shorter events, 17.0 us)
Async XLA Ops:
  3.2 17.9 %collective-permute-start.1 = (bf16[1040,256]{1,0:T(8,128)(2,1)}, bf16[1040,256]{1,0:T(8,128)(2,1)}, u32[]{:S(2)}, u32[]{:S(2)}) collective-permute-start(bf16[1040,256]{1,0:T(8,128)(2,1)} %own_piece.1.refs_0_.first), channel_id=1, source_target_pairs={{0,2},{1,3},{2,0},{3,1},{4,6},{5,7},{6,4},{7,5},{8,10},{9,11},{10,... | collective-permute-start | bytes 1597448 | tf_op jit(solution)/shard_map/ppermute | solution.py:185
  5.4 14.4 %collective-permute-start.3 = (bf16[1040,256]{1,0:T(8,128)(2,1)}, bf16[1040,256]{1,0:T(8,128)(2,1)}, u32[]{:S(2)}, u32[]{:S(2)}) collective-permute-start(bf16[1040,256]{1,0:T(8,128)(2,1)} %own_piece.1.refs_0_.first), channel_id=1, source_target_pairs={{2,4},{3,5},{4,2},{5,3},{10,12},{11,13},{12,10},{13,11},{18,20},{1... | collective-permute-start | bytes 1597448 | tf_op jit(solution)/shard_map/ppermute | solution.py:185
  9.7 24.1 %collective-permute-start.13 = (bf16[4,1,2,512,128]{4,3,2,1,0:T(8,128)(2,1)}, bf16[4,1,2,512,128]{4,3,2,1,0:T(8,128)(2,1)S(1)}, u32[]{:S(2)}, u32[]{:S(2)}) collective-permute-start(bf16[4,1,2,512,128]{4,3,2,1,0:T(8,128)(2,1)} %pack.2.first), channel_id=1, source_target_pairs={{0,1},{1,0},{2,3},{3,2},{4,5},{5,4},{6,7},{7,6},{8,9},{9,8},{10,11... | collective-permute-start | bytes 3145736 | tf_op jit(solution)/shard_map/ppermute | solution.py:76
  13.6 13.5 %collective-permute-start.9 = (bf16[768,512]{1,0:T(8,128)(2,1)}, bf16[768,512]{1,0:T(8,128)(2,1)}, u32[]{:S(2)}, u32[]{:S(2)}) collective-permute-start(bf16[768,512]{1,0:T(8,128)(2,1)} %get-tuple-element.19), channel_id=1, source_target_pairs={{0,8},{8,16},{16,24},{1,9},{9,17},{17,25},{2,10},{10,18},{18,26},{... | collective-permute-start | bytes 2359304 | tf_op jit(solution)/shard_map/ppermute | solution.py:589
  17.9 13.9 %collective-permute-start.10 = (bf16[768,512]{1,0:T(8,128)(2,1)}, bf16[768,512]{1,0:T(8,128)(2,1)}, u32[]{:S(2)}, u32[]{:S(2)}) collective-permute-start(bf16[768,512]{1,0:T(8,128)(2,1)} %get-tuple-element.18), channel_id=1, source_target_pairs={{8,0},{16,8},{24,16},{9,1},{17,9},{25,17},{10,2},{18,10},{26,18},{... | collective-permute-start | bytes 2359304 | tf_op jit(solution)/shard_map/ppermute | solution.py:589
  19.8 17.2 %collective-permute-start.4 = (bf16[1040,256]{1,0:T(8,128)(2,1)}, bf16[1040,256]{1,0:T(8,128)(2,1)}, u32[]{:S(2)}, u32[]{:S(2)}) collective-permute-start(bf16[1040,256]{1,0:T(8,128)(2,1)} %collective-permute-done.3), channel_id=1, source_target_pairs={{2,0},{3,1},{4,6},{5,7},{10,8},{11,9},{12,14},{13,15},{18,16},{19,... | collective-permute-start | bytes 1597448 | tf_op jit(solution)/shard_map/ppermute | solution.py:185
  21.1 15.9 %collective-permute-start.6 = (bf16[1040,256]{1,0:T(8,128)(2,1)}, bf16[1040,256]{1,0:T(8,128)(2,1)S(1)}, u32[]{:S(2)}, u32[]{:S(2)}) collective-permute-start(bf16[1040,256]{1,0:T(8,128)(2,1)} %collective-permute-done.1.refs_2_), channel_id=1, source_target_pairs={{2,4},{3,5},{4,2},{5,3},{10,12},{11,13},{12,10},{13,11},{18,20},{1... | collective-permute-start | bytes 1597448 | tf_op jit(solution)/shard_map/ppermute | solution.py:185
  37.0 3.1 %copy-start.5 = (bf16[1040,256]{1,0:T(8,128)(2,1)}, bf16[1040,256]{1,0:T(8,128)(2,1)S(1)}, u32[]{:S(2)}) copy-start(bf16[1040,256]{1,0:T(8,128)(2,1)S(1)} %collective-permute-done.6.refs_1_) | copy-start | bytes 1597444
  37.0 1.8 copy-start.2
  38.8 1.3 copy-start.3
  40.2 52.9 %all-to-all-start = ((bf16[4,2,2,512,128]{4,3,2,1,0:T(8,128)(2,1)}), bf16[4,2,2,512,128]{4,3,2,1,0:T(8,128)(2,1)S(1)}, u32[]{:S(2)}, u32[]{:S(2)}) async-start(bf16[4,2,2,512,128]{4,3,2,1,0:T(8,128)(2,1)} %copy-done.3), calls=%async_computation | async-start | bytes 4194304 | tf_op jit(solution)/shard_map/all_to_all | solution.py:158
  45.3 40.7 %collective-permute-start.14 = (bf16[4,1,2,512,128]{4,3,2,1,0:T(8,128)(2,1)}, bf16[4,1,2,512,128]{4,3,2,1,0:T(8,128)(2,1)}, u32[]{:S(2)}, u32[]{:S(2)}) collective-permute-start(bf16[4,1,2,512,128]{4,3,2,1,0:T(8,128)(2,1)} %get-tuple-element.11), channel_id=1, source_target_pairs={{0,1},{1,0},{2,3},{3,2},{4,5},{5,4},{6,7},{7,6},{8,9},{9,8},{10,11... | collective-permute-start | bytes 3145736 | tf_op jit(solution)/shard_map/ppermute | solution.py:76
  45.3 55.1 %collective-permute-start = (bf16[1040,256]{1,0:T(8,128)(2,1)}, bf16[1040,256]{1,0:T(8,128)(2,1)}, u32[]{:S(2)}, u32[]{:S(2)}) collective-permute-start(bf16[1040,256]{1,0:T(8,128)(2,1)} %own_piece.1.refs_0_.first), channel_id=1, source_target_pairs={{0,1},{1,0},{2,3},{3,2},{4,5},{5,4},{6,7},{7,6},{8,9},{9,8},{10,11... | collective-permute-start | bytes 1597448 | tf_op jit(solution)/shard_map/ppermute | solution.py:76
  46.7 36.3 %collective-permute-start.7 = (bf16[1040,256]{1,0:T(8,128)(2,1)}, bf16[1040,256]{1,0:T(8,128)(2,1)S(1)}, u32[]{:S(2)}, u32[]{:S(2)}) collective-permute-start(bf16[1040,256]{1,0:T(8,128)(2,1)} %copy-done.5), channel_id=1, source_target_pairs={{2,0},{3,1},{4,6},{5,7},{10,8},{11,9},{12,14},{13,15},{18,16},{19,... | collective-permute-start | bytes 1597448 | tf_op jit(solution)/shard_map/ppermute | solution.py:185
  48.1 52.3 %collective-permute-start.2 = (bf16[1040,256]{1,0:T(8,128)(2,1)}, bf16[1040,256]{1,0:T(8,128)(2,1)}, u32[]{:S(2)}, u32[]{:S(2)}) collective-permute-start(bf16[1040,256]{1,0:T(8,128)(2,1)} %collective-permute-done.1.refs_2_), channel_id=1, source_target_pairs={{0,1},{1,0},{2,3},{3,2},{4,5},{5,4},{6,7},{7,6},{8,9},{9,8},{10,11... | collective-permute-start | bytes 1597448 | tf_op jit(solution)/shard_map/ppermute | solution.py:76
  50.4 52.9 %collective-permute-start.5 = (bf16[1040,256]{1,0:T(8,128)(2,1)}, bf16[1040,256]{1,0:T(8,128)(2,1)}, u32[]{:S(2)}, u32[]{:S(2)}) collective-permute-start(bf16[1040,256]{1,0:T(8,128)(2,1)} %add.189.refs_4_), channel_id=1, source_target_pairs={{0,1},{1,0},{2,3},{3,2},{4,5},{5,4},{6,7},{7,6},{8,9},{9,8},{10,11... | collective-permute-start | bytes 1597448 | tf_op jit(solution)/shard_map/ppermute | solution.py:76
  85.0 29.6 %collective-permute-start.8 = (bf16[1040,256]{1,0:T(8,128)(2,1)}, bf16[1040,256]{1,0:T(8,128)(2,1)}, u32[]{:S(2)}, u32[]{:S(2)}) collective-permute-start(bf16[1040,256]{1,0:T(8,128)(2,1)} %add.190.refs_6_), channel_id=1, source_target_pairs={{0,1},{1,0},{2,3},{3,2},{4,5},{5,4},{6,7},{7,6},{8,9},{9,8},{10,11... | collective-permute-start | bytes 1597448 | tf_op jit(solution)/shard_map/ppermute | solution.py:76
  93.0 1.6 copy-start
  94.6 1.3 copy-start.1
  95.9 60.3 %all-to-all-start.1 = ((bf16[4,2,2,512,128]{4,3,2,1,0:T(8,128)(2,1)}), bf16[4,2,2,512,128]{4,3,2,1,0:T(8,128)(2,1)}, u32[]{:S(2)}, u32[]{:S(2)}) async-start(bf16[4,2,2,512,128]{4,3,2,1,0:T(8,128)(2,1)} %copy-done.1), calls=%async_computation.1 | async-start | bytes 4194304 | tf_op jit(solution)/shard_map/all_to_all | solution.py:158
  100.4 34.1 %copy-start.7 = (s32[8]{0:T(128)S(1)}, s32[8]{0:T(128)}, u32[]{:S(2)}) copy-start(s32[8]{0:T(128)} %stack.35.owners) | copy-start | bytes 100
  100.4 34.1 %copy-start.8 = (f32[4]{0:T(128)S(1)}, f32[4]{0:T(128)}, u32[]{:S(2)}) copy-start(f32[4]{0:T(128)} %coef.1) | copy-start | bytes 52
  119.6 10.6 %collective-permute-start.11 = (bf16[2,512,256]{2,1,0:T(8,128)(2,1)}, bf16[2,512,256]{2,1,0:T(8,128)(2,1)S(1)}, u32[]{:S(2)}, u32[]{:S(2)}) collective-permute-start(bf16[2,512,256]{2,1,0:T(8,128)(2,1)} %get-tuple-element.8), channel_id=1, source_target_pairs={{0,8},{8,16},{16,24},{1,9},{9,17},{17,25},{2,10},{10,18},{18,26},{... | collective-permute-start | bytes 1572872 | tf_op jit(solution)/shard_map/ppermute | solution.py:589
  123.7 10.7 %collective-permute-start.12 = (bf16[2,512,256]{2,1,0:T(8,128)(2,1)}, bf16[2,512,256]{2,1,0:T(8,128)(2,1)S(1)}, u32[]{:S(2)}, u32[]{:S(2)}) collective-permute-start(bf16[2,512,256]{2,1,0:T(8,128)(2,1)} %get-tuple-element.9), channel_id=1, source_target_pairs={{8,0},{16,8},{24,16},{9,1},{17,9},{25,17},{10,2},{18,10},{26,18},{... | collective-permute-start | bytes 1572872 | tf_op jit(solution)/shard_map/ppermute | solution.py:589
  126.5 29.7 %copy-start.6 = (f32[4,128]{1,0:T(4,128)S(1)}, f32[4,128]{1,0:T(4,128)}, u32[]{:S(2)}) copy-start(f32[4,128]{1,0:T(4,128)} %core.1) | copy-start | bytes 6148
  156.2 2.2 %copy-start.4 = (bf16[8,512,512]{2,1,0:T(8,128)(2,1)S(1)}, bf16[8,512,512]{2,1,0:T(8,128)(2,1)}, u32[]{:S(2)}) copy-start(bf16[8,512,512]{2,1,0:T(8,128)(2,1)} %chebyshev.1.kernel_t) | copy-start | bytes 12582916
  163.6 10.1 %all-to-all-start.2 = ((f32[8,24,128]{2,1,0:T(8,128)}), f32[8,24,128]{2,1,0:T(8,128)S(1)}, u32[]{:S(2)}, u32[]{:S(2)}) async-start(f32[8,24,128]{2,1,0:T(8,128)} %project.1), calls=%async_computation.2 | async-start | bytes 196608 | tf_op jit(solution)/shard_map/all_to_all | solution.py:668

commit v2 on v1

--- a/solution.py
+++ b/solution.py
@@ -112,15 +112,17 @@
         store.wait()
 
 
-def pack(me, peers, basis, first, col_count, wanted):
+def pack(me, peers, basis, first, col_count, wanted, spare=0):
     outer, _ = lines_of(col_count)
     entries = basis.shape[0]
     number = sum(len(group) for group in wanted) * outer
     return list(pl.pallas_call(
         functools.partial(pack_kernel, entries, col_count, wanted),
         out_shape=tuple(
-            jax.ShapeDtypeStruct((outer, len(group)) + basis.shape[1:], basis.dtype)
-            for group in wanted
+            jax.ShapeDtypeStruct(
+                (outer, len(group) + (spare if i == 0 else 0)) + basis.shape[1:], basis.dtype
+            )
+            for i, group in enumerate(wanted)
         ),
         in_specs=[SMEM, SMEM, HBM, HBM],
         out_specs=(HBM,) * len(wanted),
@@ -136,42 +138,72 @@
     )(me, peers, basis, first))
 
 
-def after(block, *others):
+def join_kernel(fills, block, *refs):
+    sources, (out, held, in_sems, out_sems) = refs[:fills], refs[-4:]
+    units = out.shape[1]
+    loads = [pltpu.make_async_copy(sources[i], held.at[i], in_sems.at[i]) for i in range(fills)]
+    stores = [
+        pltpu.make_async_copy(held.at[i], out.at[:, pl.ds(units - fills + i, 1)], out_sems.at[i])
+        for i in range(fills)
+    ]
+    for load in loads:
+        load.start()
+    for load, store in zip(loads, stores):
+        load.wait()
+        store.start()
+    for store in stores:
+        store.wait()
+
+
+def join(block, fills, *others):
     return pl.pallas_call(
-        lambda *refs: None,
+        functools.partial(join_kernel, len(fills)),
         out_shape=jax.ShapeDtypeStruct(block.shape, block.dtype),
-        in_specs=[HBM] + [ANY] * len(others),
+        in_specs=[HBM] + [ANY] * (len(fills) + len(others)),
         out_specs=HBM,
         input_output_aliases={0: 0},
-        compiler_params=pltpu.CompilerParams(vmem_limit_bytes=MIB),
-        name="after",
-    )(block, *others)
-
-
-def exchange(me, peers, basis, own, awaited):
+        scratch_shapes=[
+            pltpu.VMEM((max(len(fills), 1), block.shape[0], 1) + block.shape[2:], block.dtype),
+            pltpu.SemaphoreType.DMA((max(len(fills), 1),)),
+            pltpu.SemaphoreType.DMA((max(len(fills), 1),)),
+        ],
+        compiler_params=pltpu.CompilerParams(vmem_limit_bytes=62 * MIB),
+        name="join",
+    )(block, *fills, *others)
+
+
+def unit_of(t, k, inner):
+    if t == 0:
+        return 0, k
+    return (0, CAP + t - 1) if k == 0 else (1, (k - 1) * (inner - 1) + t - 1)
+
+
+def exchange(me, peers, basis, own, awaited, handed):
     count = lax.axis_size("col")
     outer, inner = lines_of(count)
     groups = [[line * inner + place for line in range(outer)] for place in range(inner)]
 
-    def between_lines(blocks, *others):
-        block = jnp.concatenate(blocks, axis=1)
+    def between_lines(block):
         return lax.all_to_all(
-            after(block, *others), "col", split_axis=0, concat_axis=0,
-            axis_index_groups=groups, tiled=True,
+            block, "col", split_axis=0, concat_axis=0, axis_index_groups=groups, tiled=True
         )
 
     here = [(0, k) for k in range(CAP)]
     ahead = [[(t, 0)] for t in range(1, inner)]
     rest = [[(t, k)] for k in range(1, CAP) for t in range(1, inner)]
     sent = pack(me, peers, basis, own, count, ahead) if ahead else []
-    to_lines, *later = pack(me, peers, basis, sent[0] if ahead else own, count, [here] + rest)
-    swapped = {
-        group[0]: swap_along(block, group[0][0]) for block, group in zip(sent + later, ahead + rest)
-    }
-    parts = [between_lines([to_lines], *awaited, *[swapped[group[0]] for group in ahead])]
-    for t in range(1, inner):
-        parts.append(between_lines([swapped[t, k] for k in range(CAP)], parts[-1]))
-    return [part.reshape((outer * CAP,) + part.shape[2:]) for part in parts]
+    first, *later = pack(
+        me, peers, basis, sent[0] if ahead else own, count, [here] + rest, spare=len(ahead)
+    )
+    swapped = [swap_along(block, group[0][0]) for block, group in zip(sent, ahead)]
+    parts = [between_lines(join(first, swapped, *awaited))]
+    if rest:
+        swapped = [
+            swap_along(join(block, [], *handed), group[0][0]) for block, group in zip(later, rest)
+        ]
+        last = swapped[0] if len(swapped) == 1 else jnp.concatenate(swapped, axis=1)
+        parts.append(between_lines(join(last, [], parts[0])))
+    return parts
 
 
 def gather_pieces(own):
@@ -198,13 +230,13 @@
             (across + handed, jnp.where(within, a ^ 3, a ^ 2)),
             (far + last, jnp.where(within, a ^ 2, a ^ 3)),
         ]
-        awaited = [far, handed]
+        awaited, end = [far, handed], [last]
     else:
         lines = [(own, a)] + [
             (move(own, [(x, partner(x, t, outer)) for x in range(outer)]), partner(a, -t, outer))
             for t in range(1, outer)
         ]
-        awaited = [block for block, _ in lines[1:]]
+        awaited, end = [block for block, _ in lines[1:]], []
     pieces, owners = [], []
     for block, line in lines:
         pieces.append(block)
@@ -212,7 +244,7 @@
         for t in range(1, inner):
             pieces.append(swap_along(block, t))
             owners.append(line * inner + partner(b, -t, inner))
-    return pieces, jnp.stack(owners).astype(jnp.int32), awaited
+    return pieces, jnp.stack(owners).astype(jnp.int32), awaited, end
 
 
 def edge_kernel(col_count, depth, owners, *refs):
@@ -377,17 +409,23 @@
 
 
 def entry_loads(order, parts, pair, sems):
-    size = parts[0].shape[0]
+    outer, units = parts[0].shape[:2]
+    inner = units - CAP + 1
 
     def load(p):
-        return pltpu.make_async_copy(parts[0].at[0], pair.at[p], sems.at[p])
+        return pltpu.make_async_copy(parts[0].at[0, 0], pair.at[p], sems.at[p])
 
     def start(p, carry):
         n = order[p]
-        for t, part in enumerate(parts):
-            @pl.when((n >= t * size) & (n < (t + 1) * size))
-            def _():
-                pltpu.make_async_copy(part.at[n - t * size], pair.at[p], sems.at[p]).start()
+        line = lax.rem(lax.div(n, CAP), outer)
+        for t in range(inner):
+            for k in range(CAP):
+                part, unit = unit_of(t, k, inner)
+
+                @pl.when((lax.div(n, CAP * outer) == t) & (lax.rem(n, CAP) == k))
+                def _():
+                    source = parts[part].at[line, unit]
+                    pltpu.make_async_copy(source, pair.at[p], sems.at[p]).start()
 
         return carry
 
@@ -460,7 +498,7 @@
 
 def project(plan, order, kernel_t, core, parts, col_count):
     slots = col_count * CAP
-    entry = parts[0].shape[1:]
+    entry = parts[0].shape[2:]
     sent = sent_rows(slots, core.shape[0])
     blocks = kernel_t.shape[0]
     return pl.pallas_call(
@@ -475,7 +513,7 @@
             pltpu.SemaphoreType.DMA((blocks,)),
             pltpu.SemaphoreType.DMA((slots,)),
         ],
-        compiler_params=pltpu.CompilerParams(vmem_limit_bytes=20 * MIB),
+        compiler_params=pltpu.CompilerParams(vmem_limit_bytes=62 * MIB),
         name="project",
     )(plan, order, kernel_t, core, *parts)
 
@@ -557,9 +595,9 @@
         store(b).wait()
 
 
-def update(plan, order, tile_of, contributions, collect, parts, tiles, blocks, cols):
-    slots = len(parts) * parts[0].shape[0]
-    entry = parts[0].shape[1:]
+def update(plan, order, tile_of, contributions, collect, parts, col_count, tiles, blocks, cols):
+    slots = col_count * CAP
+    entry = parts[0].shape[2:]
     all_tiles = (collect.shape[0], P_SIZE)
     return pl.pallas_call(
         functools.partial(update_kernel, blocks, tiles),
@@ -578,7 +616,7 @@
             pltpu.SemaphoreType.DMA((slots,)),
             pltpu.SemaphoreType.DMA((blocks,)),
         ],
-        compiler_params=pltpu.CompilerParams(vmem_limit_bytes=24 * MIB),
+        compiler_params=pltpu.CompilerParams(vmem_limit_bytes=62 * MIB),
         name="update",
     )(plan, order, tile_of, contributions, collect, *parts)
 
@@ -652,10 +690,10 @@
     me = lax.axis_index("col").astype(jnp.int32)
 
     own = own_piece(peers, tile_block, tile_count, band_pattern, hamiltonian.reshape(-1, W))
-    pieces, owners, awaited = gather_pieces(own)
+    pieces, owners, awaited, end = gather_pieces(own)
     v_low = shift(start_columns[-DEG * W :], "row", 1)
     v_high = shift(start_columns[: DEG * W], "row", -1)
-    parts = exchange(me[None], peers, basis_values, own, awaited + [v_low, v_high])
+    parts = exchange(me[None], peers, basis_values, own, awaited + [v_low, v_high], end)
 
     first, last, lists = edge_blocks(owners, pieces, col_count, DEG - 1)
     h_low = shift(last, "row", 1)
@@ -668,7 +706,7 @@
     contributions = lax.all_to_all(partial, "col", split_axis=0, concat_axis=0, tiled=True)
     contributions = contributions.reshape(-1, P_SIZE)
     return update(
-        plan, order, tile_of, contributions, collect, parts, tiles, blocks, cols
+        plan, order, tile_of, contributions, collect, parts, col_count, tiles, blocks, cols
     )
 
 

time: 182 us -> 188 us (1.033)
  the two profiles are of different devices: /device:TPU:1 before, /device:TPU:2 now
where the time goes in v2:
time: 188 us; the launch traced here: 185 us
  waiting for transfers between devices  85.3 us (45%)
  Pallas kernels  46.8 us (25%)
  starting transfers between devices  38.5 us (20%)
  local copies, waits for them, and re-layouts  8.88 us (5%)
  other arithmetic  4.42 us (2%)
    ppermute x5, waiting for transfers between devices, move(): return lax.ppermute(block, 'col', pairs)  45 us
    ppermute x6, waiting for transfers between devices, swap_along(): return lax.ppermute(block, 'col', pairs)  29.1 us
    pallas_call x1, Pallas kernels, chebyshev(): pl.pallas_call(functools.partial(cheb_kernel, blocks), out_shape=jax.Shap...  21.4 us
    ppermute x4, starting transfers between devices, shift(): return lax.ppermute(block, axis, pairs)  11.1 us
    all_to_all x2, starting transfers between devices, between_lines(): lax.all_to_all(block, 'col', split_axis=0, concat_axis=0, axis_index_grou...  10.2 us
    ppermute x6, starting transfers between devices, swap_along(): return lax.ppermute(block, 'col', pairs)  7.01 us
    all_to_all x1, waiting for transfers between devices, shards(): lax.all_to_all(partial, 'col', split_axis=0, concat_axis=0, tiled=True)  6.41 us
    pallas_call x1, Pallas kernels, update(): pl.pallas_call(functools.partial(update_kernel, blocks, tiles), out_shape...  6.36 us
  transfers between devices with their start and end apart: 18, of which 9 were waited for; matrix products, arithmetic and copies ran while one was open for 5% of the time, Pallas kernels for 17%

profile of v2, /device:TPU:2, one launch (start us, length us, event | category | flops | bytes accessed | tf_op | source)
XLA Modules:
  0.0 184.9 jit_solution(11241276501337183956)
XLA Ops:
  0.6 2.6 %own_piece.1.refs_0_.first = bf16[1040,256]{1,0:T(8,128)(2,1)} custom-call(s32[16]{0:T(128)} %bitcast.30, s32[16]{0:T(128)} %named.1, s32[4]{0:T(128)} %counts.1, s32[2]{0:T(128)} %pattern.1, bf16[1024,256]{1,0:T(8,128)(2,1)} %bitcast.24), custom_call_target="tpu_custom_call" | custom-call | tf_op jit(solution)/shard_map/own_piece/pallas_call | solution.py:56
  3.2 1.6 collective-permute-start.1
  5.6 2.8 %pack.2.first = bf16[4,1,2,512,128]{4,3,2,1,0:T(8,128)(2,1)} custom-call(s32[1]{0:T(128)} %bitcast.11.me, s32[16]{0:T(128)} %bitcast.31, bf16[16,2,512,128]{3,2,1,0:T(8,128)(2,1)} %basis.3, bf16[1040,256]{1,0:T(8,128)(2,1)} %own_piece.1.refs_0_.first), custom_call_target="tpu_custom_call" | custom-call | tf_op jit(solution)/shard_map/pack/pallas_call | solution.py:119
  8.3 1.6 collective-permute-start.13
  9.9 2.6 %fusion.12 = (bf16[768,512]{1,0:T(8,128)(2,1)}, bf16[768,512]{1,0:T(8,128)(2,1)}) fusion(bf16[4096,512]{1,0:T(8,128)(2,1)} %v_mid.1), kind=kLoop, calls=%fused_computation.54 | loop fusion | bytes 3145728 | tf_op jit(solution)/shard_map/slice | solution.py:695
  12.5 1.9 %collective-permute-start.9 = (bf16[768,512]{1,0:T(8,128)(2,1)}, bf16[768,512]{1,0:T(8,128)(2,1)S(1)}, u32[]{:S(2)}, u32[]{:S(2)}) collective-permute-start(bf16[768,512]{1,0:T(8,128)(2,1)} %get-tuple-element.19), channel_id=1, source_target_pairs={{0,8},{8,16},{16,24},{1,9},{9,17},{17,25},{2,10},{10,18},{18,26},{... | collective-permute-start | bytes 2359304 | tf_op jit(solution)/shard_map/ppermute | solution.py:627
  14.5 3.6 %collective-permute-start.10 = (bf16[768,512]{1,0:T(8,128)(2,1)}, bf16[768,512]{1,0:T(8,128)(2,1)}, u32[]{:S(2)}, u32[]{:S(2)}) collective-permute-start(bf16[768,512]{1,0:T(8,128)(2,1)} %get-tuple-element.18), channel_id=1, source_target_pairs={{8,0},{16,8},{24,16},{9,1},{17,9},{25,17},{10,2},{18,10},{26,18},{... | collective-permute-start | bytes 2359304 | tf_op jit(solution)/shard_map/ppermute | solution.py:627
  18.1 1.3 collective-permute-start.4
  20.1 3.6 %pack.3 = (bf16[4,3,2,512,128]{4,3,2,1,0:T(8,128)(2,1)}, bf16[4,1,2,512,128]{4,3,2,1,0:T(8,128)(2,1)}) custom-call(s32[1]{0:T(128)} %bitcast.11.me, s32[16]{0:T(128)} %bitcast.32, bf16[16,2,512,128]{3,2,1,0:T(8,128)(2,1)} %basis.3, bf16[4,1,2,512,128]{4,3,2,1,0:T(8,128)(2,1)} %pack.2.first), custom_call_target="tpu_custom_call" | custom-call | tf_op jit(solution)/shard_map/pack/pallas_call | solution.py:119
  23.7 2.4 %collective-permute-done.9.v_low.refs_3_ = bf16[768,512]{1,0:T(8,128)(2,1)S(1)} collective-permute-done((bf16[768,512]{1,0:T(8,128)(2,1)}, bf16[768,512]{1,0:T(8,128)(2,1)S(1)}, u32[]{:S(2)}, u32[]{:S(2)}) %collective-permute-start.9) | collective-permute-done | bytes 786464 | tf_op jit(solution)/shard_map/ppermute | solution.py:627
  26.0 1.9 %collective-permute-done.10.v_high.refs_4_ = bf16[768,512]{1,0:T(8,128)(2,1)} collective-permute-done((bf16[768,512]{1,0:T(8,128)(2,1)}, bf16[768,512]{1,0:T(8,128)(2,1)}, u32[]{:S(2)}, u32[]{:S(2)}) %collective-permute-start.10) | collective-permute-done | bytes 786464 | tf_op jit(solution)/shard_map/ppermute | solution.py:627
  27.9 5.4 %collective-permute-done.13.refs_0_ = bf16[4,1,2,512,128]{4,3,2,1,0:T(8,128)(2,1)} collective-permute-done((bf16[4,1,2,512,128]{4,3,2,1,0:T(8,128)(2,1)}, bf16[4,1,2,512,128]{4,3,2,1,0:T(8,128)(2,1)}, u32[]{:S(2)}, u32[]{:S(2)}) %collective-permute-start.13) | collective-permute-done | bytes 1048608 | tf_op jit(solution)/shard_map/ppermute | solution.py:76
  33.3 2.5 %collective-permute-done.4.refs_2_ = bf16[1040,256]{1,0:T(8,128)(2,1)} collective-permute-done((bf16[1040,256]{1,0:T(8,128)(2,1)S(1)}, bf16[1040,256]{1,0:T(8,128)(2,1)}, u32[]{:S(2)}, u32[]{:S(2)}) %collective-permute-start.4) | collective-permute-done | bytes 532512 | tf_op jit(solution)/shard_map/ppermute | solution.py:217
  36.7 2.2 %join.3 = bf16[4,3,2,512,128]{4,3,2,1,0:T(8,128)(2,1)} custom-call(bf16[4,3,2,512,128]{4,3,2,1,0:T(8,128)(2,1)} %get-tuple-element.10.block, bf16[4,1,2,512,128]{4,3,2,1,0:T(8,128)(2,1)} %collective-permute-done.13.refs_0_, bf16[1040,256]{1,0:T(8,128)(2,1)} %copy-done.10, ...), custom_call_target="tpu_custom_call", output_to_operand_aliasing={{}: (0, {})} | custom-call | tf_op jit(solution)/shard_map/join/pallas_call | solution.py:159
  38.9 6.0 %all-to-all-start = ((bf16[4,3,2,512,128]{4,3,2,1,0:T(8,128)(2,1)}), bf16[4,3,2,512,128]{4,3,2,1,0:T(8,128)(2,1)}, u32[]{:S(2)}, u32[]{:S(2)}) async-start(bf16[4,3,2,512,128]{4,3,2,1,0:T(8,128)(2,1)} %join.3), calls=%async_computation | async-start | bytes 6291456 | tf_op jit(solution)/shard_map/all_to_all | solution.py:187
  44.9 1.2 collective-permute-start
  47.0 1.3 collective-permute-start.7
  49.3 1.2 add.189.refs_4_
  50.5 1.2 collective-permute-start.5
  51.7 42.5 %collective-permute-done.7.refs_0_ = bf16[1040,256]{1,0:T(8,128)(2,1)S(1)} collective-permute-done((bf16[1040,256]{1,0:T(8,128)(2,1)S(1)}, bf16[1040,256]{1,0:T(8,128)(2,1)S(1)}, u32[]{:S(2)}, u32[]{:S(2)}) %collective-permute-start.7) | collective-permute-done | bytes 532512 | tf_op jit(solution)/shard_map/ppermute | solution.py:217
  95.1 2.1 %collective-permute-start.14 = (bf16[4,1,2,512,128]{4,3,2,1,0:T(8,128)(2,1)}, bf16[4,1,2,512,128]{4,3,2,1,0:T(8,128)(2,1)}, u32[]{:S(2)}, u32[]{:S(2)}) collective-permute-start(bf16[4,1,2,512,128]{4,3,2,1,0:T(8,128)(2,1)} %join.4), channel_id=1, source_target_pairs={{0,1},{1,0},{2,3},{3,2},{4,5},{5,4},{6,7},{7,6},{8,9},{9,8},{10,11... | collective-permute-start | bytes 3145736 | tf_op jit(solution)/shard_map/ppermute | solution.py:76
  97.2 12.8 %collective-permute-done.8.refs_7_ = bf16[1040,256]{1,0:T(8,128)(2,1)} collective-permute-done((bf16[1040,256]{1,0:T(8,128)(2,1)S(1)}, bf16[1040,256]{1,0:T(8,128)(2,1)}, u32[]{:S(2)}, u32[]{:S(2)}) %collective-permute-start.8) | collective-permute-done | bytes 532512 | tf_op jit(solution)/shard_map/ppermute | solution.py:76
  110.1 3.1 %edge_blocks.1 = (bf16[2,512,256]{2,1,0:T(8,128)(2,1)}, bf16[2,512,256]{2,1,0:T(8,128)(2,1)}, bf16[8,16,256]{2,1,0:T(8,128)(2,1)}) custom-call(s32[8]{0:T(128)} %stack.35.owners, bf16[1040,256]{1,0:T(8,128)(2,1)} %own_piece.1.refs_0_.first, bf16[1040,256]{1,0:T(8,128)(2,1)} %collective-permute-done.refs_1_, ...), custom_call_target="tpu_custom_call" | custom-call | tf_op jit(solution)/shard_map/edge_blocks/pallas_call | solution.py:279
  115.3 1.9 %collective-permute-start.11 = (bf16[2,512,256]{2,1,0:T(8,128)(2,1)}, bf16[2,512,256]{2,1,0:T(8,128)(2,1)}, u32[]{:S(2)}, u32[]{:S(2)}) collective-permute-start(bf16[2,512,256]{2,1,0:T(8,128)(2,1)} %get-tuple-element.8), channel_id=1, source_target_pairs={{0,8},{8,16},{16,24},{1,9},{9,17},{17,25},{2,10},{10,18},{18,26},{... | collective-permute-start | bytes 1572872 | tf_op jit(solution)/shard_map/ppermute | solution.py:627
  117.2 3.6 %collective-permute-start.12 = (bf16[2,512,256]{2,1,0:T(8,128)(2,1)}, bf16[2,512,256]{2,1,0:T(8,128)(2,1)}, u32[]{:S(2)}, u32[]{:S(2)}) collective-permute-start(bf16[2,512,256]{2,1,0:T(8,128)(2,1)} %get-tuple-element.9), channel_id=1, source_target_pairs={{8,0},{16,8},{24,16},{9,1},{17,9},{25,17},{10,2},{18,10},{26,18},{... | collective-permute-start | bytes 1572872 | tf_op jit(solution)/shard_map/ppermute | solution.py:627
  120.8 10.9 %collective-permute-done.14.block = bf16[4,1,2,512,128]{4,3,2,1,0:T(8,128)(2,1)} collective-permute-done((bf16[4,1,2,512,128]{4,3,2,1,0:T(8,128)(2,1)}, bf16[4,1,2,512,128]{4,3,2,1,0:T(8,128)(2,1)}, u32[]{:S(2)}, u32[]{:S(2)}) %collective-permute-start.14) | collective-permute-done | bytes 1048608 | tf_op jit(solution)/shard_map/ppermute | solution.py:76
  131.8 4.3 %all-to-all-start.1 = ((bf16[4,1,2,512,128]{4,3,2,1,0:T(8,128)(2,1)}), bf16[4,1,2,512,128]{4,3,2,1,0:T(8,128)(2,1)}, u32[]{:S(2)}, u32[]{:S(2)}) async-start(bf16[4,1,2,512,128]{4,3,2,1,0:T(8,128)(2,1)} %join.5), calls=%async_computation.1 | async-start | bytes 2097152 | tf_op jit(solution)/shard_map/all_to_all | solution.py:187
  139.6 21.4 %chebyshev.1.kernel_t = bf16[8,512,512]{2,1,0:T(8,128)(2,1)} custom-call(f32[4]{0:T(128)S(1)} %copy-done.9, s32[8]{0:T(128)S(1)} %copy-done.8, bf16[768,512]{1,0:T(8,128)(2,1)S(1)} %copy-done.7, bf16[4096,512]{1,0:T(8,128)(2,1)} %v_mid.1, bf16[768,512]{1,0:T(8,128)(2,1)} %collective-permute-done.10.v_high.refs_4_, ...), custom_call_target="tpu_custom_call" | custom-call | flops 10871635968 | bytes 16777216 | tf_op jit(solution)/shard_map/chebyshev/pallas_call | solution.py:388
  161.5 4.7 %project.1 = f32[8,24,128]{2,1,0:T(8,128)} custom-call(s32[26]{0:T(128)} %pad_add_fusion.1.plan, s32[16]{0:T(128)} %select_reduce_fusion.2.order, bf16[8,512,512]{2,1,0:T(8,128)(2,1)} %chebyshev.1.kernel_t, f32[4,128]{1,0:T(4,128)} %core.1, bf16[4,3,2,512,128]{4,3,2,1,0:T(8,128)(2,1)} %all-to-all-done.refs_0_, ...), custom_call_target="tpu_custom_call" | custom-call | tf_op jit(solution)/shard_map/project/pallas_call | solution.py:504
  166.3 4.5 %all-to-all-start.2 = ((f32[8,24,128]{2,1,0:T(8,128)}), f32[8,24,128]{2,1,0:T(8,128)S(1)}, u32[]{:S(2)}, u32[]{:S(2)}) async-start(f32[8,24,128]{2,1,0:T(8,128)} %project.1), calls=%async_computation.2 | async-start | bytes 196608 | tf_op jit(solution)/shard_map/all_to_all | solution.py:706
  171.5 6.4 %all-to-all-done.2 = f32[8,24,128]{2,1,0:T(8,128)S(1)} async-done(((f32[8,24,128]{2,1,0:T(8,128)}), f32[8,24,128]{2,1,0:T(8,128)S(1)}, u32[]{:S(2)}, u32[]{:S(2)}) %all-to-all-start.2) | async-done | bytes 98336 | tf_op jit(solution)/shard_map/all_to_all | solution.py:706
  178.6 6.4 %update.1 = (f32[4,128]{1,0:T(4,128)}, bf16[4096,512]{1,0:T(8,128)(2,1)}) custom-call(s32[26]{0:T(128)} %pad_add_fusion.1.plan, s32[16]{0:T(128)} %select_reduce_fusion.2.order, s32[16]{0:T(128)} %reshape.279.tile_of, f32[192,128]{1,0:T(8,128)} %bitcast.25, f32[32,192]{1,0:T(8,128)} %convert_reduce_fusion.collect, ...), custom_call_target="tpu_custom_call" | custom-call | tf_op jit(solution)/shard_map/update/pallas_call | solution.py:602
  (87 shorter events, 12.4 us)
Async XLA Ops:
  3.2 16.2 %collective-permute-start.1 = (bf16[1040,256]{1,0:T(8,128)(2,1)}, bf16[1040,256]{1,0:T(8,128)(2,1)}, u32[]{:S(2)}, u32[]{:S(2)}) collective-permute-start(bf16[1040,256]{1,0:T(8,128)(2,1)} %own_piece.1.refs_0_.first), channel_id=1, source_target_pairs={{0,2},{1,3},{2,0},{3,1},{4,6},{5,7},{6,4},{7,5},{8,10},{9,11},{10,... | collective-permute-start | bytes 1597448 | tf_op jit(solution)/shard_map/ppermute | solution.py:217
  4.9 13.2 %collective-permute-start.3 = (bf16[1040,256]{1,0:T(8,128)(2,1)}, bf16[1040,256]{1,0:T(8,128)(2,1)S(1)}, u32[]{:S(2)}, u32[]{:S(2)}) collective-permute-start(bf16[1040,256]{1,0:T(8,128)(2,1)} %own_piece.1.refs_0_.first), channel_id=1, source_target_pairs={{2,4},{3,5},{4,2},{5,3},{10,12},{11,13},{12,10},{13,11},{18,20},{1... | collective-permute-start | bytes 1597448 | tf_op jit(solution)/shard_map/ppermute | solution.py:217
  8.3 25.0 %collective-permute-start.13 = (bf16[4,1,2,512,128]{4,3,2,1,0:T(8,128)(2,1)}, bf16[4,1,2,512,128]{4,3,2,1,0:T(8,128)(2,1)}, u32[]{:S(2)}, u32[]{:S(2)}) collective-permute-start(bf16[4,1,2,512,128]{4,3,2,1,0:T(8,128)(2,1)} %pack.2.first), channel_id=1, source_target_pairs={{0,1},{1,0},{2,3},{3,2},{4,5},{5,4},{6,7},{7,6},{8,9},{9,8},{10,11... | collective-permute-start | bytes 3145736 | tf_op jit(solution)/shard_map/ppermute | solution.py:76
  12.5 13.5 %collective-permute-start.9 = (bf16[768,512]{1,0:T(8,128)(2,1)}, bf16[768,512]{1,0:T(8,128)(2,1)S(1)}, u32[]{:S(2)}, u32[]{:S(2)}) collective-permute-start(bf16[768,512]{1,0:T(8,128)(2,1)} %get-tuple-element.19), channel_id=1, source_target_pairs={{0,8},{8,16},{16,24},{1,9},{9,17},{17,25},{2,10},{10,18},{18,26},{... | collective-permute-start | bytes 2359304 | tf_op jit(solution)/shard_map/ppermute | solution.py:627
  14.5 13.5 %collective-permute-start.10 = (bf16[768,512]{1,0:T(8,128)(2,1)}, bf16[768,512]{1,0:T(8,128)(2,1)}, u32[]{:S(2)}, u32[]{:S(2)}) collective-permute-start(bf16[768,512]{1,0:T(8,128)(2,1)} %get-tuple-element.18), channel_id=1, source_target_pairs={{8,0},{16,8},{24,16},{9,1},{17,9},{25,17},{10,2},{18,10},{26,18},{... | collective-permute-start | bytes 2359304 | tf_op jit(solution)/shard_map/ppermute | solution.py:627
  18.1 17.7 %collective-permute-start.4 = (bf16[1040,256]{1,0:T(8,128)(2,1)S(1)}, bf16[1040,256]{1,0:T(8,128)(2,1)}, u32[]{:S(2)}, u32[]{:S(2)}) collective-permute-start(bf16[1040,256]{1,0:T(8,128)(2,1)S(1)} %collective-permute-done.3), channel_id=1, source_target_pairs={{2,0},{3,1},{4,6},{5,7},{10,8},{11,9},{12,14},{13,15},{18,16},{19,... | collective-permute-start | bytes 1597448 | tf_op jit(solution)/shard_map/ppermute | solution.py:217
  19.4 16.4 %collective-permute-start.6 = (bf16[1040,256]{1,0:T(8,128)(2,1)}, bf16[1040,256]{1,0:T(8,128)(2,1)S(1)}, u32[]{:S(2)}, u32[]{:S(2)}) collective-permute-start(bf16[1040,256]{1,0:T(8,128)(2,1)} %collective-permute-done.1.refs_2_), channel_id=1, source_target_pairs={{2,4},{3,5},{4,2},{5,3},{10,12},{11,13},{12,10},{13,11},{18,20},{1... | collective-permute-start | bytes 1597448 | tf_op jit(solution)/shard_map/ppermute | solution.py:217
  26.0 9.8 %copy-start.6 = (bf16[768,512]{1,0:T(8,128)(2,1)}, bf16[768,512]{1,0:T(8,128)(2,1)S(1)}, u32[]{:S(2)}) copy-start(bf16[768,512]{1,0:T(8,128)(2,1)S(1)} %collective-permute-done.9.v_low.refs_3_) | copy-start | bytes 2359300
  35.8 0.8 copy-start.10
  38.9 6.0 %copy-start = (bf16[1040,256]{1,0:T(8,128)(2,1)S(1)}, bf16[1040,256]{1,0:T(8,128)(2,1)}, u32[]{:S(2)}) copy-start(bf16[1040,256]{1,0:T(8,128)(2,1)} %own_piece.1.refs_0_.first) | copy-start | bytes 1597444
  38.9 8.1 %copy-start.11 = (bf16[1040,256]{1,0:T(8,128)(2,1)S(1)}, bf16[1040,256]{1,0:T(8,128)(2,1)}, u32[]{:S(2)}) copy-start(bf16[1040,256]{1,0:T(8,128)(2,1)} %copy-done.10) | copy-start | bytes 1597444
  38.9 92.8 %all-to-all-start = ((bf16[4,3,2,512,128]{4,3,2,1,0:T(8,128)(2,1)}), bf16[4,3,2,512,128]{4,3,2,1,0:T(8,128)(2,1)}, u32[]{:S(2)}, u32[]{:S(2)}) async-start(bf16[4,3,2,512,128]{4,3,2,1,0:T(8,128)(2,1)} %join.3), calls=%async_computation | async-start | bytes 6291456 | tf_op jit(solution)/shard_map/all_to_all | solution.py:187
  44.9 52.3 %collective-permute-start = (bf16[1040,256]{1,0:T(8,128)(2,1)S(1)}, bf16[1040,256]{1,0:T(8,128)(2,1)}, u32[]{:S(2)}, u32[]{:S(2)}) collective-permute-start(bf16[1040,256]{1,0:T(8,128)(2,1)S(1)} %copy-done), channel_id=1, source_target_pairs={{0,1},{1,0},{2,3},{3,2},{4,5},{5,4},{6,7},{7,6},{8,9},{9,8},{10,11... | collective-permute-start | bytes 1597448 | tf_op jit(solution)/shard_map/ppermute | solution.py:76
  47.0 47.2 %collective-permute-start.7 = (bf16[1040,256]{1,0:T(8,128)(2,1)S(1)}, bf16[1040,256]{1,0:T(8,128)(2,1)S(1)}, u32[]{:S(2)}, u32[]{:S(2)}) collective-permute-start(bf16[1040,256]{1,0:T(8,128)(2,1)S(1)} %copy-done.11), channel_id=1, source_target_pairs={{2,0},{3,1},{4,6},{5,7},{10,8},{11,9},{12,14},{13,15},{18,16},{19,... | collective-permute-start | bytes 1597448 | tf_op jit(solution)/shard_map/ppermute | solution.py:217
  48.3 48.9 %collective-permute-start.2 = (bf16[1040,256]{1,0:T(8,128)(2,1)}, bf16[1040,256]{1,0:T(8,128)(2,1)}, u32[]{:S(2)}, u32[]{:S(2)}) collective-permute-start(bf16[1040,256]{1,0:T(8,128)(2,1)} %collective-permute-done.1.refs_2_), channel_id=1, source_target_pairs={{0,1},{1,0},{2,3},{3,2},{4,5},{5,4},{6,7},{7,6},{8,9},{9,8},{10,11... | collective-permute-start | bytes 1597448 | tf_op jit(solution)/shard_map/ppermute | solution.py:76
  50.5 59.6 %copy-start.2 = (bf16[1040,256]{1,0:T(8,128)(2,1)}, bf16[1040,256]{1,0:T(8,128)(2,1)S(1)}, u32[]{:S(2)}) copy-start(bf16[1040,256]{1,0:T(8,128)(2,1)S(1)} %add.189.refs_4_) | copy-start | bytes 1597444
  50.5 46.8 %collective-permute-start.5 = (bf16[1040,256]{1,0:T(8,128)(2,1)S(1)}, bf16[1040,256]{1,0:T(8,128)(2,1)}, u32[]{:S(2)}, u32[]{:S(2)}) collective-permute-start(bf16[1040,256]{1,0:T(8,128)(2,1)S(1)} %add.189.refs_4_), channel_id=1, source_target_pairs={{0,1},{1,0},{2,3},{3,2},{4,5},{5,4},{6,7},{7,6},{8,9},{9,8},{10,11... | collective-permute-start | bytes 1597448 | tf_op jit(solution)/shard_map/ppermute | solution.py:76
  94.2 0.8 copy-start.12
  95.0 15.1 %copy-start.4 = (bf16[1040,256]{1,0:T(8,128)(2,1)}, bf16[1040,256]{1,0:T(8,128)(2,1)S(1)}, u32[]{:S(2)}) copy-start(bf16[1040,256]{1,0:T(8,128)(2,1)S(1)} %add.190.refs_6_) | copy-start | bytes 1597444
  95.0 15.1 %collective-permute-start.8 = (bf16[1040,256]{1,0:T(8,128)(2,1)S(1)}, bf16[1040,256]{1,0:T(8,128)(2,1)}, u32[]{:S(2)}, u32[]{:S(2)}) collective-permute-start(bf16[1040,256]{1,0:T(8,128)(2,1)S(1)} %add.190.refs_6_), channel_id=1, source_target_pairs={{0,1},{1,0},{2,3},{3,2},{4,5},{5,4},{6,7},{7,6},{8,9},{9,8},{10,11... | collective-permute-start | bytes 1597448 | tf_op jit(solution)/shard_map/ppermute | solution.py:76
  95.1 36.6 %collective-permute-start.14 = (bf16[4,1,2,512,128]{4,3,2,1,0:T(8,128)(2,1)}, bf16[4,1,2,512,128]{4,3,2,1,0:T(8,128)(2,1)}, u32[]{:S(2)}, u32[]{:S(2)}) collective-permute-start(bf16[4,1,2,512,128]{4,3,2,1,0:T(8,128)(2,1)} %join.4), channel_id=1, source_target_pairs={{0,1},{1,0},{2,3},{3,2},{4,5},{5,4},{6,7},{7,6},{8,9},{9,8},{10,11... | collective-permute-start | bytes 3145736 | tf_op jit(solution)/shard_map/ppermute | solution.py:76
  113.2 25.2 %copy-start.1 = (bf16[1040,256]{1,0:T(8,128)(2,1)S(1)}, bf16[1040,256]{1,0:T(8,128)(2,1)}, u32[]{:S(2)}) copy-start(bf16[1040,256]{1,0:T(8,128)(2,1)} %own_piece.1.refs_0_.first) | copy-start | bytes 1597444
  113.2 25.2 %copy-start.3 = (bf16[1040,256]{1,0:T(8,128)(2,1)S(1)}, bf16[1040,256]{1,0:T(8,128)(2,1)}, u32[]{:S(2)}) copy-start(bf16[1040,256]{1,0:T(8,128)(2,1)} %copy-done.2) | copy-start | bytes 1597444
  113.2 25.2 %copy-start.5 = (bf16[1040,256]{1,0:T(8,128)(2,1)S(1)}, bf16[1040,256]{1,0:T(8,128)(2,1)}, u32[]{:S(2)}) copy-start(bf16[1040,256]{1,0:T(8,128)(2,1)} %copy-done.4) | copy-start | bytes 1597444
  113.3 25.2 %copy-start.8 = (s32[8]{0:T(128)S(1)}, s32[8]{0:T(128)}, u32[]{:S(2)}) copy-start(s32[8]{0:T(128)} %stack.35.owners) | copy-start | bytes 100
  113.3 25.2 %copy-start.9 = (f32[4]{0:T(128)S(1)}, f32[4]{0:T(128)}, u32[]{:S(2)}) copy-start(f32[4]{0:T(128)} %coef.1) | copy-start | bytes 52
  115.3 23.1 %collective-permute-start.11 = (bf16[2,512,256]{2,1,0:T(8,128)(2,1)}, bf16[2,512,256]{2,1,0:T(8,128)(2,1)}, u32[]{:S(2)}, u32[]{:S(2)}) collective-permute-start(bf16[2,512,256]{2,1,0:T(8,128)(2,1)} %get-tuple-element.8), channel_id=1, source_target_pairs={{0,8},{8,16},{16,24},{1,9},{9,17},{17,25},{2,10},{10,18},{18,26},{... | collective-permute-start | bytes 1572872 | tf_op jit(solution)/shard_map/ppermute | solution.py:627
  117.2 21.2 %collective-permute-start.12 = (bf16[2,512,256]{2,1,0:T(8,128)(2,1)}, bf16[2,512,256]{2,1,0:T(8,128)(2,1)}, u32[]{:S(2)}, u32[]{:S(2)}) collective-permute-start(bf16[2,512,256]{2,1,0:T(8,128)(2,1)} %get-tuple-element.9), channel_id=1, source_target_pairs={{8,0},{16,8},{24,16},{9,1},{17,9},{25,17},{10,2},{18,10},{26,18},{... | collective-permute-start | bytes 1572872 | tf_op jit(solution)/shard_map/ppermute | solution.py:627
  131.8 29.8 %all-to-all-start.1 = ((bf16[4,1,2,512,128]{4,3,2,1,0:T(8,128)(2,1)}), bf16[4,1,2,512,128]{4,3,2,1,0:T(8,128)(2,1)}, u32[]{:S(2)}, u32[]{:S(2)}) async-start(bf16[4,1,2,512,128]{4,3,2,1,0:T(8,128)(2,1)} %join.5), calls=%async_computation.1 | async-start | bytes 2097152 | tf_op jit(solution)/shard_map/all_to_all | solution.py:187
  138.4 1.1 copy-start.7
  166.3 11.7 %all-to-all-start.2 = ((f32[8,24,128]{2,1,0:T(8,128)}), f32[8,24,128]{2,1,0:T(8,128)S(1)}, u32[]{:S(2)}, u32[]{:S(2)}) async-start(f32[8,24,128]{2,1,0:T(8,128)} %project.1), calls=%async_computation.2 | async-start | bytes 196608 | tf_op jit(solution)/shard_map/all_to_all | solution.py:706
  177.9 0.6 copy-start.13

commit v3 on v1

--- a/solution.py
+++ b/solution.py
@@ -143,7 +143,7 @@
         in_specs=[HBM] + [ANY] * len(others),
         out_specs=HBM,
         input_output_aliases={0: 0},
-        compiler_params=pltpu.CompilerParams(vmem_limit_bytes=MIB),
+        compiler_params=pltpu.CompilerParams(vmem_limit_bytes=62 * MIB),
         name="after",
     )(block, *others)
 
@@ -257,59 +257,66 @@
     )(owners, *pieces)
 
 
-def cheb_kernel(blocks, coef, owners, v_low, v_mid, v_high, h_low, h_high, *refs):
-    *pieces, out, vext, hraw, hcat, cheb_1, cheb_2, total, kern, sems, psems, osems = refs
-    halo_v = DEG
-    halo_h = DEG - 1
-    held = (pieces[0].shape[0] - LISTS) // (2 * W)
-    h_copies = [
-        pltpu.make_async_copy(h_low, hraw.at[pl.ds(0, halo_h)], sems.at[0]),
-        pltpu.make_async_copy(h_high, hraw.at[pl.ds(halo_h + blocks, halo_h)], sems.at[1]),
-    ]
-    v_copies = [
-        pltpu.make_async_copy(v_low, vext.at[pl.ds(0, halo_v * W)], sems.at[2]),
-        pltpu.make_async_copy(v_mid, vext.at[pl.ds(halo_v * W, blocks * W)], sems.at[3]),
-        pltpu.make_async_copy(v_high, vext.at[pl.ds((halo_v + blocks) * W, halo_v * W)], sems.at[4]),
-    ]
-
-    def each_piece(act):
-        for i, piece in enumerate(pieces):
-            @pl.when(owners[i] >= 0)
-            def _():
-                for k in range(held):
-                    act(pltpu.make_async_copy(
-                        piece.at[pl.ds(k * 2 * W, 2 * W)],
-                        hraw.at[halo_h + owners[i] * held + k],
-                        psems.at[i, k],
-                    ))
-
-    each_piece(lambda copy: copy.start())
-    for copy in h_copies + v_copies:
-        copy.start()
-    each_piece(lambda copy: copy.wait())
-    for copy in h_copies:
-        copy.wait()
+def rows_of(j, count=1):
+    return pl.ds(j * W if isinstance(j, int) else pl.multiple_of(j * W, W), count * W)
+
+
+def band_builder(source, target):
     rows = lax.broadcasted_iota(jnp.int32, (W, W), 0)
     cols = lax.broadcasted_iota(jnp.int32, (W, W), 1)
     upper = jnp.where(rows <= cols, 1.0, 0.0).astype(jnp.bfloat16)
 
     def build(j, carry):
-        coupling = hraw[j, W:]
+        coupling = source[j, W:]
         lower_band = coupling * upper
-        hcat[j, :, 0:W] = lower_band
-        hcat[j, :, W : 2 * W] = hraw[j, :W]
-        hcat[j, :, 2 * W : 3 * W] = coupling - lower_band
+        target[j, :, 0:W] = lower_band
+        target[j, :, W : 2 * W] = source[j, :W]
+        target[j, :, 2 * W : 3 * W] = coupling - lower_band
         return carry
 
-    lax.fori_loop(0, blocks + 2 * halo_h, build, 0, unroll=2)
+    return build
+
+
+def inner_kernel(blocks, coef, owners, v_low, v_mid, v_high, *refs):
+    (
+        *pieces, out, edge_1, edge_2, edge_total,
+        vext, hraw, hcat, cheb_1, cheb_2, total, kern, sems, psems, osems, esems,
+    ) = refs
+    held = (pieces[0].shape[0] - LISTS) // (2 * W)
+    v_copies = [
+        pltpu.make_async_copy(v_low.at[rows_of(DEG - 1)], vext.at[rows_of(0)], sems.at[0]),
+        pltpu.make_async_copy(v_mid, vext.at[rows_of(1, blocks)], sems.at[1]),
+        pltpu.make_async_copy(v_high.at[rows_of(0)], vext.at[rows_of(blocks + 1)], sems.at[2]),
+    ]
+
+    def each_piece(act):
+        for i, piece in enumerate(pieces):
+            for k in range(held):
+                act(pltpu.make_async_copy(
+                    piece.at[pl.ds(k * 2 * W, 2 * W)],
+                    hraw.at[owners[i] * held + k],
+                    psems.at[i, k],
+                ))
+
+    each_piece(lambda copy: copy.start())
+    for copy in v_copies:
+        copy.start()
+    each_piece(lambda copy: copy.wait())
+    lax.fori_loop(0, blocks, band_builder(hraw, hcat), 0, unroll=2)
     for copy in v_copies:
         copy.wait()
 
-    def rows_of(j, count=1):
-        return pl.ds(pl.multiple_of(j * W, W), count * W)
-
     def band(source, j, row):
         return jnp.dot(hcat[j], source[rows_of(row, 3), :], preferred_element_type=jnp.float32)
+
+    def edges(source, target, at):
+        size = source.shape[0] // W
+        return [
+            pltpu.make_async_copy(
+                source.at[rows_of(place, 2)], target.at[rows_of(2 * i, 2)], esems.at[at, i]
+            )
+            for i, place in enumerate((0, size - 2))
+        ]
 
     def first(j, carry):
         value = band(vext, j, j)
@@ -317,7 +324,7 @@
         total[rows_of(j), :] = value
         return carry
 
-    lax.fori_loop(0, blocks + 4, first, 0, unroll=2)
+    lax.fori_loop(0, blocks, first, 0, unroll=2)
 
     def second(j, carry):
         begin = vext[rows_of(j + 2), :].astype(jnp.float32)
@@ -328,7 +335,12 @@
         )
         return carry
 
-    lax.fori_loop(0, blocks + 2, second, 0, unroll=2)
+    lax.fori_loop(0, blocks - 2, second, 0, unroll=2)
+    outgoing = (
+        edges(cheb_1, edge_1, 0) + edges(cheb_2, edge_2, 1) + edges(total, edge_total, 2)
+    )
+    for copy in outgoing:
+        copy.start()
 
     def store(j):
         return pltpu.make_async_copy(kern.at[j], out.at[j], osems.at[j])
@@ -336,44 +348,148 @@
     def third(j, carry):
         for half in range(KB // W):
             i = j * (KB // W) + half
-            value = total[rows_of(i + 2), :] + (2.0 * coef[3]) * band(cheb_2, i + 2, i)
+            value = total[rows_of(i), :] + (2.0 * coef[3]) * band(cheb_2, i, i - 2)
             kern[j, :, half * W : (half + 1) * W] = value.astype(jnp.bfloat16).T
         store(j).start()
         return carry
 
-    lax.fori_loop(0, blocks // (KB // W), third, 0)
-    for j in range(blocks // (KB // W)):
+    last = blocks // (KB // W) - 1
+    lax.fori_loop(1, last, third, 0)
+    for j in range(1, last):
         store(j).wait()
-
-
-def chebyshev(coefficients, owners, v_low, v_mid, v_high, h_low, h_high, pieces):
+    for copy in outgoing:
+        copy.wait()
+
+
+def chebyshev_inner(coefficients, owners, v_low, v_mid, v_high, pieces):
     blocks = v_mid.shape[0] // W
     cols = v_mid.shape[1]
-    ext = blocks + 2 * (DEG - 1)
-    flops = 2 * W * 3 * W * cols * (3 * blocks + 6)
+    flops = 2 * W * 3 * W * cols * (3 * blocks - 6)
     result = (blocks * W // KB, cols, KB)
     held = (pieces[0].shape[0] - LISTS) // (2 * W)
     return pl.pallas_call(
-        functools.partial(cheb_kernel, blocks),
-        out_shape=jax.ShapeDtypeStruct(result, jnp.bfloat16),
-        in_specs=[SMEM] * 2 + [ANY] * (5 + len(pieces)),
-        out_specs=HBM,
+        functools.partial(inner_kernel, blocks),
+        out_shape=(
+            jax.ShapeDtypeStruct(result, jnp.bfloat16),
+            jax.ShapeDtypeStruct((4 * W, cols), jnp.bfloat16),
+            jax.ShapeDtypeStruct((4 * W, cols), jnp.bfloat16),
+            jax.ShapeDtypeStruct((4 * W, cols), jnp.float32),
+        ),
+        in_specs=[SMEM] * 2 + [HBM] * (3 + len(pieces)),
+        out_specs=(HBM,) * 4,
         scratch_shapes=[
-            pltpu.VMEM(((blocks + 2 * DEG) * W, cols), jnp.bfloat16),
-            pltpu.VMEM((ext, 2 * W, W), jnp.bfloat16),
-            pltpu.VMEM((ext, W, 3 * W), jnp.bfloat16),
-            pltpu.VMEM((ext * W, cols), jnp.bfloat16),
             pltpu.VMEM(((blocks + 2) * W, cols), jnp.bfloat16),
-            pltpu.VMEM((ext * W, cols), jnp.float32),
+            pltpu.VMEM((blocks, 2 * W, W), jnp.bfloat16),
+            pltpu.VMEM((blocks, W, 3 * W), jnp.bfloat16),
+            pltpu.VMEM((blocks * W, cols), jnp.bfloat16),
+            pltpu.VMEM(((blocks - 2) * W, cols), jnp.bfloat16),
+            pltpu.VMEM((blocks * W, cols), jnp.float32),
             pltpu.VMEM(result, jnp.bfloat16),
-            pltpu.SemaphoreType.DMA((5,)),
+            pltpu.SemaphoreType.DMA((3,)),
             pltpu.SemaphoreType.DMA((len(pieces), held)),
             pltpu.SemaphoreType.DMA((result[0],)),
+            pltpu.SemaphoreType.DMA((3, 2)),
         ],
-        compiler_params=pltpu.CompilerParams(vmem_limit_bytes=48 * MIB),
+        compiler_params=pltpu.CompilerParams(vmem_limit_bytes=62 * MIB),
         cost_estimate=pl.CostEstimate(flops=flops, bytes_accessed=16 * MIB, transcendentals=0),
-        name="chebyshev",
-    )(coefficients, owners, v_low, v_mid, v_high, h_low, h_high, *pieces)
+        name="chebyshev_inner",
+    )(coefficients, owners, v_low, v_mid, v_high, *pieces)
+
+
+def outer_kernel(
+    blocks, coef, kernel_in, v_low, v_mid, v_high, h_low, h_first, h_last, h_high,
+    edge_1, edge_2, edge_total, out,
+    v, hraw, hcat, cheb_1, cheb_2, total, kern, sems, osems,
+):
+    last = kern.shape[0] - 1
+    end = out.shape[0] - 1
+    copies = [
+        (h_low, hraw.at[pl.ds(0, 2)]),
+        (h_first, hraw.at[pl.ds(2, 2)]),
+        (h_last, hraw.at[pl.ds(4, 2)]),
+        (h_high, hraw.at[pl.ds(6, 2)]),
+        (v_low, v.at[0, rows_of(0, 3)]),
+        (v_mid.at[rows_of(0)], v.at[0, rows_of(3)]),
+        (v_mid.at[rows_of(blocks - 1)], v.at[1, rows_of(0)]),
+        (v_high, v.at[1, rows_of(1, 3)]),
+        (edge_1.at[rows_of(0, 2)], cheb_1.at[0, rows_of(2, 2)]),
+        (edge_1.at[rows_of(2, 2)], cheb_1.at[1, rows_of(0, 2)]),
+        (edge_2.at[rows_of(0, 2)], cheb_2.at[0, rows_of(2, 2)]),
+        (edge_2.at[rows_of(2, 2)], cheb_2.at[1, rows_of(0, 2)]),
+        (edge_total.at[rows_of(0, 2)], total.at[0]),
+        (edge_total.at[rows_of(2, 2)], total.at[1]),
+    ]
+    copies = [
+        pltpu.make_async_copy(source, target, sems.at[i])
+        for i, (source, target) in enumerate(copies)
+    ]
+    for copy in copies:
+        copy.start()
+    for copy in copies:
+        copy.wait()
+    lax.fori_loop(0, 8, band_builder(hraw, hcat), 0, unroll=2)
+
+    def band(side, j, source, row):
+        return jnp.dot(
+            hcat[4 * side + j], source[side, rows_of(row, 3), :], preferred_element_type=jnp.float32
+        )
+
+    for side, places in ((0, (0, 1)), (1, (2, 3))):
+        for j in places:
+            value = band(side, j, v, j - 2 * side)
+            cheb_1[side, rows_of(j), :] = value.astype(jnp.bfloat16)
+    for side, places in ((0, ((1, 0), (2, 1))), (1, ((2, 3), (1, 2)))):
+        for j, place in places:
+            begin = v[side, rows_of(place + 2 - 4 * side), :].astype(jnp.float32)
+            value = 2.0 * band(side, j, cheb_1, j - 1) - begin
+            cheb_2[side, rows_of(place), :] = value.astype(jnp.bfloat16)
+            if (j, place) == places[1]:
+                within = rows_of(side)
+                total[side, within, :] = (
+                    coef[0] * begin + (coef[1] - coef[3]) * total[side, within, :] + coef[2] * value
+                )
+    for side in range(2):
+        for half in range(2):
+            j = 2 + half if side == 0 else half
+            value = total[side, rows_of(half), :] + (2.0 * coef[3]) * band(side, j, cheb_2, half)
+            kern[side, :, half * W : (half + 1) * W] = value.astype(jnp.bfloat16).T
+    stores = [
+        pltpu.make_async_copy(kern.at[0], out.at[0], osems.at[0]),
+        pltpu.make_async_copy(kern.at[last], out.at[end], osems.at[1]),
+    ]
+    for store in stores:
+        store.start()
+    for store in stores:
+        store.wait()
+
+
+def chebyshev_outer(coefficients, inner, v_low, v_mid, v_high, h_low, h_first, h_last, h_high):
+    kernel_t, edge_1, edge_2, edge_total = inner
+    blocks = v_mid.shape[0] // W
+    cols = v_mid.shape[1]
+    return pl.pallas_call(
+        functools.partial(outer_kernel, blocks),
+        out_shape=jax.ShapeDtypeStruct(kernel_t.shape, kernel_t.dtype),
+        in_specs=[SMEM] + [HBM] * 11,
+        out_specs=HBM,
+        input_output_aliases={1: 0},
+        scratch_shapes=[
+            pltpu.VMEM((2, 4 * W, cols), jnp.bfloat16),
+            pltpu.VMEM((8, 2 * W, W), jnp.bfloat16),
+            pltpu.VMEM((8, W, 3 * W), jnp.bfloat16),
+            pltpu.VMEM((2, 4 * W, cols), jnp.bfloat16),
+            pltpu.VMEM((2, 4 * W, cols), jnp.bfloat16),
+            pltpu.VMEM((2, 2 * W, cols), jnp.float32),
+            pltpu.VMEM((2, cols, KB), jnp.bfloat16),
+            pltpu.SemaphoreType.DMA((14,)),
+            pltpu.SemaphoreType.DMA((2,)),
+        ],
+        compiler_params=pltpu.CompilerParams(vmem_limit_bytes=62 * MIB),
+        name="chebyshev_outer",
+    )(
+        coefficients, kernel_t, v_low, v_mid, v_high, h_low, h_first, h_last, h_high,
+        edge_1, edge_2, edge_total,
+    )
 
 
 def entry_loads(order, parts, pair, sems):
@@ -475,7 +591,7 @@
             pltpu.SemaphoreType.DMA((blocks,)),
             pltpu.SemaphoreType.DMA((slots,)),
         ],
-        compiler_params=pltpu.CompilerParams(vmem_limit_bytes=20 * MIB),
+        compiler_params=pltpu.CompilerParams(vmem_limit_bytes=62 * MIB),
         name="project",
     )(plan, order, kernel_t, core, *parts)
 
@@ -578,7 +694,7 @@
             pltpu.SemaphoreType.DMA((slots,)),
             pltpu.SemaphoreType.DMA((blocks,)),
         ],
-        compiler_params=pltpu.CompilerParams(vmem_limit_bytes=24 * MIB),
+        compiler_params=pltpu.CompilerParams(vmem_limit_bytes=62 * MIB),
         name="update",
     )(plan, order, tile_of, contributions, collect, *parts)
 
@@ -660,8 +776,9 @@
     first, last, lists = edge_blocks(owners, pieces, col_count, DEG - 1)
     h_low = shift(last, "row", 1)
     h_high = shift(first, "row", -1)
-    kernel_t = chebyshev(
-        coefficients, owners, v_low, start_columns, v_high, h_low, h_high, pieces
+    inner = chebyshev_inner(coefficients, owners, v_low, start_columns, v_high, pieces)
+    kernel_t = chebyshev_outer(
+        coefficients, inner, v_low, start_columns, v_high, h_low, first, last, h_high
     )
     collect, plan, order, tile_of = make_plan(lists[:, 0], me, entries, tiles, col_count, blocks)
     partial = project(plan, order, kernel_t, core_density, parts, col_count)

time: 182 us -> 180 us (0.989)
  the two profiles are of different devices: /device:TPU:1 before, /device:TPU:2 now
where the time goes in v3:
time: 180 us; the launch traced here: 178 us
  waiting for transfers between devices  71.1 us (39%)
  Pallas kernels  49.7 us (28%)
  starting transfers between devices  38.9 us (22%)
  local copies, waits for them, and re-layouts  8.84 us (5%)
  other arithmetic  8.17 us (5%)
    ppermute x5, waiting for transfers between devices, move(): return lax.ppermute(block, 'col', pairs)  42.3 us
    pallas_call x1, Pallas kernels, chebyshev_inner(): pl.pallas_call(functools.partial(inner_kernel, blocks), out_shape=(jax.Sh...  18.3 us
    ppermute x6, waiting for transfers between devices, swap_along(): return lax.ppermute(block, 'col', pairs)  18.3 us
    ppermute x4, starting transfers between devices, shift(): return lax.ppermute(block, axis, pairs)  11.1 us
    all_to_all x2, starting transfers between devices, between_lines(): lax.all_to_all(after(block, *others), 'col', split_axis=0, concat_axis=0,...  10.2 us
    pallas_call x1, Pallas kernels, chebyshev_outer(): pl.pallas_call(functools.partial(outer_kernel, blocks), out_shape=jax.Sha...  8.13 us
    pallas_call x1, Pallas kernels, update(): pl.pallas_call(functools.partial(update_kernel, blocks, tiles), out_shape...  6.52 us
    ppermute x5, starting transfers between devices, move(): return lax.ppermute(block, 'col', pairs)  6.41 us
  transfers between devices with their start and end apart: 18, of which 8 were waited for; matrix products, arithmetic and copies ran while one was open for 8% of the time, Pallas kernels for 20%

profile of v3, /device:TPU:2, one launch (start us, length us, event | category | flops | bytes accessed | tf_op | source)
XLA Modules:
  0.0 177.7 jit_solution(13219123099764045139)
XLA Ops:
  0.6 2.6 %own_piece.1.refs_0_.first = bf16[1040,256]{1,0:T(8,128)(2,1)} custom-call(s32[16]{0:T(128)} %bitcast.32, s32[16]{0:T(128)} %named.1, s32[4]{0:T(128)} %counts.1, s32[2]{0:T(128)} %pattern.1, bf16[1024,256]{1,0:T(8,128)(2,1)} %bitcast.26), custom_call_target="tpu_custom_call" | custom-call | tf_op jit(solution)/shard_map/own_piece/pallas_call | solution.py:56
  3.2 1.6 collective-permute-start.1
  4.9 1.5 collective-permute-start.3
  6.4 2.7 %pack.2.first = bf16[4,1,2,512,128]{4,3,2,1,0:T(8,128)(2,1)} custom-call(s32[1]{0:T(128)} %bitcast.11.me, s32[16]{0:T(128)} %bitcast.33, bf16[16,2,512,128]{3,2,1,0:T(8,128)(2,1)} %basis.3, bf16[1040,256]{1,0:T(8,128)(2,1)} %own_piece.1.refs_0_.first), custom_call_target="tpu_custom_call" | custom-call | tf_op jit(solution)/shard_map/pack/pallas_call | solution.py:119
  9.1 1.6 collective-permute-start.13
  10.7 2.6 %fusion.12 = (bf16[768,512]{1,0:T(8,128)(2,1)}, bf16[768,512]{1,0:T(8,128)(2,1)}) fusion(bf16[4096,512]{1,0:T(8,128)(2,1)} %v_mid.3), kind=kLoop, calls=%fused_computation.55 | loop fusion | bytes 3145728 | tf_op jit(solution)/shard_map/slice | solution.py:773
  13.3 1.9 %collective-permute-start.9 = (bf16[768,512]{1,0:T(8,128)(2,1)}, bf16[768,512]{1,0:T(8,128)(2,1)}, u32[]{:S(2)}, u32[]{:S(2)}) collective-permute-start(bf16[768,512]{1,0:T(8,128)(2,1)} %get-tuple-element.27), channel_id=1, source_target_pairs={{0,8},{8,16},{16,24},{1,9},{9,17},{17,25},{2,10},{10,18},{18,26},{... | collective-permute-start | bytes 2359304 | tf_op jit(solution)/shard_map/ppermute | solution.py:705
  15.3 3.6 %collective-permute-start.10 = (bf16[768,512]{1,0:T(8,128)(2,1)}, bf16[768,512]{1,0:T(8,128)(2,1)}, u32[]{:S(2)}, u32[]{:S(2)}) collective-permute-start(bf16[768,512]{1,0:T(8,128)(2,1)} %get-tuple-element.26), channel_id=1, source_target_pairs={{8,0},{16,8},{24,16},{9,1},{17,9},{25,17},{10,2},{18,10},{26,18},{... | collective-permute-start | bytes 2359304 | tf_op jit(solution)/shard_map/ppermute | solution.py:705
  18.9 1.3 collective-permute-start.4
  20.9 3.6 %pack.3 = (bf16[4,2,2,512,128]{4,3,2,1,0:T(8,128)(2,1)}, bf16[4,1,2,512,128]{4,3,2,1,0:T(8,128)(2,1)}) custom-call(s32[1]{0:T(128)} %bitcast.11.me, s32[16]{0:T(128)} %bitcast.34, bf16[16,2,512,128]{3,2,1,0:T(8,128)(2,1)} %basis.3, bf16[4,1,2,512,128]{4,3,2,1,0:T(8,128)(2,1)} %pack.2.first), custom_call_target="tpu_custom_call" | custom-call | tf_op jit(solution)/shard_map/pack/pallas_call | solution.py:119
  24.5 2.4 %collective-permute-done.9.v_low.refs_3_ = bf16[768,512]{1,0:T(8,128)(2,1)} collective-permute-done((bf16[768,512]{1,0:T(8,128)(2,1)}, bf16[768,512]{1,0:T(8,128)(2,1)}, u32[]{:S(2)}, u32[]{:S(2)}) %collective-permute-start.9) | collective-permute-done | bytes 786464 | tf_op jit(solution)/shard_map/ppermute | solution.py:705
  26.9 1.8 collective-permute-done.10.v_high.refs_4_
  28.7 5.3 %collective-permute-done.13.refs_5_ = bf16[4,1,2,512,128]{4,3,2,1,0:T(8,128)(2,1)S(1)} collective-permute-done((bf16[4,1,2,512,128]{4,3,2,1,0:T(8,128)(2,1)}, bf16[4,1,2,512,128]{4,3,2,1,0:T(8,128)(2,1)S(1)}, u32[]{:S(2)}, u32[]{:S(2)}) %collective-permute-start.13) | collective-permute-done | bytes 1048608 | tf_op jit(solution)/shard_map/ppermute | solution.py:76
  34.0 2.0 %collective-permute-done.4.refs_2_ = bf16[1040,256]{1,0:T(8,128)(2,1)} collective-permute-done((bf16[1040,256]{1,0:T(8,128)(2,1)}, bf16[1040,256]{1,0:T(8,128)(2,1)}, u32[]{:S(2)}, u32[]{:S(2)}) %collective-permute-start.4) | collective-permute-done | bytes 532512 | tf_op jit(solution)/shard_map/ppermute | solution.py:185
  36.8 5.8 %all-to-all-start = ((bf16[4,2,2,512,128]{4,3,2,1,0:T(8,128)(2,1)}), bf16[4,2,2,512,128]{4,3,2,1,0:T(8,128)(2,1)}, u32[]{:S(2)}, u32[]{:S(2)}) async-start(bf16[4,2,2,512,128]{4,3,2,1,0:T(8,128)(2,1)} %after.2), calls=%async_computation | async-start | bytes 4194304 | tf_op jit(solution)/shard_map/all_to_all | solution.py:158
  45.5 1.3 collective-permute-start.7
  46.8 1.3 collective-permute-start.2
  48.1 1.3 add.189.refs_4_
  50.3 40.3 %collective-permute-done.7 = bf16[1040,256]{1,0:T(8,128)(2,1)S(1)} collective-permute-done((bf16[1040,256]{1,0:T(8,128)(2,1)S(1)}, bf16[1040,256]{1,0:T(8,128)(2,1)S(1)}, u32[]{:S(2)}, u32[]{:S(2)}) %collective-permute-start.7) | collective-permute-done | bytes 532512 | tf_op jit(solution)/shard_map/ppermute | solution.py:185
  91.6 2.8 %pad_maximum_fusion.refs_0_ = bf16[4,2,2,512,128]{4,3,2,1,0:T(8,128)(2,1)} fusion(bf16[4,1,2,512,128]{4,3,2,1,0:T(8,128)(2,1)} %collective-permute-done.14, bf16[4,1,2,512,128]{4,3,2,1,0:T(8,128)(2,1)S(1)} %copy-done.2), kind=kLoop, calls=%fused_computation | loop fusion | flops 1048576 | bytes 4194304 | tf_op jit(solution)/shard_map/concatenate | solution.py:157
  94.4 4.5 %all-to-all-start.1 = ((bf16[4,2,2,512,128]{4,3,2,1,0:T(8,128)(2,1)}), bf16[4,2,2,512,128]{4,3,2,1,0:T(8,128)(2,1)}, u32[]{:S(2)}, u32[]{:S(2)}) async-start(bf16[4,2,2,512,128]{4,3,2,1,0:T(8,128)(2,1)} %after.3), calls=%async_computation.1 | async-start | bytes 4194304 | tf_op jit(solution)/shard_map/all_to_all | solution.py:158
  98.9 4.2 %collective-permute-done.5.refs_5_ = bf16[1040,256]{1,0:T(8,128)(2,1)} collective-permute-done((bf16[1040,256]{1,0:T(8,128)(2,1)S(1)}, bf16[1040,256]{1,0:T(8,128)(2,1)}, u32[]{:S(2)}, u32[]{:S(2)}) %collective-permute-start.5) | collective-permute-done | bytes 532512 | tf_op jit(solution)/shard_map/ppermute | solution.py:76
  103.2 8.7 %collective-permute-done.8.refs_7_ = bf16[1040,256]{1,0:T(8,128)(2,1)S(1)} collective-permute-done((bf16[1040,256]{1,0:T(8,128)(2,1)}, bf16[1040,256]{1,0:T(8,128)(2,1)S(1)}, u32[]{:S(2)}, u32[]{:S(2)}) %collective-permute-start.8) | collective-permute-done | bytes 532512 | tf_op jit(solution)/shard_map/ppermute | solution.py:76
  112.7 3.0 %edge_blocks.1 = (bf16[2,512,256]{2,1,0:T(8,128)(2,1)}, bf16[2,512,256]{2,1,0:T(8,128)(2,1)}, bf16[8,16,256]{2,1,0:T(8,128)(2,1)}) custom-call(s32[8]{0:T(128)} %stack.35.owners, bf16[1040,256]{1,0:T(8,128)(2,1)} %own_piece.1.refs_0_.first, bf16[1040,256]{1,0:T(8,128)(2,1)} %collective-permute-done.refs_1_, ...), custom_call_target="tpu_custom_call" | custom-call | tf_op jit(solution)/shard_map/edge_blocks/pallas_call | solution.py:247
  118.4 1.9 %collective-permute-start.11 = (bf16[2,512,256]{2,1,0:T(8,128)(2,1)}, bf16[2,512,256]{2,1,0:T(8,128)(2,1)S(1)}, u32[]{:S(2)}, u32[]{:S(2)}) collective-permute-start(bf16[2,512,256]{2,1,0:T(8,128)(2,1)} %get-tuple-element.13.h_last), channel_id=1, source_target_pairs={{0,8},{8,16},{16,24},{1,9},{9,17},{17,25},{2,10},{10,18},{18,26},{... | collective-permute-start | bytes 1572872 | tf_op jit(solution)/shard_map/ppermute | solution.py:705
  120.3 3.6 %collective-permute-start.12 = (bf16[2,512,256]{2,1,0:T(8,128)(2,1)}, bf16[2,512,256]{2,1,0:T(8,128)(2,1)S(1)}, u32[]{:S(2)}, u32[]{:S(2)}) collective-permute-start(bf16[2,512,256]{2,1,0:T(8,128)(2,1)} %get-tuple-element.14.h_first), channel_id=1, source_target_pairs={{8,0},{16,8},{24,16},{9,1},{17,9},{25,17},{10,2},{18,10},{26,18},{... | collective-permute-start | bytes 1572872 | tf_op jit(solution)/shard_map/ppermute | solution.py:705
  125.7 18.3 %chebyshev_inner.1 = (bf16[8,512,512]{2,1,0:T(8,128)(2,1)}, bf16[1024,512]{1,0:T(8,128)(2,1)}, bf16[1024,512]{1,0:T(8,128)(2,1)}, f32[1024,512]{1,0:T(8,128)}) custom-call(f32[4]{0:T(128)} %coef.3, s32[8]{0:T(128)} %stack.35.owners, bf16[768,512]{1,0:T(8,128)(2,1)} %collective-permute-done.9.v_low.refs_3_, bf16[4096,512]{1,0:T(8,128)(2,1)} %v_mid.3, ...), custom_call_target="tpu_custom_call" | custom-call | flops 8455716864 | bytes 16777216 | tf_op jit(solution)/shard_map/chebyshev_inner/pallas_call | solution.py:370
  145.1 8.1 %chebyshev_outer.1.kernel_t = bf16[8,512,512]{2,1,0:T(8,128)(2,1)} custom-call(f32[4]{0:T(128)} %coef.3, bf16[8,512,512]{2,1,0:T(8,128)(2,1)} %get-tuple-element.12.kernel_in, bf16[768,512]{1,0:T(8,128)(2,1)} %collective-permute-done.9.v_low.refs_3_, bf16[4096,512]{1,0:T(8,128)(2,1)} %v_mid.3, ...), custom_call_target="tpu_custom_call", output_to_operand_aliasing={{}: (1, {})} | custom-call | tf_op jit(solution)/shard_map/chebyshev_outer/pallas_call | solution.py:470
  153.2 4.8 %project.1 = f32[8,24,128]{2,1,0:T(8,128)} custom-call(s32[26]{0:T(128)} %pad_add_fusion.1.plan, s32[16]{0:T(128)} %select_reduce_fusion.2.order, bf16[8,512,512]{2,1,0:T(8,128)(2,1)} %chebyshev_outer.1.kernel_t, f32[4,128]{1,0:T(4,128)} %core.1, bf16[8,2,512,128]{3,2,1,0:T(8,128)(2,1)} %bitcast.12.refs_0_, bf16[8,2,512,128]{3,2,1,0:T(8,128)(2,1)} %bitcast.13.refs_1_), custom_call_target="tpu_custom_call" | custom-call | tf_op jit(solution)/shard_map/project/pallas_call | solution.py:582
  158.0 5.4 %all-to-all-start.2 = ((f32[8,24,128]{2,1,0:T(8,128)}), f32[8,24,128]{2,1,0:T(8,128)S(1)}, u32[]{:S(2)}, u32[]{:S(2)}) async-start(f32[8,24,128]{2,1,0:T(8,128)} %project.1), calls=%async_computation.2 | async-start | bytes 196608 | tf_op jit(solution)/shard_map/all_to_all | solution.py:785
  164.1 6.4 %all-to-all-done.2 = f32[8,24,128]{2,1,0:T(8,128)S(1)} async-done(((f32[8,24,128]{2,1,0:T(8,128)}), f32[8,24,128]{2,1,0:T(8,128)S(1)}, u32[]{:S(2)}, u32[]{:S(2)}) %all-to-all-start.2) | async-done | bytes 98336 | tf_op jit(solution)/shard_map/all_to_all | solution.py:785
  171.2 6.5 %update.1 = (f32[4,128]{1,0:T(4,128)}, bf16[4096,512]{1,0:T(8,128)(2,1)}) custom-call(s32[26]{0:T(128)} %pad_add_fusion.1.plan, s32[16]{0:T(128)} %select_reduce_fusion.2.order, s32[16]{0:T(128)} %reshape.285.tile_of, f32[192,128]{1,0:T(8,128)} %bitcast.27, f32[32,192]{1,0:T(8,128)} %convert_reduce_fusion.collect, bf16[8,2,512,128]{3,2,1,0:T(8,128)(2,1)} %bitcast.12.refs_0_, ...), custom_call_target="tpu_custom_call" | custom-call | tf_op jit(solution)/shard_map/update/pallas_call | solution.py:680
  (80 shorter events, 13.9 us)
Async XLA Ops:
  3.2 17.0 %collective-permute-start.1 = (bf16[1040,256]{1,0:T(8,128)(2,1)}, bf16[1040,256]{1,0:T(8,128)(2,1)}, u32[]{:S(2)}, u32[]{:S(2)}) collective-permute-start(bf16[1040,256]{1,0:T(8,128)(2,1)} %own_piece.1.refs_0_.first), channel_id=1, source_target_pairs={{0,2},{1,3},{2,0},{3,1},{4,6},{5,7},{6,4},{7,5},{8,10},{9,11},{10,... | collective-permute-start | bytes 1597448 | tf_op jit(solution)/shard_map/ppermute | solution.py:185
  4.9 14.1 %collective-permute-start.3 = (bf16[1040,256]{1,0:T(8,128)(2,1)}, bf16[1040,256]{1,0:T(8,128)(2,1)}, u32[]{:S(2)}, u32[]{:S(2)}) collective-permute-start(bf16[1040,256]{1,0:T(8,128)(2,1)} %own_piece.1.refs_0_.first), channel_id=1, source_target_pairs={{2,4},{3,5},{4,2},{5,3},{10,12},{11,13},{12,10},{13,11},{18,20},{1... | collective-permute-start | bytes 1597448 | tf_op jit(solution)/shard_map/ppermute | solution.py:185
  9.1 24.9 %collective-permute-start.13 = (bf16[4,1,2,512,128]{4,3,2,1,0:T(8,128)(2,1)}, bf16[4,1,2,512,128]{4,3,2,1,0:T(8,128)(2,1)S(1)}, u32[]{:S(2)}, u32[]{:S(2)}) collective-permute-start(bf16[4,1,2,512,128]{4,3,2,1,0:T(8,128)(2,1)} %pack.2.first), channel_id=1, source_target_pairs={{0,1},{1,0},{2,3},{3,2},{4,5},{5,4},{6,7},{7,6},{8,9},{9,8},{10,11... | collective-permute-start | bytes 3145736 | tf_op jit(solution)/shard_map/ppermute | solution.py:76
  13.3 13.6 %collective-permute-start.9 = (bf16[768,512]{1,0:T(8,128)(2,1)}, bf16[768,512]{1,0:T(8,128)(2,1)}, u32[]{:S(2)}, u32[]{:S(2)}) collective-permute-start(bf16[768,512]{1,0:T(8,128)(2,1)} %get-tuple-element.27), channel_id=1, source_target_pairs={{0,8},{8,16},{16,24},{1,9},{9,17},{17,25},{2,10},{10,18},{18,26},{... | collective-permute-start | bytes 2359304 | tf_op jit(solution)/shard_map/ppermute | solution.py:705
  15.3 13.5 %collective-permute-start.10 = (bf16[768,512]{1,0:T(8,128)(2,1)}, bf16[768,512]{1,0:T(8,128)(2,1)}, u32[]{:S(2)}, u32[]{:S(2)}) collective-permute-start(bf16[768,512]{1,0:T(8,128)(2,1)} %get-tuple-element.26), channel_id=1, source_target_pairs={{8,0},{16,8},{24,16},{9,1},{17,9},{25,17},{10,2},{18,10},{26,18},{... | collective-permute-start | bytes 2359304 | tf_op jit(solution)/shard_map/ppermute | solution.py:705
  18.9 17.1 %collective-permute-start.4 = (bf16[1040,256]{1,0:T(8,128)(2,1)}, bf16[1040,256]{1,0:T(8,128)(2,1)}, u32[]{:S(2)}, u32[]{:S(2)}) collective-permute-start(bf16[1040,256]{1,0:T(8,128)(2,1)} %collective-permute-done.3), channel_id=1, source_target_pairs={{2,0},{3,1},{4,6},{5,7},{10,8},{11,9},{12,14},{13,15},{18,16},{19,... | collective-permute-start | bytes 1597448 | tf_op jit(solution)/shard_map/ppermute | solution.py:185
  20.2 15.7 %collective-permute-start.6 = (bf16[1040,256]{1,0:T(8,128)(2,1)}, bf16[1040,256]{1,0:T(8,128)(2,1)S(1)}, u32[]{:S(2)}, u32[]{:S(2)}) collective-permute-start(bf16[1040,256]{1,0:T(8,128)(2,1)} %collective-permute-done.1.refs_2_), channel_id=1, source_target_pairs={{2,4},{3,5},{4,2},{5,3},{10,12},{11,13},{12,10},{13,11},{18,20},{1... | collective-permute-start | bytes 1597448 | tf_op jit(solution)/shard_map/ppermute | solution.py:185
  34.0 2.0 %copy-start.1 = (bf16[4,1,2,512,128]{4,3,2,1,0:T(8,128)(2,1)}, bf16[4,1,2,512,128]{4,3,2,1,0:T(8,128)(2,1)S(1)}, u32[]{:S(2)}) copy-start(bf16[4,1,2,512,128]{4,3,2,1,0:T(8,128)(2,1)S(1)} %collective-permute-done.13.refs_5_) | copy-start | bytes 3145732
  36.0 0.8 copy-start.3
  36.8 7.0 %copy-start = (bf16[1040,256]{1,0:T(8,128)(2,1)S(1)}, bf16[1040,256]{1,0:T(8,128)(2,1)}, u32[]{:S(2)}) copy-start(bf16[1040,256]{1,0:T(8,128)(2,1)} %own_piece.1.refs_0_.first) | copy-start | bytes 1597444
  36.8 8.7 %copy-start.4 = (bf16[1040,256]{1,0:T(8,128)(2,1)S(1)}, bf16[1040,256]{1,0:T(8,128)(2,1)}, u32[]{:S(2)}) copy-start(bf16[1040,256]{1,0:T(8,128)(2,1)} %copy-done.3) | copy-start | bytes 1597444
  36.8 57.6 %all-to-all-start = ((bf16[4,2,2,512,128]{4,3,2,1,0:T(8,128)(2,1)}), bf16[4,2,2,512,128]{4,3,2,1,0:T(8,128)(2,1)}, u32[]{:S(2)}, u32[]{:S(2)}) async-start(bf16[4,2,2,512,128]{4,3,2,1,0:T(8,128)(2,1)} %after.2), calls=%async_computation | async-start | bytes 4194304 | tf_op jit(solution)/shard_map/all_to_all | solution.py:158
  42.5 49.1 %copy-start.2 = (bf16[4,1,2,512,128]{4,3,2,1,0:T(8,128)(2,1)S(1)}, bf16[4,1,2,512,128]{4,3,2,1,0:T(8,128)(2,1)}, u32[]{:S(2)}) copy-start(bf16[4,1,2,512,128]{4,3,2,1,0:T(8,128)(2,1)} %copy-done.1) | copy-start | bytes 3145732
  42.5 49.1 %collective-permute-start.14 = (bf16[4,1,2,512,128]{4,3,2,1,0:T(8,128)(2,1)}, bf16[4,1,2,512,128]{4,3,2,1,0:T(8,128)(2,1)}, u32[]{:S(2)}, u32[]{:S(2)}) collective-permute-start(bf16[4,1,2,512,128]{4,3,2,1,0:T(8,128)(2,1)} %get-tuple-element.19), channel_id=1, source_target_pairs={{0,1},{1,0},{2,3},{3,2},{4,5},{5,4},{6,7},{7,6},{8,9},{9,8},{10,11... | collective-permute-start | bytes 3145736 | tf_op jit(solution)/shard_map/ppermute | solution.py:76
  43.8 55.1 %collective-permute-start = (bf16[1040,256]{1,0:T(8,128)(2,1)S(1)}, bf16[1040,256]{1,0:T(8,128)(2,1)}, u32[]{:S(2)}, u32[]{:S(2)}) collective-permute-start(bf16[1040,256]{1,0:T(8,128)(2,1)S(1)} %copy-done), channel_id=1, source_target_pairs={{0,1},{1,0},{2,3},{3,2},{4,5},{5,4},{6,7},{7,6},{8,9},{9,8},{10,11... | collective-permute-start | bytes 1597448 | tf_op jit(solution)/shard_map/ppermute | solution.py:76
  45.5 45.1 %collective-permute-start.7 = (bf16[1040,256]{1,0:T(8,128)(2,1)S(1)}, bf16[1040,256]{1,0:T(8,128)(2,1)S(1)}, u32[]{:S(2)}, u32[]{:S(2)}) collective-permute-start(bf16[1040,256]{1,0:T(8,128)(2,1)S(1)} %copy-done.4), channel_id=1, source_target_pairs={{2,0},{3,1},{4,6},{5,7},{10,8},{11,9},{12,14},{13,15},{18,16},{19,... | collective-permute-start | bytes 1597448 | tf_op jit(solution)/shard_map/ppermute | solution.py:185
  46.8 52.1 %collective-permute-start.2 = (bf16[1040,256]{1,0:T(8,128)(2,1)}, bf16[1040,256]{1,0:T(8,128)(2,1)}, u32[]{:S(2)}, u32[]{:S(2)}) collective-permute-start(bf16[1040,256]{1,0:T(8,128)(2,1)} %collective-permute-done.1.refs_2_), channel_id=1, source_target_pairs={{0,1},{1,0},{2,3},{3,2},{4,5},{5,4},{6,7},{7,6},{8,9},{9,8},{10,11... | collective-permute-start | bytes 1597448 | tf_op jit(solution)/shard_map/ppermute | solution.py:76
  49.5 44.9 %copy-start.5 = (bf16[1040,256]{1,0:T(8,128)(2,1)}, bf16[1040,256]{1,0:T(8,128)(2,1)S(1)}, u32[]{:S(2)}) copy-start(bf16[1040,256]{1,0:T(8,128)(2,1)S(1)} %add.189.refs_4_) | copy-start | bytes 1597444
  49.5 53.7 %collective-permute-start.5 = (bf16[1040,256]{1,0:T(8,128)(2,1)S(1)}, bf16[1040,256]{1,0:T(8,128)(2,1)}, u32[]{:S(2)}, u32[]{:S(2)}) collective-permute-start(bf16[1040,256]{1,0:T(8,128)(2,1)S(1)} %add.189.refs_4_), channel_id=1, source_target_pairs={{0,1},{1,0},{2,3},{3,2},{4,5},{5,4},{6,7},{7,6},{8,9},{9,8},{10,11... | collective-permute-start | bytes 1597448 | tf_op jit(solution)/shard_map/ppermute | solution.py:76
  91.6 20.3 %collective-permute-start.8 = (bf16[1040,256]{1,0:T(8,128)(2,1)}, bf16[1040,256]{1,0:T(8,128)(2,1)S(1)}, u32[]{:S(2)}, u32[]{:S(2)}) collective-permute-start(bf16[1040,256]{1,0:T(8,128)(2,1)} %add.190.refs_6_), channel_id=1, source_target_pairs={{0,1},{1,0},{2,3},{3,2},{4,5},{5,4},{6,7},{7,6},{8,9},{9,8},{10,11... | collective-permute-start | bytes 1597448 | tf_op jit(solution)/shard_map/ppermute | solution.py:76
  94.4 58.8 %all-to-all-start.1 = ((bf16[4,2,2,512,128]{4,3,2,1,0:T(8,128)(2,1)}), bf16[4,2,2,512,128]{4,3,2,1,0:T(8,128)(2,1)}, u32[]{:S(2)}, u32[]{:S(2)}) async-start(bf16[4,2,2,512,128]{4,3,2,1,0:T(8,128)(2,1)} %after.3), calls=%async_computation.1 | async-start | bytes 4194304 | tf_op jit(solution)/shard_map/all_to_all | solution.py:158
  111.9 0.8 copy-start.6
  118.4 25.6 %collective-permute-start.11 = (bf16[2,512,256]{2,1,0:T(8,128)(2,1)}, bf16[2,512,256]{2,1,0:T(8,128)(2,1)S(1)}, u32[]{:S(2)}, u32[]{:S(2)}) collective-permute-start(bf16[2,512,256]{2,1,0:T(8,128)(2,1)} %get-tuple-element.13.h_last), channel_id=1, source_target_pairs={{0,8},{8,16},{16,24},{1,9},{9,17},{17,25},{2,10},{10,18},{18,26},{... | collective-permute-start | bytes 1572872 | tf_op jit(solution)/shard_map/ppermute | solution.py:705
  120.3 23.7 %collective-permute-start.12 = (bf16[2,512,256]{2,1,0:T(8,128)(2,1)}, bf16[2,512,256]{2,1,0:T(8,128)(2,1)S(1)}, u32[]{:S(2)}, u32[]{:S(2)}) collective-permute-start(bf16[2,512,256]{2,1,0:T(8,128)(2,1)} %get-tuple-element.14.h_first), channel_id=1, source_target_pairs={{8,0},{16,8},{24,16},{9,1},{17,9},{25,17},{10,2},{18,10},{26,18},{... | collective-permute-start | bytes 1572872 | tf_op jit(solution)/shard_map/ppermute | solution.py:705
  144.1 0.8 copy-start.7
  144.1 1.0 copy-start.8
  158.0 12.6 %all-to-all-start.2 = ((f32[8,24,128]{2,1,0:T(8,128)}), f32[8,24,128]{2,1,0:T(8,128)S(1)}, u32[]{:S(2)}, u32[]{:S(2)}) async-start(f32[8,24,128]{2,1,0:T(8,128)} %project.1), calls=%async_computation.2 | async-start | bytes 196608 | tf_op jit(solution)/shard_map/all_to_all | solution.py:785
  170.5 0.6 copy-start.9

commit v4 on v3

--- a/solution.py
+++ b/solution.py
@@ -15,7 +15,7 @@
 CAP = 2
 P_SIZE = 128
 MIB = 1 << 20
-LISTS = 16
+LISTS = 8
 
 exchange_factor = (3.0 / math.pi) ** (1.0 / 3.0)
 HBM = pl.BlockSpec(memory_space=pltpu.HBM)
@@ -30,20 +30,20 @@
     return (me + j) % count
 
 
-def piece_kernel(peers, named, counts, pattern, ham, piece, blocks, sems):
-    rows = ham.shape[0]
-    load = pltpu.make_async_copy(ham, blocks.at[pl.ds(0, rows)], sems.at[0])
+def piece_kernel(peers, named, counts, pattern, ham, piece, lists, blocks, sems):
+    load = pltpu.make_async_copy(ham, blocks, sems.at[0])
     load.start()
-    lane = lax.broadcasted_iota(jnp.int32, (LISTS, W), 1)
-    lists = jnp.zeros((LISTS, W), jnp.int32)
+    lane = lax.broadcasted_iota(jnp.int32, (LISTS, P_SIZE), 1)
+    row = jnp.zeros((LISTS, P_SIZE), jnp.int32)
     at = 0
     for ref in (peers, named, counts):
         for i in range(ref.shape[0]):
-            lists = jnp.where(lane == at, ref[i], lists)
+            row = jnp.where(lane == at, ref[i], row)
             at += 1
-    blocks[rows:] = lists.astype(jnp.float32).astype(jnp.bfloat16)
+    for c in range(lists.shape[0]):
+        lists[c] = row
     load.wait()
-    for i in range(rows // (2 * W)):
+    for i in range(ham.shape[0] // (2 * W)):
         coupling = slice((2 * i + 1) * W, (2 * i + 2) * W)
         blocks[coupling] = blocks[coupling] * pattern[i].astype(jnp.bfloat16)
     store = pltpu.make_async_copy(blocks, piece, sems.at[1])
@@ -51,14 +51,16 @@
     store.wait()
 
 
-def own_piece(peers, named, counts, pattern, ham):
-    piece = (ham.shape[0] + LISTS, W)
+def own_piece(peers, named, counts, pattern, ham, col_count):
     return pl.pallas_call(
         piece_kernel,
-        out_shape=jax.ShapeDtypeStruct(piece, ham.dtype),
+        out_shape=(
+            jax.ShapeDtypeStruct(ham.shape, ham.dtype),
+            jax.ShapeDtypeStruct((col_count, LISTS, P_SIZE), jnp.int32),
+        ),
         in_specs=[SMEM] * 4 + [HBM],
-        out_specs=HBM,
-        scratch_shapes=[pltpu.VMEM(piece, ham.dtype), pltpu.SemaphoreType.DMA((2,))],
+        out_specs=(HBM, VMEM),
+        scratch_shapes=[pltpu.VMEM(ham.shape, ham.dtype), pltpu.SemaphoreType.DMA((2,))],
         compiler_params=pltpu.CompilerParams(vmem_limit_bytes=62 * MIB),
         name="own_piece",
     )(peers, named, counts, pattern, ham)
@@ -216,9 +218,8 @@
 
 
 def edge_kernel(col_count, depth, owners, *refs):
-    pieces, (first, last, lists, sems, list_sems) = refs[:-5], refs[-5:]
-    rows = pieces[0].shape[0] - LISTS
-    held = rows // (2 * W)
+    pieces, (first, last, sems) = refs[:-3], refs[-3:]
+    held = pieces[0].shape[0] // (2 * W)
     total = col_count * held
 
     def each(act):
@@ -232,12 +233,6 @@
                     def _():
                         act(copy)
 
-            @pl.when(owners[i] >= 0)
-            def _():
-                act(pltpu.make_async_copy(
-                    piece.at[pl.ds(rows, LISTS)], lists.at[owners[i]], list_sems.at[i]
-                ))
-
     each(lambda copy: copy.start())
     each(lambda copy: copy.wait())
 
@@ -246,13 +241,11 @@
     shape = jax.ShapeDtypeStruct((depth, 2 * W, W), pieces[0].dtype)
     return pl.pallas_call(
         functools.partial(edge_kernel, col_count, depth),
-        out_shape=(shape, shape, jax.ShapeDtypeStruct((col_count, LISTS, W), pieces[0].dtype)),
+        out_shape=(shape, shape),
         in_specs=[SMEM] + [HBM] * len(pieces),
-        out_specs=(VMEM, VMEM, VMEM),
-        scratch_shapes=[
-            pltpu.SemaphoreType.DMA((2, depth)),
-            pltpu.SemaphoreType.DMA((len(pieces),)),
-        ],
+        out_specs=(VMEM, VMEM),
+        scratch_shapes=[pltpu.SemaphoreType.DMA((2, depth))],
+        compiler_params=pltpu.CompilerParams(vmem_limit_bytes=62 * MIB),
         name="edge_blocks",
     )(owners, *pieces)
 
@@ -282,7 +275,7 @@
         *pieces, out, edge_1, edge_2, edge_total,
         vext, hraw, hcat, cheb_1, cheb_2, total, kern, sems, psems, osems, esems,
     ) = refs
-    held = (pieces[0].shape[0] - LISTS) // (2 * W)
+    held = pieces[0].shape[0] // (2 * W)
     v_copies = [
         pltpu.make_async_copy(v_low.at[rows_of(DEG - 1)], vext.at[rows_of(0)], sems.at[0]),
         pltpu.make_async_copy(v_mid, vext.at[rows_of(1, blocks)], sems.at[1]),
@@ -302,7 +295,8 @@
     for copy in v_copies:
         copy.start()
     each_piece(lambda copy: copy.wait())
-    lax.fori_loop(0, blocks, band_builder(hraw, hcat), 0, unroll=2)
+    build = band_builder(hraw, hcat)
+    build(0, 0)
     for copy in v_copies:
         copy.wait()
 
@@ -320,11 +314,12 @@
 
     def first(j, carry):
         value = band(vext, j, j)
+        build(jnp.minimum(j + 1, blocks - 1), 0)
         cheb_1[rows_of(j), :] = value.astype(jnp.bfloat16)
         total[rows_of(j), :] = value
         return carry
 
-    lax.fori_loop(0, blocks, first, 0, unroll=2)
+    lax.fori_loop(0, blocks, first, 0, unroll=4)
 
     def second(j, carry):
         begin = vext[rows_of(j + 2), :].astype(jnp.float32)
@@ -335,7 +330,7 @@
         )
         return carry
 
-    lax.fori_loop(0, blocks - 2, second, 0, unroll=2)
+    lax.fori_loop(0, blocks - 2, second, 0, unroll=4)
     outgoing = (
         edges(cheb_1, edge_1, 0) + edges(cheb_2, edge_2, 1) + edges(total, edge_total, 2)
     )
@@ -354,7 +349,7 @@
         return carry
 
     last = blocks // (KB // W) - 1
-    lax.fori_loop(1, last, third, 0)
+    lax.fori_loop(1, last, third, 0, unroll=2)
     for j in range(1, last):
         store(j).wait()
     for copy in outgoing:
@@ -366,7 +361,7 @@
     cols = v_mid.shape[1]
     flops = 2 * W * 3 * W * cols * (3 * blocks - 6)
     result = (blocks * W // KB, cols, KB)
-    held = (pieces[0].shape[0] - LISTS) // (2 * W)
+    held = pieces[0].shape[0] // (2 * W)
     return pl.pallas_call(
         functools.partial(inner_kernel, blocks),
         out_shape=(
@@ -403,41 +398,59 @@
 ):
     last = kern.shape[0] - 1
     end = out.shape[0] - 1
-    copies = [
-        (h_low, hraw.at[pl.ds(0, 2)]),
-        (h_first, hraw.at[pl.ds(2, 2)]),
-        (h_last, hraw.at[pl.ds(4, 2)]),
-        (h_high, hraw.at[pl.ds(6, 2)]),
-        (v_low, v.at[0, rows_of(0, 3)]),
-        (v_mid.at[rows_of(0)], v.at[0, rows_of(3)]),
-        (v_mid.at[rows_of(blocks - 1)], v.at[1, rows_of(0)]),
-        (v_high, v.at[1, rows_of(1, 3)]),
-        (edge_1.at[rows_of(0, 2)], cheb_1.at[0, rows_of(2, 2)]),
-        (edge_1.at[rows_of(2, 2)], cheb_1.at[1, rows_of(0, 2)]),
-        (edge_2.at[rows_of(0, 2)], cheb_2.at[0, rows_of(2, 2)]),
-        (edge_2.at[rows_of(2, 2)], cheb_2.at[1, rows_of(0, 2)]),
-        (edge_total.at[rows_of(0, 2)], total.at[0]),
-        (edge_total.at[rows_of(2, 2)], total.at[1]),
+    stages = [
+        [
+            (h_low, hraw.at[pl.ds(0, 2)]),
+            (v_low, v.at[0, rows_of(0, 3)]),
+            (v_mid.at[rows_of(0)], v.at[0, rows_of(3)]),
+            (h_high, hraw.at[pl.ds(6, 2)]),
+            (v_mid.at[rows_of(blocks - 1)], v.at[1, rows_of(0)]),
+            (v_high, v.at[1, rows_of(1, 3)]),
+        ],
+        [
+            (h_first, hraw.at[pl.ds(2, 2)]),
+            (h_last, hraw.at[pl.ds(4, 2)]),
+            (edge_1.at[rows_of(0, 2)], cheb_1.at[0, rows_of(2, 2)]),
+            (edge_1.at[rows_of(2, 2)], cheb_1.at[1, rows_of(0, 2)]),
+        ],
+        [
+            (edge_2.at[rows_of(0, 2)], cheb_2.at[0, rows_of(2, 2)]),
+            (edge_2.at[rows_of(2, 2)], cheb_2.at[1, rows_of(0, 2)]),
+            (edge_total.at[rows_of(0, 2)], total.at[0]),
+            (edge_total.at[rows_of(2, 2)], total.at[1]),
+        ],
     ]
-    copies = [
-        pltpu.make_async_copy(source, target, sems.at[i])
-        for i, (source, target) in enumerate(copies)
-    ]
-    for copy in copies:
-        copy.start()
-    for copy in copies:
-        copy.wait()
-    lax.fori_loop(0, 8, band_builder(hraw, hcat), 0, unroll=2)
+    at = 0
+    for i, stage in enumerate(stages):
+        stages[i] = [
+            pltpu.make_async_copy(source, target, sems.at[at + n])
+            for n, (source, target) in enumerate(stage)
+        ]
+        at += len(stage)
+        for copy in stages[i]:
+            copy.start()
+    build = band_builder(hraw, hcat)
+
+    def arrived(i):
+        for copy in stages[i]:
+            copy.wait()
 
     def band(side, j, source, row):
         return jnp.dot(
             hcat[4 * side + j], source[side, rows_of(row, 3), :], preferred_element_type=jnp.float32
         )
 
+    arrived(0)
+    for j in (0, 1, 6, 7):
+        build(j, 0)
     for side, places in ((0, (0, 1)), (1, (2, 3))):
         for j in places:
             value = band(side, j, v, j - 2 * side)
             cheb_1[side, rows_of(j), :] = value.astype(jnp.bfloat16)
+    arrived(1)
+    for j in (2, 3, 4, 5):
+        build(j, 0)
+    arrived(2)
     for side, places in ((0, ((1, 0), (2, 1))), (1, ((2, 3), (1, 2)))):
         for j, place in places:
             begin = v[side, rows_of(place + 2 - 4 * side), :].astype(jnp.float32)
@@ -708,7 +721,7 @@
 def make_plan(lists, me, entries, tiles, col_count, blocks):
     slots = col_count * CAP
     sent = sent_rows(slots, tiles)
-    lists = lists[:, : 2 * entries + tiles].astype(jnp.int32)
+    lists = lists[:, : 2 * entries + tiles]
     peers, named, counts = lists[:, :entries], lists[:, entries : 2 * entries], lists[:, 2 * entries :]
     index = jnp.arange(entries, dtype=jnp.int32)
     home = jnp.arange(col_count, dtype=jnp.int32)[:, None]
@@ -767,13 +780,16 @@
     peers = tile_peer[:, 0]
     me = lax.axis_index("col").astype(jnp.int32)
 
-    own = own_piece(peers, tile_block, tile_count, band_pattern, hamiltonian.reshape(-1, W))
+    own, lists = own_piece(
+        peers, tile_block, tile_count, band_pattern, hamiltonian.reshape(-1, W), col_count
+    )
+    lists = lax.all_to_all(lists, "col", split_axis=0, concat_axis=0, tiled=True)
     pieces, owners, awaited = gather_pieces(own)
     v_low = shift(start_columns[-DEG * W :], "row", 1)
     v_high = shift(start_columns[: DEG * W], "row", -1)
-    parts = exchange(me[None], peers, basis_values, own, awaited + [v_low, v_high])
-
-    first, last, lists = edge_blocks(owners, pieces, col_count, DEG - 1)
+    parts = exchange(me[None], peers, basis_values, own, awaited + [v_low, v_high, lists])
+
+    first, last = edge_blocks(owners, pieces, col_count, DEG - 1)
     h_low = shift(last, "row", 1)
     h_high = shift(first, "row", -1)
     inner = chebyshev_inner(coefficients, owners, v_low, start_columns, v_high, pieces)

time: 180 us -> 205 us (1.14)
  waiting for transfers between devices: 71.1 us -> 91.9 us
  starting transfers between devices: 38.9 us -> 46.5 us
  Pallas kernels: 49.7 us -> 47.2 us
    all_to_all x2, waiting for transfers between devices: 0.01 us -> 19.8 us  [between_lines(): lax.all_to_all(after(block, *others), 'col', split_axis=0, concat_axis=0,...]
    ppermute x5, waiting for transfers between devices: 42.3 us -> 30 us  [move(): return lax.ppermute(block, 'col', pairs)]
    ppermute x6, waiting for transfers between devices: 18.3 us -> 30.4 us  [swap_along(): return lax.ppermute(block, 'col', pairs)]
    all_to_all x0 -> x1, starting transfers between devices: none -> 7.64 us  [shards(): lax.all_to_all(lists, 'col', split_axis=0, concat_axis=0, tiled=True)]
    all_to_all x0 -> x1, waiting for transfers between devices: none -> 5.34 us  [shards(): lax.all_to_all(lists, 'col', split_axis=0, concat_axis=0, tiled=True)]
    ppermute x4, waiting for transfers between devices: 4.17 us -> 0.01 us  [shift(): return lax.ppermute(block, axis, pairs)]
    unnamed x22 -> x25, local copies, waits for them, and re-layouts: 3.27 us -> 4.49 us
  transfers between devices with their start and end apart: 18 -> 19, of which waited for: 8 -> 6; matrix products, arithmetic and copies ran while one was open for 8% -> 6% of each run, Pallas kernels for 20% -> 16%
where the time goes in v4:
time: 205 us; the launch traced here: 204 us
  waiting for transfers between devices  91.9 us (45%)
  Pallas kernels  47.2 us (23%)
  starting transfers between devices  46.5 us (23%)
  local copies, waits for them, and re-layouts  10 us (5%)
  other arithmetic  7.29 us (4%)
    ppermute x6, waiting for transfers between devices, swap_along(): return lax.ppermute(block, 'col', pairs)  30.4 us
    ppermute x5, waiting for transfers between devices, move(): return lax.ppermute(block, 'col', pairs)  30 us
    all_to_all x2, waiting for transfers between devices, between_lines(): lax.all_to_all(after(block, *others), 'col', split_axis=0, concat_axis=0,...  19.8 us
    pallas_call x1, Pallas kernels, chebyshev_inner(): pl.pallas_call(functools.partial(inner_kernel, blocks), out_shape=(jax.Sh...  16.4 us
    ppermute x4, starting transfers between devices, shift(): return lax.ppermute(block, axis, pairs)  11.1 us
    all_to_all x2, starting transfers between devices, between_lines(): lax.all_to_all(after(block, *others), 'col', split_axis=0, concat_axis=0,...  9.04 us
    all_to_all x1, starting transfers between devices, shards(): lax.all_to_all(lists, 'col', split_axis=0, concat_axis=0, tiled=True)  7.64 us
    ppermute x5, starting transfers between devices, move(): return lax.ppermute(block, 'col', pairs)  7.14 us
  transfers between devices with their start and end apart: 19, of which 6 were waited for; matrix products, arithmetic and copies ran while one was open for 6% of the time, Pallas kernels for 16%

profile of v4, /device:TPU:2, one launch (start us, length us, event | category | flops | bytes accessed | tf_op | source)
XLA Modules:
  0.0 203.9 jit_solution(2090735434771078607)
XLA Ops:
  0.6 3.2 %own_piece.1 = (bf16[1024,256]{1,0:T(8,128)(2,1)}, s32[8,8,128]{2,1,0:T(8,128)}) custom-call(s32[16]{0:T(128)} %bitcast.32, s32[16]{0:T(128)} %named.1, s32[4]{0:T(128)} %counts.1, s32[2]{0:T(128)} %pattern.1, bf16[1024,256]{1,0:T(8,128)(2,1)} %bitcast.24), custom_call_target="tpu_custom_call" | custom-call | tf_op jit(solution)/shard_map/own_piece/pallas_call | solution.py:55
  3.8 1.6 collective-permute-start.3
  5.5 1.5 collective-permute-start.5
  6.9 2.8 %pack.2.first = bf16[4,1,2,512,128]{4,3,2,1,0:T(8,128)(2,1)} custom-call(s32[1]{0:T(128)} %bitcast.4.me, s32[16]{0:T(128)} %bitcast.33, bf16[16,2,512,128]{3,2,1,0:T(8,128)(2,1)} %basis.3, bf16[1024,256]{1,0:T(8,128)(2,1)} %get-tuple-element.13.refs_0_.first), custom_call_target="tpu_custom_call" | custom-call | tf_op jit(solution)/shard_map/pack/pallas_call | solution.py:121
  9.7 1.6 collective-permute-start.13
  11.3 2.6 %fusion.12 = (bf16[768,512]{1,0:T(8,128)(2,1)}, bf16[768,512]{1,0:T(8,128)(2,1)}) fusion(bf16[4096,512]{1,0:T(8,128)(2,1)} %v_mid.3), kind=kLoop, calls=%fused_computation.53 | loop fusion | bytes 3145728 | tf_op jit(solution)/shard_map/slice | solution.py:789
  13.9 1.9 collective-permute-start
  15.8 3.6 %collective-permute-start.1 = (bf16[768,512]{1,0:T(8,128)(2,1)}, bf16[768,512]{1,0:T(8,128)(2,1)}, u32[]{:S(2)}, u32[]{:S(2)}) collective-permute-start(bf16[768,512]{1,0:T(8,128)(2,1)} %get-tuple-element.28), channel_id=1, source_target_pairs={{8,0},{16,8},{24,16},{9,1},{17,9},{25,17},{10,2},{18,10},{26,18},{... | collective-permute-start | bytes 2359304 | tf_op jit(solution)/shard_map/ppermute | solution.py:718
  19.5 1.5 collective-permute-start.8
  22.2 7.6 %all-to-all-start = ((s32[8,8,128]{2,1,0:T(8,128)}), s32[8,8,128]{2,1,0:T(8,128)S(1)}, u32[]{:S(2)}, u32[]{:S(2)}) async-start(s32[8,8,128]{2,1,0:T(8,128)} %get-tuple-element.12), calls=%async_computation | async-start | bytes 65536 | tf_op jit(solution)/shard_map/all_to_all | solution.py:786
  29.9 3.6 %pack.3 = (bf16[4,2,2,512,128]{4,3,2,1,0:T(8,128)(2,1)}, bf16[4,1,2,512,128]{4,3,2,1,0:T(8,128)(2,1)}) custom-call(s32[1]{0:T(128)} %bitcast.4.me, s32[16]{0:T(128)} %bitcast.34, bf16[16,2,512,128]{3,2,1,0:T(8,128)(2,1)} %basis.3, bf16[4,1,2,512,128]{4,3,2,1,0:T(8,128)(2,1)} %pack.2.first), custom_call_target="tpu_custom_call" | custom-call | tf_op jit(solution)/shard_map/pack/pallas_call | solution.py:121
  33.5 5.3 %all-to-all-done.refs_5_ = s32[8,8,128]{2,1,0:T(8,128)S(1)} async-done(((s32[8,8,128]{2,1,0:T(8,128)}), s32[8,8,128]{2,1,0:T(8,128)S(1)}, u32[]{:S(2)}, u32[]{:S(2)}) %all-to-all-start) | async-done | bytes 32800 | tf_op jit(solution)/shard_map/all_to_all | solution.py:786
  40.1 4.6 %all-to-all-start.1 = ((bf16[4,2,2,512,128]{4,3,2,1,0:T(8,128)(2,1)}), bf16[4,2,2,512,128]{4,3,2,1,0:T(8,128)(2,1)}, u32[]{:S(2)}, u32[]{:S(2)}) async-start(bf16[4,2,2,512,128]{4,3,2,1,0:T(8,128)(2,1)} %after.2), calls=%async_computation.1 | async-start | bytes 4194304 | tf_op jit(solution)/shard_map/all_to_all | solution.py:160
  44.6 1.5 collective-permute-start.14
  47.6 23.4 %collective-permute-done.14 = bf16[4,1,2,512,128]{4,3,2,1,0:T(8,128)(2,1)S(1)} collective-permute-done((bf16[4,1,2,512,128]{4,3,2,1,0:T(8,128)(2,1)}, bf16[4,1,2,512,128]{4,3,2,1,0:T(8,128)(2,1)S(1)}, u32[]{:S(2)}, u32[]{:S(2)}) %collective-permute-start.14) | collective-permute-done | bytes 1048608 | tf_op jit(solution)/shard_map/ppermute | solution.py:78
  71.0 1.5 pad_maximum_fusion.refs_0_
  72.6 19.8 %all-to-all-done.1.refs_1_ = bf16[4,2,2,512,128]{4,3,2,1,0:T(8,128)(2,1)} async-done(((bf16[4,2,2,512,128]{4,3,2,1,0:T(8,128)(2,1)}), bf16[4,2,2,512,128]{4,3,2,1,0:T(8,128)(2,1)}, u32[]{:S(2)}, u32[]{:S(2)}) %all-to-all-start.1) | async-done | bytes 2097184 | tf_op jit(solution)/shard_map/all_to_all | solution.py:160
  92.4 4.5 %all-to-all-start.2 = ((bf16[4,2,2,512,128]{4,3,2,1,0:T(8,128)(2,1)}), bf16[4,2,2,512,128]{4,3,2,1,0:T(8,128)(2,1)}, u32[]{:S(2)}, u32[]{:S(2)}) async-start(bf16[4,2,2,512,128]{4,3,2,1,0:T(8,128)(2,1)} %after.3), calls=%async_computation.2 | async-start | bytes 4194304 | tf_op jit(solution)/shard_map/all_to_all | solution.py:160
  98.3 1.3 collective-permute-start.9
  101.1 1.3 add.195.refs_4_
  103.6 30.0 %collective-permute-done.9 = bf16[1024,256]{1,0:T(8,128)(2,1)} collective-permute-done((bf16[1024,256]{1,0:T(8,128)(2,1)}, bf16[1024,256]{1,0:T(8,128)(2,1)}, u32[]{:S(2)}, u32[]{:S(2)}) %collective-permute-start.9) | collective-permute-done | bytes 524320 | tf_op jit(solution)/shard_map/ppermute | solution.py:187
  133.5 1.3 add.196.refs_6_
  140.0 7.0 %collective-permute-done.10.refs_7_ = bf16[1024,256]{1,0:T(8,128)(2,1)} collective-permute-done((bf16[1024,256]{1,0:T(8,128)(2,1)S(1)}, bf16[1024,256]{1,0:T(8,128)(2,1)}, u32[]{:S(2)}, u32[]{:S(2)}) %collective-permute-start.10) | collective-permute-done | bytes 524320 | tf_op jit(solution)/shard_map/ppermute | solution.py:78
  147.0 2.9 %edge_blocks.1 = (bf16[2,512,256]{2,1,0:T(8,128)(2,1)}, bf16[2,512,256]{2,1,0:T(8,128)(2,1)}) custom-call(s32[8]{0:T(128)} %stack.35.owners, bf16[1024,256]{1,0:T(8,128)(2,1)} %get-tuple-element.13.refs_0_.first, bf16[1024,256]{1,0:T(8,128)(2,1)} %collective-permute-done.2.refs_1_, bf16[1024,256]{1,0:T(8,128)(2,1)} %collective-permute-done.3.refs_2_, ...), custom_call_target="tpu_custom_call" | custom-call | tf_op jit(solution)/shard_map/edge_blocks/pallas_call | solution.py:242
  149.9 1.9 collective-permute-start.11
  151.8 3.6 %collective-permute-start.12 = (bf16[2,512,256]{2,1,0:T(8,128)(2,1)}, bf16[2,512,256]{2,1,0:T(8,128)(2,1)S(1)}, u32[]{:S(2)}, u32[]{:S(2)}) collective-permute-start(bf16[2,512,256]{2,1,0:T(8,128)(2,1)} %get-tuple-element.16.h_first), channel_id=1, source_target_pairs={{8,0},{16,8},{24,16},{9,1},{17,9},{25,17},{10,2},{18,10},{26,18},{... | collective-permute-start | bytes 1572872 | tf_op jit(solution)/shard_map/ppermute | solution.py:718
  155.5 16.4 %chebyshev_inner.1 = (bf16[8,512,512]{2,1,0:T(8,128)(2,1)}, bf16[1024,512]{1,0:T(8,128)(2,1)}, bf16[1024,512]{1,0:T(8,128)(2,1)}, f32[1024,512]{1,0:T(8,128)}) custom-call(f32[4]{0:T(128)} %coef.3, s32[8]{0:T(128)} %stack.35.owners, bf16[768,512]{1,0:T(8,128)(2,1)} %copy-done.2, bf16[4096,512]{1,0:T(8,128)(2,1)} %v_mid.3, ...), custom_call_target="tpu_custom_call" | custom-call | flops 8455716864 | bytes 16777216 | tf_op jit(solution)/shard_map/chebyshev_inner/pallas_call | solution.py:365
  172.9 7.1 %chebyshev_outer.1.kernel_t = bf16[8,512,512]{2,1,0:T(8,128)(2,1)} custom-call(f32[4]{0:T(128)} %coef.3, bf16[8,512,512]{2,1,0:T(8,128)(2,1)} %get-tuple-element.14.kernel_in, bf16[768,512]{1,0:T(8,128)(2,1)} %copy-done.2, bf16[4096,512]{1,0:T(8,128)(2,1)} %v_mid.3, ...), custom_call_target="tpu_custom_call", output_to_operand_aliasing={{}: (1, {})} | custom-call | tf_op jit(solution)/shard_map/chebyshev_outer/pallas_call | solution.py:483
  180.0 4.7 %project.1 = f32[8,24,128]{2,1,0:T(8,128)} custom-call(s32[26]{0:T(128)} %pad_add_fusion.1.plan, s32[16]{0:T(128)} %select_reduce_fusion.2.order, bf16[8,512,512]{2,1,0:T(8,128)(2,1)} %chebyshev_outer.1.kernel_t, f32[4,128]{1,0:T(4,128)} %core.1, bf16[8,2,512,128]{3,2,1,0:T(8,128)(2,1)} %bitcast.13.refs_0_, bf16[8,2,512,128]{3,2,1,0:T(8,128)(2,1)} %bitcast.14.refs_1_), custom_call_target="tpu_custom_call" | custom-call | tf_op jit(solution)/shard_map/project/pallas_call | solution.py:595
  184.8 4.7 %all-to-all-start.3 = ((f32[8,24,128]{2,1,0:T(8,128)}), f32[8,24,128]{2,1,0:T(8,128)S(1)}, u32[]{:S(2)}, u32[]{:S(2)}) async-start(f32[8,24,128]{2,1,0:T(8,128)} %project.1), calls=%async_computation.3 | async-start | bytes 196608 | tf_op jit(solution)/shard_map/all_to_all | solution.py:801
  190.2 6.4 %all-to-all-done.3 = f32[8,24,128]{2,1,0:T(8,128)S(1)} async-done(((f32[8,24,128]{2,1,0:T(8,128)}), f32[8,24,128]{2,1,0:T(8,128)S(1)}, u32[]{:S(2)}, u32[]{:S(2)}) %all-to-all-start.3) | async-done | bytes 98336 | tf_op jit(solution)/shard_map/all_to_all | solution.py:801
  197.3 6.6 %update.1 = (f32[4,128]{1,0:T(4,128)}, bf16[4096,512]{1,0:T(8,128)(2,1)}) custom-call(s32[26]{0:T(128)} %pad_add_fusion.1.plan, s32[16]{0:T(128)} %select_reduce_fusion.2.order, s32[16]{0:T(128)} %reshape.285.tile_of, f32[192,128]{1,0:T(8,128)} %bitcast.25, f32[32,192]{1,0:T(8,128)} %convert_reduce_fusion.collect, bf16[8,2,512,128]{3,2,1,0:T(8,128)(2,1)} %bitcast.13.refs_0_, ...), custom_call_target="tpu_custom_call" | custom-call | tf_op jit(solution)/shard_map/update/pallas_call | solution.py:693
  (84 shorter events, 15.6 us)
Async XLA Ops:
  3.8 15.7 %collective-permute-start.3 = (bf16[1024,256]{1,0:T(8,128)(2,1)}, bf16[1024,256]{1,0:T(8,128)(2,1)}, u32[]{:S(2)}, u32[]{:S(2)}) collective-permute-start(bf16[1024,256]{1,0:T(8,128)(2,1)} %get-tuple-element.13.refs_0_.first), channel_id=1, source_target_pairs={{0,2},{1,3},{2,0},{3,1},{4,6},{5,7},{6,4},{7,5},{8,10},{9,11},{10,... | collective-permute-start | bytes 1572872 | tf_op jit(solution)/shard_map/ppermute | solution.py:187
  5.5 15.5 %collective-permute-start.5 = (bf16[1024,256]{1,0:T(8,128)(2,1)}, bf16[1024,256]{1,0:T(8,128)(2,1)}, u32[]{:S(2)}, u32[]{:S(2)}) collective-permute-start(bf16[1024,256]{1,0:T(8,128)(2,1)} %get-tuple-element.13.refs_0_.first), channel_id=1, source_target_pairs={{2,4},{3,5},{4,2},{5,3},{10,12},{11,13},{12,10},{13,11},{18,20},{1... | collective-permute-start | bytes 1572872 | tf_op jit(solution)/shard_map/ppermute | solution.py:187
  9.7 29.2 %collective-permute-start.13 = (bf16[4,1,2,512,128]{4,3,2,1,0:T(8,128)(2,1)}, bf16[4,1,2,512,128]{4,3,2,1,0:T(8,128)(2,1)S(1)}, u32[]{:S(2)}, u32[]{:S(2)}) collective-permute-start(bf16[4,1,2,512,128]{4,3,2,1,0:T(8,128)(2,1)} %pack.2.first), channel_id=1, source_target_pairs={{0,1},{1,0},{2,3},{3,2},{4,5},{5,4},{6,7},{7,6},{8,9},{9,8},{10,11... | collective-permute-start | bytes 3145736 | tf_op jit(solution)/shard_map/ppermute | solution.py:78
  13.9 24.9 %collective-permute-start = (bf16[768,512]{1,0:T(8,128)(2,1)}, bf16[768,512]{1,0:T(8,128)(2,1)S(1)}, u32[]{:S(2)}, u32[]{:S(2)}) collective-permute-start(bf16[768,512]{1,0:T(8,128)(2,1)} %get-tuple-element.29), channel_id=1, source_target_pairs={{0,8},{8,16},{16,24},{1,9},{9,17},{17,25},{2,10},{10,18},{18,26},{... | collective-permute-start | bytes 2359304 | tf_op jit(solution)/shard_map/ppermute | solution.py:718
  15.8 23.0 %collective-permute-start.1 = (bf16[768,512]{1,0:T(8,128)(2,1)}, bf16[768,512]{1,0:T(8,128)(2,1)}, u32[]{:S(2)}, u32[]{:S(2)}) collective-permute-start(bf16[768,512]{1,0:T(8,128)(2,1)} %get-tuple-element.28), channel_id=1, source_target_pairs={{8,0},{16,8},{24,16},{9,1},{17,9},{25,17},{10,2},{18,10},{26,18},{... | collective-permute-start | bytes 2359304 | tf_op jit(solution)/shard_map/ppermute | solution.py:718
  19.5 19.3 %collective-permute-start.8 = (bf16[1024,256]{1,0:T(8,128)(2,1)}, bf16[1024,256]{1,0:T(8,128)(2,1)}, u32[]{:S(2)}, u32[]{:S(2)}) collective-permute-start(bf16[1024,256]{1,0:T(8,128)(2,1)} %collective-permute-done.3.refs_2_), channel_id=1, source_target_pairs={{2,4},{3,5},{4,2},{5,3},{10,12},{11,13},{12,10},{13,11},{18,20},{1... | collective-permute-start | bytes 1572872 | tf_op jit(solution)/shard_map/ppermute | solution.py:187
  21.0 17.9 %collective-permute-start.6 = (bf16[1024,256]{1,0:T(8,128)(2,1)}, bf16[1024,256]{1,0:T(8,128)(2,1)}, u32[]{:S(2)}, u32[]{:S(2)}) collective-permute-start(bf16[1024,256]{1,0:T(8,128)(2,1)} %collective-permute-done.5), channel_id=1, source_target_pairs={{2,0},{3,1},{4,6},{5,7},{10,8},{11,9},{12,14},{13,15},{18,16},{19,... | collective-permute-start | bytes 1572872 | tf_op jit(solution)/shard_map/ppermute | solution.py:187
  22.2 16.5 %all-to-all-start = ((s32[8,8,128]{2,1,0:T(8,128)}), s32[8,8,128]{2,1,0:T(8,128)S(1)}, u32[]{:S(2)}, u32[]{:S(2)}) async-start(s32[8,8,128]{2,1,0:T(8,128)} %get-tuple-element.12), calls=%async_computation | async-start | bytes 65536 | tf_op jit(solution)/shard_map/all_to_all | solution.py:786
  38.8 0.6 copy-start.11
  38.8 0.9 copy-start.2
  38.8 1.2 copy-start
  40.1 6.1 %copy-start.3 = (bf16[1024,256]{1,0:T(8,128)(2,1)S(1)}, bf16[1024,256]{1,0:T(8,128)(2,1)}, u32[]{:S(2)}) copy-start(bf16[1024,256]{1,0:T(8,128)(2,1)} %get-tuple-element.13.refs_0_.first) | copy-start | bytes 1572868
  40.1 31.0 %copy-start.1 = (bf16[4,1,2,512,128]{4,3,2,1,0:T(8,128)(2,1)S(1)}, bf16[4,1,2,512,128]{4,3,2,1,0:T(8,128)(2,1)}, u32[]{:S(2)}) copy-start(bf16[4,1,2,512,128]{4,3,2,1,0:T(8,128)(2,1)} %copy-done) | copy-start | bytes 3145732
  40.1 52.3 %all-to-all-start.1 = ((bf16[4,2,2,512,128]{4,3,2,1,0:T(8,128)(2,1)}), bf16[4,2,2,512,128]{4,3,2,1,0:T(8,128)(2,1)}, u32[]{:S(2)}, u32[]{:S(2)}) async-start(bf16[4,2,2,512,128]{4,3,2,1,0:T(8,128)(2,1)} %after.2), calls=%async_computation.1 | async-start | bytes 4194304 | tf_op jit(solution)/shard_map/all_to_all | solution.py:160
  44.6 26.4 %collective-permute-start.14 = (bf16[4,1,2,512,128]{4,3,2,1,0:T(8,128)(2,1)}, bf16[4,1,2,512,128]{4,3,2,1,0:T(8,128)(2,1)S(1)}, u32[]{:S(2)}, u32[]{:S(2)}) collective-permute-start(bf16[4,1,2,512,128]{4,3,2,1,0:T(8,128)(2,1)} %get-tuple-element.21), channel_id=1, source_target_pairs={{0,1},{1,0},{2,3},{3,2},{4,5},{5,4},{6,7},{7,6},{8,9},{9,8},{10,11... | collective-permute-start | bytes 3145736 | tf_op jit(solution)/shard_map/ppermute | solution.py:78
  46.1 92.3 %collective-permute-start.2 = (bf16[1024,256]{1,0:T(8,128)(2,1)S(1)}, bf16[1024,256]{1,0:T(8,128)(2,1)}, u32[]{:S(2)}, u32[]{:S(2)}) collective-permute-start(bf16[1024,256]{1,0:T(8,128)(2,1)S(1)} %copy-done.3), channel_id=1, source_target_pairs={{0,1},{1,0},{2,3},{3,2},{4,5},{5,4},{6,7},{7,6},{8,9},{9,8},{10,11... | collective-permute-start | bytes 1572872 | tf_op jit(solution)/shard_map/ppermute | solution.py:78
  92.4 87.6 %all-to-all-start.2 = ((bf16[4,2,2,512,128]{4,3,2,1,0:T(8,128)(2,1)}), bf16[4,2,2,512,128]{4,3,2,1,0:T(8,128)(2,1)}, u32[]{:S(2)}, u32[]{:S(2)}) async-start(bf16[4,2,2,512,128]{4,3,2,1,0:T(8,128)(2,1)} %after.3), calls=%async_computation.2 | async-start | bytes 4194304 | tf_op jit(solution)/shard_map/all_to_all | solution.py:160
  98.3 35.2 %collective-permute-start.9 = (bf16[1024,256]{1,0:T(8,128)(2,1)}, bf16[1024,256]{1,0:T(8,128)(2,1)}, u32[]{:S(2)}, u32[]{:S(2)}) collective-permute-start(bf16[1024,256]{1,0:T(8,128)(2,1)} %collective-permute-done.8.refs_1_), channel_id=1, source_target_pairs={{2,0},{3,1},{4,6},{5,7},{10,8},{11,9},{12,14},{13,15},{18,16},{19,... | collective-permute-start | bytes 1572872 | tf_op jit(solution)/shard_map/ppermute | solution.py:187
  100.1 38.3 %collective-permute-start.4 = (bf16[1024,256]{1,0:T(8,128)(2,1)}, bf16[1024,256]{1,0:T(8,128)(2,1)S(1)}, u32[]{:S(2)}, u32[]{:S(2)}) collective-permute-start(bf16[1024,256]{1,0:T(8,128)(2,1)} %collective-permute-done.3.refs_2_), channel_id=1, source_target_pairs={{0,1},{1,0},{2,3},{3,2},{4,5},{5,4},{6,7},{7,6},{8,9},{9,8},{10,11... | collective-permute-start | bytes 1572872 | tf_op jit(solution)/shard_map/ppermute | solution.py:78
  102.4 44.6 %copy-start.4 = (bf16[1024,256]{1,0:T(8,128)(2,1)}, bf16[1024,256]{1,0:T(8,128)(2,1)S(1)}, u32[]{:S(2)}) copy-start(bf16[1024,256]{1,0:T(8,128)(2,1)S(1)} %add.195.refs_4_) | copy-start | bytes 1572868
  102.4 36.0 %collective-permute-start.7 = (bf16[1024,256]{1,0:T(8,128)(2,1)S(1)}, bf16[1024,256]{1,0:T(8,128)(2,1)S(1)}, u32[]{:S(2)}, u32[]{:S(2)}) collective-permute-start(bf16[1024,256]{1,0:T(8,128)(2,1)S(1)} %add.195.refs_4_), channel_id=1, source_target_pairs={{0,1},{1,0},{2,3},{3,2},{4,5},{5,4},{6,7},{7,6},{8,9},{9,8},{10,11... | collective-permute-start | bytes 1572872 | tf_op jit(solution)/shard_map/ppermute | solution.py:78
  134.9 12.2 %copy-start.5 = (bf16[1024,256]{1,0:T(8,128)(2,1)}, bf16[1024,256]{1,0:T(8,128)(2,1)S(1)}, u32[]{:S(2)}) copy-start(bf16[1024,256]{1,0:T(8,128)(2,1)S(1)} %add.196.refs_6_) | copy-start | bytes 1572868
  134.9 12.1 %collective-permute-start.10 = (bf16[1024,256]{1,0:T(8,128)(2,1)S(1)}, bf16[1024,256]{1,0:T(8,128)(2,1)}, u32[]{:S(2)}, u32[]{:S(2)}) collective-permute-start(bf16[1024,256]{1,0:T(8,128)(2,1)S(1)} %add.196.refs_6_), channel_id=1, source_target_pairs={{0,1},{1,0},{2,3},{3,2},{4,5},{5,4},{6,7},{7,6},{8,9},{9,8},{10,11... | collective-permute-start | bytes 1572872 | tf_op jit(solution)/shard_map/ppermute | solution.py:78
  138.4 0.8 copy-start.6
  139.2 0.8 copy-start.7
  149.9 22.0 %collective-permute-start.11 = (bf16[2,512,256]{2,1,0:T(8,128)(2,1)}, bf16[2,512,256]{2,1,0:T(8,128)(2,1)S(1)}, u32[]{:S(2)}, u32[]{:S(2)}) collective-permute-start(bf16[2,512,256]{2,1,0:T(8,128)(2,1)} %get-tuple-element.15.h_last), channel_id=1, source_target_pairs={{0,8},{8,16},{16,24},{1,9},{9,17},{17,25},{2,10},{10,18},{18,26},{... | collective-permute-start | bytes 1572872 | tf_op jit(solution)/shard_map/ppermute | solution.py:718
  151.8 20.1 %collective-permute-start.12 = (bf16[2,512,256]{2,1,0:T(8,128)(2,1)}, bf16[2,512,256]{2,1,0:T(8,128)(2,1)S(1)}, u32[]{:S(2)}, u32[]{:S(2)}) collective-permute-start(bf16[2,512,256]{2,1,0:T(8,128)(2,1)} %get-tuple-element.16.h_first), channel_id=1, source_target_pairs={{8,0},{16,8},{24,16},{9,1},{17,9},{25,17},{10,2},{18,10},{26,18},{... | collective-permute-start | bytes 1572872 | tf_op jit(solution)/shard_map/ppermute | solution.py:718
  171.9 0.8 copy-start.8
  171.9 1.0 copy-start.9
  184.8 11.9 %all-to-all-start.3 = ((f32[8,24,128]{2,1,0:T(8,128)}), f32[8,24,128]{2,1,0:T(8,128)S(1)}, u32[]{:S(2)}, u32[]{:S(2)}) async-start(f32[8,24,128]{2,1,0:T(8,128)} %project.1), calls=%async_computation.3 | async-start | bytes 196608 | tf_op jit(solution)/shard_map/all_to_all | solution.py:801
  196.6 0.6 copy-start.10

commit v5 on v4

--- a/solution.py
+++ b/solution.py
@@ -150,7 +150,7 @@
     )(block, *others)
 
 
-def exchange(me, peers, basis, own, awaited):
+def exchange(me, peers, basis, own, awaited, handed):
     count = lax.axis_size("col")
     outer, inner = lines_of(count)
     groups = [[line * inner + place for line in range(outer)] for place in range(inner)]
@@ -172,7 +172,7 @@
     }
     parts = [between_lines([to_lines], *awaited, *[swapped[group[0]] for group in ahead])]
     for t in range(1, inner):
-        parts.append(between_lines([swapped[t, k] for k in range(CAP)], parts[-1]))
+        parts.append(between_lines([swapped[t, k] for k in range(CAP)], parts[-1], *handed))
     return [part.reshape((outer * CAP,) + part.shape[2:]) for part in parts]
 
 
@@ -200,13 +200,13 @@
             (across + handed, jnp.where(within, a ^ 3, a ^ 2)),
             (far + last, jnp.where(within, a ^ 2, a ^ 3)),
         ]
-        awaited = [far, handed]
+        awaited, ends = [far, handed], [last]
     else:
         lines = [(own, a)] + [
             (move(own, [(x, partner(x, t, outer)) for x in range(outer)]), partner(a, -t, outer))
             for t in range(1, outer)
         ]
-        awaited = [block for block, _ in lines[1:]]
+        awaited, ends = [block for block, _ in lines[1:]], []
     pieces, owners = [], []
     for block, line in lines:
         pieces.append(block)
@@ -214,7 +214,8 @@
         for t in range(1, inner):
             pieces.append(swap_along(block, t))
             owners.append(line * inner + partner(b, -t, inner))
-    return pieces, jnp.stack(owners).astype(jnp.int32), awaited
+    ends += [piece for piece in pieces[: 2 * inner] if all(piece is not block for block, _ in lines)]
+    return pieces, jnp.stack(owners).astype(jnp.int32), awaited, ends
 
 
 def edge_kernel(col_count, depth, owners, *refs):
@@ -784,10 +785,10 @@
         peers, tile_block, tile_count, band_pattern, hamiltonian.reshape(-1, W), col_count
     )
     lists = lax.all_to_all(lists, "col", split_axis=0, concat_axis=0, tiled=True)
-    pieces, owners, awaited = gather_pieces(own)
+    pieces, owners, awaited, handed = gather_pieces(own)
     v_low = shift(start_columns[-DEG * W :], "row", 1)
     v_high = shift(start_columns[: DEG * W], "row", -1)
-    parts = exchange(me[None], peers, basis_values, own, awaited + [v_low, v_high, lists])
+    parts = exchange(me[None], peers, basis_values, own, awaited + [v_low, v_high, lists], handed)
 
     first, last = edge_blocks(owners, pieces, col_count, DEG - 1)
     h_low = shift(last, "row", 1)

time: 205 us -> 184 us (0.90)
  waiting for transfers between devices: 91.9 us -> 69.1 us
    ppermute x5, waiting for transfers between devices: 30 us -> 0.01 us  [move(): return lax.ppermute(block, 'col', pairs)]
    ppermute x6, waiting for transfers between devices: 30.4 us -> 56.5 us  [swap_along(): return lax.ppermute(block, 'col', pairs)]
    all_to_all x2, waiting for transfers between devices: 19.8 us -> 0.89 us  [between_lines(): lax.all_to_all(after(block, *others), 'col', split_axis=0, concat_axis=0,...]
    unnamed x25 -> x27, local copies, waits for them, and re-layouts: 4.49 us -> 2.9 us
  transfers between devices with their start and end apart: 19 -> 19, of which waited for: 6 -> 8; matrix products, arithmetic and copies ran while one was open for 6% -> 8% of each run, Pallas kernels for 16% -> 18%
where the time goes in v5:
time: 184 us; the launch traced here: 182 us
  waiting for transfers between devices  69.1 us (38%)
  Pallas kernels  47.7 us (26%)
  starting transfers between devices  47.5 us (26%)
  other arithmetic  8.55 us (5%)
  local copies, waits for them, and re-layouts  8.45 us (5%)
    ppermute x6, waiting for transfers between devices, swap_along(): return lax.ppermute(block, 'col', pairs)  56.5 us
    pallas_call x1, Pallas kernels, chebyshev_inner(): pl.pallas_call(functools.partial(inner_kernel, blocks), out_shape=(jax.Sh...  16.4 us
    ppermute x4, starting transfers between devices, shift(): return lax.ppermute(block, axis, pairs)  11.1 us
    all_to_all x2, starting transfers between devices, between_lines(): lax.all_to_all(after(block, *others), 'col', split_axis=0, concat_axis=0,...  9.22 us
    all_to_all x1, starting transfers between devices, shards(): lax.all_to_all(lists, 'col', split_axis=0, concat_axis=0, tiled=True)  7.61 us
    ppermute x6, starting transfers between devices, swap_along(): return lax.ppermute(block, 'col', pairs)  7.25 us
    ppermute x5, starting transfers between devices, move(): return lax.ppermute(block, 'col', pairs)  7.17 us
    pallas_call x1, Pallas kernels, chebyshev_outer(): pl.pallas_call(functools.partial(outer_kernel, blocks), out_shape=jax.Sha...  7.07 us
  transfers between devices with their start and end apart: 19, of which 8 were waited for; matrix products, arithmetic and copies ran while one was open for 8% of the time, Pallas kernels for 18%

profile of v5, /device:TPU:2, one launch (start us, length us, event | category | flops | bytes accessed | tf_op | source)
XLA Modules:
  0.0 182.3 jit_solution(3425124411073485324)
XLA Ops:
  0.6 3.2 %own_piece.1 = (bf16[1024,256]{1,0:T(8,128)(2,1)}, s32[8,8,128]{2,1,0:T(8,128)}) custom-call(s32[16]{0:T(128)} %bitcast.32, s32[16]{0:T(128)} %named.1, s32[4]{0:T(128)} %counts.1, s32[2]{0:T(128)} %pattern.1, bf16[1024,256]{1,0:T(8,128)(2,1)} %bitcast.24), custom_call_target="tpu_custom_call" | custom-call | tf_op jit(solution)/shard_map/own_piece/pallas_call | solution.py:55
  3.8 1.6 collective-permute-start.3
  5.5 1.5 collective-permute-start.5
  7.0 2.8 %pack.2.first = bf16[4,1,2,512,128]{4,3,2,1,0:T(8,128)(2,1)} custom-call(s32[1]{0:T(128)} %bitcast.4.me, s32[16]{0:T(128)} %bitcast.33, bf16[16,2,512,128]{3,2,1,0:T(8,128)(2,1)} %basis.3, bf16[1024,256]{1,0:T(8,128)(2,1)} %get-tuple-element.13.refs_0_.first), custom_call_target="tpu_custom_call" | custom-call | tf_op jit(solution)/shard_map/pack/pallas_call | solution.py:121
  9.7 1.6 collective-permute-start.13
  11.3 2.6 %fusion.12 = (bf16[768,512]{1,0:T(8,128)(2,1)}, bf16[768,512]{1,0:T(8,128)(2,1)}) fusion(bf16[4096,512]{1,0:T(8,128)(2,1)} %v_mid.3), kind=kLoop, calls=%fused_computation.53 | loop fusion | bytes 3145728 | tf_op jit(solution)/shard_map/slice | solution.py:790
  13.9 1.9 %collective-permute-start = (bf16[768,512]{1,0:T(8,128)(2,1)}, bf16[768,512]{1,0:T(8,128)(2,1)S(1)}, u32[]{:S(2)}, u32[]{:S(2)}) collective-permute-start(bf16[768,512]{1,0:T(8,128)(2,1)} %get-tuple-element.29), channel_id=1, source_target_pairs={{0,8},{8,16},{16,24},{1,9},{9,17},{17,25},{2,10},{10,18},{18,26},{... | collective-permute-start | bytes 2359304 | tf_op jit(solution)/shard_map/ppermute | solution.py:719
  15.9 3.6 %collective-permute-start.1 = (bf16[768,512]{1,0:T(8,128)(2,1)}, bf16[768,512]{1,0:T(8,128)(2,1)}, u32[]{:S(2)}, u32[]{:S(2)}) collective-permute-start(bf16[768,512]{1,0:T(8,128)(2,1)} %get-tuple-element.28), channel_id=1, source_target_pairs={{8,0},{16,8},{24,16},{9,1},{17,9},{25,17},{10,2},{18,10},{26,18},{... | collective-permute-start | bytes 2359304 | tf_op jit(solution)/shard_map/ppermute | solution.py:719
  19.5 1.5 collective-permute-start.8
  22.3 7.6 %all-to-all-start = ((s32[8,8,128]{2,1,0:T(8,128)}), s32[8,8,128]{2,1,0:T(8,128)S(1)}, u32[]{:S(2)}, u32[]{:S(2)}) async-start(s32[8,8,128]{2,1,0:T(8,128)} %get-tuple-element.12), calls=%async_computation | async-start | bytes 65536 | tf_op jit(solution)/shard_map/all_to_all | solution.py:787
  29.9 3.6 %pack.3 = (bf16[4,2,2,512,128]{4,3,2,1,0:T(8,128)(2,1)}, bf16[4,1,2,512,128]{4,3,2,1,0:T(8,128)(2,1)}) custom-call(s32[1]{0:T(128)} %bitcast.4.me, s32[16]{0:T(128)} %bitcast.34, bf16[16,2,512,128]{3,2,1,0:T(8,128)(2,1)} %basis.3, bf16[4,1,2,512,128]{4,3,2,1,0:T(8,128)(2,1)} %pack.2.first), custom_call_target="tpu_custom_call" | custom-call | tf_op jit(solution)/shard_map/pack/pallas_call | solution.py:121
  33.5 5.3 %all-to-all-done.refs_5_ = s32[8,8,128]{2,1,0:T(8,128)S(1)} async-done(((s32[8,8,128]{2,1,0:T(8,128)}), s32[8,8,128]{2,1,0:T(8,128)S(1)}, u32[]{:S(2)}, u32[]{:S(2)}) %all-to-all-start) | async-done | bytes 32800 | tf_op jit(solution)/shard_map/all_to_all | solution.py:787
  40.1 4.6 %all-to-all-start.1 = ((bf16[4,2,2,512,128]{4,3,2,1,0:T(8,128)(2,1)}), bf16[4,2,2,512,128]{4,3,2,1,0:T(8,128)(2,1)}, u32[]{:S(2)}, u32[]{:S(2)}) async-start(bf16[4,2,2,512,128]{4,3,2,1,0:T(8,128)(2,1)} %after.2), calls=%async_computation.1 | async-start | bytes 4194304 | tf_op jit(solution)/shard_map/all_to_all | solution.py:160
  44.7 1.5 collective-permute-start.14
  46.8 1.4 collective-permute-start.4
  50.4 20.7 %collective-permute-done.14 = bf16[4,1,2,512,128]{4,3,2,1,0:T(8,128)(2,1)} collective-permute-done((bf16[4,1,2,512,128]{4,3,2,1,0:T(8,128)(2,1)}, bf16[4,1,2,512,128]{4,3,2,1,0:T(8,128)(2,1)}, u32[]{:S(2)}, u32[]{:S(2)}) %collective-permute-start.14) | collective-permute-done | bytes 1048608 | tf_op jit(solution)/shard_map/ppermute | solution.py:78
  71.2 2.8 %pad_maximum_fusion.refs_0_ = bf16[4,2,2,512,128]{4,3,2,1,0:T(8,128)(2,1)} fusion(bf16[4,1,2,512,128]{4,3,2,1,0:T(8,128)(2,1)} %collective-permute-done.14, bf16[4,1,2,512,128]{4,3,2,1,0:T(8,128)(2,1)S(1)} %copy-done.1), kind=kLoop, calls=%fused_computation | loop fusion | flops 1048576 | bytes 4194304 | tf_op jit(solution)/shard_map/concatenate | solution.py:159
  74.0 8.3 %collective-permute-done.2.refs_1_.refs_3_ = bf16[1024,256]{1,0:T(8,128)(2,1)S(1)} collective-permute-done((bf16[1024,256]{1,0:T(8,128)(2,1)S(1)}, bf16[1024,256]{1,0:T(8,128)(2,1)S(1)}, u32[]{:S(2)}, u32[]{:S(2)}) %collective-permute-start.2) | collective-permute-done | bytes 524320 | tf_op jit(solution)/shard_map/ppermute | solution.py:78
  82.3 9.3 %collective-permute-done.4.refs_3_.refs_4_ = bf16[1024,256]{1,0:T(8,128)(2,1)S(1)} collective-permute-done((bf16[1024,256]{1,0:T(8,128)(2,1)}, bf16[1024,256]{1,0:T(8,128)(2,1)S(1)}, u32[]{:S(2)}, u32[]{:S(2)}) %collective-permute-start.4) | collective-permute-done | bytes 524320 | tf_op jit(solution)/shard_map/ppermute | solution.py:78
  92.5 4.6 %all-to-all-start.2 = ((bf16[4,2,2,512,128]{4,3,2,1,0:T(8,128)(2,1)}), bf16[4,2,2,512,128]{4,3,2,1,0:T(8,128)(2,1)}, u32[]{:S(2)}, u32[]{:S(2)}) async-start(bf16[4,2,2,512,128]{4,3,2,1,0:T(8,128)(2,1)} %after.3), calls=%async_computation.2 | async-start | bytes 4194304 | tf_op jit(solution)/shard_map/all_to_all | solution.py:160
  99.0 1.3 add.195.refs_4_
  106.4 8.9 %collective-permute-done.7.refs_5_ = bf16[1024,256]{1,0:T(8,128)(2,1)S(1)} collective-permute-done((bf16[1024,256]{1,0:T(8,128)(2,1)S(1)}, bf16[1024,256]{1,0:T(8,128)(2,1)S(1)}, u32[]{:S(2)}, u32[]{:S(2)}) %collective-permute-start.7) | collective-permute-done | bytes 524320 | tf_op jit(solution)/shard_map/ppermute | solution.py:78
  115.3 9.2 %collective-permute-done.10.refs_7_ = bf16[1024,256]{1,0:T(8,128)(2,1)} collective-permute-done((bf16[1024,256]{1,0:T(8,128)(2,1)S(1)}, bf16[1024,256]{1,0:T(8,128)(2,1)}, u32[]{:S(2)}, u32[]{:S(2)}) %collective-permute-start.10) | collective-permute-done | bytes 524320 | tf_op jit(solution)/shard_map/ppermute | solution.py:78
  124.5 2.9 %edge_blocks.1 = (bf16[2,512,256]{2,1,0:T(8,128)(2,1)}, bf16[2,512,256]{2,1,0:T(8,128)(2,1)}) custom-call(s32[8]{0:T(128)} %stack.35.owners, bf16[1024,256]{1,0:T(8,128)(2,1)} %get-tuple-element.13.refs_0_.first, bf16[1024,256]{1,0:T(8,128)(2,1)} %copy-done.6, bf16[1024,256]{1,0:T(8,128)(2,1)} %collective-permute-done.3.refs_2_, ...), custom_call_target="tpu_custom_call" | custom-call | tf_op jit(solution)/shard_map/edge_blocks/pallas_call | solution.py:243
  127.4 1.9 %collective-permute-start.11 = (bf16[2,512,256]{2,1,0:T(8,128)(2,1)}, bf16[2,512,256]{2,1,0:T(8,128)(2,1)S(1)}, u32[]{:S(2)}, u32[]{:S(2)}) collective-permute-start(bf16[2,512,256]{2,1,0:T(8,128)(2,1)} %get-tuple-element.15.h_last), channel_id=1, source_target_pairs={{0,8},{8,16},{16,24},{1,9},{9,17},{17,25},{2,10},{10,18},{18,26},{... | collective-permute-start | bytes 1572872 | tf_op jit(solution)/shard_map/ppermute | solution.py:719
  129.3 3.6 %collective-permute-start.12 = (bf16[2,512,256]{2,1,0:T(8,128)(2,1)}, bf16[2,512,256]{2,1,0:T(8,128)(2,1)S(1)}, u32[]{:S(2)}, u32[]{:S(2)}) collective-permute-start(bf16[2,512,256]{2,1,0:T(8,128)(2,1)} %get-tuple-element.16.h_first), channel_id=1, source_target_pairs={{8,0},{16,8},{24,16},{9,1},{17,9},{25,17},{10,2},{18,10},{26,18},{... | collective-permute-start | bytes 1572872 | tf_op jit(solution)/shard_map/ppermute | solution.py:719
  133.0 16.4 %chebyshev_inner.1 = (bf16[8,512,512]{2,1,0:T(8,128)(2,1)}, bf16[1024,512]{1,0:T(8,128)(2,1)}, bf16[1024,512]{1,0:T(8,128)(2,1)}, f32[1024,512]{1,0:T(8,128)}) custom-call(f32[4]{0:T(128)} %coef.3, s32[8]{0:T(128)} %stack.35.owners, bf16[768,512]{1,0:T(8,128)(2,1)} %copy-done.2, bf16[4096,512]{1,0:T(8,128)(2,1)} %v_mid.3, ...), custom_call_target="tpu_custom_call" | custom-call | flops 8455716864 | bytes 16777216 | tf_op jit(solution)/shard_map/chebyshev_inner/pallas_call | solution.py:366
  150.4 7.1 %chebyshev_outer.1.kernel_t = bf16[8,512,512]{2,1,0:T(8,128)(2,1)} custom-call(f32[4]{0:T(128)} %coef.3, bf16[8,512,512]{2,1,0:T(8,128)(2,1)} %get-tuple-element.14.kernel_in, bf16[768,512]{1,0:T(8,128)(2,1)} %copy-done.2, bf16[4096,512]{1,0:T(8,128)(2,1)} %v_mid.3, ...), custom_call_target="tpu_custom_call", output_to_operand_aliasing={{}: (1, {})} | custom-call | tf_op jit(solution)/shard_map/chebyshev_outer/pallas_call | solution.py:484
  157.5 5.0 %project.1 = f32[8,24,128]{2,1,0:T(8,128)} custom-call(s32[26]{0:T(128)} %pad_add_fusion.1.plan, s32[16]{0:T(128)} %select_reduce_fusion.2.order, bf16[8,512,512]{2,1,0:T(8,128)(2,1)} %chebyshev_outer.1.kernel_t, f32[4,128]{1,0:T(4,128)} %core.1, bf16[8,2,512,128]{3,2,1,0:T(8,128)(2,1)} %bitcast.13.refs_0_, bf16[8,2,512,128]{3,2,1,0:T(8,128)(2,1)} %bitcast.14.refs_1_), custom_call_target="tpu_custom_call" | custom-call | tf_op jit(solution)/shard_map/project/pallas_call | solution.py:596
  162.5 5.2 %all-to-all-start.3 = ((f32[8,24,128]{2,1,0:T(8,128)}), f32[8,24,128]{2,1,0:T(8,128)S(1)}, u32[]{:S(2)}, u32[]{:S(2)}) async-start(f32[8,24,128]{2,1,0:T(8,128)} %project.1), calls=%async_computation.3 | async-start | bytes 196608 | tf_op jit(solution)/shard_map/all_to_all | solution.py:802
  168.4 6.4 %all-to-all-done.3 = f32[8,24,128]{2,1,0:T(8,128)S(1)} async-done(((f32[8,24,128]{2,1,0:T(8,128)}), f32[8,24,128]{2,1,0:T(8,128)S(1)}, u32[]{:S(2)}, u32[]{:S(2)}) %all-to-all-start.3) | async-done | bytes 98336 | tf_op jit(solution)/shard_map/all_to_all | solution.py:802
  175.4 6.9 %update.1 = (f32[4,128]{1,0:T(4,128)}, bf16[4096,512]{1,0:T(8,128)(2,1)}) custom-call(s32[26]{0:T(128)} %pad_add_fusion.1.plan, s32[16]{0:T(128)} %select_reduce_fusion.2.order, s32[16]{0:T(128)} %reshape.285.tile_of, f32[192,128]{1,0:T(8,128)} %bitcast.25, f32[32,192]{1,0:T(8,128)} %convert_reduce_fusion.collect, bf16[8,2,512,128]{3,2,1,0:T(8,128)(2,1)} %bitcast.13.refs_0_, ...), custom_call_target="tpu_custom_call" | custom-call | tf_op jit(solution)/shard_map/update/pallas_call | solution.py:694
  (86 shorter events, 16.5 us)
Async XLA Ops:
  3.8 15.7 %collective-permute-start.3 = (bf16[1024,256]{1,0:T(8,128)(2,1)}, bf16[1024,256]{1,0:T(8,128)(2,1)}, u32[]{:S(2)}, u32[]{:S(2)}) collective-permute-start(bf16[1024,256]{1,0:T(8,128)(2,1)} %get-tuple-element.13.refs_0_.first), channel_id=1, source_target_pairs={{0,2},{1,3},{2,0},{3,1},{4,6},{5,7},{6,4},{7,5},{8,10},{9,11},{10,... | collective-permute-start | bytes 1572872 | tf_op jit(solution)/shard_map/ppermute | solution.py:187
  5.5 15.5 %collective-permute-start.5 = (bf16[1024,256]{1,0:T(8,128)(2,1)}, bf16[1024,256]{1,0:T(8,128)(2,1)}, u32[]{:S(2)}, u32[]{:S(2)}) collective-permute-start(bf16[1024,256]{1,0:T(8,128)(2,1)} %get-tuple-element.13.refs_0_.first), channel_id=1, source_target_pairs={{2,4},{3,5},{4,2},{5,3},{10,12},{11,13},{12,10},{13,11},{18,20},{1... | collective-permute-start | bytes 1572872 | tf_op jit(solution)/shard_map/ppermute | solution.py:187
  9.7 29.1 %collective-permute-start.13 = (bf16[4,1,2,512,128]{4,3,2,1,0:T(8,128)(2,1)}, bf16[4,1,2,512,128]{4,3,2,1,0:T(8,128)(2,1)S(1)}, u32[]{:S(2)}, u32[]{:S(2)}) collective-permute-start(bf16[4,1,2,512,128]{4,3,2,1,0:T(8,128)(2,1)} %pack.2.first), channel_id=1, source_target_pairs={{0,1},{1,0},{2,3},{3,2},{4,5},{5,4},{6,7},{7,6},{8,9},{9,8},{10,11... | collective-permute-start | bytes 3145736 | tf_op jit(solution)/shard_map/ppermute | solution.py:78
  13.9 24.9 %collective-permute-start = (bf16[768,512]{1,0:T(8,128)(2,1)}, bf16[768,512]{1,0:T(8,128)(2,1)S(1)}, u32[]{:S(2)}, u32[]{:S(2)}) collective-permute-start(bf16[768,512]{1,0:T(8,128)(2,1)} %get-tuple-element.29), channel_id=1, source_target_pairs={{0,8},{8,16},{16,24},{1,9},{9,17},{17,25},{2,10},{10,18},{18,26},{... | collective-permute-start | bytes 2359304 | tf_op jit(solution)/shard_map/ppermute | solution.py:719
  15.9 23.0 %collective-permute-start.1 = (bf16[768,512]{1,0:T(8,128)(2,1)}, bf16[768,512]{1,0:T(8,128)(2,1)}, u32[]{:S(2)}, u32[]{:S(2)}) collective-permute-start(bf16[768,512]{1,0:T(8,128)(2,1)} %get-tuple-element.28), channel_id=1, source_target_pairs={{8,0},{16,8},{24,16},{9,1},{17,9},{25,17},{10,2},{18,10},{26,18},{... | collective-permute-start | bytes 2359304 | tf_op jit(solution)/shard_map/ppermute | solution.py:719
  19.5 19.3 %collective-permute-start.8 = (bf16[1024,256]{1,0:T(8,128)(2,1)}, bf16[1024,256]{1,0:T(8,128)(2,1)}, u32[]{:S(2)}, u32[]{:S(2)}) collective-permute-start(bf16[1024,256]{1,0:T(8,128)(2,1)} %collective-permute-done.3.refs_2_), channel_id=1, source_target_pairs={{2,4},{3,5},{4,2},{5,3},{10,12},{11,13},{12,10},{13,11},{18,20},{1... | collective-permute-start | bytes 1572872 | tf_op jit(solution)/shard_map/ppermute | solution.py:187
  21.0 17.8 %collective-permute-start.6 = (bf16[1024,256]{1,0:T(8,128)(2,1)}, bf16[1024,256]{1,0:T(8,128)(2,1)}, u32[]{:S(2)}, u32[]{:S(2)}) collective-permute-start(bf16[1024,256]{1,0:T(8,128)(2,1)} %collective-permute-done.5), channel_id=1, source_target_pairs={{2,0},{3,1},{4,6},{5,7},{10,8},{11,9},{12,14},{13,15},{18,16},{19,... | collective-permute-start | bytes 1572872 | tf_op jit(solution)/shard_map/ppermute | solution.py:187
  22.3 16.5 %all-to-all-start = ((s32[8,8,128]{2,1,0:T(8,128)}), s32[8,8,128]{2,1,0:T(8,128)S(1)}, u32[]{:S(2)}, u32[]{:S(2)}) async-start(s32[8,8,128]{2,1,0:T(8,128)} %get-tuple-element.12), calls=%async_computation | async-start | bytes 65536 | tf_op jit(solution)/shard_map/all_to_all | solution.py:787
  38.8 0.6 copy-start.12
  38.8 0.9 copy-start.2
  38.9 1.2 copy-start
  40.1 6.1 %copy-start.3 = (bf16[1024,256]{1,0:T(8,128)(2,1)S(1)}, bf16[1024,256]{1,0:T(8,128)(2,1)}, u32[]{:S(2)}) copy-start(bf16[1024,256]{1,0:T(8,128)(2,1)} %get-tuple-element.13.refs_0_.first) | copy-start | bytes 1572868
  40.1 31.1 %copy-start.1 = (bf16[4,1,2,512,128]{4,3,2,1,0:T(8,128)(2,1)S(1)}, bf16[4,1,2,512,128]{4,3,2,1,0:T(8,128)(2,1)}, u32[]{:S(2)}) copy-start(bf16[4,1,2,512,128]{4,3,2,1,0:T(8,128)(2,1)} %copy-done) | copy-start | bytes 3145732
  40.1 52.4 %all-to-all-start.1 = ((bf16[4,2,2,512,128]{4,3,2,1,0:T(8,128)(2,1)}), bf16[4,2,2,512,128]{4,3,2,1,0:T(8,128)(2,1)}, u32[]{:S(2)}, u32[]{:S(2)}) async-start(bf16[4,2,2,512,128]{4,3,2,1,0:T(8,128)(2,1)} %after.2), calls=%async_computation.1 | async-start | bytes 4194304 | tf_op jit(solution)/shard_map/all_to_all | solution.py:160
  44.7 26.5 %collective-permute-start.14 = (bf16[4,1,2,512,128]{4,3,2,1,0:T(8,128)(2,1)}, bf16[4,1,2,512,128]{4,3,2,1,0:T(8,128)(2,1)}, u32[]{:S(2)}, u32[]{:S(2)}) collective-permute-start(bf16[4,1,2,512,128]{4,3,2,1,0:T(8,128)(2,1)} %get-tuple-element.21), channel_id=1, source_target_pairs={{0,1},{1,0},{2,3},{3,2},{4,5},{5,4},{6,7},{7,6},{8,9},{9,8},{10,11... | collective-permute-start | bytes 3145736 | tf_op jit(solution)/shard_map/ppermute | solution.py:78
  46.2 36.1 %collective-permute-start.2 = (bf16[1024,256]{1,0:T(8,128)(2,1)S(1)}, bf16[1024,256]{1,0:T(8,128)(2,1)S(1)}, u32[]{:S(2)}, u32[]{:S(2)}) collective-permute-start(bf16[1024,256]{1,0:T(8,128)(2,1)S(1)} %copy-done.3), channel_id=1, source_target_pairs={{0,1},{1,0},{2,3},{3,2},{4,5},{5,4},{6,7},{7,6},{8,9},{9,8},{10,11... | collective-permute-start | bytes 1572872 | tf_op jit(solution)/shard_map/ppermute | solution.py:78
  46.8 44.8 %collective-permute-start.4 = (bf16[1024,256]{1,0:T(8,128)(2,1)}, bf16[1024,256]{1,0:T(8,128)(2,1)S(1)}, u32[]{:S(2)}, u32[]{:S(2)}) collective-permute-start(bf16[1024,256]{1,0:T(8,128)(2,1)} %collective-permute-done.3.refs_2_), channel_id=1, source_target_pairs={{0,1},{1,0},{2,3},{3,2},{4,5},{5,4},{6,7},{7,6},{8,9},{9,8},{10,11... | collective-permute-start | bytes 1572872 | tf_op jit(solution)/shard_map/ppermute | solution.py:78
  48.2 43.4 %collective-permute-start.9 = (bf16[1024,256]{1,0:T(8,128)(2,1)}, bf16[1024,256]{1,0:T(8,128)(2,1)}, u32[]{:S(2)}, u32[]{:S(2)}) collective-permute-start(bf16[1024,256]{1,0:T(8,128)(2,1)} %collective-permute-done.8.refs_1_), channel_id=1, source_target_pairs={{2,0},{3,1},{4,6},{5,7},{10,8},{11,9},{12,14},{13,15},{18,16},{19,... | collective-permute-start | bytes 1572872 | tf_op jit(solution)/shard_map/ppermute | solution.py:187
  82.3 10.1 %copy-start.6 = (bf16[1024,256]{1,0:T(8,128)(2,1)}, bf16[1024,256]{1,0:T(8,128)(2,1)S(1)}, u32[]{:S(2)}) copy-start(bf16[1024,256]{1,0:T(8,128)(2,1)S(1)} %collective-permute-done.2.refs_1_.refs_3_) | copy-start | bytes 1572868
  91.6 0.9 copy-start.7
  92.5 65.1 %all-to-all-start.2 = ((bf16[4,2,2,512,128]{4,3,2,1,0:T(8,128)(2,1)}), bf16[4,2,2,512,128]{4,3,2,1,0:T(8,128)(2,1)}, u32[]{:S(2)}, u32[]{:S(2)}) async-start(bf16[4,2,2,512,128]{4,3,2,1,0:T(8,128)(2,1)} %after.3), calls=%async_computation.2 | async-start | bytes 4194304 | tf_op jit(solution)/shard_map/all_to_all | solution.py:160
  100.4 24.1 %copy-start.4 = (bf16[1024,256]{1,0:T(8,128)(2,1)}, bf16[1024,256]{1,0:T(8,128)(2,1)S(1)}, u32[]{:S(2)}) copy-start(bf16[1024,256]{1,0:T(8,128)(2,1)S(1)} %add.195.refs_4_) | copy-start | bytes 1572868
  100.4 14.9 %collective-permute-start.7 = (bf16[1024,256]{1,0:T(8,128)(2,1)S(1)}, bf16[1024,256]{1,0:T(8,128)(2,1)S(1)}, u32[]{:S(2)}, u32[]{:S(2)}) collective-permute-start(bf16[1024,256]{1,0:T(8,128)(2,1)S(1)} %add.195.refs_4_), channel_id=1, source_target_pairs={{0,1},{1,0},{2,3},{3,2},{4,5},{5,4},{6,7},{7,6},{8,9},{9,8},{10,11... | collective-permute-start | bytes 1572872 | tf_op jit(solution)/shard_map/ppermute | solution.py:78
  102.8 21.8 %copy-start.5 = (bf16[1024,256]{1,0:T(8,128)(2,1)}, bf16[1024,256]{1,0:T(8,128)(2,1)S(1)}, u32[]{:S(2)}) copy-start(bf16[1024,256]{1,0:T(8,128)(2,1)S(1)} %add.196.refs_6_) | copy-start | bytes 1572868
  102.8 21.7 %collective-permute-start.10 = (bf16[1024,256]{1,0:T(8,128)(2,1)S(1)}, bf16[1024,256]{1,0:T(8,128)(2,1)}, u32[]{:S(2)}, u32[]{:S(2)}) collective-permute-start(bf16[1024,256]{1,0:T(8,128)(2,1)S(1)} %add.196.refs_6_), channel_id=1, source_target_pairs={{0,1},{1,0},{2,3},{3,2},{4,5},{5,4},{6,7},{7,6},{8,9},{9,8},{10,11... | collective-permute-start | bytes 1572872 | tf_op jit(solution)/shard_map/ppermute | solution.py:78
  115.3 9.2 %copy-start.8 = (bf16[1024,256]{1,0:T(8,128)(2,1)}, bf16[1024,256]{1,0:T(8,128)(2,1)S(1)}, u32[]{:S(2)}) copy-start(bf16[1024,256]{1,0:T(8,128)(2,1)S(1)} %collective-permute-done.7.refs_5_) | copy-start | bytes 1572868
  127.4 22.0 %collective-permute-start.11 = (bf16[2,512,256]{2,1,0:T(8,128)(2,1)}, bf16[2,512,256]{2,1,0:T(8,128)(2,1)S(1)}, u32[]{:S(2)}, u32[]{:S(2)}) collective-permute-start(bf16[2,512,256]{2,1,0:T(8,128)(2,1)} %get-tuple-element.15.h_last), channel_id=1, source_target_pairs={{0,8},{8,16},{16,24},{1,9},{9,17},{17,25},{2,10},{10,18},{18,26},{... | collective-permute-start | bytes 1572872 | tf_op jit(solution)/shard_map/ppermute | solution.py:719
  129.3 20.0 %collective-permute-start.12 = (bf16[2,512,256]{2,1,0:T(8,128)(2,1)}, bf16[2,512,256]{2,1,0:T(8,128)(2,1)S(1)}, u32[]{:S(2)}, u32[]{:S(2)}) collective-permute-start(bf16[2,512,256]{2,1,0:T(8,128)(2,1)} %get-tuple-element.16.h_first), channel_id=1, source_target_pairs={{8,0},{16,8},{24,16},{9,1},{17,9},{25,17},{10,2},{18,10},{26,18},{... | collective-permute-start | bytes 1572872 | tf_op jit(solution)/shard_map/ppermute | solution.py:719
  149.4 0.8 copy-start.9
  149.4 1.0 copy-start.10
  162.5 12.3 %all-to-all-start.3 = ((f32[8,24,128]{2,1,0:T(8,128)}), f32[8,24,128]{2,1,0:T(8,128)S(1)}, u32[]{:S(2)}, u32[]{:S(2)}) async-start(f32[8,24,128]{2,1,0:T(8,128)} %project.1), calls=%async_computation.3 | async-start | bytes 196608 | tf_op jit(solution)/shard_map/all_to_all | solution.py:802
  174.8 0.6 copy-start.11

commit v6 on v5

--- a/solution.py
+++ b/solution.py
@@ -214,7 +214,7 @@
         for t in range(1, inner):
             pieces.append(swap_along(block, t))
             owners.append(line * inner + partner(b, -t, inner))
-    ends += [piece for piece in pieces[: 2 * inner] if all(piece is not block for block, _ in lines)]
+    ends += [piece for piece in pieces[: 3 * inner] if all(piece is not block for block, _ in lines)]
     return pieces, jnp.stack(owners).astype(jnp.int32), awaited, ends
 
 

time: 184 us -> 183 us (level)
  waiting for transfers between devices: 69.1 us -> 67 us
  transfers between devices with their start and end apart: 19 -> 19, of which waited for: 8 -> 7; matrix products, arithmetic and copies ran while one was open for 8% -> 8% of each run, Pallas kernels for 18% -> 18%
where the time goes in v6:
time: 183 us; the launch traced here: 181 us
  waiting for transfers between devices  67 us (37%)
  Pallas kernels  48.6 us (27%)
  starting transfers between devices  45.9 us (25%)
  other arithmetic  9.33 us (5%)
  local copies, waits for them, and re-layouts  9.21 us (5%)
    ppermute x6, waiting for transfers between devices, swap_along(): return lax.ppermute(block, 'col', pairs)  55.2 us
    pallas_call x1, Pallas kernels, chebyshev_inner(): pl.pallas_call(functools.partial(inner_kernel, blocks), out_shape=(jax.Sh...  16.4 us
    ppermute x4, starting transfers between devices, shift(): return lax.ppermute(block, axis, pairs)  11.1 us
    all_to_all x2, starting transfers between devices, between_lines(): lax.all_to_all(after(block, *others), 'col', split_axis=0, concat_axis=0,...  9.29 us
    all_to_all x1, starting transfers between devices, shards(): lax.all_to_all(lists, 'col', split_axis=0, concat_axis=0, tiled=True)  7.57 us
    pallas_call x1, Pallas kernels, update(): pl.pallas_call(functools.partial(update_kernel, blocks, tiles), out_shape...  7.41 us
    ppermute x5, starting transfers between devices, move(): return lax.ppermute(block, 'col', pairs)  7.17 us
    pallas_call x1, Pallas kernels, chebyshev_outer(): pl.pallas_call(functools.partial(outer_kernel, blocks), out_shape=jax.Sha...  7.07 us
  transfers between devices with their start and end apart: 19, of which 7 were waited for; matrix products, arithmetic and copies ran while one was open for 8% of the time, Pallas kernels for 18%

profile of v6, /device:TPU:2, one launch (start us, length us, event | category | flops | bytes accessed | tf_op | source)
XLA Modules:
  0.0 181.1 jit_solution(5784154811077274033)
XLA Ops:
  0.6 3.2 %own_piece.1 = (bf16[1024,256]{1,0:T(8,128)(2,1)}, s32[8,8,128]{2,1,0:T(8,128)}) custom-call(s32[16]{0:T(128)} %bitcast.32, s32[16]{0:T(128)} %named.1, s32[4]{0:T(128)} %counts.1, s32[2]{0:T(128)} %pattern.1, bf16[1024,256]{1,0:T(8,128)(2,1)} %bitcast.24), custom_call_target="tpu_custom_call" | custom-call | tf_op jit(solution)/shard_map/own_piece/pallas_call | solution.py:55
  3.8 1.6 collective-permute-start.3
  5.5 1.5 collective-permute-start.5
  6.9 2.8 %pack.2.first = bf16[4,1,2,512,128]{4,3,2,1,0:T(8,128)(2,1)} custom-call(s32[1]{0:T(128)} %bitcast.4.me, s32[16]{0:T(128)} %bitcast.33, bf16[16,2,512,128]{3,2,1,0:T(8,128)(2,1)} %basis.3, bf16[1024,256]{1,0:T(8,128)(2,1)} %get-tuple-element.13.refs_0_.first), custom_call_target="tpu_custom_call" | custom-call | tf_op jit(solution)/shard_map/pack/pallas_call | solution.py:121
  9.7 1.6 collective-permute-start.13
  11.3 2.6 %fusion.12 = (bf16[768,512]{1,0:T(8,128)(2,1)}, bf16[768,512]{1,0:T(8,128)(2,1)}) fusion(bf16[4096,512]{1,0:T(8,128)(2,1)} %v_mid.3), kind=kLoop, calls=%fused_computation.53 | loop fusion | bytes 3145728 | tf_op jit(solution)/shard_map/slice | solution.py:790
  13.9 1.9 %collective-permute-start = (bf16[768,512]{1,0:T(8,128)(2,1)}, bf16[768,512]{1,0:T(8,128)(2,1)S(1)}, u32[]{:S(2)}, u32[]{:S(2)}) collective-permute-start(bf16[768,512]{1,0:T(8,128)(2,1)} %get-tuple-element.29), channel_id=1, source_target_pairs={{0,8},{8,16},{16,24},{1,9},{9,17},{17,25},{2,10},{10,18},{18,26},{... | collective-permute-start | bytes 2359304 | tf_op jit(solution)/shard_map/ppermute | solution.py:719
  15.8 3.6 %collective-permute-start.1 = (bf16[768,512]{1,0:T(8,128)(2,1)}, bf16[768,512]{1,0:T(8,128)(2,1)}, u32[]{:S(2)}, u32[]{:S(2)}) collective-permute-start(bf16[768,512]{1,0:T(8,128)(2,1)} %get-tuple-element.28), channel_id=1, source_target_pairs={{8,0},{16,8},{24,16},{9,1},{17,9},{25,17},{10,2},{18,10},{26,18},{... | collective-permute-start | bytes 2359304 | tf_op jit(solution)/shard_map/ppermute | solution.py:719
  19.5 1.5 collective-permute-start.8
  22.3 7.6 %all-to-all-start = ((s32[8,8,128]{2,1,0:T(8,128)}), s32[8,8,128]{2,1,0:T(8,128)S(1)}, u32[]{:S(2)}, u32[]{:S(2)}) async-start(s32[8,8,128]{2,1,0:T(8,128)} %get-tuple-element.12), calls=%async_computation | async-start | bytes 65536 | tf_op jit(solution)/shard_map/all_to_all | solution.py:787
  29.9 3.6 %pack.3 = (bf16[4,2,2,512,128]{4,3,2,1,0:T(8,128)(2,1)}, bf16[4,1,2,512,128]{4,3,2,1,0:T(8,128)(2,1)}) custom-call(s32[1]{0:T(128)} %bitcast.4.me, s32[16]{0:T(128)} %bitcast.34, bf16[16,2,512,128]{3,2,1,0:T(8,128)(2,1)} %basis.3, bf16[4,1,2,512,128]{4,3,2,1,0:T(8,128)(2,1)} %pack.2.first), custom_call_target="tpu_custom_call" | custom-call | tf_op jit(solution)/shard_map/pack/pallas_call | solution.py:121
  33.4 5.4 %all-to-all-done.refs_5_ = s32[8,8,128]{2,1,0:T(8,128)S(1)} async-done(((s32[8,8,128]{2,1,0:T(8,128)}), s32[8,8,128]{2,1,0:T(8,128)S(1)}, u32[]{:S(2)}, u32[]{:S(2)}) %all-to-all-start) | async-done | bytes 32800 | tf_op jit(solution)/shard_map/all_to_all | solution.py:787
  40.1 4.6 %all-to-all-start.1 = ((bf16[4,2,2,512,128]{4,3,2,1,0:T(8,128)(2,1)}), bf16[4,2,2,512,128]{4,3,2,1,0:T(8,128)(2,1)}, u32[]{:S(2)}, u32[]{:S(2)}) async-start(bf16[4,2,2,512,128]{4,3,2,1,0:T(8,128)(2,1)} %after.2), calls=%async_computation.1 | async-start | bytes 4194304 | tf_op jit(solution)/shard_map/all_to_all | solution.py:160
  44.6 1.5 collective-permute-start.14
  46.7 1.4 collective-permute-start.4
  48.2 2.1 %add.195.refs_4_ = bf16[1024,256]{1,0:T(8,128)(2,1)} add(bf16[1024,256]{1,0:T(8,128)(2,1)} %collective-permute-done.5, bf16[1024,256]{1,0:T(8,128)(2,1)} %collective-permute-done.6.refs_2_) | non-fusion elementwise | flops 262144 | bytes 1572864 | tf_op jit(solution)/shard_map/add | solution.py:200
  53.1 18.0 %collective-permute-done.14 = bf16[4,1,2,512,128]{4,3,2,1,0:T(8,128)(2,1)} collective-permute-done((bf16[4,1,2,512,128]{4,3,2,1,0:T(8,128)(2,1)}, bf16[4,1,2,512,128]{4,3,2,1,0:T(8,128)(2,1)}, u32[]{:S(2)}, u32[]{:S(2)}) %collective-permute-start.14) | collective-permute-done | bytes 1048608 | tf_op jit(solution)/shard_map/ppermute | solution.py:78
  71.1 2.8 %pad_maximum_fusion.refs_0_ = bf16[4,2,2,512,128]{4,3,2,1,0:T(8,128)(2,1)} fusion(bf16[4,1,2,512,128]{4,3,2,1,0:T(8,128)(2,1)} %collective-permute-done.14, bf16[4,1,2,512,128]{4,3,2,1,0:T(8,128)(2,1)S(1)} %copy-done.1), kind=kLoop, calls=%fused_computation | loop fusion | flops 1048576 | bytes 4194304 | tf_op jit(solution)/shard_map/concatenate | solution.py:159
  73.9 8.4 %collective-permute-done.2.refs_1_.refs_3_ = bf16[1024,256]{1,0:T(8,128)(2,1)S(1)} collective-permute-done((bf16[1024,256]{1,0:T(8,128)(2,1)S(1)}, bf16[1024,256]{1,0:T(8,128)(2,1)S(1)}, u32[]{:S(2)}, u32[]{:S(2)}) %collective-permute-start.2) | collective-permute-done | bytes 524320 | tf_op jit(solution)/shard_map/ppermute | solution.py:78
  82.3 11.2 %collective-permute-done.4.refs_3_.refs_4_ = bf16[1024,256]{1,0:T(8,128)(2,1)S(1)} collective-permute-done((bf16[1024,256]{1,0:T(8,128)(2,1)}, bf16[1024,256]{1,0:T(8,128)(2,1)S(1)}, u32[]{:S(2)}, u32[]{:S(2)}) %collective-permute-start.4) | collective-permute-done | bytes 524320 | tf_op jit(solution)/shard_map/ppermute | solution.py:78
  93.5 9.3 %collective-permute-done.7.refs_5_ = bf16[1024,256]{1,0:T(8,128)(2,1)} collective-permute-done((bf16[1024,256]{1,0:T(8,128)(2,1)}, bf16[1024,256]{1,0:T(8,128)(2,1)}, u32[]{:S(2)}, u32[]{:S(2)}) %collective-permute-start.7) | collective-permute-done | bytes 524320 | tf_op jit(solution)/shard_map/ppermute | solution.py:78
  102.9 4.7 %all-to-all-start.2 = ((bf16[4,2,2,512,128]{4,3,2,1,0:T(8,128)(2,1)}), bf16[4,2,2,512,128]{4,3,2,1,0:T(8,128)(2,1)}, u32[]{:S(2)}, u32[]{:S(2)}) async-start(bf16[4,2,2,512,128]{4,3,2,1,0:T(8,128)(2,1)} %after.3), calls=%async_computation.2 | async-start | bytes 4194304 | tf_op jit(solution)/shard_map/all_to_all | solution.py:160
  114.4 8.3 %collective-permute-done.10.refs_7_ = bf16[1024,256]{1,0:T(8,128)(2,1)S(1)} collective-permute-done((bf16[1024,256]{1,0:T(8,128)(2,1)S(1)}, bf16[1024,256]{1,0:T(8,128)(2,1)S(1)}, u32[]{:S(2)}, u32[]{:S(2)}) %collective-permute-start.10) | collective-permute-done | bytes 524320 | tf_op jit(solution)/shard_map/ppermute | solution.py:78
  123.5 2.9 %edge_blocks.1 = (bf16[2,512,256]{2,1,0:T(8,128)(2,1)}, bf16[2,512,256]{2,1,0:T(8,128)(2,1)}) custom-call(s32[8]{0:T(128)} %stack.35.owners, bf16[1024,256]{1,0:T(8,128)(2,1)} %get-tuple-element.13.refs_0_.first, bf16[1024,256]{1,0:T(8,128)(2,1)} %copy-done.4, bf16[1024,256]{1,0:T(8,128)(2,1)} %collective-permute-done.3.refs_2_, ...), custom_call_target="tpu_custom_call" | custom-call | tf_op jit(solution)/shard_map/edge_blocks/pallas_call | solution.py:243
  126.4 1.9 %collective-permute-start.11 = (bf16[2,512,256]{2,1,0:T(8,128)(2,1)}, bf16[2,512,256]{2,1,0:T(8,128)(2,1)S(1)}, u32[]{:S(2)}, u32[]{:S(2)}) collective-permute-start(bf16[2,512,256]{2,1,0:T(8,128)(2,1)} %get-tuple-element.15.h_last), channel_id=1, source_target_pairs={{0,8},{8,16},{16,24},{1,9},{9,17},{17,25},{2,10},{10,18},{18,26},{... | collective-permute-start | bytes 1572872 | tf_op jit(solution)/shard_map/ppermute | solution.py:719
  128.3 3.6 %collective-permute-start.12 = (bf16[2,512,256]{2,1,0:T(8,128)(2,1)}, bf16[2,512,256]{2,1,0:T(8,128)(2,1)S(1)}, u32[]{:S(2)}, u32[]{:S(2)}) collective-permute-start(bf16[2,512,256]{2,1,0:T(8,128)(2,1)} %get-tuple-element.16.h_first), channel_id=1, source_target_pairs={{8,0},{16,8},{24,16},{9,1},{17,9},{25,17},{10,2},{18,10},{26,18},{... | collective-permute-start | bytes 1572872 | tf_op jit(solution)/shard_map/ppermute | solution.py:719
  132.0 16.4 %chebyshev_inner.1 = (bf16[8,512,512]{2,1,0:T(8,128)(2,1)}, bf16[1024,512]{1,0:T(8,128)(2,1)}, bf16[1024,512]{1,0:T(8,128)(2,1)}, f32[1024,512]{1,0:T(8,128)}) custom-call(f32[4]{0:T(128)} %coef.3, s32[8]{0:T(128)} %stack.35.owners, bf16[768,512]{1,0:T(8,128)(2,1)} %copy-done.2, bf16[4096,512]{1,0:T(8,128)(2,1)} %v_mid.3, ...), custom_call_target="tpu_custom_call" | custom-call | flops 8455716864 | bytes 16777216 | tf_op jit(solution)/shard_map/chebyshev_inner/pallas_call | solution.py:366
  149.4 7.1 %chebyshev_outer.1.kernel_t = bf16[8,512,512]{2,1,0:T(8,128)(2,1)} custom-call(f32[4]{0:T(128)} %coef.3, bf16[8,512,512]{2,1,0:T(8,128)(2,1)} %get-tuple-element.14.kernel_in, bf16[768,512]{1,0:T(8,128)(2,1)} %copy-done.2, bf16[4096,512]{1,0:T(8,128)(2,1)} %v_mid.3, ...), custom_call_target="tpu_custom_call", output_to_operand_aliasing={{}: (1, {})} | custom-call | tf_op jit(solution)/shard_map/chebyshev_outer/pallas_call | solution.py:484
  156.5 5.4 %project.1 = f32[8,24,128]{2,1,0:T(8,128)} custom-call(s32[26]{0:T(128)} %pad_add_fusion.1.plan, s32[16]{0:T(128)} %select_reduce_fusion.2.order, bf16[8,512,512]{2,1,0:T(8,128)(2,1)} %chebyshev_outer.1.kernel_t, f32[4,128]{1,0:T(4,128)} %core.1, bf16[8,2,512,128]{3,2,1,0:T(8,128)(2,1)} %bitcast.13.refs_0_, bf16[8,2,512,128]{3,2,1,0:T(8,128)(2,1)} %bitcast.14.refs_1_), custom_call_target="tpu_custom_call" | custom-call | tf_op jit(solution)/shard_map/project/pallas_call | solution.py:596
  161.8 4.0 %all-to-all-start.3 = ((f32[8,24,128]{2,1,0:T(8,128)}), f32[8,24,128]{2,1,0:T(8,128)S(1)}, u32[]{:S(2)}, u32[]{:S(2)}) async-start(f32[8,24,128]{2,1,0:T(8,128)} %project.1), calls=%async_computation.3 | async-start | bytes 196608 | tf_op jit(solution)/shard_map/all_to_all | solution.py:802
  166.6 6.4 %all-to-all-done.3 = f32[8,24,128]{2,1,0:T(8,128)S(1)} async-done(((f32[8,24,128]{2,1,0:T(8,128)}), f32[8,24,128]{2,1,0:T(8,128)S(1)}, u32[]{:S(2)}, u32[]{:S(2)}) %all-to-all-start.3) | async-done | bytes 98336 | tf_op jit(solution)/shard_map/all_to_all | solution.py:802
  173.6 7.4 %update.1 = (f32[4,128]{1,0:T(4,128)}, bf16[4096,512]{1,0:T(8,128)(2,1)}) custom-call(s32[26]{0:T(128)} %pad_add_fusion.1.plan, s32[16]{0:T(128)} %select_reduce_fusion.2.order, s32[16]{0:T(128)} %reshape.285.tile_of, f32[192,128]{1,0:T(8,128)} %bitcast.25, f32[32,192]{1,0:T(8,128)} %convert_reduce_fusion.collect, bf16[8,2,512,128]{3,2,1,0:T(8,128)(2,1)} %bitcast.13.refs_0_, ...), custom_call_target="tpu_custom_call" | custom-call | tf_op jit(solution)/shard_map/update/pallas_call | solution.py:694
  (84 shorter events, 15.9 us)
Async XLA Ops:
  3.8 15.7 %collective-permute-start.3 = (bf16[1024,256]{1,0:T(8,128)(2,1)}, bf16[1024,256]{1,0:T(8,128)(2,1)}, u32[]{:S(2)}, u32[]{:S(2)}) collective-permute-start(bf16[1024,256]{1,0:T(8,128)(2,1)} %get-tuple-element.13.refs_0_.first), channel_id=1, source_target_pairs={{0,2},{1,3},{2,0},{3,1},{4,6},{5,7},{6,4},{7,5},{8,10},{9,11},{10,... | collective-permute-start | bytes 1572872 | tf_op jit(solution)/shard_map/ppermute | solution.py:187
  5.5 15.5 %collective-permute-start.5 = (bf16[1024,256]{1,0:T(8,128)(2,1)}, bf16[1024,256]{1,0:T(8,128)(2,1)}, u32[]{:S(2)}, u32[]{:S(2)}) collective-permute-start(bf16[1024,256]{1,0:T(8,128)(2,1)} %get-tuple-element.13.refs_0_.first), channel_id=1, source_target_pairs={{2,4},{3,5},{4,2},{5,3},{10,12},{11,13},{12,10},{13,11},{18,20},{1... | collective-permute-start | bytes 1572872 | tf_op jit(solution)/shard_map/ppermute | solution.py:187
  9.7 29.1 %collective-permute-start.13 = (bf16[4,1,2,512,128]{4,3,2,1,0:T(8,128)(2,1)}, bf16[4,1,2,512,128]{4,3,2,1,0:T(8,128)(2,1)S(1)}, u32[]{:S(2)}, u32[]{:S(2)}) collective-permute-start(bf16[4,1,2,512,128]{4,3,2,1,0:T(8,128)(2,1)} %pack.2.first), channel_id=1, source_target_pairs={{0,1},{1,0},{2,3},{3,2},{4,5},{5,4},{6,7},{7,6},{8,9},{9,8},{10,11... | collective-permute-start | bytes 3145736 | tf_op jit(solution)/shard_map/ppermute | solution.py:78
  13.9 24.9 %collective-permute-start = (bf16[768,512]{1,0:T(8,128)(2,1)}, bf16[768,512]{1,0:T(8,128)(2,1)S(1)}, u32[]{:S(2)}, u32[]{:S(2)}) collective-permute-start(bf16[768,512]{1,0:T(8,128)(2,1)} %get-tuple-element.29), channel_id=1, source_target_pairs={{0,8},{8,16},{16,24},{1,9},{9,17},{17,25},{2,10},{10,18},{18,26},{... | collective-permute-start | bytes 2359304 | tf_op jit(solution)/shard_map/ppermute | solution.py:719
  15.8 23.0 %collective-permute-start.1 = (bf16[768,512]{1,0:T(8,128)(2,1)}, bf16[768,512]{1,0:T(8,128)(2,1)}, u32[]{:S(2)}, u32[]{:S(2)}) collective-permute-start(bf16[768,512]{1,0:T(8,128)(2,1)} %get-tuple-element.28), channel_id=1, source_target_pairs={{8,0},{16,8},{24,16},{9,1},{17,9},{25,17},{10,2},{18,10},{26,18},{... | collective-permute-start | bytes 2359304 | tf_op jit(solution)/shard_map/ppermute | solution.py:719
  19.5 19.3 %collective-permute-start.8 = (bf16[1024,256]{1,0:T(8,128)(2,1)}, bf16[1024,256]{1,0:T(8,128)(2,1)}, u32[]{:S(2)}, u32[]{:S(2)}) collective-permute-start(bf16[1024,256]{1,0:T(8,128)(2,1)} %collective-permute-done.3.refs_2_), channel_id=1, source_target_pairs={{2,4},{3,5},{4,2},{5,3},{10,12},{11,13},{12,10},{13,11},{18,20},{1... | collective-permute-start | bytes 1572872 | tf_op jit(solution)/shard_map/ppermute | solution.py:187
  21.0 17.8 %collective-permute-start.6 = (bf16[1024,256]{1,0:T(8,128)(2,1)}, bf16[1024,256]{1,0:T(8,128)(2,1)}, u32[]{:S(2)}, u32[]{:S(2)}) collective-permute-start(bf16[1024,256]{1,0:T(8,128)(2,1)} %collective-permute-done.5), channel_id=1, source_target_pairs={{2,0},{3,1},{4,6},{5,7},{10,8},{11,9},{12,14},{13,15},{18,16},{19,... | collective-permute-start | bytes 1572872 | tf_op jit(solution)/shard_map/ppermute | solution.py:187
  22.3 16.5 %all-to-all-start = ((s32[8,8,128]{2,1,0:T(8,128)}), s32[8,8,128]{2,1,0:T(8,128)S(1)}, u32[]{:S(2)}, u32[]{:S(2)}) async-start(s32[8,8,128]{2,1,0:T(8,128)} %get-tuple-element.12), calls=%async_computation | async-start | bytes 65536 | tf_op jit(solution)/shard_map/all_to_all | solution.py:787
  38.8 0.6 copy-start.11
  38.8 0.9 copy-start.2
  38.8 1.2 copy-start
  40.1 6.1 %copy-start.3 = (bf16[1024,256]{1,0:T(8,128)(2,1)S(1)}, bf16[1024,256]{1,0:T(8,128)(2,1)}, u32[]{:S(2)}) copy-start(bf16[1024,256]{1,0:T(8,128)(2,1)} %get-tuple-element.13.refs_0_.first) | copy-start | bytes 1572868
  40.1 31.1 %copy-start.1 = (bf16[4,1,2,512,128]{4,3,2,1,0:T(8,128)(2,1)S(1)}, bf16[4,1,2,512,128]{4,3,2,1,0:T(8,128)(2,1)}, u32[]{:S(2)}) copy-start(bf16[4,1,2,512,128]{4,3,2,1,0:T(8,128)(2,1)} %copy-done) | copy-start | bytes 3145732
  40.1 62.8 %all-to-all-start.1 = ((bf16[4,2,2,512,128]{4,3,2,1,0:T(8,128)(2,1)}), bf16[4,2,2,512,128]{4,3,2,1,0:T(8,128)(2,1)}, u32[]{:S(2)}, u32[]{:S(2)}) async-start(bf16[4,2,2,512,128]{4,3,2,1,0:T(8,128)(2,1)} %after.2), calls=%async_computation.1 | async-start | bytes 4194304 | tf_op jit(solution)/shard_map/all_to_all | solution.py:160
  44.6 26.5 %collective-permute-start.14 = (bf16[4,1,2,512,128]{4,3,2,1,0:T(8,128)(2,1)}, bf16[4,1,2,512,128]{4,3,2,1,0:T(8,128)(2,1)}, u32[]{:S(2)}, u32[]{:S(2)}) collective-permute-start(bf16[4,1,2,512,128]{4,3,2,1,0:T(8,128)(2,1)} %get-tuple-element.21), channel_id=1, source_target_pairs={{0,1},{1,0},{2,3},{3,2},{4,5},{5,4},{6,7},{7,6},{8,9},{9,8},{10,11... | collective-permute-start | bytes 3145736 | tf_op jit(solution)/shard_map/ppermute | solution.py:78
  46.1 36.1 %collective-permute-start.2 = (bf16[1024,256]{1,0:T(8,128)(2,1)S(1)}, bf16[1024,256]{1,0:T(8,128)(2,1)S(1)}, u32[]{:S(2)}, u32[]{:S(2)}) collective-permute-start(bf16[1024,256]{1,0:T(8,128)(2,1)S(1)} %copy-done.3), channel_id=1, source_target_pairs={{0,1},{1,0},{2,3},{3,2},{4,5},{5,4},{6,7},{7,6},{8,9},{9,8},{10,11... | collective-permute-start | bytes 1572872 | tf_op jit(solution)/shard_map/ppermute | solution.py:78
  46.7 46.7 %collective-permute-start.4 = (bf16[1024,256]{1,0:T(8,128)(2,1)}, bf16[1024,256]{1,0:T(8,128)(2,1)S(1)}, u32[]{:S(2)}, u32[]{:S(2)}) collective-permute-start(bf16[1024,256]{1,0:T(8,128)(2,1)} %collective-permute-done.3.refs_2_), channel_id=1, source_target_pairs={{0,1},{1,0},{2,3},{3,2},{4,5},{5,4},{6,7},{7,6},{8,9},{9,8},{10,11... | collective-permute-start | bytes 1572872 | tf_op jit(solution)/shard_map/ppermute | solution.py:78
  50.3 52.5 %collective-permute-start.7 = (bf16[1024,256]{1,0:T(8,128)(2,1)}, bf16[1024,256]{1,0:T(8,128)(2,1)}, u32[]{:S(2)}, u32[]{:S(2)}) collective-permute-start(bf16[1024,256]{1,0:T(8,128)(2,1)} %add.195.refs_4_), channel_id=1, source_target_pairs={{0,1},{1,0},{2,3},{3,2},{4,5},{5,4},{6,7},{7,6},{8,9},{9,8},{10,11... | collective-permute-start | bytes 1572872 | tf_op jit(solution)/shard_map/ppermute | solution.py:78
  50.9 42.6 %collective-permute-start.9 = (bf16[1024,256]{1,0:T(8,128)(2,1)}, bf16[1024,256]{1,0:T(8,128)(2,1)}, u32[]{:S(2)}, u32[]{:S(2)}) collective-permute-start(bf16[1024,256]{1,0:T(8,128)(2,1)} %collective-permute-done.8.refs_1_), channel_id=1, source_target_pairs={{2,0},{3,1},{4,6},{5,7},{10,8},{11,9},{12,14},{13,15},{18,16},{19,... | collective-permute-start | bytes 1572872 | tf_op jit(solution)/shard_map/ppermute | solution.py:187
  82.3 20.6 %copy-start.4 = (bf16[1024,256]{1,0:T(8,128)(2,1)}, bf16[1024,256]{1,0:T(8,128)(2,1)S(1)}, u32[]{:S(2)}) copy-start(bf16[1024,256]{1,0:T(8,128)(2,1)S(1)} %collective-permute-done.2.refs_1_.refs_3_) | copy-start | bytes 1572868
  93.5 9.4 %copy-start.5 = (bf16[1024,256]{1,0:T(8,128)(2,1)}, bf16[1024,256]{1,0:T(8,128)(2,1)S(1)}, u32[]{:S(2)}) copy-start(bf16[1024,256]{1,0:T(8,128)(2,1)S(1)} %collective-permute-done.4.refs_3_.refs_4_) | copy-start | bytes 1572868
  102.9 53.6 %all-to-all-start.2 = ((bf16[4,2,2,512,128]{4,3,2,1,0:T(8,128)(2,1)}), bf16[4,2,2,512,128]{4,3,2,1,0:T(8,128)(2,1)}, u32[]{:S(2)}, u32[]{:S(2)}) async-start(bf16[4,2,2,512,128]{4,3,2,1,0:T(8,128)(2,1)} %after.3), calls=%async_computation.2 | async-start | bytes 4194304 | tf_op jit(solution)/shard_map/all_to_all | solution.py:160
  110.9 11.8 %copy-start.6 = (bf16[1024,256]{1,0:T(8,128)(2,1)}, bf16[1024,256]{1,0:T(8,128)(2,1)S(1)}, u32[]{:S(2)}) copy-start(bf16[1024,256]{1,0:T(8,128)(2,1)S(1)} %add.196.refs_6_) | copy-start | bytes 1572868
  110.9 11.8 %collective-permute-start.10 = (bf16[1024,256]{1,0:T(8,128)(2,1)S(1)}, bf16[1024,256]{1,0:T(8,128)(2,1)S(1)}, u32[]{:S(2)}, u32[]{:S(2)}) collective-permute-start(bf16[1024,256]{1,0:T(8,128)(2,1)S(1)} %add.196.refs_6_), channel_id=1, source_target_pairs={{0,1},{1,0},{2,3},{3,2},{4,5},{5,4},{6,7},{7,6},{8,9},{9,8},{10,11... | collective-permute-start | bytes 1572872 | tf_op jit(solution)/shard_map/ppermute | solution.py:78
  122.7 0.8 copy-start.7
  126.4 22.0 %collective-permute-start.11 = (bf16[2,512,256]{2,1,0:T(8,128)(2,1)}, bf16[2,512,256]{2,1,0:T(8,128)(2,1)S(1)}, u32[]{:S(2)}, u32[]{:S(2)}) collective-permute-start(bf16[2,512,256]{2,1,0:T(8,128)(2,1)} %get-tuple-element.15.h_last), channel_id=1, source_target_pairs={{0,8},{8,16},{16,24},{1,9},{9,17},{17,25},{2,10},{10,18},{18,26},{... | collective-permute-start | bytes 1572872 | tf_op jit(solution)/shard_map/ppermute | solution.py:719
  128.3 20.0 %collective-permute-start.12 = (bf16[2,512,256]{2,1,0:T(8,128)(2,1)}, bf16[2,512,256]{2,1,0:T(8,128)(2,1)S(1)}, u32[]{:S(2)}, u32[]{:S(2)}) collective-permute-start(bf16[2,512,256]{2,1,0:T(8,128)(2,1)} %get-tuple-element.16.h_first), channel_id=1, source_target_pairs={{8,0},{16,8},{24,16},{9,1},{17,9},{25,17},{10,2},{18,10},{26,18},{... | collective-permute-start | bytes 1572872 | tf_op jit(solution)/shard_map/ppermute | solution.py:719
  148.3 0.8 copy-start.8
  148.4 1.0 copy-start.9
  161.8 11.2 %all-to-all-start.3 = ((f32[8,24,128]{2,1,0:T(8,128)}), f32[8,24,128]{2,1,0:T(8,128)S(1)}, u32[]{:S(2)}, u32[]{:S(2)}) async-start(f32[8,24,128]{2,1,0:T(8,128)} %project.1), calls=%async_computation.3 | async-start | bytes 196608 | tf_op jit(solution)/shard_map/all_to_all | solution.py:802
  173.0 0.6 copy-start.10

commit v7 on v6

--- a/solution.py
+++ b/solution.py
@@ -150,7 +150,7 @@
     )(block, *others)
 
 
-def exchange(me, peers, basis, own, awaited, handed):
+def exchange(me, peers, basis, own, early, awaited, handed):
     count = lax.axis_size("col")
     outer, inner = lines_of(count)
     groups = [[line * inner + place for line in range(outer)] for place in range(inner)]
@@ -166,7 +166,7 @@
     ahead = [[(t, 0)] for t in range(1, inner)]
     rest = [[(t, k)] for k in range(1, CAP) for t in range(1, inner)]
     sent = pack(me, peers, basis, own, count, ahead) if ahead else []
-    to_lines, *later = pack(me, peers, basis, sent[0] if ahead else own, count, [here] + rest)
+    to_lines, *later = pack(me, peers, basis, early, count, [here] + rest)
     swapped = {
         group[0]: swap_along(block, group[0][0]) for block, group in zip(sent + later, ahead + rest)
     }
@@ -637,46 +637,44 @@
         rows = pl.ds(pl.multiple_of(b * KB, KB), KB)
         return pltpu.make_async_copy(stage.at[b], update_out.at[rows], osems.at[b])
 
+    most = jnp.maximum(live - 1, 0)
+
+    @pl.when(live == 0)
+    def _():
+        pair[0] = jnp.zeros(pair.shape[1:], jnp.bfloat16)
+
+    def arrived(p, carry):
+        load(p).wait()
+        return carry
+
+    lax.fori_loop(0, live, arrived, 0)
+
+    def two(p, last):
+        sides = []
+        for place in (p, p + 1):
+            at = jnp.minimum(place, most)
+            weight = potential[pl.ds(tile_of[order[at]], 1), :] * (place < last).astype(jnp.float32)
+            sides.append((pair[at, 0], (pair[at, 1].astype(jnp.float32) * weight).astype(jnp.bfloat16)))
+        return lax.dot_general(
+            jnp.concatenate([rows for rows, _ in sides], axis=1),
+            jnp.concatenate([weighted for _, weighted in sides], axis=1),
+            (((1,), (1,)), ((), ())),
+            preferred_element_type=jnp.float32,
+        )
+
     def step(b, carry):
         first, last = plan[slots + b], plan[slots + b + 1]
-
-        @pl.when(first == last)
-        def _():
-            stage[b] = jnp.zeros(stage.shape[1:], jnp.bfloat16)
-
-        def body(i, p, q):
-            weight_p = potential[pl.ds(tile_of[order[p]], 1), :]
-            weight_q = potential[pl.ds(tile_of[order[q]], 1), :] * (q - p).astype(jnp.float32)
-            weighted = jnp.concatenate(
-                [
-                    (pair[p, 1].astype(jnp.float32) * weight_p).astype(jnp.bfloat16),
-                    (pair[q, 1].astype(jnp.float32) * weight_q).astype(jnp.bfloat16),
-                ],
-                axis=1,
-            )
-            block = lax.dot_general(
-                jnp.concatenate([pair[p, 0], pair[q, 0]], axis=1),
-                weighted,
-                (((1,), (1,)), ((), ())),
-                preferred_element_type=jnp.float32,
-            )
-
-            @pl.when(last - first <= 2)
-            def _():
-                stage[b] = (block * scale).astype(jnp.bfloat16)
-
-            @pl.when((last - first > 2) & (i == 0))
-            def _():
-                acc[...] = block
-
-            @pl.when(i > 0)
-            def _():
-                acc[...] += block
-
-        by_twos(first, last, load, body)
+        stage[b] = (two(first, last) * scale).astype(jnp.bfloat16)
 
         @pl.when(last - first > 2)
         def _():
+            acc[...] = two(first, last)
+
+            def more(i, carry):
+                acc[...] += two(first + 2 * i, last)
+                return carry
+
+            lax.fori_loop(1, (last - first + 1) // 2, more, 0)
             stage[b] = (acc[...] * scale).astype(jnp.bfloat16)
 
         store(b).start()
@@ -788,7 +786,8 @@
     pieces, owners, awaited, handed = gather_pieces(own)
     v_low = shift(start_columns[-DEG * W :], "row", 1)
     v_high = shift(start_columns[: DEG * W], "row", -1)
-    parts = exchange(me[None], peers, basis_values, own, awaited + [v_low, v_high, lists], handed)
+    parts = exchange(me[None], peers, basis_values, own, pieces[min(1, len(pieces) - 1)],
+        awaited + [v_low, v_high, lists], handed)
 
     first, last = edge_blocks(owners, pieces, col_count, DEG - 1)
     h_low = shift(last, "row", 1)

time: 183 us -> 180 us (0.984)
  waiting for transfers between devices: 67 us -> 63.8 us
    ppermute x6, waiting for transfers between devices: 55.2 us -> 46.1 us  [swap_along(): return lax.ppermute(block, 'col', pairs)]
    all_to_all x1, waiting for transfers between devices: 5.37 us -> 8.37 us  [shards(): lax.all_to_all(lists, 'col', split_axis=0, concat_axis=0, tiled=True)]
    all_to_all x1, starting transfers between devices: 4.05 us -> 6.1 us  [shards(): lax.all_to_all(partial, 'col', split_axis=0, concat_axis=0, tiled=True)]
  transfers between devices with their start and end apart: 19 -> 19, of which waited for: 7 -> 9; matrix products, arithmetic and copies ran while one was open for 8% -> 8% of each run, Pallas kernels for 18% -> 18%
where the time goes in v7:
time: 180 us; the launch traced here: 179 us
  waiting for transfers between devices  63.8 us (35%)
  Pallas kernels  49.2 us (27%)
  starting transfers between devices  47.5 us (26%)
  local copies, waits for them, and re-layouts  9.01 us (5%)
  other arithmetic  8.54 us (5%)
    ppermute x6, waiting for transfers between devices, swap_along(): return lax.ppermute(block, 'col', pairs)  46.1 us
    pallas_call x1, Pallas kernels, chebyshev_inner(): pl.pallas_call(functools.partial(inner_kernel, blocks), out_shape=(jax.Sh...  16.4 us
    ppermute x4, starting transfers between devices, shift(): return lax.ppermute(block, axis, pairs)  9.6 us
    all_to_all x2, starting transfers between devices, between_lines(): lax.all_to_all(after(block, *others), 'col', split_axis=0, concat_axis=0,...  9.24 us
    pallas_call x1, Pallas kernels, update(): pl.pallas_call(functools.partial(update_kernel, blocks, tiles), out_shape...  8.38 us
    all_to_all x1, waiting for transfers between devices, shards(): lax.all_to_all(lists, 'col', split_axis=0, concat_axis=0, tiled=True)  8.37 us
    all_to_all x1, starting transfers between devices, shards(): lax.all_to_all(lists, 'col', split_axis=0, concat_axis=0, tiled=True)  8.12 us
    ppermute x6, starting transfers between devices, swap_along(): return lax.ppermute(block, 'col', pairs)  7.29 us
  transfers between devices with their start and end apart: 19, of which 9 were waited for; matrix products, arithmetic and copies ran while one was open for 8% of the time, Pallas kernels for 18%

profile of v7, /device:TPU:2, one launch (start us, length us, event | category | flops | bytes accessed | tf_op | source)
XLA Modules:
  0.0 179.1 jit_solution(12423507253035309097)
XLA Ops:
  0.6 3.2 %own_piece.1 = (bf16[1024,256]{1,0:T(8,128)(2,1)}, s32[8,8,128]{2,1,0:T(8,128)}) custom-call(s32[16]{0:T(128)} %bitcast.32, s32[16]{0:T(128)} %named.1, s32[4]{0:T(128)} %counts.1, s32[2]{0:T(128)} %pattern.1, bf16[1024,256]{1,0:T(8,128)(2,1)} %bitcast.24), custom_call_target="tpu_custom_call" | custom-call | tf_op jit(solution)/shard_map/own_piece/pallas_call | solution.py:55
  3.8 1.6 collective-permute-start.3
  5.5 1.5 collective-permute-start.5
  6.9 1.5 collective-permute-start.2
  8.4 2.8 %pack.3 = bf16[4,1,2,512,128]{4,3,2,1,0:T(8,128)(2,1)} custom-call(s32[1]{0:T(128)} %bitcast.4.me, s32[16]{0:T(128)} %bitcast.33, bf16[16,2,512,128]{3,2,1,0:T(8,128)(2,1)} %basis.3, bf16[1024,256]{1,0:T(8,128)(2,1)} %get-tuple-element.13.refs_0_.first), custom_call_target="tpu_custom_call" | custom-call | tf_op jit(solution)/shard_map/pack/pallas_call | solution.py:121
  11.8 2.6 %fusion.12 = (bf16[768,512]{1,0:T(8,128)(2,1)}, bf16[768,512]{1,0:T(8,128)(2,1)}) fusion(bf16[4096,512]{1,0:T(8,128)(2,1)} %v_mid.3), kind=kLoop, calls=%fused_computation.53 | loop fusion | bytes 3145728 | tf_op jit(solution)/shard_map/slice | solution.py:788
  14.4 1.9 %collective-permute-start = (bf16[768,512]{1,0:T(8,128)(2,1)}, bf16[768,512]{1,0:T(8,128)(2,1)}, u32[]{:S(2)}, u32[]{:S(2)}) collective-permute-start(bf16[768,512]{1,0:T(8,128)(2,1)} %get-tuple-element.29), channel_id=1, source_target_pairs={{0,8},{8,16},{16,24},{1,9},{9,17},{17,25},{2,10},{10,18},{18,26},{... | collective-permute-start | bytes 2359304 | tf_op jit(solution)/shard_map/ppermute | solution.py:717
  16.3 1.5 collective-permute-done.3.refs_2_
  17.9 2.1 %collective-permute-start.1 = (bf16[768,512]{1,0:T(8,128)(2,1)}, bf16[768,512]{1,0:T(8,128)(2,1)}, u32[]{:S(2)}, u32[]{:S(2)}) collective-permute-start(bf16[768,512]{1,0:T(8,128)(2,1)} %get-tuple-element.28), channel_id=1, source_target_pairs={{8,0},{16,8},{24,16},{9,1},{17,9},{25,17},{10,2},{18,10},{26,18},{... | collective-permute-start | bytes 2359304 | tf_op jit(solution)/shard_map/ppermute | solution.py:717
  20.0 1.5 collective-permute-start.8
  23.3 8.1 %all-to-all-start = ((s32[8,8,128]{2,1,0:T(8,128)}), s32[8,8,128]{2,1,0:T(8,128)S(1)}, u32[]{:S(2)}, u32[]{:S(2)}) async-start(s32[8,8,128]{2,1,0:T(8,128)} %get-tuple-element.12), calls=%async_computation | async-start | bytes 65536 | tf_op jit(solution)/shard_map/all_to_all | solution.py:785
  31.4 3.6 %pack.2 = (bf16[4,2,2,512,128]{4,3,2,1,0:T(8,128)(2,1)}, bf16[4,1,2,512,128]{4,3,2,1,0:T(8,128)(2,1)}) custom-call(s32[1]{0:T(128)} %bitcast.4.me, s32[16]{0:T(128)} %bitcast.34, bf16[16,2,512,128]{3,2,1,0:T(8,128)(2,1)} %basis.3, bf16[1024,256]{1,0:T(8,128)(2,1)} %copy-done), custom_call_target="tpu_custom_call" | custom-call | tf_op jit(solution)/shard_map/pack/pallas_call | solution.py:121
  35.0 8.4 %all-to-all-done.refs_5_ = s32[8,8,128]{2,1,0:T(8,128)S(1)} async-done(((s32[8,8,128]{2,1,0:T(8,128)}), s32[8,8,128]{2,1,0:T(8,128)S(1)}, u32[]{:S(2)}, u32[]{:S(2)}) %all-to-all-start) | async-done | bytes 32800 | tf_op jit(solution)/shard_map/all_to_all | solution.py:785
  44.4 4.8 %all-to-all-start.1 = ((bf16[4,2,2,512,128]{4,3,2,1,0:T(8,128)(2,1)}), bf16[4,2,2,512,128]{4,3,2,1,0:T(8,128)(2,1)}, u32[]{:S(2)}, u32[]{:S(2)}) async-start(bf16[4,2,2,512,128]{4,3,2,1,0:T(8,128)(2,1)} %after.2), calls=%async_computation.1 | async-start | bytes 4194304 | tf_op jit(solution)/shard_map/all_to_all | solution.py:160
  49.2 1.5 collective-permute-start.14
  52.5 1.6 collective-permute-start.7
  56.4 19.2 %collective-permute-done.14 = bf16[4,1,2,512,128]{4,3,2,1,0:T(8,128)(2,1)} collective-permute-done((bf16[4,1,2,512,128]{4,3,2,1,0:T(8,128)(2,1)}, bf16[4,1,2,512,128]{4,3,2,1,0:T(8,128)(2,1)}, u32[]{:S(2)}, u32[]{:S(2)}) %collective-permute-start.14) | collective-permute-done | bytes 1048608 | tf_op jit(solution)/shard_map/ppermute | solution.py:78
  75.6 2.8 %pad_maximum_fusion.refs_0_ = bf16[4,2,2,512,128]{4,3,2,1,0:T(8,128)(2,1)} fusion(bf16[4,1,2,512,128]{4,3,2,1,0:T(8,128)(2,1)} %collective-permute-done.14, bf16[4,1,2,512,128]{4,3,2,1,0:T(8,128)(2,1)S(1)} %copy-done.2), kind=kLoop, calls=%fused_computation | loop fusion | flops 1048576 | bytes 4194304 | tf_op jit(solution)/shard_map/concatenate | solution.py:159
  78.4 8.4 %collective-permute-done.4.refs_3_.refs_4_ = bf16[1024,256]{1,0:T(8,128)(2,1)S(1)} collective-permute-done((bf16[1024,256]{1,0:T(8,128)(2,1)}, bf16[1024,256]{1,0:T(8,128)(2,1)S(1)}, u32[]{:S(2)}, u32[]{:S(2)}) %collective-permute-start.4) | collective-permute-done | bytes 524320 | tf_op jit(solution)/shard_map/ppermute | solution.py:78
  86.7 8.7 %collective-permute-done.7.refs_5_ = bf16[1024,256]{1,0:T(8,128)(2,1)S(1)} collective-permute-done((bf16[1024,256]{1,0:T(8,128)(2,1)S(1)}, bf16[1024,256]{1,0:T(8,128)(2,1)S(1)}, u32[]{:S(2)}, u32[]{:S(2)}) %collective-permute-start.7) | collective-permute-done | bytes 524320 | tf_op jit(solution)/shard_map/ppermute | solution.py:78
  96.8 4.5 %all-to-all-start.2 = ((bf16[4,2,2,512,128]{4,3,2,1,0:T(8,128)(2,1)}), bf16[4,2,2,512,128]{4,3,2,1,0:T(8,128)(2,1)}, u32[]{:S(2)}, u32[]{:S(2)}) async-start(bf16[4,2,2,512,128]{4,3,2,1,0:T(8,128)(2,1)} %after.3), calls=%async_computation.2 | async-start | bytes 4194304 | tf_op jit(solution)/shard_map/all_to_all | solution.py:160
  104.6 1.6 collective-permute-start.10
  108.7 9.4 %collective-permute-done.10.refs_7_ = bf16[1024,256]{1,0:T(8,128)(2,1)S(1)} collective-permute-done((bf16[1024,256]{1,0:T(8,128)(2,1)S(1)}, bf16[1024,256]{1,0:T(8,128)(2,1)S(1)}, u32[]{:S(2)}, u32[]{:S(2)}) %collective-permute-start.10) | collective-permute-done | bytes 524320 | tf_op jit(solution)/shard_map/ppermute | solution.py:78
  118.9 2.9 %edge_blocks.1 = (bf16[2,512,256]{2,1,0:T(8,128)(2,1)}, bf16[2,512,256]{2,1,0:T(8,128)(2,1)}) custom-call(s32[8]{0:T(128)} %stack.35.owners, bf16[1024,256]{1,0:T(8,128)(2,1)} %get-tuple-element.13.refs_0_.first, bf16[1024,256]{1,0:T(8,128)(2,1)} %copy-done, bf16[1024,256]{1,0:T(8,128)(2,1)} %collective-permute-done.3.refs_2_, bf16[1024,256]{1,0:T(8,128)(2,1)} %copy-done.3, ...), custom_call_target="tpu_custom_call" | custom-call | tf_op jit(solution)/shard_map/edge_blocks/pallas_call | solution.py:243
  121.8 1.9 %collective-permute-start.11 = (bf16[2,512,256]{2,1,0:T(8,128)(2,1)}, bf16[2,512,256]{2,1,0:T(8,128)(2,1)S(1)}, u32[]{:S(2)}, u32[]{:S(2)}) collective-permute-start(bf16[2,512,256]{2,1,0:T(8,128)(2,1)} %get-tuple-element.15.h_last), channel_id=1, source_target_pairs={{0,8},{8,16},{16,24},{1,9},{9,17},{17,25},{2,10},{10,18},{18,26},{... | collective-permute-start | bytes 1572872 | tf_op jit(solution)/shard_map/ppermute | solution.py:717
  123.7 3.6 %collective-permute-start.12 = (bf16[2,512,256]{2,1,0:T(8,128)(2,1)}, bf16[2,512,256]{2,1,0:T(8,128)(2,1)S(1)}, u32[]{:S(2)}, u32[]{:S(2)}) collective-permute-start(bf16[2,512,256]{2,1,0:T(8,128)(2,1)} %get-tuple-element.16.h_first), channel_id=1, source_target_pairs={{8,0},{16,8},{24,16},{9,1},{17,9},{25,17},{10,2},{18,10},{26,18},{... | collective-permute-start | bytes 1572872 | tf_op jit(solution)/shard_map/ppermute | solution.py:717
  127.4 16.4 %chebyshev_inner.1 = (bf16[8,512,512]{2,1,0:T(8,128)(2,1)}, bf16[1024,512]{1,0:T(8,128)(2,1)}, bf16[1024,512]{1,0:T(8,128)(2,1)}, f32[1024,512]{1,0:T(8,128)}) custom-call(f32[4]{0:T(128)} %coef.3, s32[8]{0:T(128)} %stack.35.owners, bf16[768,512]{1,0:T(8,128)(2,1)} %collective-permute-done.v_low.refs_3_, bf16[4096,512]{1,0:T(8,128)(2,1)} %v_mid.3, ...), custom_call_target="tpu_custom_call" | custom-call | flops 8455716864 | bytes 16777216 | tf_op jit(solution)/shard_map/chebyshev_inner/pallas_call | solution.py:366
  144.8 7.1 %chebyshev_outer.1.kernel_t = bf16[8,512,512]{2,1,0:T(8,128)(2,1)} custom-call(f32[4]{0:T(128)} %coef.3, bf16[8,512,512]{2,1,0:T(8,128)(2,1)} %get-tuple-element.14.kernel_in, bf16[768,512]{1,0:T(8,128)(2,1)} %collective-permute-done.v_low.refs_3_, bf16[4096,512]{1,0:T(8,128)(2,1)} %v_mid.3, ...), custom_call_target="tpu_custom_call", output_to_operand_aliasing={{}: (1, {})} | custom-call | tf_op jit(solution)/shard_map/chebyshev_outer/pallas_call | solution.py:484
  151.9 5.0 %project.1 = f32[8,24,128]{2,1,0:T(8,128)} custom-call(s32[26]{0:T(128)} %pad_add_fusion.1.plan, s32[16]{0:T(128)} %select_reduce_fusion.2.order, bf16[8,512,512]{2,1,0:T(8,128)(2,1)} %chebyshev_outer.1.kernel_t, f32[4,128]{1,0:T(4,128)} %core.1, bf16[8,2,512,128]{3,2,1,0:T(8,128)(2,1)} %bitcast.13.refs_0_, bf16[8,2,512,128]{3,2,1,0:T(8,128)(2,1)} %bitcast.14.refs_1_), custom_call_target="tpu_custom_call" | custom-call | tf_op jit(solution)/shard_map/project/pallas_call | solution.py:596
  156.9 6.1 %all-to-all-start.3 = ((f32[8,24,128]{2,1,0:T(8,128)}), f32[8,24,128]{2,1,0:T(8,128)S(1)}, u32[]{:S(2)}, u32[]{:S(2)}) async-start(f32[8,24,128]{2,1,0:T(8,128)} %project.1), calls=%async_computation.3 | async-start | bytes 196608 | tf_op jit(solution)/shard_map/all_to_all | solution.py:801
  163.7 6.4 %all-to-all-done.3 = f32[8,24,128]{2,1,0:T(8,128)S(1)} async-done(((f32[8,24,128]{2,1,0:T(8,128)}), f32[8,24,128]{2,1,0:T(8,128)S(1)}, u32[]{:S(2)}, u32[]{:S(2)}) %all-to-all-start.3) | async-done | bytes 98336 | tf_op jit(solution)/shard_map/all_to_all | solution.py:801
  170.7 8.4 %update.1 = (f32[4,128]{1,0:T(4,128)}, bf16[4096,512]{1,0:T(8,128)(2,1)}) custom-call(s32[26]{0:T(128)} %pad_add_fusion.1.plan, s32[16]{0:T(128)} %select_reduce_fusion.2.order, s32[16]{0:T(128)} %reshape.285.tile_of, f32[192,128]{1,0:T(8,128)} %bitcast.25, f32[32,192]{1,0:T(8,128)} %convert_reduce_fusion.collect, bf16[8,2,512,128]{3,2,1,0:T(8,128)(2,1)} %bitcast.13.refs_0_, ...), custom_call_target="tpu_custom_call" | custom-call | tf_op jit(solution)/shard_map/update/pallas_call | solution.py:692
  (84 shorter events, 17.7 us)
Async XLA Ops:
  3.8 14.0 %collective-permute-start.3 = (bf16[1024,256]{1,0:T(8,128)(2,1)}, bf16[1024,256]{1,0:T(8,128)(2,1)}, u32[]{:S(2)}, u32[]{:S(2)}) collective-permute-start(bf16[1024,256]{1,0:T(8,128)(2,1)} %get-tuple-element.13.refs_0_.first), channel_id=1, source_target_pairs={{0,2},{1,3},{2,0},{3,1},{4,6},{5,7},{6,4},{7,5},{8,10},{9,11},{10,... | collective-permute-start | bytes 1572872 | tf_op jit(solution)/shard_map/ppermute | solution.py:187
  5.5 14.5 %collective-permute-start.5 = (bf16[1024,256]{1,0:T(8,128)(2,1)}, bf16[1024,256]{1,0:T(8,128)(2,1)}, u32[]{:S(2)}, u32[]{:S(2)}) collective-permute-start(bf16[1024,256]{1,0:T(8,128)(2,1)} %get-tuple-element.13.refs_0_.first), channel_id=1, source_target_pairs={{2,4},{3,5},{4,2},{5,3},{10,12},{11,13},{12,10},{13,11},{18,20},{1... | collective-permute-start | bytes 1572872 | tf_op jit(solution)/shard_map/ppermute | solution.py:187
  6.9 15.1 %collective-permute-start.2 = (bf16[1024,256]{1,0:T(8,128)(2,1)}, bf16[1024,256]{1,0:T(8,128)(2,1)S(1)}, u32[]{:S(2)}, u32[]{:S(2)}) collective-permute-start(bf16[1024,256]{1,0:T(8,128)(2,1)} %get-tuple-element.13.refs_0_.first), channel_id=1, source_target_pairs={{0,1},{1,0},{2,3},{3,2},{4,5},{5,4},{6,7},{7,6},{8,9},{9,8},{10,11... | collective-permute-start | bytes 1572872 | tf_op jit(solution)/shard_map/ppermute | solution.py:78
  11.2 32.2 %collective-permute-start.13 = (bf16[4,1,2,512,128]{4,3,2,1,0:T(8,128)(2,1)}, bf16[4,1,2,512,128]{4,3,2,1,0:T(8,128)(2,1)S(1)}, u32[]{:S(2)}, u32[]{:S(2)}) collective-permute-start(bf16[4,1,2,512,128]{4,3,2,1,0:T(8,128)(2,1)} %pack.3), channel_id=1, source_target_pairs={{0,1},{1,0},{2,3},{3,2},{4,5},{5,4},{6,7},{7,6},{8,9},{9,8},{10,11... | collective-permute-start | bytes 3145736 | tf_op jit(solution)/shard_map/ppermute | solution.py:78
  14.4 28.9 %collective-permute-start = (bf16[768,512]{1,0:T(8,128)(2,1)}, bf16[768,512]{1,0:T(8,128)(2,1)}, u32[]{:S(2)}, u32[]{:S(2)}) collective-permute-start(bf16[768,512]{1,0:T(8,128)(2,1)} %get-tuple-element.29), channel_id=1, source_target_pairs={{0,8},{8,16},{16,24},{1,9},{9,17},{17,25},{2,10},{10,18},{18,26},{... | collective-permute-start | bytes 2359304 | tf_op jit(solution)/shard_map/ppermute | solution.py:717
  17.9 25.5 %collective-permute-start.1 = (bf16[768,512]{1,0:T(8,128)(2,1)}, bf16[768,512]{1,0:T(8,128)(2,1)}, u32[]{:S(2)}, u32[]{:S(2)}) collective-permute-start(bf16[768,512]{1,0:T(8,128)(2,1)} %get-tuple-element.28), channel_id=1, source_target_pairs={{8,0},{16,8},{24,16},{9,1},{17,9},{25,17},{10,2},{18,10},{26,18},{... | collective-permute-start | bytes 2359304 | tf_op jit(solution)/shard_map/ppermute | solution.py:717
  20.0 23.3 %collective-permute-start.8 = (bf16[1024,256]{1,0:T(8,128)(2,1)}, bf16[1024,256]{1,0:T(8,128)(2,1)}, u32[]{:S(2)}, u32[]{:S(2)}) collective-permute-start(bf16[1024,256]{1,0:T(8,128)(2,1)} %collective-permute-done.3.refs_2_), channel_id=1, source_target_pairs={{2,4},{3,5},{4,2},{5,3},{10,12},{11,13},{12,10},{13,11},{18,20},{1... | collective-permute-start | bytes 1572872 | tf_op jit(solution)/shard_map/ppermute | solution.py:187
  22.0 9.4 %copy-start = (bf16[1024,256]{1,0:T(8,128)(2,1)}, bf16[1024,256]{1,0:T(8,128)(2,1)S(1)}, u32[]{:S(2)}) copy-start(bf16[1024,256]{1,0:T(8,128)(2,1)S(1)} %collective-permute-done.2.refs_1_.first.refs_3_) | copy-start | bytes 1572868
  22.0 21.4 %collective-permute-start.6 = (bf16[1024,256]{1,0:T(8,128)(2,1)}, bf16[1024,256]{1,0:T(8,128)(2,1)}, u32[]{:S(2)}, u32[]{:S(2)}) collective-permute-start(bf16[1024,256]{1,0:T(8,128)(2,1)} %collective-permute-done.5), channel_id=1, source_target_pairs={{2,0},{3,1},{4,6},{5,7},{10,8},{11,9},{12,14},{13,15},{18,16},{19,... | collective-permute-start | bytes 1572872 | tf_op jit(solution)/shard_map/ppermute | solution.py:187
  23.3 20.1 %all-to-all-start = ((s32[8,8,128]{2,1,0:T(8,128)}), s32[8,8,128]{2,1,0:T(8,128)S(1)}, u32[]{:S(2)}, u32[]{:S(2)}) async-start(s32[8,8,128]{2,1,0:T(8,128)} %get-tuple-element.12), calls=%async_computation | async-start | bytes 65536 | tf_op jit(solution)/shard_map/all_to_all | solution.py:785
  43.3 0.6 copy-start.11
  43.4 1.0 copy-start.1
  44.4 31.2 %copy-start.2 = (bf16[4,1,2,512,128]{4,3,2,1,0:T(8,128)(2,1)S(1)}, bf16[4,1,2,512,128]{4,3,2,1,0:T(8,128)(2,1)}, u32[]{:S(2)}) copy-start(bf16[4,1,2,512,128]{4,3,2,1,0:T(8,128)(2,1)} %copy-done.1) | copy-start | bytes 3145732
  44.4 52.4 %all-to-all-start.1 = ((bf16[4,2,2,512,128]{4,3,2,1,0:T(8,128)(2,1)}), bf16[4,2,2,512,128]{4,3,2,1,0:T(8,128)(2,1)}, u32[]{:S(2)}, u32[]{:S(2)}) async-start(bf16[4,2,2,512,128]{4,3,2,1,0:T(8,128)(2,1)} %after.2), calls=%async_computation.1 | async-start | bytes 4194304 | tf_op jit(solution)/shard_map/all_to_all | solution.py:160
  49.2 26.4 %collective-permute-start.14 = (bf16[4,1,2,512,128]{4,3,2,1,0:T(8,128)(2,1)}, bf16[4,1,2,512,128]{4,3,2,1,0:T(8,128)(2,1)}, u32[]{:S(2)}, u32[]{:S(2)}) collective-permute-start(bf16[4,1,2,512,128]{4,3,2,1,0:T(8,128)(2,1)} %get-tuple-element.21), channel_id=1, source_target_pairs={{0,1},{1,0},{2,3},{3,2},{4,5},{5,4},{6,7},{7,6},{8,9},{9,8},{10,11... | collective-permute-start | bytes 3145736 | tf_op jit(solution)/shard_map/ppermute | solution.py:78
  50.7 36.0 %collective-permute-start.4 = (bf16[1024,256]{1,0:T(8,128)(2,1)}, bf16[1024,256]{1,0:T(8,128)(2,1)S(1)}, u32[]{:S(2)}, u32[]{:S(2)}) collective-permute-start(bf16[1024,256]{1,0:T(8,128)(2,1)} %collective-permute-done.3.refs_2_), channel_id=1, source_target_pairs={{0,1},{1,0},{2,3},{3,2},{4,5},{5,4},{6,7},{7,6},{8,9},{9,8},{10,11... | collective-permute-start | bytes 1572872 | tf_op jit(solution)/shard_map/ppermute | solution.py:78
  52.5 25.8 %copy-start.4 = (bf16[1024,256]{1,0:T(8,128)(2,1)}, bf16[1024,256]{1,0:T(8,128)(2,1)S(1)}, u32[]{:S(2)}) copy-start(bf16[1024,256]{1,0:T(8,128)(2,1)S(1)} %add.195.refs_4_) | copy-start | bytes 1572868
  52.5 42.9 %collective-permute-start.7 = (bf16[1024,256]{1,0:T(8,128)(2,1)S(1)}, bf16[1024,256]{1,0:T(8,128)(2,1)S(1)}, u32[]{:S(2)}, u32[]{:S(2)}) collective-permute-start(bf16[1024,256]{1,0:T(8,128)(2,1)S(1)} %add.195.refs_4_), channel_id=1, source_target_pairs={{0,1},{1,0},{2,3},{3,2},{4,5},{5,4},{6,7},{7,6},{8,9},{9,8},{10,11... | collective-permute-start | bytes 1572872 | tf_op jit(solution)/shard_map/ppermute | solution.py:78
  54.1 32.6 %collective-permute-start.9 = (bf16[1024,256]{1,0:T(8,128)(2,1)}, bf16[1024,256]{1,0:T(8,128)(2,1)}, u32[]{:S(2)}, u32[]{:S(2)}) collective-permute-start(bf16[1024,256]{1,0:T(8,128)(2,1)} %collective-permute-done.8.refs_1_), channel_id=1, source_target_pairs={{2,0},{3,1},{4,6},{5,7},{10,8},{11,9},{12,14},{13,15},{18,16},{19,... | collective-permute-start | bytes 1572872 | tf_op jit(solution)/shard_map/ppermute | solution.py:187
  86.7 10.1 %copy-start.3 = (bf16[1024,256]{1,0:T(8,128)(2,1)}, bf16[1024,256]{1,0:T(8,128)(2,1)S(1)}, u32[]{:S(2)}) copy-start(bf16[1024,256]{1,0:T(8,128)(2,1)S(1)} %collective-permute-done.4.refs_3_.refs_4_) | copy-start | bytes 1572868
  95.4 1.4 copy-start.5
  96.8 55.0 %all-to-all-start.2 = ((bf16[4,2,2,512,128]{4,3,2,1,0:T(8,128)(2,1)}), bf16[4,2,2,512,128]{4,3,2,1,0:T(8,128)(2,1)}, u32[]{:S(2)}, u32[]{:S(2)}) async-start(bf16[4,2,2,512,128]{4,3,2,1,0:T(8,128)(2,1)} %after.3), calls=%async_computation.2 | async-start | bytes 4194304 | tf_op jit(solution)/shard_map/all_to_all | solution.py:160
  104.6 13.5 %copy-start.6 = (bf16[1024,256]{1,0:T(8,128)(2,1)}, bf16[1024,256]{1,0:T(8,128)(2,1)S(1)}, u32[]{:S(2)}) copy-start(bf16[1024,256]{1,0:T(8,128)(2,1)S(1)} %add.196.refs_6_) | copy-start | bytes 1572868
  104.6 13.4 %collective-permute-start.10 = (bf16[1024,256]{1,0:T(8,128)(2,1)S(1)}, bf16[1024,256]{1,0:T(8,128)(2,1)S(1)}, u32[]{:S(2)}, u32[]{:S(2)}) collective-permute-start(bf16[1024,256]{1,0:T(8,128)(2,1)S(1)} %add.196.refs_6_), channel_id=1, source_target_pairs={{0,1},{1,0},{2,3},{3,2},{4,5},{5,4},{6,7},{7,6},{8,9},{9,8},{10,11... | collective-permute-start | bytes 1572872 | tf_op jit(solution)/shard_map/ppermute | solution.py:78
  118.1 0.8 copy-start.7
  121.8 22.0 %collective-permute-start.11 = (bf16[2,512,256]{2,1,0:T(8,128)(2,1)}, bf16[2,512,256]{2,1,0:T(8,128)(2,1)S(1)}, u32[]{:S(2)}, u32[]{:S(2)}) collective-permute-start(bf16[2,512,256]{2,1,0:T(8,128)(2,1)} %get-tuple-element.15.h_last), channel_id=1, source_target_pairs={{0,8},{8,16},{16,24},{1,9},{9,17},{17,25},{2,10},{10,18},{18,26},{... | collective-permute-start | bytes 1572872 | tf_op jit(solution)/shard_map/ppermute | solution.py:717
  123.7 20.0 %collective-permute-start.12 = (bf16[2,512,256]{2,1,0:T(8,128)(2,1)}, bf16[2,512,256]{2,1,0:T(8,128)(2,1)S(1)}, u32[]{:S(2)}, u32[]{:S(2)}) collective-permute-start(bf16[2,512,256]{2,1,0:T(8,128)(2,1)} %get-tuple-element.16.h_first), channel_id=1, source_target_pairs={{8,0},{16,8},{24,16},{9,1},{17,9},{25,17},{10,2},{18,10},{26,18},{... | collective-permute-start | bytes 1572872 | tf_op jit(solution)/shard_map/ppermute | solution.py:717
  143.8 0.8 copy-start.8
  143.8 1.0 copy-start.9
  156.9 13.2 %all-to-all-start.3 = ((f32[8,24,128]{2,1,0:T(8,128)}), f32[8,24,128]{2,1,0:T(8,128)S(1)}, u32[]{:S(2)}, u32[]{:S(2)}) async-start(f32[8,24,128]{2,1,0:T(8,128)} %project.1), calls=%async_computation.3 | async-start | bytes 196608 | tf_op jit(solution)/shard_map/all_to_all | solution.py:801
  170.1 0.6 copy-start.10

commit v8 on v6

--- a/solution.py
+++ b/solution.py
@@ -15,7 +15,7 @@
 CAP = 2
 P_SIZE = 128
 MIB = 1 << 20
-LISTS = 8
+LISTS = 16
 
 exchange_factor = (3.0 / math.pi) ** (1.0 / 3.0)
 HBM = pl.BlockSpec(memory_space=pltpu.HBM)
@@ -30,20 +30,20 @@
     return (me + j) % count
 
 
-def piece_kernel(peers, named, counts, pattern, ham, piece, lists, blocks, sems):
-    load = pltpu.make_async_copy(ham, blocks, sems.at[0])
+def piece_kernel(peers, named, counts, pattern, ham, piece, blocks, sems):
+    rows = ham.shape[0]
+    load = pltpu.make_async_copy(ham, blocks.at[pl.ds(0, rows)], sems.at[0])
     load.start()
-    lane = lax.broadcasted_iota(jnp.int32, (LISTS, P_SIZE), 1)
-    row = jnp.zeros((LISTS, P_SIZE), jnp.int32)
+    lane = lax.broadcasted_iota(jnp.int32, (LISTS, W), 1)
+    lists = jnp.zeros((LISTS, W), jnp.int32)
     at = 0
     for ref in (peers, named, counts):
         for i in range(ref.shape[0]):
-            row = jnp.where(lane == at, ref[i], row)
+            lists = jnp.where(lane == at, ref[i], lists)
             at += 1
-    for c in range(lists.shape[0]):
-        lists[c] = row
+    blocks[rows:] = lists.astype(jnp.float32).astype(jnp.bfloat16)
     load.wait()
-    for i in range(ham.shape[0] // (2 * W)):
+    for i in range(rows // (2 * W)):
         coupling = slice((2 * i + 1) * W, (2 * i + 2) * W)
         blocks[coupling] = blocks[coupling] * pattern[i].astype(jnp.bfloat16)
     store = pltpu.make_async_copy(blocks, piece, sems.at[1])
@@ -51,16 +51,14 @@
     store.wait()
 
 
-def own_piece(peers, named, counts, pattern, ham, col_count):
+def own_piece(peers, named, counts, pattern, ham):
+    piece = (ham.shape[0] + LISTS, W)
     return pl.pallas_call(
         piece_kernel,
-        out_shape=(
-            jax.ShapeDtypeStruct(ham.shape, ham.dtype),
-            jax.ShapeDtypeStruct((col_count, LISTS, P_SIZE), jnp.int32),
-        ),
+        out_shape=jax.ShapeDtypeStruct(piece, ham.dtype),
         in_specs=[SMEM] * 4 + [HBM],
-        out_specs=(HBM, VMEM),
-        scratch_shapes=[pltpu.VMEM(ham.shape, ham.dtype), pltpu.SemaphoreType.DMA((2,))],
+        out_specs=HBM,
+        scratch_shapes=[pltpu.VMEM(piece, ham.dtype), pltpu.SemaphoreType.DMA((2,))],
         compiler_params=pltpu.CompilerParams(vmem_limit_bytes=62 * MIB),
         name="own_piece",
     )(peers, named, counts, pattern, ham)
@@ -150,7 +148,7 @@
     )(block, *others)
 
 
-def exchange(me, peers, basis, own, awaited, handed):
+def exchange(me, peers, basis, own, early, awaited, handed):
     count = lax.axis_size("col")
     outer, inner = lines_of(count)
     groups = [[line * inner + place for line in range(outer)] for place in range(inner)]
@@ -166,7 +164,7 @@
     ahead = [[(t, 0)] for t in range(1, inner)]
     rest = [[(t, k)] for k in range(1, CAP) for t in range(1, inner)]
     sent = pack(me, peers, basis, own, count, ahead) if ahead else []
-    to_lines, *later = pack(me, peers, basis, sent[0] if ahead else own, count, [here] + rest)
+    to_lines, *later = pack(me, peers, basis, early, count, [here] + rest)
     swapped = {
         group[0]: swap_along(block, group[0][0]) for block, group in zip(sent + later, ahead + rest)
     }
@@ -219,8 +217,9 @@
 
 
 def edge_kernel(col_count, depth, owners, *refs):
-    pieces, (first, last, sems) = refs[:-3], refs[-3:]
-    held = pieces[0].shape[0] // (2 * W)
+    pieces, (first, last, lists, sems, list_sems) = refs[:-5], refs[-5:]
+    rows = pieces[0].shape[0] - LISTS
+    held = rows // (2 * W)
     total = col_count * held
 
     def each(act):
@@ -234,6 +233,12 @@
                     def _():
                         act(copy)
 
+            @pl.when(owners[i] >= 0)
+            def _():
+                act(pltpu.make_async_copy(
+                    piece.at[pl.ds(rows, LISTS)], lists.at[owners[i]], list_sems.at[i]
+                ))
+
     each(lambda copy: copy.start())
     each(lambda copy: copy.wait())
 
@@ -242,11 +247,13 @@
     shape = jax.ShapeDtypeStruct((depth, 2 * W, W), pieces[0].dtype)
     return pl.pallas_call(
         functools.partial(edge_kernel, col_count, depth),
-        out_shape=(shape, shape),
+        out_shape=(shape, shape, jax.ShapeDtypeStruct((col_count, LISTS, W), pieces[0].dtype)),
         in_specs=[SMEM] + [HBM] * len(pieces),
-        out_specs=(VMEM, VMEM),
-        scratch_shapes=[pltpu.SemaphoreType.DMA((2, depth))],
-        compiler_params=pltpu.CompilerParams(vmem_limit_bytes=62 * MIB),
+        out_specs=(VMEM, VMEM, VMEM),
+        scratch_shapes=[
+            pltpu.SemaphoreType.DMA((2, depth)),
+            pltpu.SemaphoreType.DMA((len(pieces),)),
+        ],
         name="edge_blocks",
     )(owners, *pieces)
 
@@ -276,7 +283,7 @@
         *pieces, out, edge_1, edge_2, edge_total,
         vext, hraw, hcat, cheb_1, cheb_2, total, kern, sems, psems, osems, esems,
     ) = refs
-    held = pieces[0].shape[0] // (2 * W)
+    held = (pieces[0].shape[0] - LISTS) // (2 * W)
     v_copies = [
         pltpu.make_async_copy(v_low.at[rows_of(DEG - 1)], vext.at[rows_of(0)], sems.at[0]),
         pltpu.make_async_copy(v_mid, vext.at[rows_of(1, blocks)], sems.at[1]),
@@ -362,7 +369,7 @@
     cols = v_mid.shape[1]
     flops = 2 * W * 3 * W * cols * (3 * blocks - 6)
     result = (blocks * W // KB, cols, KB)
-    held = pieces[0].shape[0] // (2 * W)
+    held = (pieces[0].shape[0] - LISTS) // (2 * W)
     return pl.pallas_call(
         functools.partial(inner_kernel, blocks),
         out_shape=(
@@ -722,7 +729,7 @@
 def make_plan(lists, me, entries, tiles, col_count, blocks):
     slots = col_count * CAP
     sent = sent_rows(slots, tiles)
-    lists = lists[:, : 2 * entries + tiles]
+    lists = lists[:, : 2 * entries + tiles].astype(jnp.int32)
     peers, named, counts = lists[:, :entries], lists[:, entries : 2 * entries], lists[:, 2 * entries :]
     index = jnp.arange(entries, dtype=jnp.int32)
     home = jnp.arange(col_count, dtype=jnp.int32)[:, None]
@@ -781,16 +788,14 @@
     peers = tile_peer[:, 0]
     me = lax.axis_index("col").astype(jnp.int32)
 
-    own, lists = own_piece(
-        peers, tile_block, tile_count, band_pattern, hamiltonian.reshape(-1, W), col_count
-    )
-    lists = lax.all_to_all(lists, "col", split_axis=0, concat_axis=0, tiled=True)
+    own = own_piece(peers, tile_block, tile_count, band_pattern, hamiltonian.reshape(-1, W))
     pieces, owners, awaited, handed = gather_pieces(own)
     v_low = shift(start_columns[-DEG * W :], "row", 1)
     v_high = shift(start_columns[: DEG * W], "row", -1)
-    parts = exchange(me[None], peers, basis_values, own, awaited + [v_low, v_high, lists], handed)
-
-    first, last = edge_blocks(owners, pieces, col_count, DEG - 1)
+    parts = exchange(me[None], peers, basis_values, own, pieces[min(1, len(pieces) - 1)],
+        awaited + [v_low, v_high], handed)
+
+    first, last, lists = edge_blocks(owners, pieces, col_count, DEG - 1)
     h_low = shift(last, "row", 1)
     h_high = shift(first, "row", -1)
     inner = chebyshev_inner(coefficients, owners, v_low, start_columns, v_high, pieces)

time: 183 us -> 177 us (0.967)
  starting transfers between devices: 45.9 us -> 41.8 us
  Pallas kernels: 48.6 us -> 46.3 us
    ppermute x6, waiting for transfers between devices: 55.2 us -> 18.2 us  [swap_along(): return lax.ppermute(block, 'col', pairs)]
    ppermute x5, waiting for transfers between devices: 0.01 us -> 29.6 us  [move(): return lax.ppermute(block, 'col', pairs)]
    all_to_all x2, waiting for transfers between devices: 0.01 us -> 10.6 us  [between_lines(): lax.all_to_all(after(block, *others), 'col', split_axis=0, concat_axis=0,...]
    all_to_all x1 -> x0, starting transfers between devices: 7.57 us -> none  [shards(): lax.all_to_all(lists, 'col', split_axis=0, concat_axis=0, tiled=True)]
    all_to_all x1 -> x0, waiting for transfers between devices: 5.37 us -> none  [shards(): lax.all_to_all(lists, 'col', split_axis=0, concat_axis=0, tiled=True)]
    all_to_all x2, starting transfers between devices: 9.29 us -> 14.6 us  [between_lines(): lax.all_to_all(after(block, *others), 'col', split_axis=0, concat_axis=0,...]
    ppermute x4, waiting for transfers between devices: 0.01 us -> 3.42 us  [shift(): return lax.ppermute(block, axis, pairs)]
    unnamed x25 -> x20, local copies, waits for them, and re-layouts: 3.67 us -> 3.19 us
  transfers between devices with their start and end apart: 19 -> 18, of which waited for: 7 -> 9; matrix products, arithmetic and copies ran while one was open for 8% -> 8% of each run, Pallas kernels for 18% -> 19%
where the time goes in v8:
time: 177 us; the launch traced here: 175 us
  waiting for transfers between devices  68.1 us (38%)
  Pallas kernels  46.3 us (26%)
  starting transfers between devices  41.8 us (24%)
  other arithmetic  9.33 us (5%)
  local copies, waits for them, and re-layouts  8.7 us (5%)
    ppermute x5, waiting for transfers between devices, move(): return lax.ppermute(block, 'col', pairs)  29.6 us
    ppermute x6, waiting for transfers between devices, swap_along(): return lax.ppermute(block, 'col', pairs)  18.2 us
    pallas_call x1, Pallas kernels, chebyshev_inner(): pl.pallas_call(functools.partial(inner_kernel, blocks), out_shape=(jax.Sh...  16.4 us
    all_to_all x2, starting transfers between devices, between_lines(): lax.all_to_all(after(block, *others), 'col', split_axis=0, concat_axis=0,...  14.6 us
    all_to_all x2, waiting for transfers between devices, between_lines(): lax.all_to_all(after(block, *others), 'col', split_axis=0, concat_axis=0,...  10.6 us
    ppermute x4, starting transfers between devices, shift(): return lax.ppermute(block, axis, pairs)  9.37 us
    ppermute x6, starting transfers between devices, swap_along(): return lax.ppermute(block, 'col', pairs)  7.35 us
    ppermute x5, starting transfers between devices, move(): return lax.ppermute(block, 'col', pairs)  7.08 us
  transfers between devices with their start and end apart: 18, of which 9 were waited for; matrix products, arithmetic and copies ran while one was open for 8% of the time, Pallas kernels for 19%

profile of v8, /device:TPU:2, one launch (start us, length us, event | category | flops | bytes accessed | tf_op | source)
XLA Modules:
  0.0 175.1 jit_solution(5954384506986105033)
XLA Ops:
  0.6 2.6 %own_piece.1.refs_0_.first = bf16[1040,256]{1,0:T(8,128)(2,1)} custom-call(s32[16]{0:T(128)} %bitcast.32, s32[16]{0:T(128)} %named.1, s32[4]{0:T(128)} %counts.1, s32[2]{0:T(128)} %pattern.1, bf16[1024,256]{1,0:T(8,128)(2,1)} %bitcast.26), custom_call_target="tpu_custom_call" | custom-call | tf_op jit(solution)/shard_map/own_piece/pallas_call | solution.py:56
  3.2 1.6 collective-permute-start
  4.8 1.6 collective-permute-start.1
  6.4 1.5 collective-permute-start.3
  7.8 2.7 %pack.3 = bf16[4,1,2,512,128]{4,3,2,1,0:T(8,128)(2,1)} custom-call(s32[1]{0:T(128)} %bitcast.11.me, s32[16]{0:T(128)} %bitcast.33, bf16[16,2,512,128]{3,2,1,0:T(8,128)(2,1)} %basis.3, bf16[1040,256]{1,0:T(8,128)(2,1)} %own_piece.1.refs_0_.first), custom_call_target="tpu_custom_call" | custom-call | tf_op jit(solution)/shard_map/pack/pallas_call | solution.py:119
  11.2 2.6 %fusion.12 = (bf16[768,512]{1,0:T(8,128)(2,1)}, bf16[768,512]{1,0:T(8,128)(2,1)}) fusion(bf16[4096,512]{1,0:T(8,128)(2,1)} %v_mid.3), kind=kLoop, calls=%fused_computation.55 | loop fusion | bytes 3145728 | tf_op jit(solution)/shard_map/slice | solution.py:794
  13.8 1.9 %collective-permute-start.9 = (bf16[768,512]{1,0:T(8,128)(2,1)}, bf16[768,512]{1,0:T(8,128)(2,1)}, u32[]{:S(2)}, u32[]{:S(2)}) collective-permute-start(bf16[768,512]{1,0:T(8,128)(2,1)} %get-tuple-element.27), channel_id=1, source_target_pairs={{0,8},{8,16},{16,24},{1,9},{9,17},{17,25},{2,10},{10,18},{18,26},{... | collective-permute-start | bytes 2359304 | tf_op jit(solution)/shard_map/ppermute | solution.py:726
  15.7 2.8 %collective-permute-done.refs_1_.first.refs_3_ = bf16[1040,256]{1,0:T(8,128)(2,1)S(1)} collective-permute-done((bf16[1040,256]{1,0:T(8,128)(2,1)}, bf16[1040,256]{1,0:T(8,128)(2,1)S(1)}, u32[]{:S(2)}, u32[]{:S(2)}) %collective-permute-start) | collective-permute-done | bytes 532512 | tf_op jit(solution)/shard_map/ppermute | solution.py:76
  18.5 1.9 %collective-permute-start.10 = (bf16[768,512]{1,0:T(8,128)(2,1)}, bf16[768,512]{1,0:T(8,128)(2,1)}, u32[]{:S(2)}, u32[]{:S(2)}) collective-permute-start(bf16[768,512]{1,0:T(8,128)(2,1)} %get-tuple-element.26), channel_id=1, source_target_pairs={{8,0},{16,8},{24,16},{9,1},{17,9},{25,17},{10,2},{18,10},{26,18},{... | collective-permute-start | bytes 2359304 | tf_op jit(solution)/shard_map/ppermute | solution.py:726
  21.7 1.5 collective-permute-start.6
  23.2 3.6 %pack.2 = (bf16[4,2,2,512,128]{4,3,2,1,0:T(8,128)(2,1)}, bf16[4,1,2,512,128]{4,3,2,1,0:T(8,128)(2,1)}) custom-call(s32[1]{0:T(128)} %bitcast.11.me, s32[16]{0:T(128)} %bitcast.34, bf16[16,2,512,128]{3,2,1,0:T(8,128)(2,1)} %basis.3, bf16[1040,256]{1,0:T(8,128)(2,1)} %copy-done), custom_call_target="tpu_custom_call" | custom-call | tf_op jit(solution)/shard_map/pack/pallas_call | solution.py:119
  27.4 2.8 %collective-permute-done.10.v_high.refs_4_ = bf16[768,512]{1,0:T(8,128)(2,1)} collective-permute-done((bf16[768,512]{1,0:T(8,128)(2,1)}, bf16[768,512]{1,0:T(8,128)(2,1)}, u32[]{:S(2)}, u32[]{:S(2)}) %collective-permute-start.10) | collective-permute-done | bytes 786464 | tf_op jit(solution)/shard_map/ppermute | solution.py:726
  30.2 9.6 %collective-permute-done.13.refs_5_ = bf16[4,1,2,512,128]{4,3,2,1,0:T(8,128)(2,1)S(1)} collective-permute-done((bf16[4,1,2,512,128]{4,3,2,1,0:T(8,128)(2,1)}, bf16[4,1,2,512,128]{4,3,2,1,0:T(8,128)(2,1)S(1)}, u32[]{:S(2)}, u32[]{:S(2)}) %collective-permute-start.13) | collective-permute-done | bytes 1048608 | tf_op jit(solution)/shard_map/ppermute | solution.py:76
  40.8 4.9 %all-to-all-start = ((bf16[4,2,2,512,128]{4,3,2,1,0:T(8,128)(2,1)}), bf16[4,2,2,512,128]{4,3,2,1,0:T(8,128)(2,1)}, u32[]{:S(2)}, u32[]{:S(2)}) async-start(bf16[4,2,2,512,128]{4,3,2,1,0:T(8,128)(2,1)} %after.2), calls=%async_computation | async-start | bytes 4194304 | tf_op jit(solution)/shard_map/all_to_all | solution.py:158
  45.7 1.5 collective-permute-start.14
  50.4 1.6 collective-permute-start.5
  52.9 29.6 %collective-permute-done.7.refs_2_ = bf16[1040,256]{1,0:T(8,128)(2,1)} collective-permute-done((bf16[1040,256]{1,0:T(8,128)(2,1)}, bf16[1040,256]{1,0:T(8,128)(2,1)}, u32[]{:S(2)}, u32[]{:S(2)}) %collective-permute-start.7) | collective-permute-done | bytes 532512 | tf_op jit(solution)/shard_map/ppermute | solution.py:185
  82.5 2.1 %add.190.refs_6_ = bf16[1040,256]{1,0:T(8,128)(2,1)} add(bf16[1040,256]{1,0:T(8,128)(2,1)} %collective-permute-done.6.refs_1_, bf16[1040,256]{1,0:T(8,128)(2,1)} %collective-permute-done.7.refs_2_) | non-fusion elementwise | flops 266240 | bytes 1597440 | tf_op jit(solution)/shard_map/add | solution.py:199
  84.6 1.5 collective-permute-start.8
  86.2 2.8 %pad_maximum_fusion.refs_0_ = bf16[4,2,2,512,128]{4,3,2,1,0:T(8,128)(2,1)} fusion(bf16[4,1,2,512,128]{4,3,2,1,0:T(8,128)(2,1)} %collective-permute-done.14, bf16[4,1,2,512,128]{4,3,2,1,0:T(8,128)(2,1)S(1)} %copy-done.2), kind=kLoop, calls=%fused_computation | loop fusion | flops 1048576 | bytes 4194304 | tf_op jit(solution)/shard_map/concatenate | solution.py:157
  88.9 5.8 %collective-permute-done.5.refs_5_ = bf16[1040,256]{1,0:T(8,128)(2,1)S(1)} collective-permute-done((bf16[1040,256]{1,0:T(8,128)(2,1)S(1)}, bf16[1040,256]{1,0:T(8,128)(2,1)S(1)}, u32[]{:S(2)}, u32[]{:S(2)}) %collective-permute-start.5) | collective-permute-done | bytes 532512 | tf_op jit(solution)/shard_map/ppermute | solution.py:76
  95.6 9.8 %all-to-all-start.1 = ((bf16[4,2,2,512,128]{4,3,2,1,0:T(8,128)(2,1)}), bf16[4,2,2,512,128]{4,3,2,1,0:T(8,128)(2,1)}, u32[]{:S(2)}, u32[]{:S(2)}) async-start(bf16[4,2,2,512,128]{4,3,2,1,0:T(8,128)(2,1)} %after.3), calls=%async_computation.1 | async-start | bytes 4194304 | tf_op jit(solution)/shard_map/all_to_all | solution.py:158
  105.4 3.1 %edge_blocks.1 = (bf16[2,512,256]{2,1,0:T(8,128)(2,1)}, bf16[2,512,256]{2,1,0:T(8,128)(2,1)}, bf16[8,16,256]{2,1,0:T(8,128)(2,1)}) custom-call(s32[8]{0:T(128)} %stack.35.owners, bf16[1040,256]{1,0:T(8,128)(2,1)} %own_piece.1.refs_0_.first, bf16[1040,256]{1,0:T(8,128)(2,1)} %copy-done, bf16[1040,256]{1,0:T(8,128)(2,1)} %collective-permute-done.1.refs_2_, ...), custom_call_target="tpu_custom_call" | custom-call | tf_op jit(solution)/shard_map/edge_blocks/pallas_call | solution.py:248
  111.0 1.9 %collective-permute-start.11 = (bf16[2,512,256]{2,1,0:T(8,128)(2,1)}, bf16[2,512,256]{2,1,0:T(8,128)(2,1)S(1)}, u32[]{:S(2)}, u32[]{:S(2)}) collective-permute-start(bf16[2,512,256]{2,1,0:T(8,128)(2,1)} %get-tuple-element.13.h_last), channel_id=1, source_target_pairs={{0,8},{8,16},{16,24},{1,9},{9,17},{17,25},{2,10},{10,18},{18,26},{... | collective-permute-start | bytes 1572872 | tf_op jit(solution)/shard_map/ppermute | solution.py:726
  113.0 3.6 %collective-permute-start.12 = (bf16[2,512,256]{2,1,0:T(8,128)(2,1)}, bf16[2,512,256]{2,1,0:T(8,128)(2,1)S(1)}, u32[]{:S(2)}, u32[]{:S(2)}) collective-permute-start(bf16[2,512,256]{2,1,0:T(8,128)(2,1)} %get-tuple-element.14.h_first), channel_id=1, source_target_pairs={{8,0},{16,8},{24,16},{9,1},{17,9},{25,17},{10,2},{18,10},{26,18},{... | collective-permute-start | bytes 1572872 | tf_op jit(solution)/shard_map/ppermute | solution.py:726
  118.4 16.4 %chebyshev_inner.1 = (bf16[8,512,512]{2,1,0:T(8,128)(2,1)}, bf16[1024,512]{1,0:T(8,128)(2,1)}, bf16[1024,512]{1,0:T(8,128)(2,1)}, f32[1024,512]{1,0:T(8,128)}) custom-call(f32[4]{0:T(128)} %coef.3, s32[8]{0:T(128)} %stack.35.owners, bf16[768,512]{1,0:T(8,128)(2,1)} %collective-permute-done.9.v_low.refs_3_, bf16[4096,512]{1,0:T(8,128)(2,1)} %v_mid.3, ...), custom_call_target="tpu_custom_call" | custom-call | flops 8455716864 | bytes 16777216 | tf_op jit(solution)/shard_map/chebyshev_inner/pallas_call | solution.py:373
  135.8 7.1 %chebyshev_outer.1.kernel_t = bf16[8,512,512]{2,1,0:T(8,128)(2,1)} custom-call(f32[4]{0:T(128)} %coef.3, bf16[8,512,512]{2,1,0:T(8,128)(2,1)} %get-tuple-element.12.kernel_in, bf16[768,512]{1,0:T(8,128)(2,1)} %collective-permute-done.9.v_low.refs_3_, bf16[4096,512]{1,0:T(8,128)(2,1)} %v_mid.3, ...), custom_call_target="tpu_custom_call", output_to_operand_aliasing={{}: (1, {})} | custom-call | tf_op jit(solution)/shard_map/chebyshev_outer/pallas_call | solution.py:491
  142.8 10.3 %all-to-all-done.1 = bf16[4,2,2,512,128]{4,3,2,1,0:T(8,128)(2,1)} async-done(((bf16[4,2,2,512,128]{4,3,2,1,0:T(8,128)(2,1)}), bf16[4,2,2,512,128]{4,3,2,1,0:T(8,128)(2,1)}, u32[]{:S(2)}, u32[]{:S(2)}) %all-to-all-start.1) | async-done | bytes 2097184 | tf_op jit(solution)/shard_map/all_to_all | solution.py:158
  153.1 4.7 %project.1 = f32[8,24,128]{2,1,0:T(8,128)} custom-call(s32[26]{0:T(128)} %pad_add_fusion.1.plan, s32[16]{0:T(128)} %select_reduce_fusion.2.order, bf16[8,512,512]{2,1,0:T(8,128)(2,1)} %chebyshev_outer.1.kernel_t, f32[4,128]{1,0:T(4,128)} %core.1, bf16[8,2,512,128]{3,2,1,0:T(8,128)(2,1)} %bitcast.12.refs_0_, bf16[8,2,512,128]{3,2,1,0:T(8,128)(2,1)} %bitcast.13.refs_1_), custom_call_target="tpu_custom_call" | custom-call | tf_op jit(solution)/shard_map/project/pallas_call | solution.py:603
  157.8 3.4 %all-to-all-start.2 = ((f32[8,24,128]{2,1,0:T(8,128)}), f32[8,24,128]{2,1,0:T(8,128)S(1)}, u32[]{:S(2)}, u32[]{:S(2)}) async-start(f32[8,24,128]{2,1,0:T(8,128)} %project.1), calls=%async_computation.2 | async-start | bytes 196608 | tf_op jit(solution)/shard_map/all_to_all | solution.py:807
  161.9 6.3 %all-to-all-done.2 = f32[8,24,128]{2,1,0:T(8,128)S(1)} async-done(((f32[8,24,128]{2,1,0:T(8,128)}), f32[8,24,128]{2,1,0:T(8,128)S(1)}, u32[]{:S(2)}, u32[]{:S(2)}) %all-to-all-start.2) | async-done | bytes 98336 | tf_op jit(solution)/shard_map/all_to_all | solution.py:807
  168.9 6.3 %update.1 = (f32[4,128]{1,0:T(4,128)}, bf16[4096,512]{1,0:T(8,128)(2,1)}) custom-call(s32[26]{0:T(128)} %pad_add_fusion.1.plan, s32[16]{0:T(128)} %select_reduce_fusion.2.order, s32[16]{0:T(128)} %reshape.285.tile_of, f32[192,128]{1,0:T(8,128)} %bitcast.27, f32[32,192]{1,0:T(8,128)} %convert_reduce_fusion.collect, bf16[8,2,512,128]{3,2,1,0:T(8,128)(2,1)} %bitcast.12.refs_0_, ...), custom_call_target="tpu_custom_call" | custom-call | tf_op jit(solution)/shard_map/update/pallas_call | solution.py:701
  (78 shorter events, 15.1 us)
Async XLA Ops:
  3.2 15.3 %collective-permute-start = (bf16[1040,256]{1,0:T(8,128)(2,1)}, bf16[1040,256]{1,0:T(8,128)(2,1)S(1)}, u32[]{:S(2)}, u32[]{:S(2)}) collective-permute-start(bf16[1040,256]{1,0:T(8,128)(2,1)} %own_piece.1.refs_0_.first), channel_id=1, source_target_pairs={{0,1},{1,0},{2,3},{3,2},{4,5},{5,4},{6,7},{7,6},{8,9},{9,8},{10,11... | collective-permute-start | bytes 1597448 | tf_op jit(solution)/shard_map/ppermute | solution.py:76
  4.8 16.9 %collective-permute-start.1 = (bf16[1040,256]{1,0:T(8,128)(2,1)}, bf16[1040,256]{1,0:T(8,128)(2,1)}, u32[]{:S(2)}, u32[]{:S(2)}) collective-permute-start(bf16[1040,256]{1,0:T(8,128)(2,1)} %own_piece.1.refs_0_.first), channel_id=1, source_target_pairs={{0,2},{1,3},{2,0},{3,1},{4,6},{5,7},{6,4},{7,5},{8,10},{9,11},{10,... | collective-permute-start | bytes 1597448 | tf_op jit(solution)/shard_map/ppermute | solution.py:185
  6.4 14.0 %collective-permute-start.3 = (bf16[1040,256]{1,0:T(8,128)(2,1)}, bf16[1040,256]{1,0:T(8,128)(2,1)}, u32[]{:S(2)}, u32[]{:S(2)}) collective-permute-start(bf16[1040,256]{1,0:T(8,128)(2,1)} %own_piece.1.refs_0_.first), channel_id=1, source_target_pairs={{2,4},{3,5},{4,2},{5,3},{10,12},{11,13},{12,10},{13,11},{18,20},{1... | collective-permute-start | bytes 1597448 | tf_op jit(solution)/shard_map/ppermute | solution.py:185
  10.6 29.2 %collective-permute-start.13 = (bf16[4,1,2,512,128]{4,3,2,1,0:T(8,128)(2,1)}, bf16[4,1,2,512,128]{4,3,2,1,0:T(8,128)(2,1)S(1)}, u32[]{:S(2)}, u32[]{:S(2)}) collective-permute-start(bf16[4,1,2,512,128]{4,3,2,1,0:T(8,128)(2,1)} %pack.3), channel_id=1, source_target_pairs={{0,1},{1,0},{2,3},{3,2},{4,5},{5,4},{6,7},{7,6},{8,9},{9,8},{10,11... | collective-permute-start | bytes 3145736 | tf_op jit(solution)/shard_map/ppermute | solution.py:76
  13.8 13.6 %collective-permute-start.9 = (bf16[768,512]{1,0:T(8,128)(2,1)}, bf16[768,512]{1,0:T(8,128)(2,1)}, u32[]{:S(2)}, u32[]{:S(2)}) collective-permute-start(bf16[768,512]{1,0:T(8,128)(2,1)} %get-tuple-element.27), channel_id=1, source_target_pairs={{0,8},{8,16},{16,24},{1,9},{9,17},{17,25},{2,10},{10,18},{18,26},{... | collective-permute-start | bytes 2359304 | tf_op jit(solution)/shard_map/ppermute | solution.py:726
  18.5 4.7 %copy-start = (bf16[1040,256]{1,0:T(8,128)(2,1)}, bf16[1040,256]{1,0:T(8,128)(2,1)S(1)}, u32[]{:S(2)}) copy-start(bf16[1040,256]{1,0:T(8,128)(2,1)S(1)} %collective-permute-done.refs_1_.first.refs_3_) | copy-start | bytes 1597444
  18.5 11.7 %collective-permute-start.10 = (bf16[768,512]{1,0:T(8,128)(2,1)}, bf16[768,512]{1,0:T(8,128)(2,1)}, u32[]{:S(2)}, u32[]{:S(2)}) collective-permute-start(bf16[768,512]{1,0:T(8,128)(2,1)} %get-tuple-element.26), channel_id=1, source_target_pairs={{8,0},{16,8},{24,16},{9,1},{17,9},{25,17},{10,2},{18,10},{26,18},{... | collective-permute-start | bytes 2359304 | tf_op jit(solution)/shard_map/ppermute | solution.py:726
  20.4 19.4 %collective-permute-start.4 = (bf16[1040,256]{1,0:T(8,128)(2,1)}, bf16[1040,256]{1,0:T(8,128)(2,1)}, u32[]{:S(2)}, u32[]{:S(2)}) collective-permute-start(bf16[1040,256]{1,0:T(8,128)(2,1)} %collective-permute-done.3), channel_id=1, source_target_pairs={{2,0},{3,1},{4,6},{5,7},{10,8},{11,9},{12,14},{13,15},{18,16},{19,... | collective-permute-start | bytes 1597448 | tf_op jit(solution)/shard_map/ppermute | solution.py:185
  21.7 18.1 %collective-permute-start.6 = (bf16[1040,256]{1,0:T(8,128)(2,1)}, bf16[1040,256]{1,0:T(8,128)(2,1)}, u32[]{:S(2)}, u32[]{:S(2)}) collective-permute-start(bf16[1040,256]{1,0:T(8,128)(2,1)} %collective-permute-done.1.refs_2_), channel_id=1, source_target_pairs={{2,4},{3,5},{4,2},{5,3},{10,12},{11,13},{12,10},{13,11},{18,20},{1... | collective-permute-start | bytes 1597448 | tf_op jit(solution)/shard_map/ppermute | solution.py:185
  39.8 1.0 copy-start.1
  40.8 54.2 %all-to-all-start = ((bf16[4,2,2,512,128]{4,3,2,1,0:T(8,128)(2,1)}), bf16[4,2,2,512,128]{4,3,2,1,0:T(8,128)(2,1)}, u32[]{:S(2)}, u32[]{:S(2)}) async-start(bf16[4,2,2,512,128]{4,3,2,1,0:T(8,128)(2,1)} %after.2), calls=%async_computation | async-start | bytes 4194304 | tf_op jit(solution)/shard_map/all_to_all | solution.py:158
  45.7 40.5 %copy-start.2 = (bf16[4,1,2,512,128]{4,3,2,1,0:T(8,128)(2,1)S(1)}, bf16[4,1,2,512,128]{4,3,2,1,0:T(8,128)(2,1)}, u32[]{:S(2)}) copy-start(bf16[4,1,2,512,128]{4,3,2,1,0:T(8,128)(2,1)} %copy-done.1) | copy-start | bytes 3145732
  45.7 40.5 %collective-permute-start.14 = (bf16[4,1,2,512,128]{4,3,2,1,0:T(8,128)(2,1)}, bf16[4,1,2,512,128]{4,3,2,1,0:T(8,128)(2,1)}, u32[]{:S(2)}, u32[]{:S(2)}) collective-permute-start(bf16[4,1,2,512,128]{4,3,2,1,0:T(8,128)(2,1)} %get-tuple-element.19), channel_id=1, source_target_pairs={{0,1},{1,0},{2,3},{3,2},{4,5},{5,4},{6,7},{7,6},{8,9},{9,8},{10,11... | collective-permute-start | bytes 3145736 | tf_op jit(solution)/shard_map/ppermute | solution.py:76
  47.2 35.3 %collective-permute-start.7 = (bf16[1040,256]{1,0:T(8,128)(2,1)}, bf16[1040,256]{1,0:T(8,128)(2,1)}, u32[]{:S(2)}, u32[]{:S(2)}) collective-permute-start(bf16[1040,256]{1,0:T(8,128)(2,1)} %collective-permute-done.6.refs_1_), channel_id=1, source_target_pairs={{2,0},{3,1},{4,6},{5,7},{10,8},{11,9},{12,14},{13,15},{18,16},{19,... | collective-permute-start | bytes 1597448 | tf_op jit(solution)/shard_map/ppermute | solution.py:185
  48.5 40.4 %collective-permute-start.2 = (bf16[1040,256]{1,0:T(8,128)(2,1)}, bf16[1040,256]{1,0:T(8,128)(2,1)S(1)}, u32[]{:S(2)}, u32[]{:S(2)}) collective-permute-start(bf16[1040,256]{1,0:T(8,128)(2,1)} %collective-permute-done.1.refs_2_), channel_id=1, source_target_pairs={{0,1},{1,0},{2,3},{3,2},{4,5},{5,4},{6,7},{7,6},{8,9},{9,8},{10,11... | collective-permute-start | bytes 1597448 | tf_op jit(solution)/shard_map/ppermute | solution.py:76
  50.4 38.5 %copy-start.5 = (bf16[1040,256]{1,0:T(8,128)(2,1)}, bf16[1040,256]{1,0:T(8,128)(2,1)S(1)}, u32[]{:S(2)}) copy-start(bf16[1040,256]{1,0:T(8,128)(2,1)S(1)} %add.189.refs_4_) | copy-start | bytes 1597444
  50.4 44.3 %collective-permute-start.5 = (bf16[1040,256]{1,0:T(8,128)(2,1)S(1)}, bf16[1040,256]{1,0:T(8,128)(2,1)S(1)}, u32[]{:S(2)}, u32[]{:S(2)}) collective-permute-start(bf16[1040,256]{1,0:T(8,128)(2,1)S(1)} %add.189.refs_4_), channel_id=1, source_target_pairs={{0,1},{1,0},{2,3},{3,2},{4,5},{5,4},{6,7},{7,6},{8,9},{9,8},{10,11... | collective-permute-start | bytes 1597448 | tf_op jit(solution)/shard_map/ppermute | solution.py:76
  84.6 20.8 %collective-permute-start.8 = (bf16[1040,256]{1,0:T(8,128)(2,1)}, bf16[1040,256]{1,0:T(8,128)(2,1)}, u32[]{:S(2)}, u32[]{:S(2)}) collective-permute-start(bf16[1040,256]{1,0:T(8,128)(2,1)} %add.190.refs_6_), channel_id=1, source_target_pairs={{0,1},{1,0},{2,3},{3,2},{4,5},{5,4},{6,7},{7,6},{8,9},{9,8},{10,11... | collective-permute-start | bytes 1597448 | tf_op jit(solution)/shard_map/ppermute | solution.py:76
  88.9 6.1 %copy-start.3 = (bf16[1040,256]{1,0:T(8,128)(2,1)}, bf16[1040,256]{1,0:T(8,128)(2,1)S(1)}, u32[]{:S(2)}) copy-start(bf16[1040,256]{1,0:T(8,128)(2,1)S(1)} %collective-permute-done.2.refs_3_.refs_4_) | copy-start | bytes 1597444
  94.8 0.8 copy-start.4
  95.6 57.6 %all-to-all-start.1 = ((bf16[4,2,2,512,128]{4,3,2,1,0:T(8,128)(2,1)}), bf16[4,2,2,512,128]{4,3,2,1,0:T(8,128)(2,1)}, u32[]{:S(2)}, u32[]{:S(2)}) async-start(bf16[4,2,2,512,128]{4,3,2,1,0:T(8,128)(2,1)} %after.3), calls=%async_computation.1 | async-start | bytes 4194304 | tf_op jit(solution)/shard_map/all_to_all | solution.py:158
  111.0 23.7 %collective-permute-start.11 = (bf16[2,512,256]{2,1,0:T(8,128)(2,1)}, bf16[2,512,256]{2,1,0:T(8,128)(2,1)S(1)}, u32[]{:S(2)}, u32[]{:S(2)}) collective-permute-start(bf16[2,512,256]{2,1,0:T(8,128)(2,1)} %get-tuple-element.13.h_last), channel_id=1, source_target_pairs={{0,8},{8,16},{16,24},{1,9},{9,17},{17,25},{2,10},{10,18},{18,26},{... | collective-permute-start | bytes 1572872 | tf_op jit(solution)/shard_map/ppermute | solution.py:726
  113.0 21.8 %collective-permute-start.12 = (bf16[2,512,256]{2,1,0:T(8,128)(2,1)}, bf16[2,512,256]{2,1,0:T(8,128)(2,1)S(1)}, u32[]{:S(2)}, u32[]{:S(2)}) collective-permute-start(bf16[2,512,256]{2,1,0:T(8,128)(2,1)} %get-tuple-element.14.h_first), channel_id=1, source_target_pairs={{8,0},{16,8},{24,16},{9,1},{17,9},{25,17},{10,2},{18,10},{26,18},{... | collective-permute-start | bytes 1572872 | tf_op jit(solution)/shard_map/ppermute | solution.py:726
  134.7 0.8 copy-start.6
  134.8 1.0 copy-start.7
  157.8 10.4 %all-to-all-start.2 = ((f32[8,24,128]{2,1,0:T(8,128)}), f32[8,24,128]{2,1,0:T(8,128)S(1)}, u32[]{:S(2)}, u32[]{:S(2)}) async-start(f32[8,24,128]{2,1,0:T(8,128)} %project.1), calls=%async_computation.2 | async-start | bytes 196608 | tf_op jit(solution)/shard_map/all_to_all | solution.py:807
  168.2 0.6 copy-start.8

commit v9 on v8

--- a/solution.py
+++ b/solution.py
@@ -148,15 +148,49 @@
     )(block, *others)
 
 
+def stack_kernel(number, *refs):
+    sources, (out, held, in_sems, out_sems) = refs[:number], refs[-4:]
+    loads = [pltpu.make_async_copy(sources[i], held.at[i], in_sems.at[i]) for i in range(number)]
+    stores = [
+        pltpu.make_async_copy(held.at[i], out.at[:, pl.ds(i, 1)], out_sems.at[i])
+        for i in range(number)
+    ]
+    for load in loads:
+        load.start()
+    for load, store in zip(loads, stores):
+        load.wait()
+        store.start()
+    for store in stores:
+        store.wait()
+
+
+def stack(blocks, *others):
+    block = blocks[0]
+    shape = (block.shape[0], len(blocks)) + block.shape[2:]
+    return pl.pallas_call(
+        functools.partial(stack_kernel, len(blocks)),
+        out_shape=jax.ShapeDtypeStruct(shape, block.dtype),
+        in_specs=[ANY] * (len(blocks) + len(others)),
+        out_specs=HBM,
+        scratch_shapes=[
+            pltpu.VMEM((len(blocks),) + block.shape, block.dtype),
+            pltpu.SemaphoreType.DMA((len(blocks),)),
+            pltpu.SemaphoreType.DMA((len(blocks),)),
+        ],
+        compiler_params=pltpu.CompilerParams(vmem_limit_bytes=62 * MIB),
+        name="stack",
+    )(*blocks, *others)
+
+
 def exchange(me, peers, basis, own, early, awaited, handed):
     count = lax.axis_size("col")
     outer, inner = lines_of(count)
     groups = [[line * inner + place for line in range(outer)] for place in range(inner)]
 
     def between_lines(blocks, *others):
-        block = jnp.concatenate(blocks, axis=1)
+        block = stack(blocks, *others) if len(blocks) > 1 else after(blocks[0], *others)
         return lax.all_to_all(
-            after(block, *others), "col", split_axis=0, concat_axis=0,
+            block, "col", split_axis=0, concat_axis=0,
             axis_index_groups=groups, tiled=True,
         )
 

time: 177 us -> 177 us (level)
  waiting for transfers between devices: 68.1 us -> 70.9 us
  Pallas kernels: 46.3 us -> 49.1 us
  other arithmetic: 9.33 us -> 6.58 us
    concatenate x1 -> x0, other arithmetic: 2.76 us -> none  [between_lines(): block = jnp.concatenate(blocks, axis=1)]
    ppermute x6, waiting for transfers between devices: 18.2 us -> 20.9 us  [swap_along(): return lax.ppermute(block, 'col', pairs)]
    pallas_call x0 -> x1, Pallas kernels: none -> 2.55 us  [stack(): pl.pallas_call(functools.partial(stack_kernel, len(blocks)), out_shape=ja...]
    all_to_all x2, starting transfers between devices: 14.6 us -> 12.7 us  [between_lines(): lax.all_to_all(block, 'col', split_axis=0, concat_axis=0, axis_index_grou...]
  transfers between devices with their start and end apart: 18 -> 18, of which waited for: 9 -> 9; matrix products, arithmetic and copies ran while one was open for 8% -> 7% of each run, Pallas kernels for 19% -> 20%
where the time goes in v9:
time: 177 us; the launch traced here: 176 us
  waiting for transfers between devices  70.9 us (40%)
  Pallas kernels  49.1 us (28%)
  starting transfers between devices  40.2 us (23%)
  local copies, waits for them, and re-layouts  8.72 us (5%)
  other arithmetic  6.58 us (4%)
    ppermute x5, waiting for transfers between devices, move(): return lax.ppermute(block, 'col', pairs)  29.6 us
    ppermute x6, waiting for transfers between devices, swap_along(): return lax.ppermute(block, 'col', pairs)  20.9 us
    pallas_call x1, Pallas kernels, chebyshev_inner(): pl.pallas_call(functools.partial(inner_kernel, blocks), out_shape=(jax.Sh...  16.4 us
    all_to_all x2, starting transfers between devices, between_lines(): lax.all_to_all(block, 'col', split_axis=0, concat_axis=0, axis_index_grou...  12.7 us
    all_to_all x2, waiting for transfers between devices, between_lines(): lax.all_to_all(block, 'col', split_axis=0, concat_axis=0, axis_index_grou...  10.6 us
    ppermute x4, starting transfers between devices, shift(): return lax.ppermute(block, axis, pairs)  9.37 us
    ppermute x6, starting transfers between devices, swap_along(): return lax.ppermute(block, 'col', pairs)  7.35 us
    ppermute x5, starting transfers between devices, move(): return lax.ppermute(block, 'col', pairs)  7.08 us
  transfers between devices with their start and end apart: 18, of which 9 were waited for; matrix products, arithmetic and copies ran while one was open for 7% of the time, Pallas kernels for 20%

profile of v9, /device:TPU:2, one launch (start us, length us, event | category | flops | bytes accessed | tf_op | source)
XLA Modules:
  0.0 176.4 jit_solution(16279471493569761869)
XLA Ops:
  0.6 2.6 %own_piece.1.refs_0_.first = bf16[1040,256]{1,0:T(8,128)(2,1)} custom-call(s32[16]{0:T(128)} %bitcast.32, s32[16]{0:T(128)} %named.1, s32[4]{0:T(128)} %counts.1, s32[2]{0:T(128)} %pattern.1, bf16[1024,256]{1,0:T(8,128)(2,1)} %bitcast.26), custom_call_target="tpu_custom_call" | custom-call | tf_op jit(solution)/shard_map/own_piece/pallas_call | solution.py:56
  3.2 1.6 collective-permute-start
  4.8 1.6 collective-permute-start.1
  6.4 1.5 collective-permute-start.3
  7.8 2.7 %pack.3 = bf16[4,1,2,512,128]{4,3,2,1,0:T(8,128)(2,1)} custom-call(s32[1]{0:T(128)} %bitcast.11.me, s32[16]{0:T(128)} %bitcast.33, bf16[16,2,512,128]{3,2,1,0:T(8,128)(2,1)} %basis.3, bf16[1040,256]{1,0:T(8,128)(2,1)} %own_piece.1.refs_0_.first), custom_call_target="tpu_custom_call" | custom-call | tf_op jit(solution)/shard_map/pack/pallas_call | solution.py:119
  11.2 2.6 %fusion.12 = (bf16[768,512]{1,0:T(8,128)(2,1)}, bf16[768,512]{1,0:T(8,128)(2,1)}) fusion(bf16[4096,512]{1,0:T(8,128)(2,1)} %v_mid.3), kind=kLoop, calls=%fused_computation.54 | loop fusion | bytes 3145728 | tf_op jit(solution)/shard_map/slice | solution.py:828
  13.8 1.9 %collective-permute-start.9 = (bf16[768,512]{1,0:T(8,128)(2,1)}, bf16[768,512]{1,0:T(8,128)(2,1)}, u32[]{:S(2)}, u32[]{:S(2)}) collective-permute-start(bf16[768,512]{1,0:T(8,128)(2,1)} %get-tuple-element.27), channel_id=1, source_target_pairs={{0,8},{8,16},{16,24},{1,9},{9,17},{17,25},{2,10},{10,18},{18,26},{... | collective-permute-start | bytes 2359304 | tf_op jit(solution)/shard_map/ppermute | solution.py:760
  15.7 2.8 %collective-permute-done.refs_1_.first.refs_4_ = bf16[1040,256]{1,0:T(8,128)(2,1)S(1)} collective-permute-done((bf16[1040,256]{1,0:T(8,128)(2,1)}, bf16[1040,256]{1,0:T(8,128)(2,1)S(1)}, u32[]{:S(2)}, u32[]{:S(2)}) %collective-permute-start) | collective-permute-done | bytes 532512 | tf_op jit(solution)/shard_map/ppermute | solution.py:76
  18.5 1.9 %collective-permute-start.10 = (bf16[768,512]{1,0:T(8,128)(2,1)}, bf16[768,512]{1,0:T(8,128)(2,1)}, u32[]{:S(2)}, u32[]{:S(2)}) collective-permute-start(bf16[768,512]{1,0:T(8,128)(2,1)} %get-tuple-element.26), channel_id=1, source_target_pairs={{8,0},{16,8},{24,16},{9,1},{17,9},{25,17},{10,2},{18,10},{26,18},{... | collective-permute-start | bytes 2359304 | tf_op jit(solution)/shard_map/ppermute | solution.py:760
  21.7 1.5 collective-permute-start.6
  23.2 3.6 %pack.2 = (bf16[4,2,2,512,128]{4,3,2,1,0:T(8,128)(2,1)}, bf16[4,1,2,512,128]{4,3,2,1,0:T(8,128)(2,1)}) custom-call(s32[1]{0:T(128)} %bitcast.11.me, s32[16]{0:T(128)} %bitcast.34, bf16[16,2,512,128]{3,2,1,0:T(8,128)(2,1)} %basis.3, bf16[1040,256]{1,0:T(8,128)(2,1)} %copy-done), custom_call_target="tpu_custom_call" | custom-call | tf_op jit(solution)/shard_map/pack/pallas_call | solution.py:119
  27.4 2.8 %collective-permute-done.10.v_high.refs_4_ = bf16[768,512]{1,0:T(8,128)(2,1)} collective-permute-done((bf16[768,512]{1,0:T(8,128)(2,1)}, bf16[768,512]{1,0:T(8,128)(2,1)}, u32[]{:S(2)}, u32[]{:S(2)}) %collective-permute-start.10) | collective-permute-done | bytes 786464 | tf_op jit(solution)/shard_map/ppermute | solution.py:760
  30.2 9.6 %collective-permute-done.13.refs_5_.refs_0_ = bf16[4,1,2,512,128]{4,3,2,1,0:T(8,128)(2,1)S(1)} collective-permute-done((bf16[4,1,2,512,128]{4,3,2,1,0:T(8,128)(2,1)}, bf16[4,1,2,512,128]{4,3,2,1,0:T(8,128)(2,1)S(1)}, u32[]{:S(2)}, u32[]{:S(2)}) %collective-permute-start.13) | collective-permute-done | bytes 1048608 | tf_op jit(solution)/shard_map/ppermute | solution.py:76
  40.8 4.9 %all-to-all-start = ((bf16[4,2,2,512,128]{4,3,2,1,0:T(8,128)(2,1)}), bf16[4,2,2,512,128]{4,3,2,1,0:T(8,128)(2,1)}, u32[]{:S(2)}, u32[]{:S(2)}) async-start(bf16[4,2,2,512,128]{4,3,2,1,0:T(8,128)(2,1)} %after.1), calls=%async_computation | async-start | bytes 4194304 | tf_op jit(solution)/shard_map/all_to_all | solution.py:192
  45.7 1.5 collective-permute-start.14
  51.3 1.6 collective-permute-start.5
  52.9 29.6 %collective-permute-done.7.refs_3_ = bf16[1040,256]{1,0:T(8,128)(2,1)S(1)} collective-permute-done((bf16[1040,256]{1,0:T(8,128)(2,1)}, bf16[1040,256]{1,0:T(8,128)(2,1)S(1)}, u32[]{:S(2)}, u32[]{:S(2)}) %collective-permute-start.7) | collective-permute-done | bytes 532512 | tf_op jit(solution)/shard_map/ppermute | solution.py:219
  82.5 2.2 %add.190.refs_6_ = bf16[1040,256]{1,0:T(8,128)(2,1)} add(bf16[1040,256]{1,0:T(8,128)(2,1)} %collective-permute-done.6.refs_1_, bf16[1040,256]{1,0:T(8,128)(2,1)S(1)} %collective-permute-done.7.refs_3_) | non-fusion elementwise | flops 266240 | bytes 1597440 | tf_op jit(solution)/shard_map/add | solution.py:233
  84.6 1.5 collective-permute-start.8
  86.2 8.5 %collective-permute-done.5.refs_5_.refs_6_ = bf16[1040,256]{1,0:T(8,128)(2,1)S(1)} collective-permute-done((bf16[1040,256]{1,0:T(8,128)(2,1)S(1)}, bf16[1040,256]{1,0:T(8,128)(2,1)S(1)}, u32[]{:S(2)}, u32[]{:S(2)}) %collective-permute-start.5) | collective-permute-done | bytes 532512 | tf_op jit(solution)/shard_map/ppermute | solution.py:76
  95.6 2.6 %stack.37 = bf16[4,2,2,512,128]{4,3,2,1,0:T(8,128)(2,1)} custom-call(bf16[4,1,2,512,128]{4,3,2,1,0:T(8,128)(2,1)} %copy-done.1, bf16[4,1,2,512,128]{4,3,2,1,0:T(8,128)(2,1)} %copy-done.6, bf16[4,2,2,512,128]{4,3,2,1,0:T(8,128)(2,1)} %all-to-all-done.refs_2_, bf16[1040,256]{1,0:T(8,128)(2,1)} %copy-done.5, bf16[1040,256]{1,0:T(8,128)(2,1)} %copy-done, ...), custom_call_target="tpu_custom_call" | custom-call | tf_op jit(solution)/shard_map/stack/pallas_call | solution.py:170
  98.1 7.9 %all-to-all-start.1 = ((bf16[4,2,2,512,128]{4,3,2,1,0:T(8,128)(2,1)}), bf16[4,2,2,512,128]{4,3,2,1,0:T(8,128)(2,1)}, u32[]{:S(2)}, u32[]{:S(2)}) async-start(bf16[4,2,2,512,128]{4,3,2,1,0:T(8,128)(2,1)} %stack.37), calls=%async_computation.1 | async-start | bytes 4194304 | tf_op jit(solution)/shard_map/all_to_all | solution.py:192
  106.1 3.0 %edge_blocks.1 = (bf16[2,512,256]{2,1,0:T(8,128)(2,1)}, bf16[2,512,256]{2,1,0:T(8,128)(2,1)}, bf16[8,16,256]{2,1,0:T(8,128)(2,1)}) custom-call(s32[8]{0:T(128)} %stack.36.owners, bf16[1040,256]{1,0:T(8,128)(2,1)} %own_piece.1.refs_0_.first, bf16[1040,256]{1,0:T(8,128)(2,1)} %copy-done, bf16[1040,256]{1,0:T(8,128)(2,1)} %collective-permute-done.1.refs_2_, ...), custom_call_target="tpu_custom_call" | custom-call | tf_op jit(solution)/shard_map/edge_blocks/pallas_call | solution.py:282
  111.8 1.9 %collective-permute-start.11 = (bf16[2,512,256]{2,1,0:T(8,128)(2,1)}, bf16[2,512,256]{2,1,0:T(8,128)(2,1)S(1)}, u32[]{:S(2)}, u32[]{:S(2)}) collective-permute-start(bf16[2,512,256]{2,1,0:T(8,128)(2,1)} %get-tuple-element.13.h_last), channel_id=1, source_target_pairs={{0,8},{8,16},{16,24},{1,9},{9,17},{17,25},{2,10},{10,18},{18,26},{... | collective-permute-start | bytes 1572872 | tf_op jit(solution)/shard_map/ppermute | solution.py:760
  113.7 3.6 %collective-permute-start.12 = (bf16[2,512,256]{2,1,0:T(8,128)(2,1)}, bf16[2,512,256]{2,1,0:T(8,128)(2,1)S(1)}, u32[]{:S(2)}, u32[]{:S(2)}) collective-permute-start(bf16[2,512,256]{2,1,0:T(8,128)(2,1)} %get-tuple-element.14.h_first), channel_id=1, source_target_pairs={{8,0},{16,8},{24,16},{9,1},{17,9},{25,17},{10,2},{18,10},{26,18},{... | collective-permute-start | bytes 1572872 | tf_op jit(solution)/shard_map/ppermute | solution.py:760
  119.1 16.4 %chebyshev_inner.1 = (bf16[8,512,512]{2,1,0:T(8,128)(2,1)}, bf16[1024,512]{1,0:T(8,128)(2,1)}, bf16[1024,512]{1,0:T(8,128)(2,1)}, f32[1024,512]{1,0:T(8,128)}) custom-call(f32[4]{0:T(128)} %coef.3, s32[8]{0:T(128)} %stack.36.owners, bf16[768,512]{1,0:T(8,128)(2,1)} %collective-permute-done.9.v_low.refs_3_, bf16[4096,512]{1,0:T(8,128)(2,1)} %v_mid.3, ...), custom_call_target="tpu_custom_call" | custom-call | flops 8455716864 | bytes 16777216 | tf_op jit(solution)/shard_map/chebyshev_inner/pallas_call | solution.py:407
  136.5 7.1 %chebyshev_outer.1.kernel_t = bf16[8,512,512]{2,1,0:T(8,128)(2,1)} custom-call(f32[4]{0:T(128)} %coef.3, bf16[8,512,512]{2,1,0:T(8,128)(2,1)} %get-tuple-element.12.kernel_in, bf16[768,512]{1,0:T(8,128)(2,1)} %collective-permute-done.9.v_low.refs_3_, bf16[4096,512]{1,0:T(8,128)(2,1)} %v_mid.3, ...), custom_call_target="tpu_custom_call", output_to_operand_aliasing={{}: (1, {})} | custom-call | tf_op jit(solution)/shard_map/chebyshev_outer/pallas_call | solution.py:525
  143.5 10.3 %all-to-all-done.1 = bf16[4,2,2,512,128]{4,3,2,1,0:T(8,128)(2,1)} async-done(((bf16[4,2,2,512,128]{4,3,2,1,0:T(8,128)(2,1)}), bf16[4,2,2,512,128]{4,3,2,1,0:T(8,128)(2,1)}, u32[]{:S(2)}, u32[]{:S(2)}) %all-to-all-start.1) | async-done | bytes 2097184 | tf_op jit(solution)/shard_map/all_to_all | solution.py:192
  153.8 4.7 %project.1 = f32[8,24,128]{2,1,0:T(8,128)} custom-call(s32[26]{0:T(128)} %pad_add_fusion.1.plan, s32[16]{0:T(128)} %select_reduce_fusion.2.order, bf16[8,512,512]{2,1,0:T(8,128)(2,1)} %chebyshev_outer.1.kernel_t, f32[4,128]{1,0:T(4,128)} %core.1, bf16[8,2,512,128]{3,2,1,0:T(8,128)(2,1)} %bitcast.12.refs_0_, bf16[8,2,512,128]{3,2,1,0:T(8,128)(2,1)} %bitcast.13.refs_1_), custom_call_target="tpu_custom_call" | custom-call | tf_op jit(solution)/shard_map/project/pallas_call | solution.py:637
  158.6 3.6 %all-to-all-start.2 = ((f32[8,24,128]{2,1,0:T(8,128)}), f32[8,24,128]{2,1,0:T(8,128)S(1)}, u32[]{:S(2)}, u32[]{:S(2)}) async-start(f32[8,24,128]{2,1,0:T(8,128)} %project.1), calls=%async_computation.2 | async-start | bytes 196608 | tf_op jit(solution)/shard_map/all_to_all | solution.py:841
  162.9 6.4 %all-to-all-done.2 = f32[8,24,128]{2,1,0:T(8,128)S(1)} async-done(((f32[8,24,128]{2,1,0:T(8,128)}), f32[8,24,128]{2,1,0:T(8,128)S(1)}, u32[]{:S(2)}, u32[]{:S(2)}) %all-to-all-start.2) | async-done | bytes 98336 | tf_op jit(solution)/shard_map/all_to_all | solution.py:841
  169.9 6.4 %update.1 = (f32[4,128]{1,0:T(4,128)}, bf16[4096,512]{1,0:T(8,128)(2,1)}) custom-call(s32[26]{0:T(128)} %pad_add_fusion.1.plan, s32[16]{0:T(128)} %select_reduce_fusion.2.order, s32[16]{0:T(128)} %reshape.285.tile_of, f32[192,128]{1,0:T(8,128)} %bitcast.27, f32[32,192]{1,0:T(8,128)} %convert_reduce_fusion.collect, bf16[8,2,512,128]{3,2,1,0:T(8,128)(2,1)} %bitcast.12.refs_0_, ...), custom_call_target="tpu_custom_call" | custom-call | tf_op jit(solution)/shard_map/update/pallas_call | solution.py:735
  (79 shorter events, 15.1 us)
Async XLA Ops:
  3.2 15.3 %collective-permute-start = (bf16[1040,256]{1,0:T(8,128)(2,1)}, bf16[1040,256]{1,0:T(8,128)(2,1)S(1)}, u32[]{:S(2)}, u32[]{:S(2)}) collective-permute-start(bf16[1040,256]{1,0:T(8,128)(2,1)} %own_piece.1.refs_0_.first), channel_id=1, source_target_pairs={{0,1},{1,0},{2,3},{3,2},{4,5},{5,4},{6,7},{7,6},{8,9},{9,8},{10,11... | collective-permute-start | bytes 1597448 | tf_op jit(solution)/shard_map/ppermute | solution.py:76
  4.8 16.9 %collective-permute-start.1 = (bf16[1040,256]{1,0:T(8,128)(2,1)}, bf16[1040,256]{1,0:T(8,128)(2,1)}, u32[]{:S(2)}, u32[]{:S(2)}) collective-permute-start(bf16[1040,256]{1,0:T(8,128)(2,1)} %own_piece.1.refs_0_.first), channel_id=1, source_target_pairs={{0,2},{1,3},{2,0},{3,1},{4,6},{5,7},{6,4},{7,5},{8,10},{9,11},{10,... | collective-permute-start | bytes 1597448 | tf_op jit(solution)/shard_map/ppermute | solution.py:219
  6.4 14.0 %collective-permute-start.3 = (bf16[1040,256]{1,0:T(8,128)(2,1)}, bf16[1040,256]{1,0:T(8,128)(2,1)}, u32[]{:S(2)}, u32[]{:S(2)}) collective-permute-start(bf16[1040,256]{1,0:T(8,128)(2,1)} %own_piece.1.refs_0_.first), channel_id=1, source_target_pairs={{2,4},{3,5},{4,2},{5,3},{10,12},{11,13},{12,10},{13,11},{18,20},{1... | collective-permute-start | bytes 1597448 | tf_op jit(solution)/shard_map/ppermute | solution.py:219
  10.6 29.2 %collective-permute-start.13 = (bf16[4,1,2,512,128]{4,3,2,1,0:T(8,128)(2,1)}, bf16[4,1,2,512,128]{4,3,2,1,0:T(8,128)(2,1)S(1)}, u32[]{:S(2)}, u32[]{:S(2)}) collective-permute-start(bf16[4,1,2,512,128]{4,3,2,1,0:T(8,128)(2,1)} %pack.3), channel_id=1, source_target_pairs={{0,1},{1,0},{2,3},{3,2},{4,5},{5,4},{6,7},{7,6},{8,9},{9,8},{10,11... | collective-permute-start | bytes 3145736 | tf_op jit(solution)/shard_map/ppermute | solution.py:76
  13.8 13.6 %collective-permute-start.9 = (bf16[768,512]{1,0:T(8,128)(2,1)}, bf16[768,512]{1,0:T(8,128)(2,1)}, u32[]{:S(2)}, u32[]{:S(2)}) collective-permute-start(bf16[768,512]{1,0:T(8,128)(2,1)} %get-tuple-element.27), channel_id=1, source_target_pairs={{0,8},{8,16},{16,24},{1,9},{9,17},{17,25},{2,10},{10,18},{18,26},{... | collective-permute-start | bytes 2359304 | tf_op jit(solution)/shard_map/ppermute | solution.py:760
  18.5 4.7 %copy-start = (bf16[1040,256]{1,0:T(8,128)(2,1)}, bf16[1040,256]{1,0:T(8,128)(2,1)S(1)}, u32[]{:S(2)}) copy-start(bf16[1040,256]{1,0:T(8,128)(2,1)S(1)} %collective-permute-done.refs_1_.first.refs_4_) | copy-start | bytes 1597444
  18.5 11.7 %collective-permute-start.10 = (bf16[768,512]{1,0:T(8,128)(2,1)}, bf16[768,512]{1,0:T(8,128)(2,1)}, u32[]{:S(2)}, u32[]{:S(2)}) collective-permute-start(bf16[768,512]{1,0:T(8,128)(2,1)} %get-tuple-element.26), channel_id=1, source_target_pairs={{8,0},{16,8},{24,16},{9,1},{17,9},{25,17},{10,2},{18,10},{26,18},{... | collective-permute-start | bytes 2359304 | tf_op jit(solution)/shard_map/ppermute | solution.py:760
  20.4 19.4 %collective-permute-start.4 = (bf16[1040,256]{1,0:T(8,128)(2,1)}, bf16[1040,256]{1,0:T(8,128)(2,1)}, u32[]{:S(2)}, u32[]{:S(2)}) collective-permute-start(bf16[1040,256]{1,0:T(8,128)(2,1)} %collective-permute-done.3), channel_id=1, source_target_pairs={{2,0},{3,1},{4,6},{5,7},{10,8},{11,9},{12,14},{13,15},{18,16},{19,... | collective-permute-start | bytes 1597448 | tf_op jit(solution)/shard_map/ppermute | solution.py:219
  21.7 18.1 %collective-permute-start.6 = (bf16[1040,256]{1,0:T(8,128)(2,1)}, bf16[1040,256]{1,0:T(8,128)(2,1)}, u32[]{:S(2)}, u32[]{:S(2)}) collective-permute-start(bf16[1040,256]{1,0:T(8,128)(2,1)} %collective-permute-done.1.refs_2_), channel_id=1, source_target_pairs={{2,4},{3,5},{4,2},{5,3},{10,12},{11,13},{12,10},{13,11},{18,20},{1... | collective-permute-start | bytes 1597448 | tf_op jit(solution)/shard_map/ppermute | solution.py:219
  39.8 1.0 copy-start.1
  40.8 54.3 %all-to-all-start = ((bf16[4,2,2,512,128]{4,3,2,1,0:T(8,128)(2,1)}), bf16[4,2,2,512,128]{4,3,2,1,0:T(8,128)(2,1)}, u32[]{:S(2)}, u32[]{:S(2)}) async-start(bf16[4,2,2,512,128]{4,3,2,1,0:T(8,128)(2,1)} %after.1), calls=%async_computation | async-start | bytes 4194304 | tf_op jit(solution)/shard_map/all_to_all | solution.py:192
  45.7 40.5 %collective-permute-start.14 = (bf16[4,1,2,512,128]{4,3,2,1,0:T(8,128)(2,1)}, bf16[4,1,2,512,128]{4,3,2,1,0:T(8,128)(2,1)S(1)}, u32[]{:S(2)}, u32[]{:S(2)}) collective-permute-start(bf16[4,1,2,512,128]{4,3,2,1,0:T(8,128)(2,1)} %get-tuple-element.19), channel_id=1, source_target_pairs={{0,1},{1,0},{2,3},{3,2},{4,5},{5,4},{6,7},{7,6},{8,9},{9,8},{10,11... | collective-permute-start | bytes 3145736 | tf_op jit(solution)/shard_map/ppermute | solution.py:76
  48.1 34.4 %collective-permute-start.7 = (bf16[1040,256]{1,0:T(8,128)(2,1)}, bf16[1040,256]{1,0:T(8,128)(2,1)S(1)}, u32[]{:S(2)}, u32[]{:S(2)}) collective-permute-start(bf16[1040,256]{1,0:T(8,128)(2,1)} %collective-permute-done.6.refs_1_), channel_id=1, source_target_pairs={{2,0},{3,1},{4,6},{5,7},{10,8},{11,9},{12,14},{13,15},{18,16},{19,... | collective-permute-start | bytes 1597448 | tf_op jit(solution)/shard_map/ppermute | solution.py:219
  49.4 36.8 %collective-permute-start.2 = (bf16[1040,256]{1,0:T(8,128)(2,1)}, bf16[1040,256]{1,0:T(8,128)(2,1)S(1)}, u32[]{:S(2)}, u32[]{:S(2)}) collective-permute-start(bf16[1040,256]{1,0:T(8,128)(2,1)} %collective-permute-done.1.refs_2_), channel_id=1, source_target_pairs={{0,1},{1,0},{2,3},{3,2},{4,5},{5,4},{6,7},{7,6},{8,9},{9,8},{10,11... | collective-permute-start | bytes 1597448 | tf_op jit(solution)/shard_map/ppermute | solution.py:76
  51.3 46.8 %copy-start.4 = (bf16[1040,256]{1,0:T(8,128)(2,1)}, bf16[1040,256]{1,0:T(8,128)(2,1)S(1)}, u32[]{:S(2)}) copy-start(bf16[1040,256]{1,0:T(8,128)(2,1)S(1)} %add.189.refs_4_) | copy-start | bytes 1597444
  51.3 43.5 %collective-permute-start.5 = (bf16[1040,256]{1,0:T(8,128)(2,1)S(1)}, bf16[1040,256]{1,0:T(8,128)(2,1)S(1)}, u32[]{:S(2)}, u32[]{:S(2)}) collective-permute-start(bf16[1040,256]{1,0:T(8,128)(2,1)S(1)} %add.189.refs_4_), channel_id=1, source_target_pairs={{0,1},{1,0},{2,3},{3,2},{4,5},{5,4},{6,7},{7,6},{8,9},{9,8},{10,11... | collective-permute-start | bytes 1597448 | tf_op jit(solution)/shard_map/ppermute | solution.py:76
  82.5 3.7 %copy-start.5 = (bf16[1040,256]{1,0:T(8,128)(2,1)}, bf16[1040,256]{1,0:T(8,128)(2,1)S(1)}, u32[]{:S(2)}) copy-start(bf16[1040,256]{1,0:T(8,128)(2,1)S(1)} %collective-permute-done.7.refs_3_) | copy-start | bytes 1597444
  84.6 21.5 %collective-permute-start.8 = (bf16[1040,256]{1,0:T(8,128)(2,1)}, bf16[1040,256]{1,0:T(8,128)(2,1)}, u32[]{:S(2)}, u32[]{:S(2)}) collective-permute-start(bf16[1040,256]{1,0:T(8,128)(2,1)} %add.190.refs_6_), channel_id=1, source_target_pairs={{0,1},{1,0},{2,3},{3,2},{4,5},{5,4},{6,7},{7,6},{8,9},{9,8},{10,11... | collective-permute-start | bytes 1597448 | tf_op jit(solution)/shard_map/ppermute | solution.py:76
  86.2 8.9 %copy-start.2 = (bf16[1040,256]{1,0:T(8,128)(2,1)}, bf16[1040,256]{1,0:T(8,128)(2,1)S(1)}, u32[]{:S(2)}) copy-start(bf16[1040,256]{1,0:T(8,128)(2,1)S(1)} %collective-permute-done.2.refs_3_.refs_5_) | copy-start | bytes 1597444
  86.2 8.6 %copy-start.6 = (bf16[4,1,2,512,128]{4,3,2,1,0:T(8,128)(2,1)}, bf16[4,1,2,512,128]{4,3,2,1,0:T(8,128)(2,1)S(1)}, u32[]{:S(2)}) copy-start(bf16[4,1,2,512,128]{4,3,2,1,0:T(8,128)(2,1)S(1)} %collective-permute-done.14.refs_1_) | copy-start | bytes 3145732
  94.8 0.8 copy-start.3
  98.1 55.7 %all-to-all-start.1 = ((bf16[4,2,2,512,128]{4,3,2,1,0:T(8,128)(2,1)}), bf16[4,2,2,512,128]{4,3,2,1,0:T(8,128)(2,1)}, u32[]{:S(2)}, u32[]{:S(2)}) async-start(bf16[4,2,2,512,128]{4,3,2,1,0:T(8,128)(2,1)} %stack.37), calls=%async_computation.1 | async-start | bytes 4194304 | tf_op jit(solution)/shard_map/all_to_all | solution.py:192
  111.8 23.7 %collective-permute-start.11 = (bf16[2,512,256]{2,1,0:T(8,128)(2,1)}, bf16[2,512,256]{2,1,0:T(8,128)(2,1)S(1)}, u32[]{:S(2)}, u32[]{:S(2)}) collective-permute-start(bf16[2,512,256]{2,1,0:T(8,128)(2,1)} %get-tuple-element.13.h_last), channel_id=1, source_target_pairs={{0,8},{8,16},{16,24},{1,9},{9,17},{17,25},{2,10},{10,18},{18,26},{... | collective-permute-start | bytes 1572872 | tf_op jit(solution)/shard_map/ppermute | solution.py:760
  113.7 21.8 %collective-permute-start.12 = (bf16[2,512,256]{2,1,0:T(8,128)(2,1)}, bf16[2,512,256]{2,1,0:T(8,128)(2,1)S(1)}, u32[]{:S(2)}, u32[]{:S(2)}) collective-permute-start(bf16[2,512,256]{2,1,0:T(8,128)(2,1)} %get-tuple-element.14.h_first), channel_id=1, source_target_pairs={{8,0},{16,8},{24,16},{9,1},{17,9},{25,17},{10,2},{18,10},{26,18},{... | collective-permute-start | bytes 1572872 | tf_op jit(solution)/shard_map/ppermute | solution.py:760
  135.4 0.8 copy-start.7
  135.5 1.0 copy-start.8
  158.6 10.8 %all-to-all-start.2 = ((f32[8,24,128]{2,1,0:T(8,128)}), f32[8,24,128]{2,1,0:T(8,128)S(1)}, u32[]{:S(2)}, u32[]{:S(2)}) async-start(f32[8,24,128]{2,1,0:T(8,128)} %project.1), calls=%async_computation.2 | async-start | bytes 196608 | tf_op jit(solution)/shard_map/all_to_all | solution.py:841
  169.3 0.6 copy-start.9

commit v10 on v8

--- a/solution.py
+++ b/solution.py
@@ -715,7 +715,7 @@
             pltpu.SemaphoreType.DMA((slots,)),
             pltpu.SemaphoreType.DMA((blocks,)),
         ],
-        compiler_params=pltpu.CompilerParams(vmem_limit_bytes=62 * MIB),
+        compiler_params=pltpu.CompilerParams(vmem_limit_bytes=24 * MIB),
         name="update",
     )(plan, order, tile_of, contributions, collect, *parts)
 

time: 177 us -> 177 us (level)
  no operation moved by 1% of the time
where the time goes in v10:
time: 177 us; the launch traced here: 175 us
  waiting for transfers between devices  69.2 us (39%)
  Pallas kernels  47.2 us (27%)
  starting transfers between devices  41.9 us (24%)
  other arithmetic  8.71 us (5%)
  local copies, waits for them, and re-layouts  7.54 us (4%)
    ppermute x5, waiting for transfers between devices, move(): return lax.ppermute(block, 'col', pairs)  29.6 us
    ppermute x6, waiting for transfers between devices, swap_along(): return lax.ppermute(block, 'col', pairs)  18.2 us
    pallas_call x1, Pallas kernels, chebyshev_inner(): pl.pallas_call(functools.partial(inner_kernel, blocks), out_shape=(jax.Sh...  16.4 us
    all_to_all x2, starting transfers between devices, between_lines(): lax.all_to_all(after(block, *others), 'col', split_axis=0, concat_axis=0,...  14.7 us
    all_to_all x2, waiting for transfers between devices, between_lines(): lax.all_to_all(after(block, *others), 'col', split_axis=0, concat_axis=0,...  11.1 us
    ppermute x4, starting transfers between devices, shift(): return lax.ppermute(block, axis, pairs)  9.38 us
    ppermute x6, starting transfers between devices, swap_along(): return lax.ppermute(block, 'col', pairs)  7.35 us
    ppermute x5, starting transfers between devices, move(): return lax.ppermute(block, 'col', pairs)  7.1 us
  transfers between devices with their start and end apart: 18, of which 9 were waited for; matrix products, arithmetic and copies ran while one was open for 8% of the time, Pallas kernels for 19%

profile of v10, /device:TPU:2, one launch (start us, length us, event | category | flops | bytes accessed | tf_op | source)
XLA Modules:
  0.0 175.4 jit_solution(15009908462523227106)
XLA Ops:
  0.6 2.6 %own_piece.1.refs_0_.first = bf16[1040,256]{1,0:T(8,128)(2,1)} custom-call(s32[16]{0:T(128)} %bitcast.32, s32[16]{0:T(128)} %named.1, s32[4]{0:T(128)} %counts.1, s32[2]{0:T(128)} %pattern.1, bf16[1024,256]{1,0:T(8,128)(2,1)} %bitcast.27), custom_call_target="tpu_custom_call" | custom-call | tf_op jit(solution)/shard_map/own_piece/pallas_call | solution.py:56
  3.2 1.6 collective-permute-start
  4.8 1.6 collective-permute-start.1
  6.4 1.5 collective-permute-start.3
  7.8 2.7 %pack.3 = bf16[4,1,2,512,128]{4,3,2,1,0:T(8,128)(2,1)} custom-call(s32[1]{0:T(128)} %bitcast.11.me, s32[16]{0:T(128)} %bitcast.33, bf16[16,2,512,128]{3,2,1,0:T(8,128)(2,1)} %basis.3, bf16[1040,256]{1,0:T(8,128)(2,1)} %own_piece.1.refs_0_.first), custom_call_target="tpu_custom_call" | custom-call | tf_op jit(solution)/shard_map/pack/pallas_call | solution.py:119
  11.2 2.6 %fusion.12 = (bf16[768,512]{1,0:T(8,128)(2,1)}, bf16[768,512]{1,0:T(8,128)(2,1)}) fusion(bf16[4096,512]{1,0:T(8,128)(2,1)} %v_mid.3), kind=kLoop, calls=%fused_computation.55 | loop fusion | bytes 3145728 | tf_op jit(solution)/shard_map/slice | solution.py:794
  13.8 1.9 %collective-permute-start.9 = (bf16[768,512]{1,0:T(8,128)(2,1)}, bf16[768,512]{1,0:T(8,128)(2,1)}, u32[]{:S(2)}, u32[]{:S(2)}) collective-permute-start(bf16[768,512]{1,0:T(8,128)(2,1)} %get-tuple-element.27), channel_id=1, source_target_pairs={{0,8},{8,16},{16,24},{1,9},{9,17},{17,25},{2,10},{10,18},{18,26},{... | collective-permute-start | bytes 2359304 | tf_op jit(solution)/shard_map/ppermute | solution.py:726
  15.7 2.8 %collective-permute-done.refs_1_.first.refs_3_ = bf16[1040,256]{1,0:T(8,128)(2,1)S(1)} collective-permute-done((bf16[1040,256]{1,0:T(8,128)(2,1)}, bf16[1040,256]{1,0:T(8,128)(2,1)S(1)}, u32[]{:S(2)}, u32[]{:S(2)}) %collective-permute-start) | collective-permute-done | bytes 532512 | tf_op jit(solution)/shard_map/ppermute | solution.py:76
  18.5 1.9 %collective-permute-start.10 = (bf16[768,512]{1,0:T(8,128)(2,1)}, bf16[768,512]{1,0:T(8,128)(2,1)}, u32[]{:S(2)}, u32[]{:S(2)}) collective-permute-start(bf16[768,512]{1,0:T(8,128)(2,1)} %get-tuple-element.26), channel_id=1, source_target_pairs={{8,0},{16,8},{24,16},{9,1},{17,9},{25,17},{10,2},{18,10},{26,18},{... | collective-permute-start | bytes 2359304 | tf_op jit(solution)/shard_map/ppermute | solution.py:726
  21.7 1.5 collective-permute-start.6
  23.2 3.6 %pack.2 = (bf16[4,2,2,512,128]{4,3,2,1,0:T(8,128)(2,1)}, bf16[4,1,2,512,128]{4,3,2,1,0:T(8,128)(2,1)}) custom-call(s32[1]{0:T(128)} %bitcast.11.me, s32[16]{0:T(128)} %bitcast.34, bf16[16,2,512,128]{3,2,1,0:T(8,128)(2,1)} %basis.3, bf16[1040,256]{1,0:T(8,128)(2,1)} %copy-done.2), custom_call_target="tpu_custom_call" | custom-call | tf_op jit(solution)/shard_map/pack/pallas_call | solution.py:119
  27.4 2.8 %collective-permute-done.10.v_high.refs_4_ = bf16[768,512]{1,0:T(8,128)(2,1)} collective-permute-done((bf16[768,512]{1,0:T(8,128)(2,1)}, bf16[768,512]{1,0:T(8,128)(2,1)}, u32[]{:S(2)}, u32[]{:S(2)}) %collective-permute-start.10) | collective-permute-done | bytes 786464 | tf_op jit(solution)/shard_map/ppermute | solution.py:726
  30.2 9.6 %collective-permute-done.13.refs_5_ = bf16[4,1,2,512,128]{4,3,2,1,0:T(8,128)(2,1)S(1)} collective-permute-done((bf16[4,1,2,512,128]{4,3,2,1,0:T(8,128)(2,1)}, bf16[4,1,2,512,128]{4,3,2,1,0:T(8,128)(2,1)S(1)}, u32[]{:S(2)}, u32[]{:S(2)}) %collective-permute-start.13) | collective-permute-done | bytes 1048608 | tf_op jit(solution)/shard_map/ppermute | solution.py:76
  40.8 4.9 %all-to-all-start = ((bf16[4,2,2,512,128]{4,3,2,1,0:T(8,128)(2,1)}), bf16[4,2,2,512,128]{4,3,2,1,0:T(8,128)(2,1)}, u32[]{:S(2)}, u32[]{:S(2)}) async-start(bf16[4,2,2,512,128]{4,3,2,1,0:T(8,128)(2,1)} %after.2), calls=%async_computation | async-start | bytes 4194304 | tf_op jit(solution)/shard_map/all_to_all | solution.py:158
  45.7 1.5 collective-permute-start.14
  50.4 1.6 collective-permute-start.5
  52.9 29.6 %collective-permute-done.7.refs_2_ = bf16[1040,256]{1,0:T(8,128)(2,1)} collective-permute-done((bf16[1040,256]{1,0:T(8,128)(2,1)}, bf16[1040,256]{1,0:T(8,128)(2,1)}, u32[]{:S(2)}, u32[]{:S(2)}) %collective-permute-start.7) | collective-permute-done | bytes 532512 | tf_op jit(solution)/shard_map/ppermute | solution.py:185
  82.5 2.1 %add.190.refs_6_ = bf16[1040,256]{1,0:T(8,128)(2,1)} add(bf16[1040,256]{1,0:T(8,128)(2,1)} %collective-permute-done.6.refs_1_, bf16[1040,256]{1,0:T(8,128)(2,1)} %collective-permute-done.7.refs_2_) | non-fusion elementwise | flops 266240 | bytes 1597440 | tf_op jit(solution)/shard_map/add | solution.py:199
  84.7 1.5 collective-permute-start.8
  86.2 2.8 %pad_maximum_fusion.refs_0_ = bf16[4,2,2,512,128]{4,3,2,1,0:T(8,128)(2,1)} fusion(bf16[4,1,2,512,128]{4,3,2,1,0:T(8,128)(2,1)} %collective-permute-done.14, bf16[4,1,2,512,128]{4,3,2,1,0:T(8,128)(2,1)S(1)} %copy-done.4), kind=kLoop, calls=%fused_computation | loop fusion | flops 1048576 | bytes 4194304 | tf_op jit(solution)/shard_map/concatenate | solution.py:157
  89.0 5.8 %collective-permute-done.5.refs_5_ = bf16[1040,256]{1,0:T(8,128)(2,1)S(1)} collective-permute-done((bf16[1040,256]{1,0:T(8,128)(2,1)S(1)}, bf16[1040,256]{1,0:T(8,128)(2,1)S(1)}, u32[]{:S(2)}, u32[]{:S(2)}) %collective-permute-start.5) | collective-permute-done | bytes 532512 | tf_op jit(solution)/shard_map/ppermute | solution.py:76
  95.6 9.8 %all-to-all-start.1 = ((bf16[4,2,2,512,128]{4,3,2,1,0:T(8,128)(2,1)}), bf16[4,2,2,512,128]{4,3,2,1,0:T(8,128)(2,1)}, u32[]{:S(2)}, u32[]{:S(2)}) async-start(bf16[4,2,2,512,128]{4,3,2,1,0:T(8,128)(2,1)} %after.3), calls=%async_computation.1 | async-start | bytes 4194304 | tf_op jit(solution)/shard_map/all_to_all | solution.py:158
  105.4 3.0 %edge_blocks.1 = (bf16[2,512,256]{2,1,0:T(8,128)(2,1)}, bf16[2,512,256]{2,1,0:T(8,128)(2,1)}, bf16[8,16,256]{2,1,0:T(8,128)(2,1)}) custom-call(s32[8]{0:T(128)} %stack.35.owners, bf16[1040,256]{1,0:T(8,128)(2,1)} %own_piece.1.refs_0_.first, bf16[1040,256]{1,0:T(8,128)(2,1)} %copy-done.2, bf16[1040,256]{1,0:T(8,128)(2,1)} %collective-permute-done.1.refs_2_, ...), custom_call_target="tpu_custom_call" | custom-call | tf_op jit(solution)/shard_map/edge_blocks/pallas_call | solution.py:248
  110.5 1.9 %collective-permute-start.11 = (bf16[2,512,256]{2,1,0:T(8,128)(2,1)}, bf16[2,512,256]{2,1,0:T(8,128)(2,1)S(1)}, u32[]{:S(2)}, u32[]{:S(2)}) collective-permute-start(bf16[2,512,256]{2,1,0:T(8,128)(2,1)} %get-tuple-element.13.h_last), channel_id=1, source_target_pairs={{0,8},{8,16},{16,24},{1,9},{9,17},{17,25},{2,10},{10,18},{18,26},{... | collective-permute-start | bytes 1572872 | tf_op jit(solution)/shard_map/ppermute | solution.py:726
  112.5 3.6 %collective-permute-start.12 = (bf16[2,512,256]{2,1,0:T(8,128)(2,1)}, bf16[2,512,256]{2,1,0:T(8,128)(2,1)S(1)}, u32[]{:S(2)}, u32[]{:S(2)}) collective-permute-start(bf16[2,512,256]{2,1,0:T(8,128)(2,1)} %get-tuple-element.14.h_first), channel_id=1, source_target_pairs={{8,0},{16,8},{24,16},{9,1},{17,9},{25,17},{10,2},{18,10},{26,18},{... | collective-permute-start | bytes 1572872 | tf_op jit(solution)/shard_map/ppermute | solution.py:726
  117.9 16.4 %chebyshev_inner.1 = (bf16[8,512,512]{2,1,0:T(8,128)(2,1)}, bf16[1024,512]{1,0:T(8,128)(2,1)}, bf16[1024,512]{1,0:T(8,128)(2,1)}, f32[1024,512]{1,0:T(8,128)}) custom-call(f32[4]{0:T(128)} %coef.3, s32[8]{0:T(128)} %stack.35.owners, bf16[768,512]{1,0:T(8,128)(2,1)} %collective-permute-done.9.v_low.refs_3_, bf16[4096,512]{1,0:T(8,128)(2,1)} %v_mid.3, ...), custom_call_target="tpu_custom_call" | custom-call | flops 8455716864 | bytes 16777216 | tf_op jit(solution)/shard_map/chebyshev_inner/pallas_call | solution.py:373
  135.3 7.1 %chebyshev_outer.1.kernel_t = bf16[8,512,512]{2,1,0:T(8,128)(2,1)} custom-call(f32[4]{0:T(128)} %coef.3, bf16[8,512,512]{2,1,0:T(8,128)(2,1)} %get-tuple-element.12.kernel_in, bf16[768,512]{1,0:T(8,128)(2,1)} %collective-permute-done.9.v_low.refs_3_, bf16[4096,512]{1,0:T(8,128)(2,1)} %v_mid.3, ...), custom_call_target="tpu_custom_call", output_to_operand_aliasing={{}: (1, {})} | custom-call | tf_op jit(solution)/shard_map/chebyshev_outer/pallas_call | solution.py:491
  142.3 10.8 %all-to-all-done.1 = bf16[4,2,2,512,128]{4,3,2,1,0:T(8,128)(2,1)} async-done(((bf16[4,2,2,512,128]{4,3,2,1,0:T(8,128)(2,1)}), bf16[4,2,2,512,128]{4,3,2,1,0:T(8,128)(2,1)}, u32[]{:S(2)}, u32[]{:S(2)}) %all-to-all-start.1) | async-done | bytes 2097184 | tf_op jit(solution)/shard_map/all_to_all | solution.py:158
  153.1 5.2 %project.1 = f32[8,24,128]{2,1,0:T(8,128)} custom-call(s32[26]{0:T(128)} %pad_add_fusion.1.plan, s32[16]{0:T(128)} %select_reduce_fusion.2.order, bf16[8,512,512]{2,1,0:T(8,128)(2,1)} %chebyshev_outer.1.kernel_t, f32[4,128]{1,0:T(4,128)} %core.1, bf16[8,2,512,128]{3,2,1,0:T(8,128)(2,1)} %bitcast.12.refs_0_, bf16[8,2,512,128]{3,2,1,0:T(8,128)(2,1)} %bitcast.13.refs_1_), custom_call_target="tpu_custom_call" | custom-call | tf_op jit(solution)/shard_map/project/pallas_call | solution.py:603
  158.3 3.4 %all-to-all-start.2 = ((f32[8,24,128]{2,1,0:T(8,128)}), f32[8,24,128]{2,1,0:T(8,128)S(1)}, u32[]{:S(2)}, u32[]{:S(2)}) async-start(f32[8,24,128]{2,1,0:T(8,128)} %project.1), calls=%async_computation.2 | async-start | bytes 196608 | tf_op jit(solution)/shard_map/all_to_all | solution.py:807
  161.8 6.9 %all-to-all-done.2 = f32[8,24,128]{2,1,0:T(8,128)S(1)} async-done(((f32[8,24,128]{2,1,0:T(8,128)}), f32[8,24,128]{2,1,0:T(8,128)S(1)}, u32[]{:S(2)}, u32[]{:S(2)}) %all-to-all-start.2) | async-done | bytes 98336 | tf_op jit(solution)/shard_map/all_to_all | solution.py:807
  168.8 6.7 %update.1 = (f32[4,128]{1,0:T(4,128)}, bf16[4096,512]{1,0:T(8,128)(2,1)}) custom-call(s32[26]{0:T(128)S(1)} %copy-done, s32[16]{0:T(128)S(1)} %copy-done.1, s32[16]{0:T(128)S(1)} %reshape.285.tile_of, f32[192,128]{1,0:T(8,128)S(1)} %bitcast.26, f32[32,192]{1,0:T(8,128)S(1)} %convert_reduce_fusion.collect, bf16[8,2,512,128]{3,2,1,0:T(8,128)(2,1)} %bitcast.12.refs_0_, ...), custom_call_target="tpu_custom_call" | custom-call | tf_op jit(solution)/shard_map/update/pallas_call | solution.py:701
  (80 shorter events, 13.3 us)
Async XLA Ops:
  3.2 15.3 %collective-permute-start = (bf16[1040,256]{1,0:T(8,128)(2,1)}, bf16[1040,256]{1,0:T(8,128)(2,1)S(1)}, u32[]{:S(2)}, u32[]{:S(2)}) collective-permute-start(bf16[1040,256]{1,0:T(8,128)(2,1)} %own_piece.1.refs_0_.first), channel_id=1, source_target_pairs={{0,1},{1,0},{2,3},{3,2},{4,5},{5,4},{6,7},{7,6},{8,9},{9,8},{10,11... | collective-permute-start | bytes 1597448 | tf_op jit(solution)/shard_map/ppermute | solution.py:76
  4.8 16.9 %collective-permute-start.1 = (bf16[1040,256]{1,0:T(8,128)(2,1)}, bf16[1040,256]{1,0:T(8,128)(2,1)}, u32[]{:S(2)}, u32[]{:S(2)}) collective-permute-start(bf16[1040,256]{1,0:T(8,128)(2,1)} %own_piece.1.refs_0_.first), channel_id=1, source_target_pairs={{0,2},{1,3},{2,0},{3,1},{4,6},{5,7},{6,4},{7,5},{8,10},{9,11},{10,... | collective-permute-start | bytes 1597448 | tf_op jit(solution)/shard_map/ppermute | solution.py:185
  6.4 14.0 %collective-permute-start.3 = (bf16[1040,256]{1,0:T(8,128)(2,1)}, bf16[1040,256]{1,0:T(8,128)(2,1)}, u32[]{:S(2)}, u32[]{:S(2)}) collective-permute-start(bf16[1040,256]{1,0:T(8,128)(2,1)} %own_piece.1.refs_0_.first), channel_id=1, source_target_pairs={{2,4},{3,5},{4,2},{5,3},{10,12},{11,13},{12,10},{13,11},{18,20},{1... | collective-permute-start | bytes 1597448 | tf_op jit(solution)/shard_map/ppermute | solution.py:185
  10.6 29.2 %collective-permute-start.13 = (bf16[4,1,2,512,128]{4,3,2,1,0:T(8,128)(2,1)}, bf16[4,1,2,512,128]{4,3,2,1,0:T(8,128)(2,1)S(1)}, u32[]{:S(2)}, u32[]{:S(2)}) collective-permute-start(bf16[4,1,2,512,128]{4,3,2,1,0:T(8,128)(2,1)} %pack.3), channel_id=1, source_target_pairs={{0,1},{1,0},{2,3},{3,2},{4,5},{5,4},{6,7},{7,6},{8,9},{9,8},{10,11... | collective-permute-start | bytes 3145736 | tf_op jit(solution)/shard_map/ppermute | solution.py:76
  13.8 13.6 %collective-permute-start.9 = (bf16[768,512]{1,0:T(8,128)(2,1)}, bf16[768,512]{1,0:T(8,128)(2,1)}, u32[]{:S(2)}, u32[]{:S(2)}) collective-permute-start(bf16[768,512]{1,0:T(8,128)(2,1)} %get-tuple-element.27), channel_id=1, source_target_pairs={{0,8},{8,16},{16,24},{1,9},{9,17},{17,25},{2,10},{10,18},{18,26},{... | collective-permute-start | bytes 2359304 | tf_op jit(solution)/shard_map/ppermute | solution.py:726
  18.5 4.7 %copy-start.2 = (bf16[1040,256]{1,0:T(8,128)(2,1)}, bf16[1040,256]{1,0:T(8,128)(2,1)S(1)}, u32[]{:S(2)}) copy-start(bf16[1040,256]{1,0:T(8,128)(2,1)S(1)} %collective-permute-done.refs_1_.first.refs_3_) | copy-start | bytes 1597444
  18.5 11.7 %collective-permute-start.10 = (bf16[768,512]{1,0:T(8,128)(2,1)}, bf16[768,512]{1,0:T(8,128)(2,1)}, u32[]{:S(2)}, u32[]{:S(2)}) collective-permute-start(bf16[768,512]{1,0:T(8,128)(2,1)} %get-tuple-element.26), channel_id=1, source_target_pairs={{8,0},{16,8},{24,16},{9,1},{17,9},{25,17},{10,2},{18,10},{26,18},{... | collective-permute-start | bytes 2359304 | tf_op jit(solution)/shard_map/ppermute | solution.py:726
  20.4 19.4 %collective-permute-start.4 = (bf16[1040,256]{1,0:T(8,128)(2,1)}, bf16[1040,256]{1,0:T(8,128)(2,1)}, u32[]{:S(2)}, u32[]{:S(2)}) collective-permute-start(bf16[1040,256]{1,0:T(8,128)(2,1)} %collective-permute-done.3), channel_id=1, source_target_pairs={{2,0},{3,1},{4,6},{5,7},{10,8},{11,9},{12,14},{13,15},{18,16},{19,... | collective-permute-start | bytes 1597448 | tf_op jit(solution)/shard_map/ppermute | solution.py:185
  21.7 18.1 %collective-permute-start.6 = (bf16[1040,256]{1,0:T(8,128)(2,1)}, bf16[1040,256]{1,0:T(8,128)(2,1)}, u32[]{:S(2)}, u32[]{:S(2)}) collective-permute-start(bf16[1040,256]{1,0:T(8,128)(2,1)} %collective-permute-done.1.refs_2_), channel_id=1, source_target_pairs={{2,4},{3,5},{4,2},{5,3},{10,12},{11,13},{12,10},{13,11},{18,20},{1... | collective-permute-start | bytes 1597448 | tf_op jit(solution)/shard_map/ppermute | solution.py:185
  39.8 1.0 copy-start.3
  40.8 54.2 %all-to-all-start = ((bf16[4,2,2,512,128]{4,3,2,1,0:T(8,128)(2,1)}), bf16[4,2,2,512,128]{4,3,2,1,0:T(8,128)(2,1)}, u32[]{:S(2)}, u32[]{:S(2)}) async-start(bf16[4,2,2,512,128]{4,3,2,1,0:T(8,128)(2,1)} %after.2), calls=%async_computation | async-start | bytes 4194304 | tf_op jit(solution)/shard_map/all_to_all | solution.py:158
  45.7 40.5 %copy-start.4 = (bf16[4,1,2,512,128]{4,3,2,1,0:T(8,128)(2,1)S(1)}, bf16[4,1,2,512,128]{4,3,2,1,0:T(8,128)(2,1)}, u32[]{:S(2)}) copy-start(bf16[4,1,2,512,128]{4,3,2,1,0:T(8,128)(2,1)} %copy-done.3) | copy-start | bytes 3145732
  45.7 40.5 %collective-permute-start.14 = (bf16[4,1,2,512,128]{4,3,2,1,0:T(8,128)(2,1)}, bf16[4,1,2,512,128]{4,3,2,1,0:T(8,128)(2,1)}, u32[]{:S(2)}, u32[]{:S(2)}) collective-permute-start(bf16[4,1,2,512,128]{4,3,2,1,0:T(8,128)(2,1)} %get-tuple-element.19), channel_id=1, source_target_pairs={{0,1},{1,0},{2,3},{3,2},{4,5},{5,4},{6,7},{7,6},{8,9},{9,8},{10,11... | collective-permute-start | bytes 3145736 | tf_op jit(solution)/shard_map/ppermute | solution.py:76
  47.2 35.3 %collective-permute-start.7 = (bf16[1040,256]{1,0:T(8,128)(2,1)}, bf16[1040,256]{1,0:T(8,128)(2,1)}, u32[]{:S(2)}, u32[]{:S(2)}) collective-permute-start(bf16[1040,256]{1,0:T(8,128)(2,1)} %collective-permute-done.6.refs_1_), channel_id=1, source_target_pairs={{2,0},{3,1},{4,6},{5,7},{10,8},{11,9},{12,14},{13,15},{18,16},{19,... | collective-permute-start | bytes 1597448 | tf_op jit(solution)/shard_map/ppermute | solution.py:185
  48.5 40.5 %collective-permute-start.2 = (bf16[1040,256]{1,0:T(8,128)(2,1)}, bf16[1040,256]{1,0:T(8,128)(2,1)S(1)}, u32[]{:S(2)}, u32[]{:S(2)}) collective-permute-start(bf16[1040,256]{1,0:T(8,128)(2,1)} %collective-permute-done.1.refs_2_), channel_id=1, source_target_pairs={{0,1},{1,0},{2,3},{3,2},{4,5},{5,4},{6,7},{7,6},{8,9},{9,8},{10,11... | collective-permute-start | bytes 1597448 | tf_op jit(solution)/shard_map/ppermute | solution.py:76
  50.4 38.5 %copy-start.7 = (bf16[1040,256]{1,0:T(8,128)(2,1)}, bf16[1040,256]{1,0:T(8,128)(2,1)S(1)}, u32[]{:S(2)}) copy-start(bf16[1040,256]{1,0:T(8,128)(2,1)S(1)} %add.189.refs_4_) | copy-start | bytes 1597444
  50.4 44.3 %collective-permute-start.5 = (bf16[1040,256]{1,0:T(8,128)(2,1)S(1)}, bf16[1040,256]{1,0:T(8,128)(2,1)S(1)}, u32[]{:S(2)}, u32[]{:S(2)}) collective-permute-start(bf16[1040,256]{1,0:T(8,128)(2,1)S(1)} %add.189.refs_4_), channel_id=1, source_target_pairs={{0,1},{1,0},{2,3},{3,2},{4,5},{5,4},{6,7},{7,6},{8,9},{9,8},{10,11... | collective-permute-start | bytes 1597448 | tf_op jit(solution)/shard_map/ppermute | solution.py:76
  84.7 20.8 %collective-permute-start.8 = (bf16[1040,256]{1,0:T(8,128)(2,1)}, bf16[1040,256]{1,0:T(8,128)(2,1)}, u32[]{:S(2)}, u32[]{:S(2)}) collective-permute-start(bf16[1040,256]{1,0:T(8,128)(2,1)} %add.190.refs_6_), channel_id=1, source_target_pairs={{0,1},{1,0},{2,3},{3,2},{4,5},{5,4},{6,7},{7,6},{8,9},{9,8},{10,11... | collective-permute-start | bytes 1597448 | tf_op jit(solution)/shard_map/ppermute | solution.py:76
  89.0 6.1 %copy-start.5 = (bf16[1040,256]{1,0:T(8,128)(2,1)}, bf16[1040,256]{1,0:T(8,128)(2,1)S(1)}, u32[]{:S(2)}) copy-start(bf16[1040,256]{1,0:T(8,128)(2,1)S(1)} %collective-permute-done.2.refs_3_.refs_4_) | copy-start | bytes 1597444
  94.8 0.8 copy-start.6
  95.6 57.6 %all-to-all-start.1 = ((bf16[4,2,2,512,128]{4,3,2,1,0:T(8,128)(2,1)}), bf16[4,2,2,512,128]{4,3,2,1,0:T(8,128)(2,1)}, u32[]{:S(2)}, u32[]{:S(2)}) async-start(bf16[4,2,2,512,128]{4,3,2,1,0:T(8,128)(2,1)} %after.3), calls=%async_computation.1 | async-start | bytes 4194304 | tf_op jit(solution)/shard_map/all_to_all | solution.py:158
  110.5 23.7 %collective-permute-start.11 = (bf16[2,512,256]{2,1,0:T(8,128)(2,1)}, bf16[2,512,256]{2,1,0:T(8,128)(2,1)S(1)}, u32[]{:S(2)}, u32[]{:S(2)}) collective-permute-start(bf16[2,512,256]{2,1,0:T(8,128)(2,1)} %get-tuple-element.13.h_last), channel_id=1, source_target_pairs={{0,8},{8,16},{16,24},{1,9},{9,17},{17,25},{2,10},{10,18},{18,26},{... | collective-permute-start | bytes 1572872 | tf_op jit(solution)/shard_map/ppermute | solution.py:726
  112.5 21.8 %collective-permute-start.12 = (bf16[2,512,256]{2,1,0:T(8,128)(2,1)}, bf16[2,512,256]{2,1,0:T(8,128)(2,1)S(1)}, u32[]{:S(2)}, u32[]{:S(2)}) collective-permute-start(bf16[2,512,256]{2,1,0:T(8,128)(2,1)} %get-tuple-element.14.h_first), channel_id=1, source_target_pairs={{8,0},{16,8},{24,16},{9,1},{17,9},{25,17},{10,2},{18,10},{26,18},{... | collective-permute-start | bytes 1572872 | tf_op jit(solution)/shard_map/ppermute | solution.py:726
  134.2 0.8 copy-start.8
  134.3 1.0 copy-start.9
  153.1 15.6 %copy-start = (s32[26]{0:T(128)S(1)}, s32[26]{0:T(128)}, u32[]{:S(2)}) copy-start(s32[26]{0:T(128)} %pad_add_fusion.1.plan) | copy-start | bytes 316
  153.1 15.6 %copy-start.1 = (s32[16]{0:T(128)S(1)}, s32[16]{0:T(128)}, u32[]{:S(2)}) copy-start(s32[16]{0:T(128)} %select_reduce_fusion.2.order) | copy-start | bytes 196
  158.3 10.4 %all-to-all-start.2 = ((f32[8,24,128]{2,1,0:T(8,128)}), f32[8,24,128]{2,1,0:T(8,128)S(1)}, u32[]{:S(2)}, u32[]{:S(2)}) async-start(f32[8,24,128]{2,1,0:T(8,128)} %project.1), calls=%async_computation.2 | async-start | bytes 196608 | tf_op jit(solution)/shard_map/all_to_all | solution.py:807

commit v11 on v10

--- a/solution.py
+++ b/solution.py
@@ -143,7 +143,7 @@
         in_specs=[HBM] + [ANY] * len(others),
         out_specs=HBM,
         input_output_aliases={0: 0},
-        compiler_params=pltpu.CompilerParams(vmem_limit_bytes=62 * MIB),
+        compiler_params=pltpu.CompilerParams(vmem_limit_bytes=59 * MIB),
         name="after",
     )(block, *others)
 

time: 177 us -> 173 us (0.977)
  waiting for transfers between devices: 69.2 us -> 61.9 us
  local copies, waits for them, and re-layouts: 7.54 us -> 10.5 us
    all_to_all x2, waiting for transfers between devices: 11.1 us -> 4.47 us  [between_lines(): lax.all_to_all(after(block, *others), 'col', split_axis=0, concat_axis=0,...]
    unnamed x22 -> x26, local copies, waits for them, and re-layouts: 2.56 us -> 5.54 us
  transfers between devices with their start and end apart: 18 -> 18, of which waited for: 9 -> 8; matrix products, arithmetic and copies ran while one was open for 8% -> 9% of each run, Pallas kernels for 19% -> 19%
where the time goes in v11:
time: 173 us; the launch traced here: 172 us
  waiting for transfers between devices  61.9 us (36%)
  Pallas kernels  48.1 us (28%)
  starting transfers between devices  40.8 us (24%)
  local copies, waits for them, and re-layouts  10.5 us (6%)
  other arithmetic  9.75 us (6%)
    ppermute x5, waiting for transfers between devices, move(): return lax.ppermute(block, 'col', pairs)  29.2 us
    ppermute x6, waiting for transfers between devices, swap_along(): return lax.ppermute(block, 'col', pairs)  17.9 us
    pallas_call x1, Pallas kernels, chebyshev_inner(): pl.pallas_call(functools.partial(inner_kernel, blocks), out_shape=(jax.Sh...  16.4 us
    all_to_all x2, starting transfers between devices, between_lines(): lax.all_to_all(after(block, *others), 'col', split_axis=0, concat_axis=0,...  13.6 us
    ppermute x4, starting transfers between devices, shift(): return lax.ppermute(block, axis, pairs)  9.38 us
    ppermute x6, starting transfers between devices, swap_along(): return lax.ppermute(block, 'col', pairs)  7.29 us
    pallas_call x1, Pallas kernels, update(): pl.pallas_call(functools.partial(update_kernel, blocks, tiles), out_shape...  7.25 us
    ppermute x5, starting transfers between devices, move(): return lax.ppermute(block, 'col', pairs)  7.11 us
  transfers between devices with their start and end apart: 18, of which 8 were waited for; matrix products, arithmetic and copies ran while one was open for 9% of the time, Pallas kernels for 19%

profile of v11, /device:TPU:2, one launch (start us, length us, event | category | flops | bytes accessed | tf_op | source)
XLA Modules:
  0.0 171.8 jit_solution(10446483118668366179)
XLA Ops:
  0.6 2.6 %own_piece.1.refs_0_.first = bf16[1040,256]{1,0:T(8,128)(2,1)} custom-call(s32[16]{0:T(128)} %bitcast.34, s32[16]{0:T(128)} %named.1, s32[4]{0:T(128)} %counts.1, s32[2]{0:T(128)} %pattern.1, bf16[1024,256]{1,0:T(8,128)(2,1)} %bitcast.29), custom_call_target="tpu_custom_call" | custom-call | tf_op jit(solution)/shard_map/own_piece/pallas_call | solution.py:56
  3.2 1.6 collective-permute-start
  4.8 1.6 collective-permute-start.1
  7.8 2.7 %pack.3 = bf16[4,1,2,512,128]{4,3,2,1,0:T(8,128)(2,1)} custom-call(s32[1]{0:T(128)} %bitcast.11.me, s32[16]{0:T(128)} %bitcast.35, bf16[16,2,512,128]{3,2,1,0:T(8,128)(2,1)} %basis.3, bf16[1040,256]{1,0:T(8,128)(2,1)} %own_piece.1.refs_0_.first), custom_call_target="tpu_custom_call" | custom-call | tf_op jit(solution)/shard_map/pack/pallas_call | solution.py:119
  11.2 2.6 %fusion.12 = (bf16[768,512]{1,0:T(8,128)(2,1)}, bf16[768,512]{1,0:T(8,128)(2,1)}) fusion(bf16[4096,512]{1,0:T(8,128)(2,1)} %v_mid.3), kind=kLoop, calls=%fused_computation.55 | loop fusion | bytes 3145728 | tf_op jit(solution)/shard_map/slice | solution.py:794
  13.8 1.9 %collective-permute-start.9 = (bf16[768,512]{1,0:T(8,128)(2,1)}, bf16[768,512]{1,0:T(8,128)(2,1)S(1)}, u32[]{:S(2)}, u32[]{:S(2)}) collective-permute-start(bf16[768,512]{1,0:T(8,128)(2,1)} %get-tuple-element.27), channel_id=1, source_target_pairs={{0,8},{8,16},{16,24},{1,9},{9,17},{17,25},{2,10},{10,18},{18,26},{... | collective-permute-start | bytes 2359304 | tf_op jit(solution)/shard_map/ppermute | solution.py:726
  15.7 2.8 %collective-permute-done.refs_1_.first.refs_3_ = bf16[1040,256]{1,0:T(8,128)(2,1)S(1)} collective-permute-done((bf16[1040,256]{1,0:T(8,128)(2,1)}, bf16[1040,256]{1,0:T(8,128)(2,1)S(1)}, u32[]{:S(2)}, u32[]{:S(2)}) %collective-permute-start) | collective-permute-done | bytes 532512 | tf_op jit(solution)/shard_map/ppermute | solution.py:76
  18.5 1.9 %collective-permute-start.10 = (bf16[768,512]{1,0:T(8,128)(2,1)}, bf16[768,512]{1,0:T(8,128)(2,1)}, u32[]{:S(2)}, u32[]{:S(2)}) collective-permute-start(bf16[768,512]{1,0:T(8,128)(2,1)} %get-tuple-element.26), channel_id=1, source_target_pairs={{8,0},{16,8},{24,16},{9,1},{17,9},{25,17},{10,2},{18,10},{26,18},{... | collective-permute-start | bytes 2359304 | tf_op jit(solution)/shard_map/ppermute | solution.py:726
  23.2 3.6 %pack.2 = (bf16[4,2,2,512,128]{4,3,2,1,0:T(8,128)(2,1)}, bf16[4,1,2,512,128]{4,3,2,1,0:T(8,128)(2,1)}) custom-call(s32[1]{0:T(128)} %bitcast.11.me, s32[16]{0:T(128)} %bitcast.36, bf16[16,2,512,128]{3,2,1,0:T(8,128)(2,1)} %basis.3, bf16[1040,256]{1,0:T(8,128)(2,1)} %copy-done.4), custom_call_target="tpu_custom_call" | custom-call | tf_op jit(solution)/shard_map/pack/pallas_call | solution.py:119
  27.3 2.9 %collective-permute-done.10.v_high.refs_4_ = bf16[768,512]{1,0:T(8,128)(2,1)} collective-permute-done((bf16[768,512]{1,0:T(8,128)(2,1)}, bf16[768,512]{1,0:T(8,128)(2,1)}, u32[]{:S(2)}, u32[]{:S(2)}) %collective-permute-start.10) | collective-permute-done | bytes 786464 | tf_op jit(solution)/shard_map/ppermute | solution.py:726
  30.2 9.7 %collective-permute-done.13.refs_5_ = bf16[4,1,2,512,128]{4,3,2,1,0:T(8,128)(2,1)} collective-permute-done((bf16[4,1,2,512,128]{4,3,2,1,0:T(8,128)(2,1)}, bf16[4,1,2,512,128]{4,3,2,1,0:T(8,128)(2,1)}, u32[]{:S(2)}, u32[]{:S(2)}) %collective-permute-start.13) | collective-permute-done | bytes 1048608 | tf_op jit(solution)/shard_map/ppermute | solution.py:76
  40.7 5.0 %all-to-all-start = ((bf16[4,2,2,512,128]{4,3,2,1,0:T(8,128)(2,1)}), bf16[4,2,2,512,128]{4,3,2,1,0:T(8,128)(2,1)S(1)}, u32[]{:S(2)}, u32[]{:S(2)}) async-start(bf16[4,2,2,512,128]{4,3,2,1,0:T(8,128)(2,1)} %after.2), calls=%async_computation | async-start | bytes 4194304 | tf_op jit(solution)/shard_map/all_to_all | solution.py:158
  45.7 1.5 collective-permute-start.14
  49.1 2.0 %add.189.refs_4_ = bf16[1040,256]{1,0:T(8,128)(2,1)} add(bf16[1040,256]{1,0:T(8,128)(2,1)} %collective-permute-done.3, bf16[1040,256]{1,0:T(8,128)(2,1)S(1)} %copy-done.9) | non-fusion elementwise | flops 266240 | bytes 1597440 | tf_op jit(solution)/shard_map/add | solution.py:198
  51.2 1.5 collective-permute-start.5
  53.5 29.1 %collective-permute-done.7.refs_2_ = bf16[1040,256]{1,0:T(8,128)(2,1)} collective-permute-done((bf16[1040,256]{1,0:T(8,128)(2,1)}, bf16[1040,256]{1,0:T(8,128)(2,1)}, u32[]{:S(2)}, u32[]{:S(2)}) %collective-permute-start.7) | collective-permute-done | bytes 532512 | tf_op jit(solution)/shard_map/ppermute | solution.py:185
  82.7 2.1 %add.190.refs_6_ = bf16[1040,256]{1,0:T(8,128)(2,1)} add(bf16[1040,256]{1,0:T(8,128)(2,1)} %collective-permute-done.6.refs_1_, bf16[1040,256]{1,0:T(8,128)(2,1)} %collective-permute-done.7.refs_2_) | non-fusion elementwise | flops 266240 | bytes 1597440 | tf_op jit(solution)/shard_map/add | solution.py:199
  84.8 1.5 collective-permute-start.8
  86.3 3.1 %pad_maximum_fusion.refs_0_ = bf16[4,2,2,512,128]{4,3,2,1,0:T(8,128)(2,1)} fusion(bf16[4,1,2,512,128]{4,3,2,1,0:T(8,128)(2,1)} %collective-permute-done.14, bf16[4,1,2,512,128]{4,3,2,1,0:T(8,128)(2,1)} %collective-permute-done.13.refs_5_), kind=kLoop, calls=%fused_computation | loop fusion | flops 1048576 | bytes 4194304 | tf_op jit(solution)/shard_map/concatenate | solution.py:157
  89.4 5.4 %collective-permute-done.5.refs_5_ = bf16[1040,256]{1,0:T(8,128)(2,1)S(1)} collective-permute-done((bf16[1040,256]{1,0:T(8,128)(2,1)}, bf16[1040,256]{1,0:T(8,128)(2,1)S(1)}, u32[]{:S(2)}, u32[]{:S(2)}) %collective-permute-start.5) | collective-permute-done | bytes 532512 | tf_op jit(solution)/shard_map/ppermute | solution.py:76
  97.0 8.6 %all-to-all-start.1 = ((bf16[4,2,2,512,128]{4,3,2,1,0:T(8,128)(2,1)}), bf16[4,2,2,512,128]{4,3,2,1,0:T(8,128)(2,1)}, u32[]{:S(2)}, u32[]{:S(2)}) async-start(bf16[4,2,2,512,128]{4,3,2,1,0:T(8,128)(2,1)} %after.3), calls=%async_computation.1 | async-start | bytes 4194304 | tf_op jit(solution)/shard_map/all_to_all | solution.py:158
  105.7 3.1 %edge_blocks.1 = (bf16[2,512,256]{2,1,0:T(8,128)(2,1)}, bf16[2,512,256]{2,1,0:T(8,128)(2,1)}, bf16[8,16,256]{2,1,0:T(8,128)(2,1)}) custom-call(s32[8]{0:T(128)} %stack.35.owners, bf16[1040,256]{1,0:T(8,128)(2,1)} %own_piece.1.refs_0_.first, bf16[1040,256]{1,0:T(8,128)(2,1)} %copy-done.4, bf16[1040,256]{1,0:T(8,128)(2,1)} %collective-permute-done.1.refs_2_, ...), custom_call_target="tpu_custom_call" | custom-call | tf_op jit(solution)/shard_map/edge_blocks/pallas_call | solution.py:248
  110.8 1.9 %collective-permute-start.11 = (bf16[2,512,256]{2,1,0:T(8,128)(2,1)}, bf16[2,512,256]{2,1,0:T(8,128)(2,1)S(1)}, u32[]{:S(2)}, u32[]{:S(2)}) collective-permute-start(bf16[2,512,256]{2,1,0:T(8,128)(2,1)} %get-tuple-element.13.h_last), channel_id=1, source_target_pairs={{0,8},{8,16},{16,24},{1,9},{9,17},{17,25},{2,10},{10,18},{18,26},{... | collective-permute-start | bytes 1572872 | tf_op jit(solution)/shard_map/ppermute | solution.py:726
  112.7 3.6 %collective-permute-start.12 = (bf16[2,512,256]{2,1,0:T(8,128)(2,1)}, bf16[2,512,256]{2,1,0:T(8,128)(2,1)S(1)}, u32[]{:S(2)}, u32[]{:S(2)}) collective-permute-start(bf16[2,512,256]{2,1,0:T(8,128)(2,1)} %get-tuple-element.14.h_first), channel_id=1, source_target_pairs={{8,0},{16,8},{24,16},{9,1},{17,9},{25,17},{10,2},{18,10},{26,18},{... | collective-permute-start | bytes 1572872 | tf_op jit(solution)/shard_map/ppermute | solution.py:726
  118.1 16.4 %chebyshev_inner.1 = (bf16[8,512,512]{2,1,0:T(8,128)(2,1)}, bf16[1024,512]{1,0:T(8,128)(2,1)}, bf16[1024,512]{1,0:T(8,128)(2,1)}, f32[1024,512]{1,0:T(8,128)}) custom-call(f32[4]{0:T(128)} %coef.3, s32[8]{0:T(128)} %stack.35.owners, bf16[768,512]{1,0:T(8,128)(2,1)} %copy-done.5, bf16[4096,512]{1,0:T(8,128)(2,1)} %v_mid.3, ...), custom_call_target="tpu_custom_call" | custom-call | flops 8455716864 | bytes 16777216 | tf_op jit(solution)/shard_map/chebyshev_inner/pallas_call | solution.py:373
  135.5 7.1 %chebyshev_outer.1.kernel_t = bf16[8,512,512]{2,1,0:T(8,128)(2,1)} custom-call(f32[4]{0:T(128)} %coef.3, bf16[8,512,512]{2,1,0:T(8,128)(2,1)} %get-tuple-element.12.kernel_in, bf16[768,512]{1,0:T(8,128)(2,1)} %copy-done.5, bf16[4096,512]{1,0:T(8,128)(2,1)} %v_mid.3, ...), custom_call_target="tpu_custom_call", output_to_operand_aliasing={{}: (1, {})} | custom-call | tf_op jit(solution)/shard_map/chebyshev_outer/pallas_call | solution.py:491
  142.6 4.5 %all-to-all-done.1 = bf16[4,2,2,512,128]{4,3,2,1,0:T(8,128)(2,1)} async-done(((bf16[4,2,2,512,128]{4,3,2,1,0:T(8,128)(2,1)}), bf16[4,2,2,512,128]{4,3,2,1,0:T(8,128)(2,1)}, u32[]{:S(2)}, u32[]{:S(2)}) %all-to-all-start.1) | async-done | bytes 2097184 | tf_op jit(solution)/shard_map/all_to_all | solution.py:158
  147.0 5.5 %project.1 = f32[8,24,128]{2,1,0:T(8,128)} custom-call(s32[26]{0:T(128)} %pad_add_fusion.1.plan, s32[16]{0:T(128)} %select_reduce_fusion.2.order, bf16[8,512,512]{2,1,0:T(8,128)(2,1)} %chebyshev_outer.1.kernel_t, f32[4,128]{1,0:T(4,128)} %core.1, bf16[8,2,512,128]{3,2,1,0:T(8,128)(2,1)} %bitcast.26, bf16[8,2,512,128]{3,2,1,0:T(8,128)(2,1)} %bitcast.13.refs_1_), custom_call_target="tpu_custom_call" | custom-call | tf_op jit(solution)/shard_map/project/pallas_call | solution.py:603
  152.5 3.4 %all-to-all-start.2 = ((f32[8,24,128]{2,1,0:T(8,128)}), f32[8,24,128]{2,1,0:T(8,128)S(1)}, u32[]{:S(2)}, u32[]{:S(2)}) async-start(f32[8,24,128]{2,1,0:T(8,128)} %project.1), calls=%async_computation.2 | async-start | bytes 196608 | tf_op jit(solution)/shard_map/all_to_all | solution.py:807
  156.0 6.9 %all-to-all-done.2 = f32[8,24,128]{2,1,0:T(8,128)S(1)} async-done(((f32[8,24,128]{2,1,0:T(8,128)}), f32[8,24,128]{2,1,0:T(8,128)S(1)}, u32[]{:S(2)}, u32[]{:S(2)}) %all-to-all-start.2) | async-done | bytes 98336 | tf_op jit(solution)/shard_map/all_to_all | solution.py:807
  163.0 1.6 copy-done.1
  164.6 7.3 %update.1 = (f32[4,128]{1,0:T(4,128)}, bf16[4096,512]{1,0:T(8,128)(2,1)}) custom-call(s32[26]{0:T(128)S(1)} %copy-done.2, s32[16]{0:T(128)S(1)} %copy-done.3, s32[16]{0:T(128)S(1)} %reshape.285.tile_of, f32[192,128]{1,0:T(8,128)S(1)} %bitcast.28, f32[32,192]{1,0:T(8,128)S(1)} %convert_reduce_fusion.collect, bf16[8,2,512,128]{3,2,1,0:T(8,128)(2,1)S(1)} %bitcast.27, ...), custom_call_target="tpu_custom_call" | custom-call | tf_op jit(solution)/shard_map/update/pallas_call | solution.py:701
  (84 shorter events, 15.9 us)
Async XLA Ops:
  3.2 15.3 %collective-permute-start = (bf16[1040,256]{1,0:T(8,128)(2,1)}, bf16[1040,256]{1,0:T(8,128)(2,1)S(1)}, u32[]{:S(2)}, u32[]{:S(2)}) collective-permute-start(bf16[1040,256]{1,0:T(8,128)(2,1)} %own_piece.1.refs_0_.first), channel_id=1, source_target_pairs={{0,1},{1,0},{2,3},{3,2},{4,5},{5,4},{6,7},{7,6},{8,9},{9,8},{10,11... | collective-permute-start | bytes 1597448 | tf_op jit(solution)/shard_map/ppermute | solution.py:76
  4.8 16.9 %collective-permute-start.1 = (bf16[1040,256]{1,0:T(8,128)(2,1)}, bf16[1040,256]{1,0:T(8,128)(2,1)}, u32[]{:S(2)}, u32[]{:S(2)}) collective-permute-start(bf16[1040,256]{1,0:T(8,128)(2,1)} %own_piece.1.refs_0_.first), channel_id=1, source_target_pairs={{0,2},{1,3},{2,0},{3,1},{4,6},{5,7},{6,4},{7,5},{8,10},{9,11},{10,... | collective-permute-start | bytes 1597448 | tf_op jit(solution)/shard_map/ppermute | solution.py:185
  6.4 14.0 %collective-permute-start.3 = (bf16[1040,256]{1,0:T(8,128)(2,1)}, bf16[1040,256]{1,0:T(8,128)(2,1)}, u32[]{:S(2)}, u32[]{:S(2)}) collective-permute-start(bf16[1040,256]{1,0:T(8,128)(2,1)} %own_piece.1.refs_0_.first), channel_id=1, source_target_pairs={{2,4},{3,5},{4,2},{5,3},{10,12},{11,13},{12,10},{13,11},{18,20},{1... | collective-permute-start | bytes 1597448 | tf_op jit(solution)/shard_map/ppermute | solution.py:185
  10.6 29.3 %collective-permute-start.13 = (bf16[4,1,2,512,128]{4,3,2,1,0:T(8,128)(2,1)}, bf16[4,1,2,512,128]{4,3,2,1,0:T(8,128)(2,1)}, u32[]{:S(2)}, u32[]{:S(2)}) collective-permute-start(bf16[4,1,2,512,128]{4,3,2,1,0:T(8,128)(2,1)} %pack.3), channel_id=1, source_target_pairs={{0,1},{1,0},{2,3},{3,2},{4,5},{5,4},{6,7},{7,6},{8,9},{9,8},{10,11... | collective-permute-start | bytes 3145736 | tf_op jit(solution)/shard_map/ppermute | solution.py:76
  13.8 13.5 %collective-permute-start.9 = (bf16[768,512]{1,0:T(8,128)(2,1)}, bf16[768,512]{1,0:T(8,128)(2,1)S(1)}, u32[]{:S(2)}, u32[]{:S(2)}) collective-permute-start(bf16[768,512]{1,0:T(8,128)(2,1)} %get-tuple-element.27), channel_id=1, source_target_pairs={{0,8},{8,16},{16,24},{1,9},{9,17},{17,25},{2,10},{10,18},{18,26},{... | collective-permute-start | bytes 2359304 | tf_op jit(solution)/shard_map/ppermute | solution.py:726
  18.5 4.7 %copy-start.4 = (bf16[1040,256]{1,0:T(8,128)(2,1)}, bf16[1040,256]{1,0:T(8,128)(2,1)S(1)}, u32[]{:S(2)}) copy-start(bf16[1040,256]{1,0:T(8,128)(2,1)S(1)} %collective-permute-done.refs_1_.first.refs_3_) | copy-start | bytes 1597444
  18.5 11.7 %collective-permute-start.10 = (bf16[768,512]{1,0:T(8,128)(2,1)}, bf16[768,512]{1,0:T(8,128)(2,1)}, u32[]{:S(2)}, u32[]{:S(2)}) collective-permute-start(bf16[768,512]{1,0:T(8,128)(2,1)} %get-tuple-element.26), channel_id=1, source_target_pairs={{8,0},{16,8},{24,16},{9,1},{17,9},{25,17},{10,2},{18,10},{26,18},{... | collective-permute-start | bytes 2359304 | tf_op jit(solution)/shard_map/ppermute | solution.py:726
  20.4 19.5 %collective-permute-start.4 = (bf16[1040,256]{1,0:T(8,128)(2,1)}, bf16[1040,256]{1,0:T(8,128)(2,1)S(1)}, u32[]{:S(2)}, u32[]{:S(2)}) collective-permute-start(bf16[1040,256]{1,0:T(8,128)(2,1)} %collective-permute-done.3), channel_id=1, source_target_pairs={{2,0},{3,1},{4,6},{5,7},{10,8},{11,9},{12,14},{13,15},{18,16},{19,... | collective-permute-start | bytes 1597448 | tf_op jit(solution)/shard_map/ppermute | solution.py:185
  21.7 18.2 %collective-permute-start.6 = (bf16[1040,256]{1,0:T(8,128)(2,1)}, bf16[1040,256]{1,0:T(8,128)(2,1)}, u32[]{:S(2)}, u32[]{:S(2)}) collective-permute-start(bf16[1040,256]{1,0:T(8,128)(2,1)} %collective-permute-done.1.refs_2_), channel_id=1, source_target_pairs={{2,4},{3,5},{4,2},{5,3},{10,12},{11,13},{12,10},{13,11},{18,20},{1... | collective-permute-start | bytes 1597448 | tf_op jit(solution)/shard_map/ppermute | solution.py:185
  27.3 12.6 %copy-start.5 = (bf16[768,512]{1,0:T(8,128)(2,1)}, bf16[768,512]{1,0:T(8,128)(2,1)S(1)}, u32[]{:S(2)}) copy-start(bf16[768,512]{1,0:T(8,128)(2,1)S(1)} %collective-permute-done.9.v_low.refs_3_) | copy-start | bytes 2359300
  39.9 0.8 copy-start.8
  40.7 8.4 %copy-start.9 = (bf16[1040,256]{1,0:T(8,128)(2,1)S(1)}, bf16[1040,256]{1,0:T(8,128)(2,1)}, u32[]{:S(2)}) copy-start(bf16[1040,256]{1,0:T(8,128)(2,1)} %copy-done.8) | copy-start | bytes 1597444
  40.7 54.1 %all-to-all-start = ((bf16[4,2,2,512,128]{4,3,2,1,0:T(8,128)(2,1)}), bf16[4,2,2,512,128]{4,3,2,1,0:T(8,128)(2,1)S(1)}, u32[]{:S(2)}, u32[]{:S(2)}) async-start(bf16[4,2,2,512,128]{4,3,2,1,0:T(8,128)(2,1)} %after.2), calls=%async_computation | async-start | bytes 4194304 | tf_op jit(solution)/shard_map/all_to_all | solution.py:158
  45.7 40.6 %collective-permute-start.14 = (bf16[4,1,2,512,128]{4,3,2,1,0:T(8,128)(2,1)}, bf16[4,1,2,512,128]{4,3,2,1,0:T(8,128)(2,1)}, u32[]{:S(2)}, u32[]{:S(2)}) collective-permute-start(bf16[4,1,2,512,128]{4,3,2,1,0:T(8,128)(2,1)} %get-tuple-element.19), channel_id=1, source_target_pairs={{0,1},{1,0},{2,3},{3,2},{4,5},{5,4},{6,7},{7,6},{8,9},{9,8},{10,11... | collective-permute-start | bytes 3145736 | tf_op jit(solution)/shard_map/ppermute | solution.py:76
  47.2 35.4 %collective-permute-start.7 = (bf16[1040,256]{1,0:T(8,128)(2,1)}, bf16[1040,256]{1,0:T(8,128)(2,1)}, u32[]{:S(2)}, u32[]{:S(2)}) collective-permute-start(bf16[1040,256]{1,0:T(8,128)(2,1)} %collective-permute-done.6.refs_1_), channel_id=1, source_target_pairs={{2,0},{3,1},{4,6},{5,7},{10,8},{11,9},{12,14},{13,15},{18,16},{19,... | collective-permute-start | bytes 1597448 | tf_op jit(solution)/shard_map/ppermute | solution.py:185
  48.5 40.9 %collective-permute-start.2 = (bf16[1040,256]{1,0:T(8,128)(2,1)}, bf16[1040,256]{1,0:T(8,128)(2,1)S(1)}, u32[]{:S(2)}, u32[]{:S(2)}) collective-permute-start(bf16[1040,256]{1,0:T(8,128)(2,1)} %collective-permute-done.1.refs_2_), channel_id=1, source_target_pairs={{0,1},{1,0},{2,3},{3,2},{4,5},{5,4},{6,7},{7,6},{8,9},{9,8},{10,11... | collective-permute-start | bytes 1597448 | tf_op jit(solution)/shard_map/ppermute | solution.py:76
  51.2 43.7 %collective-permute-start.5 = (bf16[1040,256]{1,0:T(8,128)(2,1)}, bf16[1040,256]{1,0:T(8,128)(2,1)S(1)}, u32[]{:S(2)}, u32[]{:S(2)}) collective-permute-start(bf16[1040,256]{1,0:T(8,128)(2,1)} %add.189.refs_4_), channel_id=1, source_target_pairs={{0,1},{1,0},{2,3},{3,2},{4,5},{5,4},{6,7},{7,6},{8,9},{9,8},{10,11... | collective-permute-start | bytes 1597448 | tf_op jit(solution)/shard_map/ppermute | solution.py:76
  84.8 20.8 %collective-permute-start.8 = (bf16[1040,256]{1,0:T(8,128)(2,1)}, bf16[1040,256]{1,0:T(8,128)(2,1)}, u32[]{:S(2)}, u32[]{:S(2)}) collective-permute-start(bf16[1040,256]{1,0:T(8,128)(2,1)} %add.190.refs_6_), channel_id=1, source_target_pairs={{0,1},{1,0},{2,3},{3,2},{4,5},{5,4},{6,7},{7,6},{8,9},{9,8},{10,11... | collective-permute-start | bytes 1597448 | tf_op jit(solution)/shard_map/ppermute | solution.py:76
  89.4 5.4 %copy-start.6 = (bf16[1040,256]{1,0:T(8,128)(2,1)}, bf16[1040,256]{1,0:T(8,128)(2,1)S(1)}, u32[]{:S(2)}) copy-start(bf16[1040,256]{1,0:T(8,128)(2,1)S(1)} %collective-permute-done.2.refs_3_.refs_4_) | copy-start | bytes 1597444
  94.8 0.8 copy-start.7
  95.6 1.3 copy-start
  97.0 50.1 %all-to-all-start.1 = ((bf16[4,2,2,512,128]{4,3,2,1,0:T(8,128)(2,1)}), bf16[4,2,2,512,128]{4,3,2,1,0:T(8,128)(2,1)}, u32[]{:S(2)}, u32[]{:S(2)}) async-start(bf16[4,2,2,512,128]{4,3,2,1,0:T(8,128)(2,1)} %after.3), calls=%async_computation.1 | async-start | bytes 4194304 | tf_op jit(solution)/shard_map/all_to_all | solution.py:158
  110.8 23.7 %collective-permute-start.11 = (bf16[2,512,256]{2,1,0:T(8,128)(2,1)}, bf16[2,512,256]{2,1,0:T(8,128)(2,1)S(1)}, u32[]{:S(2)}, u32[]{:S(2)}) collective-permute-start(bf16[2,512,256]{2,1,0:T(8,128)(2,1)} %get-tuple-element.13.h_last), channel_id=1, source_target_pairs={{0,8},{8,16},{16,24},{1,9},{9,17},{17,25},{2,10},{10,18},{18,26},{... | collective-permute-start | bytes 1572872 | tf_op jit(solution)/shard_map/ppermute | solution.py:726
  112.7 21.8 %collective-permute-start.12 = (bf16[2,512,256]{2,1,0:T(8,128)(2,1)}, bf16[2,512,256]{2,1,0:T(8,128)(2,1)S(1)}, u32[]{:S(2)}, u32[]{:S(2)}) collective-permute-start(bf16[2,512,256]{2,1,0:T(8,128)(2,1)} %get-tuple-element.14.h_first), channel_id=1, source_target_pairs={{8,0},{16,8},{24,16},{9,1},{17,9},{25,17},{10,2},{18,10},{26,18},{... | collective-permute-start | bytes 1572872 | tf_op jit(solution)/shard_map/ppermute | solution.py:726
  134.5 0.8 copy-start.10
  134.5 1.0 copy-start.11
  147.0 15.9 %copy-start.2 = (s32[26]{0:T(128)S(1)}, s32[26]{0:T(128)}, u32[]{:S(2)}) copy-start(s32[26]{0:T(128)} %pad_add_fusion.1.plan) | copy-start | bytes 316
  147.0 15.9 %copy-start.3 = (s32[16]{0:T(128)S(1)}, s32[16]{0:T(128)}, u32[]{:S(2)}) copy-start(s32[16]{0:T(128)} %select_reduce_fusion.2.order) | copy-start | bytes 196
  152.5 10.4 %all-to-all-start.2 = ((f32[8,24,128]{2,1,0:T(8,128)}), f32[8,24,128]{2,1,0:T(8,128)S(1)}, u32[]{:S(2)}, u32[]{:S(2)}) async-start(f32[8,24,128]{2,1,0:T(8,128)} %project.1), calls=%async_computation.2 | async-start | bytes 196608 | tf_op jit(solution)/shard_map/all_to_all | solution.py:807
  163.0 1.6 copy-start.1

commit v12 on v11

--- a/solution.py
+++ b/solution.py
@@ -491,7 +491,7 @@
     return pl.pallas_call(
         functools.partial(outer_kernel, blocks),
         out_shape=jax.ShapeDtypeStruct(kernel_t.shape, kernel_t.dtype),
-        in_specs=[SMEM] + [HBM] * 11,
+        in_specs=[SMEM] + [HBM] * 4 + [ANY, HBM, HBM, ANY] + [HBM] * 3,
         out_specs=HBM,
         input_output_aliases={1: 0},
         scratch_shapes=[
@@ -505,7 +505,7 @@
             pltpu.SemaphoreType.DMA((14,)),
             pltpu.SemaphoreType.DMA((2,)),
         ],
-        compiler_params=pltpu.CompilerParams(vmem_limit_bytes=62 * MIB),
+        compiler_params=pltpu.CompilerParams(vmem_limit_bytes=59 * MIB),
         name="chebyshev_outer",
     )(
         coefficients, kernel_t, v_low, v_mid, v_high, h_low, h_first, h_last, h_high,

time: 173 us -> 174 us (level); the launches traced: 172 us -> 171 us
  no operation moved by 1% of the time
where the time goes in v12:
time: 174 us; the launch traced here: 171 us
  waiting for transfers between devices  61.9 us (36%)
  Pallas kernels  47.1 us (27%)
  starting transfers between devices  40.8 us (23%)
  local copies, waits for them, and re-layouts  10.5 us (6%)
  other arithmetic  9.75 us (6%)
    ppermute x5, waiting for transfers between devices, move(): return lax.ppermute(block, 'col', pairs)  29.2 us
    ppermute x6, waiting for transfers between devices, swap_along(): return lax.ppermute(block, 'col', pairs)  17.9 us
    pallas_call x1, Pallas kernels, chebyshev_inner(): pl.pallas_call(functools.partial(inner_kernel, blocks), out_shape=(jax.Sh...  16.4 us
    all_to_all x2, starting transfers between devices, between_lines(): lax.all_to_all(after(block, *others), 'col', split_axis=0, concat_axis=0,...  13.6 us
    ppermute x4, starting transfers between devices, shift(): return lax.ppermute(block, axis, pairs)  9.38 us
    ppermute x6, starting transfers between devices, swap_along(): return lax.ppermute(block, 'col', pairs)  7.29 us
    ppermute x5, starting transfers between devices, move(): return lax.ppermute(block, 'col', pairs)  7.11 us
    pallas_call x1, Pallas kernels, chebyshev_outer(): pl.pallas_call(functools.partial(outer_kernel, blocks), out_shape=jax.Sha...  7.07 us
  transfers between devices with their start and end apart: 18, of which 8 were waited for; matrix products, arithmetic and copies ran while one was open for 9% of the time, Pallas kernels for 19%

profile of v12, /device:TPU:2, one launch (start us, length us, event | category | flops | bytes accessed | tf_op | source)
XLA Modules:
  0.0 170.9 jit_solution(10446483118668366179)
XLA Ops:
  0.6 2.6 %own_piece.1.refs_0_.first = bf16[1040,256]{1,0:T(8,128)(2,1)} custom-call(s32[16]{0:T(128)} %bitcast.34, s32[16]{0:T(128)} %named.1, s32[4]{0:T(128)} %counts.1, s32[2]{0:T(128)} %pattern.1, bf16[1024,256]{1,0:T(8,128)(2,1)} %bitcast.29), custom_call_target="tpu_custom_call" | custom-call | tf_op jit(solution)/shard_map/own_piece/pallas_call | solution.py:56
  3.2 1.6 collective-permute-start
  4.8 1.6 collective-permute-start.1
  7.8 2.7 %pack.3 = bf16[4,1,2,512,128]{4,3,2,1,0:T(8,128)(2,1)} custom-call(s32[1]{0:T(128)} %bitcast.11.me, s32[16]{0:T(128)} %bitcast.35, bf16[16,2,512,128]{3,2,1,0:T(8,128)(2,1)} %basis.3, bf16[1040,256]{1,0:T(8,128)(2,1)} %own_piece.1.refs_0_.first), custom_call_target="tpu_custom_call" | custom-call | tf_op jit(solution)/shard_map/pack/pallas_call | solution.py:119
  11.2 2.6 %fusion.12 = (bf16[768,512]{1,0:T(8,128)(2,1)}, bf16[768,512]{1,0:T(8,128)(2,1)}) fusion(bf16[4096,512]{1,0:T(8,128)(2,1)} %v_mid.3), kind=kLoop, calls=%fused_computation.55 | loop fusion | bytes 3145728 | tf_op jit(solution)/shard_map/slice | solution.py:794
  13.8 1.9 %collective-permute-start.9 = (bf16[768,512]{1,0:T(8,128)(2,1)}, bf16[768,512]{1,0:T(8,128)(2,1)S(1)}, u32[]{:S(2)}, u32[]{:S(2)}) collective-permute-start(bf16[768,512]{1,0:T(8,128)(2,1)} %get-tuple-element.27), channel_id=1, source_target_pairs={{0,8},{8,16},{16,24},{1,9},{9,17},{17,25},{2,10},{10,18},{18,26},{... | collective-permute-start | bytes 2359304 | tf_op jit(solution)/shard_map/ppermute | solution.py:726
  15.7 2.8 %collective-permute-done.refs_1_.first.refs_3_ = bf16[1040,256]{1,0:T(8,128)(2,1)S(1)} collective-permute-done((bf16[1040,256]{1,0:T(8,128)(2,1)}, bf16[1040,256]{1,0:T(8,128)(2,1)S(1)}, u32[]{:S(2)}, u32[]{:S(2)}) %collective-permute-start) | collective-permute-done | bytes 532512 | tf_op jit(solution)/shard_map/ppermute | solution.py:76
  18.5 1.9 %collective-permute-start.10 = (bf16[768,512]{1,0:T(8,128)(2,1)}, bf16[768,512]{1,0:T(8,128)(2,1)}, u32[]{:S(2)}, u32[]{:S(2)}) collective-permute-start(bf16[768,512]{1,0:T(8,128)(2,1)} %get-tuple-element.26), channel_id=1, source_target_pairs={{8,0},{16,8},{24,16},{9,1},{17,9},{25,17},{10,2},{18,10},{26,18},{... | collective-permute-start | bytes 2359304 | tf_op jit(solution)/shard_map/ppermute | solution.py:726
  23.2 3.6 %pack.2 = (bf16[4,2,2,512,128]{4,3,2,1,0:T(8,128)(2,1)}, bf16[4,1,2,512,128]{4,3,2,1,0:T(8,128)(2,1)}) custom-call(s32[1]{0:T(128)} %bitcast.11.me, s32[16]{0:T(128)} %bitcast.36, bf16[16,2,512,128]{3,2,1,0:T(8,128)(2,1)} %basis.3, bf16[1040,256]{1,0:T(8,128)(2,1)} %copy-done.4), custom_call_target="tpu_custom_call" | custom-call | tf_op jit(solution)/shard_map/pack/pallas_call | solution.py:119
  27.3 2.9 %collective-permute-done.10.v_high.refs_4_ = bf16[768,512]{1,0:T(8,128)(2,1)} collective-permute-done((bf16[768,512]{1,0:T(8,128)(2,1)}, bf16[768,512]{1,0:T(8,128)(2,1)}, u32[]{:S(2)}, u32[]{:S(2)}) %collective-permute-start.10) | collective-permute-done | bytes 786464 | tf_op jit(solution)/shard_map/ppermute | solution.py:726
  30.2 9.7 %collective-permute-done.13.refs_5_ = bf16[4,1,2,512,128]{4,3,2,1,0:T(8,128)(2,1)} collective-permute-done((bf16[4,1,2,512,128]{4,3,2,1,0:T(8,128)(2,1)}, bf16[4,1,2,512,128]{4,3,2,1,0:T(8,128)(2,1)}, u32[]{:S(2)}, u32[]{:S(2)}) %collective-permute-start.13) | collective-permute-done | bytes 1048608 | tf_op jit(solution)/shard_map/ppermute | solution.py:76
  40.7 5.0 %all-to-all-start = ((bf16[4,2,2,512,128]{4,3,2,1,0:T(8,128)(2,1)}), bf16[4,2,2,512,128]{4,3,2,1,0:T(8,128)(2,1)S(1)}, u32[]{:S(2)}, u32[]{:S(2)}) async-start(bf16[4,2,2,512,128]{4,3,2,1,0:T(8,128)(2,1)} %after.2), calls=%async_computation | async-start | bytes 4194304 | tf_op jit(solution)/shard_map/all_to_all | solution.py:158
  45.7 1.5 collective-permute-start.14
  49.1 2.0 %add.189.refs_4_ = bf16[1040,256]{1,0:T(8,128)(2,1)} add(bf16[1040,256]{1,0:T(8,128)(2,1)} %collective-permute-done.3, bf16[1040,256]{1,0:T(8,128)(2,1)S(1)} %copy-done.9) | non-fusion elementwise | flops 266240 | bytes 1597440 | tf_op jit(solution)/shard_map/add | solution.py:198
  51.2 1.5 collective-permute-start.5
  53.5 29.1 %collective-permute-done.7.refs_2_ = bf16[1040,256]{1,0:T(8,128)(2,1)} collective-permute-done((bf16[1040,256]{1,0:T(8,128)(2,1)}, bf16[1040,256]{1,0:T(8,128)(2,1)}, u32[]{:S(2)}, u32[]{:S(2)}) %collective-permute-start.7) | collective-permute-done | bytes 532512 | tf_op jit(solution)/shard_map/ppermute | solution.py:185
  82.7 2.1 %add.190.refs_6_ = bf16[1040,256]{1,0:T(8,128)(2,1)} add(bf16[1040,256]{1,0:T(8,128)(2,1)} %collective-permute-done.6.refs_1_, bf16[1040,256]{1,0:T(8,128)(2,1)} %collective-permute-done.7.refs_2_) | non-fusion elementwise | flops 266240 | bytes 1597440 | tf_op jit(solution)/shard_map/add | solution.py:199
  84.8 1.5 collective-permute-start.8
  86.3 3.1 %pad_maximum_fusion.refs_0_ = bf16[4,2,2,512,128]{4,3,2,1,0:T(8,128)(2,1)} fusion(bf16[4,1,2,512,128]{4,3,2,1,0:T(8,128)(2,1)} %collective-permute-done.14, bf16[4,1,2,512,128]{4,3,2,1,0:T(8,128)(2,1)} %collective-permute-done.13.refs_5_), kind=kLoop, calls=%fused_computation | loop fusion | flops 1048576 | bytes 4194304 | tf_op jit(solution)/shard_map/concatenate | solution.py:157
  89.4 5.4 %collective-permute-done.5.refs_5_ = bf16[1040,256]{1,0:T(8,128)(2,1)S(1)} collective-permute-done((bf16[1040,256]{1,0:T(8,128)(2,1)}, bf16[1040,256]{1,0:T(8,128)(2,1)S(1)}, u32[]{:S(2)}, u32[]{:S(2)}) %collective-permute-start.5) | collective-permute-done | bytes 532512 | tf_op jit(solution)/shard_map/ppermute | solution.py:76
  97.0 8.6 %all-to-all-start.1 = ((bf16[4,2,2,512,128]{4,3,2,1,0:T(8,128)(2,1)}), bf16[4,2,2,512,128]{4,3,2,1,0:T(8,128)(2,1)}, u32[]{:S(2)}, u32[]{:S(2)}) async-start(bf16[4,2,2,512,128]{4,3,2,1,0:T(8,128)(2,1)} %after.3), calls=%async_computation.1 | async-start | bytes 4194304 | tf_op jit(solution)/shard_map/all_to_all | solution.py:158
  105.7 3.1 %edge_blocks.1 = (bf16[2,512,256]{2,1,0:T(8,128)(2,1)}, bf16[2,512,256]{2,1,0:T(8,128)(2,1)}, bf16[8,16,256]{2,1,0:T(8,128)(2,1)}) custom-call(s32[8]{0:T(128)} %stack.35.owners, bf16[1040,256]{1,0:T(8,128)(2,1)} %own_piece.1.refs_0_.first, bf16[1040,256]{1,0:T(8,128)(2,1)} %copy-done.4, bf16[1040,256]{1,0:T(8,128)(2,1)} %collective-permute-done.1.refs_2_, ...), custom_call_target="tpu_custom_call" | custom-call | tf_op jit(solution)/shard_map/edge_blocks/pallas_call | solution.py:248
  110.8 1.9 %collective-permute-start.11 = (bf16[2,512,256]{2,1,0:T(8,128)(2,1)}, bf16[2,512,256]{2,1,0:T(8,128)(2,1)S(1)}, u32[]{:S(2)}, u32[]{:S(2)}) collective-permute-start(bf16[2,512,256]{2,1,0:T(8,128)(2,1)} %get-tuple-element.13.h_last), channel_id=1, source_target_pairs={{0,8},{8,16},{16,24},{1,9},{9,17},{17,25},{2,10},{10,18},{18,26},{... | collective-permute-start | bytes 1572872 | tf_op jit(solution)/shard_map/ppermute | solution.py:726
  112.7 3.6 %collective-permute-start.12 = (bf16[2,512,256]{2,1,0:T(8,128)(2,1)}, bf16[2,512,256]{2,1,0:T(8,128)(2,1)S(1)}, u32[]{:S(2)}, u32[]{:S(2)}) collective-permute-start(bf16[2,512,256]{2,1,0:T(8,128)(2,1)} %get-tuple-element.14.h_first), channel_id=1, source_target_pairs={{8,0},{16,8},{24,16},{9,1},{17,9},{25,17},{10,2},{18,10},{26,18},{... | collective-permute-start | bytes 1572872 | tf_op jit(solution)/shard_map/ppermute | solution.py:726
  118.1 16.4 %chebyshev_inner.1 = (bf16[8,512,512]{2,1,0:T(8,128)(2,1)}, bf16[1024,512]{1,0:T(8,128)(2,1)}, bf16[1024,512]{1,0:T(8,128)(2,1)}, f32[1024,512]{1,0:T(8,128)}) custom-call(f32[4]{0:T(128)} %coef.3, s32[8]{0:T(128)} %stack.35.owners, bf16[768,512]{1,0:T(8,128)(2,1)} %copy-done.5, bf16[4096,512]{1,0:T(8,128)(2,1)} %v_mid.3, ...), custom_call_target="tpu_custom_call" | custom-call | flops 8455716864 | bytes 16777216 | tf_op jit(solution)/shard_map/chebyshev_inner/pallas_call | solution.py:373
  135.5 7.1 %chebyshev_outer.1.kernel_t = bf16[8,512,512]{2,1,0:T(8,128)(2,1)} custom-call(f32[4]{0:T(128)} %coef.3, bf16[8,512,512]{2,1,0:T(8,128)(2,1)} %get-tuple-element.12.kernel_in, bf16[768,512]{1,0:T(8,128)(2,1)} %copy-done.5, bf16[4096,512]{1,0:T(8,128)(2,1)} %v_mid.3, ...), custom_call_target="tpu_custom_call", output_to_operand_aliasing={{}: (1, {})} | custom-call | tf_op jit(solution)/shard_map/chebyshev_outer/pallas_call | solution.py:491
  142.6 4.5 %all-to-all-done.1 = bf16[4,2,2,512,128]{4,3,2,1,0:T(8,128)(2,1)} async-done(((bf16[4,2,2,512,128]{4,3,2,1,0:T(8,128)(2,1)}), bf16[4,2,2,512,128]{4,3,2,1,0:T(8,128)(2,1)}, u32[]{:S(2)}, u32[]{:S(2)}) %all-to-all-start.1) | async-done | bytes 2097184 | tf_op jit(solution)/shard_map/all_to_all | solution.py:158
  147.0 5.2 %project.1 = f32[8,24,128]{2,1,0:T(8,128)} custom-call(s32[26]{0:T(128)} %pad_add_fusion.1.plan, s32[16]{0:T(128)} %select_reduce_fusion.2.order, bf16[8,512,512]{2,1,0:T(8,128)(2,1)} %chebyshev_outer.1.kernel_t, f32[4,128]{1,0:T(4,128)} %core.1, bf16[8,2,512,128]{3,2,1,0:T(8,128)(2,1)} %bitcast.26, bf16[8,2,512,128]{3,2,1,0:T(8,128)(2,1)} %bitcast.13.refs_1_), custom_call_target="tpu_custom_call" | custom-call | tf_op jit(solution)/shard_map/project/pallas_call | solution.py:603
  152.2 3.4 %all-to-all-start.2 = ((f32[8,24,128]{2,1,0:T(8,128)}), f32[8,24,128]{2,1,0:T(8,128)S(1)}, u32[]{:S(2)}, u32[]{:S(2)}) async-start(f32[8,24,128]{2,1,0:T(8,128)} %project.1), calls=%async_computation.2 | async-start | bytes 196608 | tf_op jit(solution)/shard_map/all_to_all | solution.py:807
  155.7 7.0 %all-to-all-done.2 = f32[8,24,128]{2,1,0:T(8,128)S(1)} async-done(((f32[8,24,128]{2,1,0:T(8,128)}), f32[8,24,128]{2,1,0:T(8,128)S(1)}, u32[]{:S(2)}, u32[]{:S(2)}) %all-to-all-start.2) | async-done | bytes 98336 | tf_op jit(solution)/shard_map/all_to_all | solution.py:807
  162.8 1.6 copy-done.1
  164.3 6.6 %update.1 = (f32[4,128]{1,0:T(4,128)}, bf16[4096,512]{1,0:T(8,128)(2,1)}) custom-call(s32[26]{0:T(128)S(1)} %copy-done.2, s32[16]{0:T(128)S(1)} %copy-done.3, s32[16]{0:T(128)S(1)} %reshape.285.tile_of, f32[192,128]{1,0:T(8,128)S(1)} %bitcast.28, f32[32,192]{1,0:T(8,128)S(1)} %convert_reduce_fusion.collect, bf16[8,2,512,128]{3,2,1,0:T(8,128)(2,1)S(1)} %bitcast.27, ...), custom_call_target="tpu_custom_call" | custom-call | tf_op jit(solution)/shard_map/update/pallas_call | solution.py:701
  (84 shorter events, 15.9 us)
Async XLA Ops:
  3.2 15.3 %collective-permute-start = (bf16[1040,256]{1,0:T(8,128)(2,1)}, bf16[1040,256]{1,0:T(8,128)(2,1)S(1)}, u32[]{:S(2)}, u32[]{:S(2)}) collective-permute-start(bf16[1040,256]{1,0:T(8,128)(2,1)} %own_piece.1.refs_0_.first), channel_id=1, source_target_pairs={{0,1},{1,0},{2,3},{3,2},{4,5},{5,4},{6,7},{7,6},{8,9},{9,8},{10,11... | collective-permute-start | bytes 1597448 | tf_op jit(solution)/shard_map/ppermute | solution.py:76
  4.8 16.9 %collective-permute-start.1 = (bf16[1040,256]{1,0:T(8,128)(2,1)}, bf16[1040,256]{1,0:T(8,128)(2,1)}, u32[]{:S(2)}, u32[]{:S(2)}) collective-permute-start(bf16[1040,256]{1,0:T(8,128)(2,1)} %own_piece.1.refs_0_.first), channel_id=1, source_target_pairs={{0,2},{1,3},{2,0},{3,1},{4,6},{5,7},{6,4},{7,5},{8,10},{9,11},{10,... | collective-permute-start | bytes 1597448 | tf_op jit(solution)/shard_map/ppermute | solution.py:185
  6.4 14.0 %collective-permute-start.3 = (bf16[1040,256]{1,0:T(8,128)(2,1)}, bf16[1040,256]{1,0:T(8,128)(2,1)}, u32[]{:S(2)}, u32[]{:S(2)}) collective-permute-start(bf16[1040,256]{1,0:T(8,128)(2,1)} %own_piece.1.refs_0_.first), channel_id=1, source_target_pairs={{2,4},{3,5},{4,2},{5,3},{10,12},{11,13},{12,10},{13,11},{18,20},{1... | collective-permute-start | bytes 1597448 | tf_op jit(solution)/shard_map/ppermute | solution.py:185
  10.6 29.3 %collective-permute-start.13 = (bf16[4,1,2,512,128]{4,3,2,1,0:T(8,128)(2,1)}, bf16[4,1,2,512,128]{4,3,2,1,0:T(8,128)(2,1)}, u32[]{:S(2)}, u32[]{:S(2)}) collective-permute-start(bf16[4,1,2,512,128]{4,3,2,1,0:T(8,128)(2,1)} %pack.3), channel_id=1, source_target_pairs={{0,1},{1,0},{2,3},{3,2},{4,5},{5,4},{6,7},{7,6},{8,9},{9,8},{10,11... | collective-permute-start | bytes 3145736 | tf_op jit(solution)/shard_map/ppermute | solution.py:76
  13.8 13.5 %collective-permute-start.9 = (bf16[768,512]{1,0:T(8,128)(2,1)}, bf16[768,512]{1,0:T(8,128)(2,1)S(1)}, u32[]{:S(2)}, u32[]{:S(2)}) collective-permute-start(bf16[768,512]{1,0:T(8,128)(2,1)} %get-tuple-element.27), channel_id=1, source_target_pairs={{0,8},{8,16},{16,24},{1,9},{9,17},{17,25},{2,10},{10,18},{18,26},{... | collective-permute-start | bytes 2359304 | tf_op jit(solution)/shard_map/ppermute | solution.py:726
  18.5 4.7 %copy-start.4 = (bf16[1040,256]{1,0:T(8,128)(2,1)}, bf16[1040,256]{1,0:T(8,128)(2,1)S(1)}, u32[]{:S(2)}) copy-start(bf16[1040,256]{1,0:T(8,128)(2,1)S(1)} %collective-permute-done.refs_1_.first.refs_3_) | copy-start | bytes 1597444
  18.5 11.7 %collective-permute-start.10 = (bf16[768,512]{1,0:T(8,128)(2,1)}, bf16[768,512]{1,0:T(8,128)(2,1)}, u32[]{:S(2)}, u32[]{:S(2)}) collective-permute-start(bf16[768,512]{1,0:T(8,128)(2,1)} %get-tuple-element.26), channel_id=1, source_target_pairs={{8,0},{16,8},{24,16},{9,1},{17,9},{25,17},{10,2},{18,10},{26,18},{... | collective-permute-start | bytes 2359304 | tf_op jit(solution)/shard_map/ppermute | solution.py:726
  20.4 19.5 %collective-permute-start.4 = (bf16[1040,256]{1,0:T(8,128)(2,1)}, bf16[1040,256]{1,0:T(8,128)(2,1)S(1)}, u32[]{:S(2)}, u32[]{:S(2)}) collective-permute-start(bf16[1040,256]{1,0:T(8,128)(2,1)} %collective-permute-done.3), channel_id=1, source_target_pairs={{2,0},{3,1},{4,6},{5,7},{10,8},{11,9},{12,14},{13,15},{18,16},{19,... | collective-permute-start | bytes 1597448 | tf_op jit(solution)/shard_map/ppermute | solution.py:185
  21.7 18.2 %collective-permute-start.6 = (bf16[1040,256]{1,0:T(8,128)(2,1)}, bf16[1040,256]{1,0:T(8,128)(2,1)}, u32[]{:S(2)}, u32[]{:S(2)}) collective-permute-start(bf16[1040,256]{1,0:T(8,128)(2,1)} %collective-permute-done.1.refs_2_), channel_id=1, source_target_pairs={{2,4},{3,5},{4,2},{5,3},{10,12},{11,13},{12,10},{13,11},{18,20},{1... | collective-permute-start | bytes 1597448 | tf_op jit(solution)/shard_map/ppermute | solution.py:185
  27.3 12.6 %copy-start.5 = (bf16[768,512]{1,0:T(8,128)(2,1)}, bf16[768,512]{1,0:T(8,128)(2,1)S(1)}, u32[]{:S(2)}) copy-start(bf16[768,512]{1,0:T(8,128)(2,1)S(1)} %collective-permute-done.9.v_low.refs_3_) | copy-start | bytes 2359300
  39.9 0.8 copy-start.8
  40.7 8.4 %copy-start.9 = (bf16[1040,256]{1,0:T(8,128)(2,1)S(1)}, bf16[1040,256]{1,0:T(8,128)(2,1)}, u32[]{:S(2)}) copy-start(bf16[1040,256]{1,0:T(8,128)(2,1)} %copy-done.8) | copy-start | bytes 1597444
  40.7 54.1 %all-to-all-start = ((bf16[4,2,2,512,128]{4,3,2,1,0:T(8,128)(2,1)}), bf16[4,2,2,512,128]{4,3,2,1,0:T(8,128)(2,1)S(1)}, u32[]{:S(2)}, u32[]{:S(2)}) async-start(bf16[4,2,2,512,128]{4,3,2,1,0:T(8,128)(2,1)} %after.2), calls=%async_computation | async-start | bytes 4194304 | tf_op jit(solution)/shard_map/all_to_all | solution.py:158
  45.7 40.6 %collective-permute-start.14 = (bf16[4,1,2,512,128]{4,3,2,1,0:T(8,128)(2,1)}, bf16[4,1,2,512,128]{4,3,2,1,0:T(8,128)(2,1)}, u32[]{:S(2)}, u32[]{:S(2)}) collective-permute-start(bf16[4,1,2,512,128]{4,3,2,1,0:T(8,128)(2,1)} %get-tuple-element.19), channel_id=1, source_target_pairs={{0,1},{1,0},{2,3},{3,2},{4,5},{5,4},{6,7},{7,6},{8,9},{9,8},{10,11... | collective-permute-start | bytes 3145736 | tf_op jit(solution)/shard_map/ppermute | solution.py:76
  47.2 35.4 %collective-permute-start.7 = (bf16[1040,256]{1,0:T(8,128)(2,1)}, bf16[1040,256]{1,0:T(8,128)(2,1)}, u32[]{:S(2)}, u32[]{:S(2)}) collective-permute-start(bf16[1040,256]{1,0:T(8,128)(2,1)} %collective-permute-done.6.refs_1_), channel_id=1, source_target_pairs={{2,0},{3,1},{4,6},{5,7},{10,8},{11,9},{12,14},{13,15},{18,16},{19,... | collective-permute-start | bytes 1597448 | tf_op jit(solution)/shard_map/ppermute | solution.py:185
  48.5 40.9 %collective-permute-start.2 = (bf16[1040,256]{1,0:T(8,128)(2,1)}, bf16[1040,256]{1,0:T(8,128)(2,1)S(1)}, u32[]{:S(2)}, u32[]{:S(2)}) collective-permute-start(bf16[1040,256]{1,0:T(8,128)(2,1)} %collective-permute-done.1.refs_2_), channel_id=1, source_target_pairs={{0,1},{1,0},{2,3},{3,2},{4,5},{5,4},{6,7},{7,6},{8,9},{9,8},{10,11... | collective-permute-start | bytes 1597448 | tf_op jit(solution)/shard_map/ppermute | solution.py:76
  51.2 43.7 %collective-permute-start.5 = (bf16[1040,256]{1,0:T(8,128)(2,1)}, bf16[1040,256]{1,0:T(8,128)(2,1)S(1)}, u32[]{:S(2)}, u32[]{:S(2)}) collective-permute-start(bf16[1040,256]{1,0:T(8,128)(2,1)} %add.189.refs_4_), channel_id=1, source_target_pairs={{0,1},{1,0},{2,3},{3,2},{4,5},{5,4},{6,7},{7,6},{8,9},{9,8},{10,11... | collective-permute-start | bytes 1597448 | tf_op jit(solution)/shard_map/ppermute | solution.py:76
  84.8 20.8 %collective-permute-start.8 = (bf16[1040,256]{1,0:T(8,128)(2,1)}, bf16[1040,256]{1,0:T(8,128)(2,1)}, u32[]{:S(2)}, u32[]{:S(2)}) collective-permute-start(bf16[1040,256]{1,0:T(8,128)(2,1)} %add.190.refs_6_), channel_id=1, source_target_pairs={{0,1},{1,0},{2,3},{3,2},{4,5},{5,4},{6,7},{7,6},{8,9},{9,8},{10,11... | collective-permute-start | bytes 1597448 | tf_op jit(solution)/shard_map/ppermute | solution.py:76
  89.4 5.4 %copy-start.6 = (bf16[1040,256]{1,0:T(8,128)(2,1)}, bf16[1040,256]{1,0:T(8,128)(2,1)S(1)}, u32[]{:S(2)}) copy-start(bf16[1040,256]{1,0:T(8,128)(2,1)S(1)} %collective-permute-done.2.refs_3_.refs_4_) | copy-start | bytes 1597444
  94.8 0.8 copy-start.7
  95.6 1.3 copy-start
  97.0 50.1 %all-to-all-start.1 = ((bf16[4,2,2,512,128]{4,3,2,1,0:T(8,128)(2,1)}), bf16[4,2,2,512,128]{4,3,2,1,0:T(8,128)(2,1)}, u32[]{:S(2)}, u32[]{:S(2)}) async-start(bf16[4,2,2,512,128]{4,3,2,1,0:T(8,128)(2,1)} %after.3), calls=%async_computation.1 | async-start | bytes 4194304 | tf_op jit(solution)/shard_map/all_to_all | solution.py:158
  110.8 23.7 %collective-permute-start.11 = (bf16[2,512,256]{2,1,0:T(8,128)(2,1)}, bf16[2,512,256]{2,1,0:T(8,128)(2,1)S(1)}, u32[]{:S(2)}, u32[]{:S(2)}) collective-permute-start(bf16[2,512,256]{2,1,0:T(8,128)(2,1)} %get-tuple-element.13.h_last), channel_id=1, source_target_pairs={{0,8},{8,16},{16,24},{1,9},{9,17},{17,25},{2,10},{10,18},{18,26},{... | collective-permute-start | bytes 1572872 | tf_op jit(solution)/shard_map/ppermute | solution.py:726
  112.7 21.8 %collective-permute-start.12 = (bf16[2,512,256]{2,1,0:T(8,128)(2,1)}, bf16[2,512,256]{2,1,0:T(8,128)(2,1)S(1)}, u32[]{:S(2)}, u32[]{:S(2)}) collective-permute-start(bf16[2,512,256]{2,1,0:T(8,128)(2,1)} %get-tuple-element.14.h_first), channel_id=1, source_target_pairs={{8,0},{16,8},{24,16},{9,1},{17,9},{25,17},{10,2},{18,10},{26,18},{... | collective-permute-start | bytes 1572872 | tf_op jit(solution)/shard_map/ppermute | solution.py:726
  134.5 0.8 copy-start.10
  134.5 1.0 copy-start.11
  147.0 15.7 %copy-start.2 = (s32[26]{0:T(128)S(1)}, s32[26]{0:T(128)}, u32[]{:S(2)}) copy-start(s32[26]{0:T(128)} %pad_add_fusion.1.plan) | copy-start | bytes 316
  147.0 15.7 %copy-start.3 = (s32[16]{0:T(128)S(1)}, s32[16]{0:T(128)}, u32[]{:S(2)}) copy-start(s32[16]{0:T(128)} %select_reduce_fusion.2.order) | copy-start | bytes 196
  152.2 10.5 %all-to-all-start.2 = ((f32[8,24,128]{2,1,0:T(8,128)}), f32[8,24,128]{2,1,0:T(8,128)S(1)}, u32[]{:S(2)}, u32[]{:S(2)}) async-start(f32[8,24,128]{2,1,0:T(8,128)} %project.1), calls=%async_computation.2 | async-start | bytes 196608 | tf_op jit(solution)/shard_map/all_to_all | solution.py:807
  162.8 1.6 copy-start.1

commit v13 on v12

--- a/solution.py
+++ b/solution.py
@@ -131,7 +131,7 @@
             pltpu.SemaphoreType.DMA((number,)),
             pltpu.SemaphoreType.DMA((number,)),
         ],
-        compiler_params=pltpu.CompilerParams(vmem_limit_bytes=62 * MIB),
+        compiler_params=pltpu.CompilerParams(vmem_limit_bytes=59 * MIB),
         name="pack",
     )(me, peers, basis, first))
 
@@ -248,7 +248,7 @@
     return pl.pallas_call(
         functools.partial(edge_kernel, col_count, depth),
         out_shape=(shape, shape, jax.ShapeDtypeStruct((col_count, LISTS, W), pieces[0].dtype)),
-        in_specs=[SMEM] + [HBM] * len(pieces),
+        in_specs=[SMEM] + [ANY] * len(pieces),
         out_specs=(VMEM, VMEM, VMEM),
         scratch_shapes=[
             pltpu.SemaphoreType.DMA((2, depth)),

time: 174 us -> 174 us (level)
  the two profiles are of different devices: /device:TPU:2 before, /device:TPU:0 now
where the time goes in v13:
time: 174 us; the launch traced here: 173 us
  waiting for transfers between devices  68.2 us (39%)
  Pallas kernels  48.2 us (28%)
  starting transfers between devices  36.3 us (21%)
  local copies, waits for them, and re-layouts  10 us (6%)
  other arithmetic  9.56 us (5%)
    ppermute x5, waiting for transfers between devices, move(): return lax.ppermute(block, 'col', pairs)  28.5 us
    ppermute x6, waiting for transfers between devices, swap_along(): return lax.ppermute(block, 'col', pairs)  24.1 us
    pallas_call x1, Pallas kernels, chebyshev_inner(): pl.pallas_call(functools.partial(inner_kernel, blocks), out_shape=(jax.Sh...  16.4 us
    all_to_all x2, starting transfers between devices, between_lines(): lax.all_to_all(after(block, *others), 'col', split_axis=0, concat_axis=0,...  12.6 us
    ppermute x6, starting transfers between devices, swap_along(): return lax.ppermute(block, 'col', pairs)  8.73 us
    all_to_all x2, waiting for transfers between devices, between_lines(): lax.all_to_all(after(block, *others), 'col', split_axis=0, concat_axis=0,...  8.59 us
    pallas_call x1, Pallas kernels, chebyshev_outer(): pl.pallas_call(functools.partial(outer_kernel, blocks), out_shape=jax.Sha...  7.07 us
    pallas_call x1, Pallas kernels, update(): pl.pallas_call(functools.partial(update_kernel, blocks, tiles), out_shape...  6.98 us
  transfers between devices with their start and end apart: 18, of which 7 were waited for; matrix products, arithmetic and copies ran while one was open for 8% of the time, Pallas kernels for 19%

profile of v13, /device:TPU:0, one launch (start us, length us, event | category | flops | bytes accessed | tf_op | source)
XLA Modules:
  0.0 173.2 jit_solution(16293535714697814532)
XLA Ops:
  0.6 2.6 %own_piece.1.refs_0_.first = bf16[1040,256]{1,0:T(8,128)(2,1)} custom-call(s32[16]{0:T(128)} %bitcast.34, s32[16]{0:T(128)} %named.1, s32[4]{0:T(128)} %counts.1, s32[2]{0:T(128)} %pattern.1, bf16[1024,256]{1,0:T(8,128)(2,1)} %bitcast.29), custom_call_target="tpu_custom_call" | custom-call | tf_op jit(solution)/shard_map/own_piece/pallas_call | solution.py:56
  3.2 3.0 %collective-permute-start = (bf16[1040,256]{1,0:T(8,128)(2,1)}, bf16[1040,256]{1,0:T(8,128)(2,1)S(1)}, u32[]{:S(2)}, u32[]{:S(2)}) collective-permute-start(bf16[1040,256]{1,0:T(8,128)(2,1)} %own_piece.1.refs_0_.first), channel_id=1, source_target_pairs={{0,1},{1,0},{2,3},{3,2},{4,5},{5,4},{6,7},{7,6},{8,9},{9,8},{10,11... | collective-permute-start | bytes 1597448 | tf_op jit(solution)/shard_map/ppermute | solution.py:76
  6.2 1.6 collective-permute-start.1
  7.8 1.5 collective-permute-start.3
  9.3 2.8 %pack.3 = bf16[4,1,2,512,128]{4,3,2,1,0:T(8,128)(2,1)} custom-call(s32[1]{0:T(128)} %bitcast.11.me, s32[16]{0:T(128)} %bitcast.35, bf16[16,2,512,128]{3,2,1,0:T(8,128)(2,1)} %basis.3, bf16[1040,256]{1,0:T(8,128)(2,1)} %own_piece.1.refs_0_.first), custom_call_target="tpu_custom_call" | custom-call | tf_op jit(solution)/shard_map/pack/pallas_call | solution.py:119
  12.6 2.4 %fusion.12 = (bf16[768,512]{1,0:T(8,128)(2,1)S(1)}, bf16[768,512]{1,0:T(8,128)(2,1)}) fusion(bf16[4096,512]{1,0:T(8,128)(2,1)} %v_mid.3), kind=kLoop, calls=%fused_computation.55 | loop fusion | bytes 3145728 | tf_op jit(solution)/shard_map/slice | solution.py:794
  15.0 1.3 collective-permute-start.9
  16.3 3.0 %collective-permute-done.refs_1_.first.refs_3_ = bf16[1040,256]{1,0:T(8,128)(2,1)S(1)} collective-permute-done((bf16[1040,256]{1,0:T(8,128)(2,1)}, bf16[1040,256]{1,0:T(8,128)(2,1)S(1)}, u32[]{:S(2)}, u32[]{:S(2)}) %collective-permute-start) | collective-permute-done | bytes 532512 | tf_op jit(solution)/shard_map/ppermute | solution.py:76
  20.7 1.3 collective-permute-start.4
  22.7 3.6 %pack.2 = (bf16[4,2,2,512,128]{4,3,2,1,0:T(8,128)(2,1)}, bf16[4,1,2,512,128]{4,3,2,1,0:T(8,128)(2,1)}) custom-call(s32[1]{0:T(128)} %bitcast.11.me, s32[16]{0:T(128)} %bitcast.36, bf16[16,2,512,128]{3,2,1,0:T(8,128)(2,1)} %basis.3, bf16[1040,256]{1,0:T(8,128)(2,1)} %copy-done.4), custom_call_target="tpu_custom_call" | custom-call | tf_op jit(solution)/shard_map/pack/pallas_call | solution.py:119
  26.3 14.7 %collective-permute-done.13.refs_5_ = bf16[4,1,2,512,128]{4,3,2,1,0:T(8,128)(2,1)S(1)} collective-permute-done((bf16[4,1,2,512,128]{4,3,2,1,0:T(8,128)(2,1)}, bf16[4,1,2,512,128]{4,3,2,1,0:T(8,128)(2,1)S(1)}, u32[]{:S(2)}, u32[]{:S(2)}) %collective-permute-start.13) | collective-permute-done | bytes 1048608 | tf_op jit(solution)/shard_map/ppermute | solution.py:76
  42.4 5.1 %all-to-all-start = ((bf16[4,2,2,512,128]{4,3,2,1,0:T(8,128)(2,1)}), bf16[4,2,2,512,128]{4,3,2,1,0:T(8,128)(2,1)S(1)}, u32[]{:S(2)}, u32[]{:S(2)}) async-start(bf16[4,2,2,512,128]{4,3,2,1,0:T(8,128)(2,1)} %after.2), calls=%async_computation | async-start | bytes 4194304 | tf_op jit(solution)/shard_map/all_to_all | solution.py:158
  47.5 1.5 collective-permute-start.14
  50.9 2.1 %add.189.refs_4_ = bf16[1040,256]{1,0:T(8,128)(2,1)} add(bf16[1040,256]{1,0:T(8,128)(2,1)} %collective-permute-done.3, bf16[1040,256]{1,0:T(8,128)(2,1)} %copy-done.10) | non-fusion elementwise | flops 266240 | bytes 1597440 | tf_op jit(solution)/shard_map/add | solution.py:198
  53.0 1.5 collective-permute-start.5
  55.5 28.5 %collective-permute-done.7.refs_2_ = bf16[1040,256]{1,0:T(8,128)(2,1)} collective-permute-done((bf16[1040,256]{1,0:T(8,128)(2,1)}, bf16[1040,256]{1,0:T(8,128)(2,1)}, u32[]{:S(2)}, u32[]{:S(2)}) %collective-permute-start.7) | collective-permute-done | bytes 532512 | tf_op jit(solution)/shard_map/ppermute | solution.py:185
  84.0 2.2 %add.190.refs_6_ = bf16[1040,256]{1,0:T(8,128)(2,1)} add(bf16[1040,256]{1,0:T(8,128)(2,1)} %copy-done.9, bf16[1040,256]{1,0:T(8,128)(2,1)} %collective-permute-done.7.refs_2_) | non-fusion elementwise | flops 266240 | bytes 1597440 | tf_op jit(solution)/shard_map/add | solution.py:199
  86.2 1.5 collective-permute-start.8
  87.7 2.8 %pad_maximum_fusion.refs_0_ = bf16[4,2,2,512,128]{4,3,2,1,0:T(8,128)(2,1)} fusion(bf16[4,1,2,512,128]{4,3,2,1,0:T(8,128)(2,1)} %collective-permute-done.14, bf16[4,1,2,512,128]{4,3,2,1,0:T(8,128)(2,1)S(1)} %copy-done.6), kind=kLoop, calls=%fused_computation | loop fusion | flops 1048576 | bytes 4194304 | tf_op jit(solution)/shard_map/concatenate | solution.py:157
  90.5 6.3 %collective-permute-done.5.refs_5_ = bf16[1040,256]{1,0:T(8,128)(2,1)} collective-permute-done((bf16[1040,256]{1,0:T(8,128)(2,1)}, bf16[1040,256]{1,0:T(8,128)(2,1)}, u32[]{:S(2)}, u32[]{:S(2)}) %collective-permute-start.5) | collective-permute-done | bytes 532512 | tf_op jit(solution)/shard_map/ppermute | solution.py:76
  96.7 1.3 copy-done
  98.1 7.6 %all-to-all-start.1 = ((bf16[4,2,2,512,128]{4,3,2,1,0:T(8,128)(2,1)}), bf16[4,2,2,512,128]{4,3,2,1,0:T(8,128)(2,1)}, u32[]{:S(2)}, u32[]{:S(2)}) async-start(bf16[4,2,2,512,128]{4,3,2,1,0:T(8,128)(2,1)} %after.3), calls=%async_computation.1 | async-start | bytes 4194304 | tf_op jit(solution)/shard_map/all_to_all | solution.py:158
  105.8 3.1 %edge_blocks.1 = (bf16[2,512,256]{2,1,0:T(8,128)(2,1)}, bf16[2,512,256]{2,1,0:T(8,128)(2,1)}, bf16[8,16,256]{2,1,0:T(8,128)(2,1)}) custom-call(s32[8]{0:T(128)} %stack.35.owners, bf16[1040,256]{1,0:T(8,128)(2,1)} %own_piece.1.refs_0_.first, bf16[1040,256]{1,0:T(8,128)(2,1)} %copy-done.4, bf16[1040,256]{1,0:T(8,128)(2,1)} %collective-permute-done.1.refs_2_, ...), custom_call_target="tpu_custom_call" | custom-call | tf_op jit(solution)/shard_map/edge_blocks/pallas_call | solution.py:248
  110.9 1.3 collective-permute-start.11
  115.3 16.4 %chebyshev_inner.1 = (bf16[8,512,512]{2,1,0:T(8,128)(2,1)}, bf16[1024,512]{1,0:T(8,128)(2,1)}, bf16[1024,512]{1,0:T(8,128)(2,1)}, f32[1024,512]{1,0:T(8,128)}) custom-call(f32[4]{0:T(128)} %coef.3, s32[8]{0:T(128)} %stack.35.owners, bf16[768,512]{1,0:T(8,128)(2,1)} %copy-done.7, bf16[4096,512]{1,0:T(8,128)(2,1)} %v_mid.3, bf16[768,512]{1,0:T(8,128)(2,1)} %copy-done.8, ...), custom_call_target="tpu_custom_call" | custom-call | flops 8455716864 | bytes 16777216 | tf_op jit(solution)/shard_map/chebyshev_inner/pallas_call | solution.py:373
  132.7 7.1 %chebyshev_outer.1.kernel_t = bf16[8,512,512]{2,1,0:T(8,128)(2,1)} custom-call(f32[4]{0:T(128)} %coef.3, bf16[8,512,512]{2,1,0:T(8,128)(2,1)} %get-tuple-element.12.kernel_in, bf16[768,512]{1,0:T(8,128)(2,1)} %copy-done.7, bf16[4096,512]{1,0:T(8,128)(2,1)} %v_mid.3, bf16[768,512]{1,0:T(8,128)(2,1)} %copy-done.8, ...), custom_call_target="tpu_custom_call", output_to_operand_aliasing={{}: (1, {})} | custom-call | tf_op jit(solution)/shard_map/chebyshev_outer/pallas_call | solution.py:491
  139.8 8.6 %all-to-all-done.1 = bf16[4,2,2,512,128]{4,3,2,1,0:T(8,128)(2,1)} async-done(((bf16[4,2,2,512,128]{4,3,2,1,0:T(8,128)(2,1)}), bf16[4,2,2,512,128]{4,3,2,1,0:T(8,128)(2,1)}, u32[]{:S(2)}, u32[]{:S(2)}) %all-to-all-start.1) | async-done | bytes 2097184 | tf_op jit(solution)/shard_map/all_to_all | solution.py:158
  148.4 5.8 %project.1 = f32[8,24,128]{2,1,0:T(8,128)} custom-call(s32[26]{0:T(128)} %pad_add_fusion.1.plan, s32[16]{0:T(128)} %select_reduce_fusion.2.order, bf16[8,512,512]{2,1,0:T(8,128)(2,1)} %chebyshev_outer.1.kernel_t, f32[4,128]{1,0:T(4,128)} %core.1, bf16[8,2,512,128]{3,2,1,0:T(8,128)(2,1)} %bitcast.26, bf16[8,2,512,128]{3,2,1,0:T(8,128)(2,1)} %bitcast.13.refs_1_), custom_call_target="tpu_custom_call" | custom-call | tf_op jit(solution)/shard_map/project/pallas_call | solution.py:603
  154.1 3.4 %all-to-all-start.2 = ((f32[8,24,128]{2,1,0:T(8,128)}), f32[8,24,128]{2,1,0:T(8,128)S(1)}, u32[]{:S(2)}, u32[]{:S(2)}) async-start(f32[8,24,128]{2,1,0:T(8,128)} %project.1), calls=%async_computation.2 | async-start | bytes 196608 | tf_op jit(solution)/shard_map/all_to_all | solution.py:807
  157.6 6.9 %all-to-all-done.2 = f32[8,24,128]{2,1,0:T(8,128)S(1)} async-done(((f32[8,24,128]{2,1,0:T(8,128)}), f32[8,24,128]{2,1,0:T(8,128)S(1)}, u32[]{:S(2)}, u32[]{:S(2)}) %all-to-all-start.2) | async-done | bytes 98336 | tf_op jit(solution)/shard_map/all_to_all | solution.py:807
  164.6 1.6 copy-done.1
  166.2 7.0 %update.1 = (f32[4,128]{1,0:T(4,128)}, bf16[4096,512]{1,0:T(8,128)(2,1)}) custom-call(s32[26]{0:T(128)S(1)} %copy-done.2, s32[16]{0:T(128)S(1)} %copy-done.3, s32[16]{0:T(128)S(1)} %reshape.285.tile_of, f32[192,128]{1,0:T(8,128)S(1)} %bitcast.28, f32[32,192]{1,0:T(8,128)S(1)} %convert_reduce_fusion.collect, bf16[8,2,512,128]{3,2,1,0:T(8,128)(2,1)S(1)} %bitcast.27, ...), custom_call_target="tpu_custom_call" | custom-call | tf_op jit(solution)/shard_map/update/pallas_call | solution.py:701
  (86 shorter events, 13.1 us)
Async XLA Ops:
  3.2 16.2 %collective-permute-start = (bf16[1040,256]{1,0:T(8,128)(2,1)}, bf16[1040,256]{1,0:T(8,128)(2,1)S(1)}, u32[]{:S(2)}, u32[]{:S(2)}) collective-permute-start(bf16[1040,256]{1,0:T(8,128)(2,1)} %own_piece.1.refs_0_.first), channel_id=1, source_target_pairs={{0,1},{1,0},{2,3},{3,2},{4,5},{5,4},{6,7},{7,6},{8,9},{9,8},{10,11... | collective-permute-start | bytes 1597448 | tf_op jit(solution)/shard_map/ppermute | solution.py:76
  6.2 15.7 %collective-permute-start.1 = (bf16[1040,256]{1,0:T(8,128)(2,1)}, bf16[1040,256]{1,0:T(8,128)(2,1)}, u32[]{:S(2)}, u32[]{:S(2)}) collective-permute-start(bf16[1040,256]{1,0:T(8,128)(2,1)} %own_piece.1.refs_0_.first), channel_id=1, source_target_pairs={{0,2},{1,3},{2,0},{3,1},{4,6},{5,7},{6,4},{7,5},{8,10},{9,11},{10,... | collective-permute-start | bytes 1597448 | tf_op jit(solution)/shard_map/ppermute | solution.py:185
  7.8 12.9 %collective-permute-start.3 = (bf16[1040,256]{1,0:T(8,128)(2,1)}, bf16[1040,256]{1,0:T(8,128)(2,1)}, u32[]{:S(2)}, u32[]{:S(2)}) collective-permute-start(bf16[1040,256]{1,0:T(8,128)(2,1)} %own_piece.1.refs_0_.first), channel_id=1, source_target_pairs={{2,4},{3,5},{4,2},{5,3},{10,12},{11,13},{12,10},{13,11},{18,20},{1... | collective-permute-start | bytes 1597448 | tf_op jit(solution)/shard_map/ppermute | solution.py:185
  12.1 29.0 %collective-permute-start.13 = (bf16[4,1,2,512,128]{4,3,2,1,0:T(8,128)(2,1)}, bf16[4,1,2,512,128]{4,3,2,1,0:T(8,128)(2,1)S(1)}, u32[]{:S(2)}, u32[]{:S(2)}) collective-permute-start(bf16[4,1,2,512,128]{4,3,2,1,0:T(8,128)(2,1)} %pack.3), channel_id=1, source_target_pairs={{0,1},{1,0},{2,3},{3,2},{4,5},{5,4},{6,7},{7,6},{8,9},{9,8},{10,11... | collective-permute-start | bytes 3145736 | tf_op jit(solution)/shard_map/ppermute | solution.py:76
  15.0 11.3 %collective-permute-start.9 = (bf16[768,512]{1,0:T(8,128)(2,1)}, bf16[768,512]{1,0:T(8,128)(2,1)S(1)}, u32[]{:S(2)}, u32[]{:S(2)}) collective-permute-start(bf16[768,512]{1,0:T(8,128)(2,1)} %get-tuple-element.27), channel_id=1, source_target_pairs={{0,8},{8,16},{16,24},{1,9},{9,17},{17,25},{2,10},{10,18},{18,26},{... | collective-permute-start | bytes 2359304 | tf_op jit(solution)/shard_map/ppermute | solution.py:726
  19.4 3.3 %copy-start.4 = (bf16[1040,256]{1,0:T(8,128)(2,1)}, bf16[1040,256]{1,0:T(8,128)(2,1)S(1)}, u32[]{:S(2)}) copy-start(bf16[1040,256]{1,0:T(8,128)(2,1)S(1)} %collective-permute-done.refs_1_.first.refs_3_) | copy-start | bytes 1597444
  19.4 6.9 %collective-permute-start.10 = (bf16[768,512]{1,0:T(8,128)(2,1)S(1)}, bf16[768,512]{1,0:T(8,128)(2,1)S(1)}, u32[]{:S(2)}, u32[]{:S(2)}) collective-permute-start(bf16[768,512]{1,0:T(8,128)(2,1)S(1)} %get-tuple-element.26), channel_id=1, source_target_pairs={{8,0},{16,8},{24,16},{9,1},{17,9},{25,17},{10,2},{18,10},{26,18},{... | collective-permute-start | bytes 2359304 | tf_op jit(solution)/shard_map/ppermute | solution.py:726
  20.7 20.3 %collective-permute-start.4 = (bf16[1040,256]{1,0:T(8,128)(2,1)}, bf16[1040,256]{1,0:T(8,128)(2,1)S(1)}, u32[]{:S(2)}, u32[]{:S(2)}) collective-permute-start(bf16[1040,256]{1,0:T(8,128)(2,1)} %collective-permute-done.3), channel_id=1, source_target_pairs={{2,0},{3,1},{4,6},{5,7},{10,8},{11,9},{12,14},{13,15},{18,16},{19,... | collective-permute-start | bytes 1597448 | tf_op jit(solution)/shard_map/ppermute | solution.py:185
  22.0 19.0 %collective-permute-start.6 = (bf16[1040,256]{1,0:T(8,128)(2,1)}, bf16[1040,256]{1,0:T(8,128)(2,1)S(1)}, u32[]{:S(2)}, u32[]{:S(2)}) collective-permute-start(bf16[1040,256]{1,0:T(8,128)(2,1)} %collective-permute-done.1.refs_2_), channel_id=1, source_target_pairs={{2,4},{3,5},{4,2},{5,3},{10,12},{11,13},{12,10},{13,11},{18,20},{1... | collective-permute-start | bytes 1597448 | tf_op jit(solution)/shard_map/ppermute | solution.py:185
  26.3 14.7 %copy-start.7 = (bf16[768,512]{1,0:T(8,128)(2,1)}, bf16[768,512]{1,0:T(8,128)(2,1)S(1)}, u32[]{:S(2)}) copy-start(bf16[768,512]{1,0:T(8,128)(2,1)S(1)} %collective-permute-done.9.v_low.refs_3_) | copy-start | bytes 2359300
  26.3 14.7 %copy-start.8 = (bf16[768,512]{1,0:T(8,128)(2,1)}, bf16[768,512]{1,0:T(8,128)(2,1)S(1)}, u32[]{:S(2)}) copy-start(bf16[768,512]{1,0:T(8,128)(2,1)S(1)} %collective-permute-done.10.v_high.refs_4_) | copy-start | bytes 2359300
  41.0 1.0 copy-start.5
  41.0 1.1 copy-start.10
  41.0 1.4 copy-start.9
  42.4 54.3 %all-to-all-start = ((bf16[4,2,2,512,128]{4,3,2,1,0:T(8,128)(2,1)}), bf16[4,2,2,512,128]{4,3,2,1,0:T(8,128)(2,1)S(1)}, u32[]{:S(2)}, u32[]{:S(2)}) async-start(bf16[4,2,2,512,128]{4,3,2,1,0:T(8,128)(2,1)} %after.2), calls=%async_computation | async-start | bytes 4194304 | tf_op jit(solution)/shard_map/all_to_all | solution.py:158
  47.5 40.2 %copy-start.6 = (bf16[4,1,2,512,128]{4,3,2,1,0:T(8,128)(2,1)S(1)}, bf16[4,1,2,512,128]{4,3,2,1,0:T(8,128)(2,1)}, u32[]{:S(2)}) copy-start(bf16[4,1,2,512,128]{4,3,2,1,0:T(8,128)(2,1)} %copy-done.5) | copy-start | bytes 3145732
  47.5 40.2 %collective-permute-start.14 = (bf16[4,1,2,512,128]{4,3,2,1,0:T(8,128)(2,1)}, bf16[4,1,2,512,128]{4,3,2,1,0:T(8,128)(2,1)}, u32[]{:S(2)}, u32[]{:S(2)}) collective-permute-start(bf16[4,1,2,512,128]{4,3,2,1,0:T(8,128)(2,1)} %get-tuple-element.19), channel_id=1, source_target_pairs={{0,1},{1,0},{2,3},{3,2},{4,5},{5,4},{6,7},{7,6},{8,9},{9,8},{10,11... | collective-permute-start | bytes 3145736 | tf_op jit(solution)/shard_map/ppermute | solution.py:76
  49.0 35.0 %collective-permute-start.7 = (bf16[1040,256]{1,0:T(8,128)(2,1)}, bf16[1040,256]{1,0:T(8,128)(2,1)}, u32[]{:S(2)}, u32[]{:S(2)}) collective-permute-start(bf16[1040,256]{1,0:T(8,128)(2,1)} %copy-done.9), channel_id=1, source_target_pairs={{2,0},{3,1},{4,6},{5,7},{10,8},{11,9},{12,14},{13,15},{18,16},{19,... | collective-permute-start | bytes 1597448 | tf_op jit(solution)/shard_map/ppermute | solution.py:185
  50.3 40.1 %collective-permute-start.2 = (bf16[1040,256]{1,0:T(8,128)(2,1)}, bf16[1040,256]{1,0:T(8,128)(2,1)}, u32[]{:S(2)}, u32[]{:S(2)}) collective-permute-start(bf16[1040,256]{1,0:T(8,128)(2,1)} %collective-permute-done.1.refs_2_), channel_id=1, source_target_pairs={{0,1},{1,0},{2,3},{3,2},{4,5},{5,4},{6,7},{7,6},{8,9},{9,8},{10,11... | collective-permute-start | bytes 1597448 | tf_op jit(solution)/shard_map/ppermute | solution.py:76
  53.0 43.7 %collective-permute-start.5 = (bf16[1040,256]{1,0:T(8,128)(2,1)}, bf16[1040,256]{1,0:T(8,128)(2,1)}, u32[]{:S(2)}, u32[]{:S(2)}) collective-permute-start(bf16[1040,256]{1,0:T(8,128)(2,1)} %add.189.refs_4_), channel_id=1, source_target_pairs={{0,1},{1,0},{2,3},{3,2},{4,5},{5,4},{6,7},{7,6},{8,9},{9,8},{10,11... | collective-permute-start | bytes 1597448 | tf_op jit(solution)/shard_map/ppermute | solution.py:76
  86.2 19.6 %collective-permute-start.8 = (bf16[1040,256]{1,0:T(8,128)(2,1)}, bf16[1040,256]{1,0:T(8,128)(2,1)}, u32[]{:S(2)}, u32[]{:S(2)}) collective-permute-start(bf16[1040,256]{1,0:T(8,128)(2,1)} %add.190.refs_6_), channel_id=1, source_target_pairs={{0,1},{1,0},{2,3},{3,2},{4,5},{5,4},{6,7},{7,6},{8,9},{9,8},{10,11... | collective-permute-start | bytes 1597448 | tf_op jit(solution)/shard_map/ppermute | solution.py:76
  96.7 1.3 copy-start
  98.1 50.3 %all-to-all-start.1 = ((bf16[4,2,2,512,128]{4,3,2,1,0:T(8,128)(2,1)}), bf16[4,2,2,512,128]{4,3,2,1,0:T(8,128)(2,1)}, u32[]{:S(2)}, u32[]{:S(2)}) async-start(bf16[4,2,2,512,128]{4,3,2,1,0:T(8,128)(2,1)} %after.3), calls=%async_computation.1 | async-start | bytes 4194304 | tf_op jit(solution)/shard_map/all_to_all | solution.py:158
  110.9 20.8 %collective-permute-start.11 = (bf16[2,512,256]{2,1,0:T(8,128)(2,1)}, bf16[2,512,256]{2,1,0:T(8,128)(2,1)S(1)}, u32[]{:S(2)}, u32[]{:S(2)}) collective-permute-start(bf16[2,512,256]{2,1,0:T(8,128)(2,1)} %get-tuple-element.13.h_last), channel_id=1, source_target_pairs={{0,8},{8,16},{16,24},{1,9},{9,17},{17,25},{2,10},{10,18},{18,26},{... | collective-permute-start | bytes 1572872 | tf_op jit(solution)/shard_map/ppermute | solution.py:726
  112.2 19.5 %collective-permute-start.12 = (bf16[2,512,256]{2,1,0:T(8,128)(2,1)}, bf16[2,512,256]{2,1,0:T(8,128)(2,1)S(1)}, u32[]{:S(2)}, u32[]{:S(2)}) collective-permute-start(bf16[2,512,256]{2,1,0:T(8,128)(2,1)} %get-tuple-element.14.h_first), channel_id=1, source_target_pairs={{8,0},{16,8},{24,16},{9,1},{17,9},{25,17},{10,2},{18,10},{26,18},{... | collective-permute-start | bytes 1572872 | tf_op jit(solution)/shard_map/ppermute | solution.py:726
  131.7 0.8 copy-start.11
  131.7 1.0 copy-start.12
  148.4 16.2 %copy-start.2 = (s32[26]{0:T(128)S(1)}, s32[26]{0:T(128)}, u32[]{:S(2)}) copy-start(s32[26]{0:T(128)} %pad_add_fusion.1.plan) | copy-start | bytes 316
  148.4 16.2 %copy-start.3 = (s32[16]{0:T(128)S(1)}, s32[16]{0:T(128)}, u32[]{:S(2)}) copy-start(s32[16]{0:T(128)} %select_reduce_fusion.2.order) | copy-start | bytes 196
  154.1 10.4 %all-to-all-start.2 = ((f32[8,24,128]{2,1,0:T(8,128)}), f32[8,24,128]{2,1,0:T(8,128)S(1)}, u32[]{:S(2)}, u32[]{:S(2)}) async-start(f32[8,24,128]{2,1,0:T(8,128)} %project.1), calls=%async_computation.2 | async-start | bytes 196608 | tf_op jit(solution)/shard_map/all_to_all | solution.py:807
  164.6 1.6 copy-start.1
